TPU v7x, 256 devices: a whole 4x4x8 slice. The times are simulated.
256 devices in a mesh: rep: 4 (over x_lo, core), fsdp: 64 (over y, x_hi, z).
Axes of the slice: x: 4 (x_hi: 2, x_lo: 2; x = x_hi * 2 + x_lo), y: 4, z: 8, core: 2. Of those that a mesh axis runs over, the one named last changes fastest.
Arguments:
- tokens: bfloat16 [196608, 4096], P(('rep', 'fsdp')), may hold values from -24 to 24
- cotangent: bfloat16 [196608, 512], P(('rep', 'fsdp')), may hold values from -0.013671875 to 0.013671875
- policy: float32 [4096, 512], P('fsdp'), may hold values from -0.09375 to 0.09375
- anchor: float32 [4096, 512], P('fsdp'), may hold values from -0.09375 to 0.09375
- moment: float32 [4096, 512], P('fsdp'), may hold values from -3 to 3
- second: float32 [4096, 512], P('fsdp'), may hold values from 0.25 to 4
- readout: float32 [512], replicated, may hold values from -6 to 6
- pair_index: int32 [512, 2], P(('rep', 'fsdp')), may hold values from 0 to 1023, as said below
- noisy_flags: int32 [512], P(('rep', 'fsdp')), may hold values 0 or 1
Outputs:
- policy_next: float32 [4096, 512], P('fsdp')
- anchor_next: float32 [4096, 512], P('fsdp')
- moment_next: float32 [4096, 512], P('fsdp')
- second_next: float32 [4096, 512], P('fsdp')
- pair_loss: float32 [512], P(('rep', 'fsdp'))
Inputs may be any that keep to these rules, and one draw needn't show every extreme that they name: Each of the 1024 sequences appears exactly once in pair_index.
All inputs are finite; a program needn't handle non-finite values. No bound on the sum of `noisy_flags` on one device may be relied on, other than what follows from the above.
Results may differ from a plain program's by a relative error of at most 0.0025.
Values may be sent and summed in bfloat16 or wider, within the bound.
No kernel may reach another device: no remote copies, remote signals or barrier semaphores. Data moves between devices by JAX's collectives and lax.ppermute only.
A program may use at most 64 MiB of HBM per device.

v0:
```python
import jax
import jax.numpy as jnp
from jax import lax
from jax.sharding import PartitionSpec as P

LEN = 192


beta_one = 0.9
beta_two = 0.95
step_count = 20
learn_rate = 0.003
adam_epsilon = 1e-08
blend_rate = 0.6
smoothing = 0.1


def adam_update(gradient, policy, anchor, moment, second):
    moment_new = beta_one * moment + (1.0 - beta_one) * gradient
    second_new = beta_two * second + (1.0 - beta_two) * gradient * gradient
    correct_one = 1.0 - beta_one**step_count
    correct_two = 1.0 - beta_two**step_count
    policy_new = policy - learn_rate * (moment_new / correct_one) / (
        jnp.sqrt(second_new / correct_two) + adam_epsilon
    )
    anchor_new = blend_rate * policy_new + (1.0 - blend_rate) * anchor
    return (policy_new, anchor_new, moment_new, second_new)


def token_scores(values, readout):
    return jnp.sum(jax.nn.log_sigmoid(values * readout[None, :]), axis=1)


def sequence_margin(policy_values, anchor_values, readout, sequence_length):
    token_gap = token_scores(policy_values, readout) - token_scores(anchor_values, readout)
    return jnp.mean(token_gap.reshape(-1, sequence_length), axis=1)


def pair_losses(margins, pair_index, noisy_flags):
    sequence_index = jnp.arange(margins.shape[0], dtype=jnp.int32)
    chosen = jnp.sum(
        jnp.where(pair_index[:, 0:1] == sequence_index[None, :], margins[None, :], 0.0), axis=1
    )
    rejected = jnp.sum(
        jnp.where(pair_index[:, 1:2] == sequence_index[None, :], margins[None, :], 0.0), axis=1
    )
    margin_gap = chosen - rejected
    logit_value = jnp.where(noisy_flags == 1, -margin_gap, margin_gap)
    return -(1.0 - smoothing) * jax.nn.log_sigmoid(logit_value) - smoothing * jax.nn.log_sigmoid(
        -logit_value
    )


def shards(tokens, cotangent, policy, anchor, moment, second, readout, pair_index, noisy_flags):
    part_sum = lax.psum_scatter(
        lax.dot_general(
            tokens, cotangent, (((0,), (0,)), ((), ())), preferred_element_type=jnp.float32
        ),
        "fsdp",
        scatter_dimension=0,
        tiled=True,
    )
    gradient = lax.psum(part_sum.astype(jnp.bfloat16), "rep").astype(jnp.float32)
    policy_next, anchor_next, moment_next, second_next = adam_update(
        gradient, policy, anchor, moment, second
    )
    policy_half = policy_next.astype(jnp.bfloat16)
    anchor_half = anchor_next.astype(jnp.bfloat16)
    policy_whole = lax.all_gather(policy_half, "fsdp", axis=0, tiled=True)
    anchor_whole = lax.all_gather(anchor_half, "fsdp", axis=0, tiled=True)
    policy_values = jnp.dot(tokens, policy_whole, preferred_element_type=jnp.float32)
    anchor_values = jnp.dot(tokens, anchor_whole, preferred_element_type=jnp.float32)
    margins_own = sequence_margin(policy_values, anchor_values, readout, LEN)
    all_margins = lax.all_gather(margins_own, ("rep", "fsdp"), axis=0, tiled=True)
    pair_loss = pair_losses(all_margins, pair_index, noisy_flags)
    return (policy_next, anchor_next, moment_next, second_next, pair_loss)


def solution(mesh):
    placed = (
        P(("rep", "fsdp"), None),
        P(("rep", "fsdp"), None),
        P("fsdp", None),
        P("fsdp", None),
        P("fsdp", None),
        P("fsdp", None),
        P(),
        P(("rep", "fsdp"), None),
        P(("rep", "fsdp")),
    )
    return jax.shard_map(
        shards,
        mesh=mesh,
        in_specs=placed,
        out_specs=(
            P("fsdp", None),
            P("fsdp", None),
            P("fsdp", None),
            P("fsdp", None),
            P(("rep", "fsdp")),
        ),
        check_vma=False,
    )
```

profile of v0, /device:TPU:1, one launch (start us, length us, event | category | flops | bytes accessed | tf_op | source)
XLA Modules:
  0.0 789.9 jit_solution(9439700475384749153)
XLA Ops:
  7.2 0.0 copy-start
  7.2 0.0 reduce-scatter.2.cloned.1.call-start
  7.2 1.1 copy-done
  8.3 8.6 %fusion.20 = f32[4096,512]{1,0:T(8,128)} fusion(bf16[768,4096]{1,0:T(8,128)(2,1)} %param.9, bf16[768,512]{1,0:T(8,128)(2,1)S(1)} %copy-done), kind=kOutput, calls=%fused_computation.38 | convolution fusion | flops 3221225472 | bytes 15466496 | tf_op jit(solution)/shard_map/dot_general | solution.py:56
  16.9 0.0 copy-start.2
  16.9 0.0 copy-start.3
  16.9 0.0 copy-start.4
  16.9 0.0 copy-start.5
  16.9 0.0 reduce-scatter.2.cloned.1.call-update
  17.0 0.0 copy-start.6
  17.0 0.0 copy-start.8
  17.0 0.0 all-reduce.3.cloned.1.call-start
  17.0 336.6 %reduce-scatter.2.cloned.1.call-done = f32[64,512]{1,0:T(8,128)} async-done(((f32[4096,512]{1,0:T(8,128)}), f32[64,512]{1,0:T(8,128)}) %reduce-scatter.2.cloned.1.call-update) | async-done | bytes 131088 | tf_op jit(solution)/shard_map/reduce_scatter | solution.py:55
  353.6 1.5 convert_element_type.12
  355.2 0.0 all-reduce.3.cloned.1.call-update
  355.2 0.0 all-gather.5.cloned.1.call-start
  355.3 82.6 %all-reduce.3.cloned.1.call-done = bf16[64,512]{1,0:T(8,128)(2,1)} async-done(((bf16[64,512]{1,0:T(8,128)(2,1)}), bf16[64,512]{1,0:T(8,128)(2,1)}) %all-reduce.3.cloned.1.call-update) | async-done | bytes 65552 | tf_op jit(solution)/shard_map/psum | solution.py:63
  437.9 0.0 copy-done.2
  437.9 0.0 copy-done.3
  437.9 0.0 copy-done.4
  437.9 1.6 fusion.16
  439.5 0.0 copy-start.1
  439.5 0.0 copy-done.5
  439.5 0.7 fusion.19
  440.2 0.0 all-gather.5.cloned.1.call-update
  440.2 0.0 all-gather.3.cloned.1.call-start
  440.3 0.5 all-gather.3.cloned.1.call-update
  440.8 0.0 copy-done.6
  440.8 0.2 slice_reduce_fusion
  441.0 126.2 %all-gather.5.cloned.1.call-done = bf16[4096,512]{1,0:T(8,128)(2,1)} async-done(((bf16[64,512]{1,0:T(8,128)(2,1)}), bf16[4096,512]{1,0:T(8,128)(2,1)}) %all-gather.5.cloned.1.call-update) | async-done | bytes 4194320 | tf_op jit(solution)/shard_map/all_gather | solution.py:70
  567.2 0.0 copy-done.8
  567.2 8.4 %fusion.1 = f32[768]{0:T(1024)S(1)} fusion(bf16[4096,512]{1,0:T(8,128)(2,1)} %all-gather.5.cloned.1.call-done, bf16[768,4096]{1,0:T(8,128)(2,1)} %param.9, f32[512]{0:T(512)S(1)} %copy-done.8), kind=kOutput, calls=%fused_computation.3 | convolution fusion | flops 3224763648 | bytes 10490880 | tf_op jit(solution)/shard_map/dot_general | solution.py:72
  575.6 0.0 copy-done.1
  575.6 0.0 copy-start.7
  575.6 120.3 %all-gather.3.cloned.1.call-done = bf16[4096,512]{1,0:T(8,128)(2,1)} async-done(((bf16[64,512]{1,0:T(8,128)(2,1)}), bf16[4096,512]{1,0:T(8,128)(2,1)}) %all-gather.3.cloned.1.call-update) | async-done | bytes 4194320 | tf_op jit(solution)/shard_map/all_gather | solution.py:69
  695.9 8.4 %fusion = f32[768]{0:T(1024)S(1)} fusion(bf16[4096,512]{1,0:T(8,128)(2,1)} %all-gather.3.cloned.1.call-done, bf16[768,4096]{1,0:T(8,128)(2,1)} %param.9, f32[512]{0:T(512)S(1)} %copy-done.8), kind=kOutput, calls=%fused_computation.2 | convolution fusion | flops 3224763648 | bytes 10490880 | tf_op jit(solution)/shard_map/dot_general | solution.py:71
  704.3 0.1 sub.18
  704.4 0.1 reduce_sum.47
  704.5 0.1 multiply_dynamic-update-slice_fusion
  704.7 77.9 %all-reduce = f32[1024]{0:T(1024)S(1)} all-reduce(f32[1024]{0:T(1024)S(1)} %multiply_dynamic-update-slice_fusion), channel_id=1, replica_groups=mesh['rep'=4,'fsdp'=64] {'rep','fsdp'}, use_global_device_ids=true, to_apply=%add | all-reduce | flops 1024 | bytes 8192
  782.6 0.2 fusion.13
  782.8 0.0 copy-done.7
  782.8 0.5 multiply_subtract_fusion
  (2 shorter events, 0.0 us)
Async XLA Ops:
  7.2 1.1 copy-start
  7.2 346.5 %reduce-scatter.2.cloned.1.call-start = ((), (), s32[]{:S(2)}) async-start(), calls=%async_computation.1 | async-start | bytes 8519680 | tf_op jit(solution)/shard_map/reduce_scatter | solution.py:55
  16.9 421.0 %copy-start.2 = (f32[64,512]{1,0:T(8,128)S(1)}, f32[64,512]{1,0:T(8,128)}, u32[]{:S(2)}) copy-start(f32[64,512]{1,0:T(8,128)} %param.11) | copy-start | bytes 393220
  16.9 421.0 %copy-start.3 = (f32[64,512]{1,0:T(8,128)S(1)}, f32[64,512]{1,0:T(8,128)}, u32[]{:S(2)}) copy-start(f32[64,512]{1,0:T(8,128)} %param.13) | copy-start | bytes 393220
  16.9 421.0 %copy-start.4 = (f32[64,512]{1,0:T(8,128)S(1)}, f32[64,512]{1,0:T(8,128)}, u32[]{:S(2)}) copy-start(f32[64,512]{1,0:T(8,128)} %param.14) | copy-start | bytes 393220
  16.9 422.6 %copy-start.5 = (f32[64,512]{1,0:T(8,128)S(1)}, f32[64,512]{1,0:T(8,128)}, u32[]{:S(2)}) copy-start(f32[64,512]{1,0:T(8,128)} %param.12) | copy-start | bytes 393220
  17.0 423.9 %copy-start.6 = (s32[2,2]{1,0:T(2,128)S(1)}, s32[2,2]{1,0:T(2,128)}, u32[]{:S(2)}) copy-start(s32[2,2]{1,0:T(2,128)} %param.16) | copy-start | bytes 52
  17.0 550.3 %copy-start.8 = (f32[512]{0:T(512)S(1)}, f32[512]{0:T(512)}, u32[]{:S(2)}) copy-start(f32[512]{0:T(512)} %param.15) | copy-start | bytes 6148
  17.0 420.9 %all-reduce.3.cloned.1.call-start = ((), (), s32[]{:S(2)}) async-start(), calls=%async_computation.2 | async-start | bytes 131072 | tf_op jit(solution)/shard_map/psum | solution.py:63
  355.2 212.0 %all-gather.5.cloned.1.call-start = ((), (), s32[]{:S(2)}) async-start(), calls=%async_computation.4 | async-start | bytes 4259840 | tf_op jit(solution)/shard_map/all_gather | solution.py:70
  439.5 136.1 %copy-start.1 = (f32[64,512]{1,0:T(8,128)}, f32[64,512]{1,0:T(8,128)S(1)}, u32[]{:S(2)}) copy-start(f32[64,512]{1,0:T(8,128)S(1)} %get-tuple-element.10) | copy-start | bytes 393220
  440.2 255.7 %all-gather.3.cloned.1.call-start = ((), (), s32[]{:S(2)}) async-start(), calls=%async_computation.3 | async-start | bytes 4259840 | tf_op jit(solution)/shard_map/all_gather | solution.py:69
  575.6 207.2 %copy-start.7 = (s32[2]{0:T(128)S(1)}, s32[2]{0:T(128)}, u32[]{:S(2)}) copy-start(s32[2]{0:T(128)} %param.17) | copy-start | bytes 28
Sparse Core Ops, SparseCore 0:
  17.1 336.5 reduce-scatter.1
  356.8 81.0 all-reduce.2
  442.0 125.2 all-gather.4
  571.2 124.7 all-gather.2
where the time goes:
time: 790 us
  waiting for transfers between devices  666 us (84%)
  blocking collectives  77.9 us (10%)
  matrix products  25.4 us (3%)
  between operations  13.9 us (2%)
    reduce_scatter x1, waiting for transfers between devices, shards(): lax.psum_scatter(lax.dot_general(tokens, cotangent, (((0,), (0,)), ((), (...  337 us
    all_gather x1, waiting for transfers between devices, shards(): anchor_whole = lax.all_gather(anchor_half, 'fsdp', axis=0, tiled=True)  126 us
    all_gather x1, waiting for transfers between devices, shards(): policy_whole = lax.all_gather(policy_half, 'fsdp', axis=0, tiled=True)  120 us
    psum x1, waiting for transfers between devices, shards(): lax.psum(part_sum.astype(jnp.bfloat16), 'rep').astype(jnp.float32)  82.6 us
    unnamed x1, blocking collectives  77.9 us
  transfers between devices with their start and end apart: 4, of which 4 were waited for; matrix products, arithmetic and copies ran while one was open for 1% of the time, Pallas kernels for 0%

commit v1 on v0

v1 whole, which is shorter than its diff:
```python
import jax
import jax.numpy as jnp
from jax import lax
from jax.sharding import Mesh
from jax.sharding import PartitionSpec as P

LEN = 192


beta_one = 0.9
beta_two = 0.95
step_count = 20
learn_rate = 0.003
adam_epsilon = 1e-08
blend_rate = 0.6
smoothing = 0.1

AXES = ("xlo", "core", "y", "xhi", "z")
PLANE = ("xlo", "y", "xhi")
SWAP = ((0, 1), (1, 0))


def adam_update(gradient, policy, anchor, moment, second):
    moment_new = beta_one * moment + (1.0 - beta_one) * gradient
    second_new = beta_two * second + (1.0 - beta_two) * gradient * gradient
    correct_one = 1.0 - beta_one**step_count
    correct_two = 1.0 - beta_two**step_count
    policy_new = policy - learn_rate * (moment_new / correct_one) / (
        jnp.sqrt(second_new / correct_two) + adam_epsilon
    )
    anchor_new = blend_rate * policy_new + (1.0 - blend_rate) * anchor
    return (policy_new, anchor_new, moment_new, second_new)


def token_scores(values, readout):
    return jnp.sum(jax.nn.log_sigmoid(values * readout[None, :]), axis=1)


def pair_losses(margins, pair_index, noisy_flags):
    sequence_index = jnp.arange(margins.shape[0], dtype=jnp.int32)
    chosen = jnp.sum(
        jnp.where(pair_index[:, 0:1] == sequence_index[None, :], margins[None, :], 0.0), axis=1
    )
    rejected = jnp.sum(
        jnp.where(pair_index[:, 1:2] == sequence_index[None, :], margins[None, :], 0.0), axis=1
    )
    margin_gap = chosen - rejected
    logit_value = jnp.where(noisy_flags == 1, -margin_gap, margin_gap)
    return -(1.0 - smoothing) * jax.nn.log_sigmoid(logit_value) - smoothing * jax.nn.log_sigmoid(
        -logit_value
    )


def gradient_product(tokens, cotangent):
    return lax.dot_general(
        tokens, cotangent, (((0,), (0,)), ((), ())), preferred_element_type=jnp.float32
    )


def shards(tokens, cotangent, policy, anchor, moment, second, readout, pair_index, noisy_flags):
    core = lax.axis_index("core")
    low = lax.axis_index("xlo")
    half = cotangent.shape[1] // 2
    rows = policy.shape[0] // 2
    features = tokens.shape[1]

    def columns(array, which):
        return lax.dynamic_slice_in_dim(array, which * half, half, axis=array.ndim - 1)

    def piece(array):
        return lax.dynamic_slice(array, (low * rows, core * half), (rows, half))

    anchor_cols = lax.all_gather(
        columns(anchor, core).astype(jnp.bfloat16), ("y", "xhi", "z"), axis=0, tiled=True
    )
    sent = gradient_product(tokens, columns(cotangent, 1 - core)).astype(jnp.bfloat16)
    arrived = lax.ppermute(sent, "core", SWAP)
    chip_sum = gradient_product(tokens, columns(cotangent, core)) + arrived.astype(jnp.float32)
    tokens_sibling = lax.ppermute(tokens, "core", SWAP)
    blocks = chip_sum.astype(jnp.bfloat16).reshape(4, 2, 8, 2, rows, half)
    blocks = blocks.transpose(3, 0, 1, 2, 4, 5).reshape(16, 8 * rows, half)
    plane = lax.all_to_all(blocks, PLANE, 0, 0, tiled=True)
    plane_sum = jnp.sum(plane.astype(jnp.float32), axis=0).astype(jnp.bfloat16)
    column = lax.all_to_all(plane_sum.reshape(8, rows, half), "z", 0, 0, tiled=True)
    gradient_piece = jnp.sum(column.astype(jnp.float32), axis=0)

    policy_piece = adam_update(
        gradient_piece, piece(policy), piece(anchor), piece(moment), piece(second)
    )[0].astype(jnp.bfloat16)
    column = lax.all_to_all(
        jnp.broadcast_to(policy_piece[None], (8, rows, half)), "z", 0, 0, tiled=True
    ).reshape(8 * rows, half)
    plane = lax.all_to_all(
        jnp.broadcast_to(column[None], (16, 8 * rows, half)), PLANE, 0, 0, tiled=True
    )
    policy_cols = (
        plane.reshape(2, 4, 2, 8, rows, half).transpose(1, 2, 3, 0, 4, 5).reshape(features, half)
    )

    other = lax.ppermute(gradient_piece, "core", SWAP)
    strip = jnp.where(
        core == 0,
        jnp.concatenate([gradient_piece, other], axis=1),
        jnp.concatenate([other, gradient_piece], axis=1),
    )
    other = lax.ppermute(strip, "xlo", SWAP)
    gradient = jnp.where(
        low == 0,
        jnp.concatenate([strip, other], axis=0),
        jnp.concatenate([other, strip], axis=0),
    )
    policy_next, anchor_next, moment_next, second_next = adam_update(
        gradient, policy, anchor, moment, second
    )

    readout_cols = columns(readout, core)

    def partial_margins(own):
        policy_values = jnp.dot(own, policy_cols, preferred_element_type=jnp.float32)
        frozen = jnp.dot(own, anchor_cols, preferred_element_type=jnp.float32)
        anchor_values = blend_rate * policy_values + (1.0 - blend_rate) * frozen
        gap = token_scores(policy_values, readout_cols) - token_scores(anchor_values, readout_cols)
        return jnp.sum(gap.reshape(-1, LEN), axis=1) / LEN

    parts = jnp.concatenate([partial_margins(tokens), partial_margins(tokens_sibling)])
    parts = lax.all_to_all(jnp.broadcast_to(parts[None], (256, 8)), AXES, 0, 0, tiled=True)
    parts = parts.reshape(2, 2, 64, 8)
    margins = (parts[:, :, :, :4] + parts[:, ::-1, :, 4:]).reshape(-1)
    pair_loss = pair_losses(margins, pair_index, noisy_flags)
    return (policy_next, anchor_next, moment_next, second_next, pair_loss)


def solution(mesh):
    fine = Mesh(mesh.devices.reshape(2, 2, 4, 2, 8), AXES)
    everywhere = AXES
    owners = ("y", "xhi", "z")
    placed = (
        P(everywhere, None),
        P(everywhere, None),
        P(owners, None),
        P(owners, None),
        P(owners, None),
        P(owners, None),
        P(),
        P(everywhere, None),
        P(everywhere),
    )
    return jax.shard_map(
        shards,
        mesh=fine,
        in_specs=placed,
        out_specs=(
            P(owners, None),
            P(owners, None),
            P(owners, None),
            P(owners, None),
            P(everywhere),
        ),
        check_vma=False,
    )
```

time: 790 us -> 222 us (0.28)
  waiting for transfers between devices: 666 us -> 110 us
  blocking collectives: 77.9 us -> 10.3 us
  starting transfers between devices: 0.16 us -> 40.4 us
  local copies, waits for them, and re-layouts: 1.39 us -> 9.84 us
    reduce_scatter x1 -> x0, waiting for transfers between devices: 337 us -> none  [shards(): lax.psum_scatter(lax.dot_general(tokens, cotangent, (((0,), (0,)), ((), (...]
    all_gather x2 -> x1, waiting for transfers between devices: 247 us -> 34 us  [shards(): lax.all_gather(columns(anchor, core).astype(jnp.bfloat16), ('y', 'xhi', '...]
    psum x1 -> x0, waiting for transfers between devices: 82.6 us -> none  [shards(): lax.psum(part_sum.astype(jnp.bfloat16), 'rep').astype(jnp.float32)]
    unnamed x1 -> x0, blocking collectives: 77.9 us -> none
    all_to_all x0 -> x4, waiting for transfers between devices: none -> 69.9 us  [the longest x1 32.4 us: shards(): plane = lax.all_to_all(blocks, PLANE, 0, 0, tiled=True)]
    all_to_all x0 -> x4, starting transfers between devices: none -> 30.7 us  [the longest x1 11.9 us: shards(): lax.all_to_all(jnp.broadcast_to(parts[None], (256, 8)), AXES, 0, 0, tiled...]
    all_to_all x0 -> x1, blocking collectives: none -> 10.3 us  [shards(): lax.all_to_all(jnp.broadcast_to(policy_piece[None], (8, rows, half)), 'z'...]
    ppermute x0 -> x4, starting transfers between devices: none -> 9.65 us  [the longest x1 4.43 us: shards(): other = lax.ppermute(gradient_piece, 'core', SWAP)]
  transfers between devices with their start and end apart: 4 -> 9, of which waited for: 4 -> 7; matrix products, arithmetic and copies ran while one was open for 1% -> 18% of each run, Pallas kernels for 0% -> 0%
where the time goes in v1:
time: 222 us
  waiting for transfers between devices  110 us (50%)
  starting transfers between devices  40.4 us (18%)
  matrix products  32.7 us (15%)
  between operations  14.3 us (6%)
  blocking collectives  10.3 us (5%)
  local copies, waits for them, and re-layouts  9.84 us (4%)
  other arithmetic  3.93 us (2%)
    all_gather x1, waiting for transfers between devices, shards(): lax.all_gather(columns(anchor, core).astype(jnp.bfloat16), ('y', 'xhi', '...  34 us
    all_to_all x1, waiting for transfers between devices, shards(): plane = lax.all_to_all(blocks, PLANE, 0, 0, tiled=True)  32.4 us
    all_to_all x1, waiting for transfers between devices, shards(): lax.all_to_all(jnp.broadcast_to(column[None], (16, 8 * rows, half)), PLAN...  18.4 us
    all_to_all x1, starting transfers between devices, shards(): lax.all_to_all(jnp.broadcast_to(parts[None], (256, 8)), AXES, 0, 0, tiled...  11.9 us
    dot_general x2, matrix products, gradient_product(): lax.dot_general(tokens, cotangent, (((0,), (0,)), ((), ())), preferred_el...  11.3 us
    all_to_all x1, waiting for transfers between devices, shards(): lax.all_to_all(jnp.broadcast_to(parts[None], (256, 8)), AXES, 0, 0, tiled...  11.2 us
    dot_general x2, matrix products, partial_margins(): frozen = jnp.dot(own, anchor_cols, preferred_element_type=jnp.float32)  11.1 us
    dot_general x2, matrix products, partial_margins(): jnp.dot(own, policy_cols, preferred_element_type=jnp.float32)  10.4 us
  transfers between devices with their start and end apart: 9, of which 7 were waited for; matrix products, arithmetic and copies ran while one was open for 18% of the time, Pallas kernels for 0%

profile of v1, /device:TPU:1, one launch (start us, length us, event | category | flops | bytes accessed | tf_op | source)
XLA Modules:
  0.0 221.8 jit_solution(5032317919100632168)
XLA Ops:
  7.2 0.0 copy-start
  7.2 1.1 copy-done
  8.3 4.6 %fusion = bf16[4096,256]{0,1:T(8,128)(2,1)S(1)} fusion(bf16[768,4096]{1,0:T(8,128)(2,1)} %param.9, bf16[768,512]{1,0:T(8,128)(2,1)S(1)} %copy-done, s32[]{:T(128)S(6)} %select_n.68), kind=kOutput, calls=%fused_computation.2 | convolution fusion | flops 1611661312 | bytes 8781828 | tf_op jit(solution)/shard_map/dot_general | solution.py:55
  12.9 3.3 %collective-permute-start = (bf16[4096,256]{0,1:T(8,128)(2,1)S(1)}, bf16[4096,256]{0,1:T(8,128)(2,1)}, u32[]{:S(2)}, u32[]{:S(2)}) collective-permute-start(bf16[4096,256]{0,1:T(8,128)(2,1)S(1)} %fusion), channel_id=1, source_target_pairs={{0,64},{64,0},{1,65},{65,1},{2,66},{66,2},{3,67},{67,3},{4,68},{68... | collective-permute-start | bytes 6291464 | tf_op jit(solution)/shard_map/ppermute | solution.py:77
  16.3 0.1 collective-permute-start.3
  16.4 5.8 %collective-permute-done = bf16[4096,256]{0,1:T(8,128)(2,1)} collective-permute-done((bf16[4096,256]{0,1:T(8,128)(2,1)S(1)}, bf16[4096,256]{0,1:T(8,128)(2,1)}, u32[]{:S(2)}, u32[]{:S(2)}) %collective-permute-start) | collective-permute-done | bytes 2097184 | tf_op jit(solution)/shard_map/ppermute | solution.py:77
  22.2 6.7 %add_convert_fusion = bf16[4096,256]{0,1:T(8,128)(2,1)} fusion(bf16[4096,256]{0,1:T(8,128)(2,1)} %collective-permute-done, bf16[768,4096]{1,0:T(8,128)(2,1)} %param.9, bf16[768,512]{1,0:T(8,128)(2,1)S(1)} %copy-done, s32[]{:T(128)S(6)} %select_n.67), kind=kOutput, calls=%fused_computation.3 | convolution fusion | flops 1613758464 | bytes 10878980 | tf_op jit(solution)/shard_map/dot_general | solution.py:55
  28.8 3.3 %copy.22 = bf16[4096,256]{1,0:T(8,128)(2,1)S(1)} copy(bf16[4096,256]{0,1:T(8,128)(2,1)} %add_convert_fusion) | data formatting | bytes 4194304 | tf_op jit(solution)/shard_map/convert_element_type | solution.py:80
  32.1 1.6 copy.23
  33.7 5.2 %all-to-all-start = ((bf16[16,256,256]{2,1,0:T(8,128)(2,1)}), bf16[16,256,256]{2,1,0:T(8,128)(2,1)S(1)}, u32[]{:S(2)}, u32[]{:S(2)}) async-start(bf16[16,256,256]{2,1,0:T(8,128)(2,1)} %bitcast.82), calls=%async_computation | async-start | bytes 4194304 | tf_op jit(solution)/shard_map/all_to_all | solution.py:82
  38.9 0.0 copy-start.2
  38.9 0.0 copy-start.3
  38.9 0.0 copy-start.4
  38.9 0.0 all-gather.2.cloned.1.call-start
  39.0 0.6 dynamic-slice_convert_fusion
  39.6 0.0 all-gather.2.cloned.1.call-update
  39.7 32.4 %all-to-all-done = bf16[16,256,256]{2,1,0:T(8,128)(2,1)S(1)} async-done(((bf16[16,256,256]{2,1,0:T(8,128)(2,1)}), bf16[16,256,256]{2,1,0:T(8,128)(2,1)S(1)}, u32[]{:S(2)}, u32[]{:S(2)}) %all-to-all-start) | async-done | bytes 2097184 | tf_op jit(solution)/shard_map/all_to_all | solution.py:82
  72.1 1.0 reduce_sum.93
  73.0 8.2 %all-to-all-start.1 = ((bf16[8,32,256]{2,1,0:T(8,128)(2,1)}), bf16[8,32,256]{2,1,0:T(8,128)(2,1)S(1)}, u32[]{:S(2)}, u32[]{:S(2)}) async-start(bf16[8,32,256]{2,1,0:T(8,128)(2,1)} %bitcast.5), calls=%async_computation.1 | async-start | bytes 262144 | tf_op jit(solution)/shard_map/all_to_all | solution.py:84
  81.2 8.0 %all-to-all-done.1 = bf16[8,32,256]{2,1,0:T(8,128)(2,1)S(1)} async-done(((bf16[8,32,256]{2,1,0:T(8,128)(2,1)}), bf16[8,32,256]{2,1,0:T(8,128)(2,1)S(1)}, u32[]{:S(2)}, u32[]{:S(2)}) %all-to-all-start.1) | async-done | bytes 131104 | tf_op jit(solution)/shard_map/all_to_all | solution.py:84
  89.3 10.3 %all_to_all.26 = bf16[8,32,256]{2,1,0:T(8,128)(2,1)S(1)} all-to-all(bf16[8,32,256]{2,1,0:T(8,128)(2,1)S(1)} %broadcast_in_dim.43), channel_id=1, replica_groups=mesh['xlo'=2,'core'=2,'y'=4,'xhi'=2,'z'=8] {'z'}, dimensions={0} | all-to-all | bytes 262144 | tf_op jit(solution)/shard_map/all_to_all | solution.py:90
  99.6 1.6 broadcast_in_dim.45
  101.2 5.4 %all-to-all-start.3 = ((bf16[16,256,256]{2,1,0:T(8,128)(2,1)}), bf16[16,256,256]{2,1,0:T(8,128)(2,1)S(1)}, u32[]{:S(2)}, u32[]{:S(2)}) async-start(bf16[16,256,256]{2,1,0:T(8,128)(2,1)} %broadcast_in_dim.45), calls=%async_computation.3 | async-start | bytes 4194304 | tf_op jit(solution)/shard_map/all_to_all | solution.py:93
  106.6 4.4 %collective-permute-start.1 = (f32[32,256]{1,0:T(8,128)S(1)}, f32[32,256]{1,0:T(8,128)S(1)}, u32[]{:S(2)}, u32[]{:S(2)}) collective-permute-start(f32[32,256]{1,0:T(8,128)S(1)} %convert_reduce_fusion), channel_id=1, source_target_pairs={{0,64},{64,0},{1,65},{65,1},{2,66},{66,2},{3,67},{67,3},{4,68},{68... | collective-permute-start | bytes 98312 | tf_op jit(solution)/shard_map/ppermute | solution.py:100
  111.0 0.2 slice_reduce_fusion
  111.2 0.1 dynamic_slice.26
  111.3 0.6 collective-permute-done.1
  111.9 1.8 collective-permute-start.2
  113.7 18.4 %all-to-all-done.3 = bf16[16,256,256]{2,1,0:T(8,128)(2,1)S(1)} async-done(((bf16[16,256,256]{2,1,0:T(8,128)(2,1)}), bf16[16,256,256]{2,1,0:T(8,128)(2,1)S(1)}, u32[]{:S(2)}, u32[]{:S(2)}) %all-to-all-start.3) | async-done | bytes 2097184 | tf_op jit(solution)/shard_map/all_to_all | solution.py:93
  132.0 0.2 copy.24
  132.3 4.8 %fusion.40 = f32[256,768]{1,0:T(8,128)S(1)} fusion(bf16[4096,256]{1,0:T(8,128)(2,1)S(1)} %bitcast.84, bf16[768,4096]{1,0:T(8,128)(2,1)} %collective-permute-done.3), kind=kOutput, calls=%fused_computation.75 | convolution fusion | flops 1610612736 | bytes 9175040 | tf_op jit(solution)/shard_map/dot_general | solution.py:119
  137.0 5.6 %fusion.5 = (f32[768]{0:T(1024)S(1)}, f32[768]{0:T(1024)S(1)}, f32[256,768]{1,0:T(8,128)S(1)}) fusion(f32[256]{0:T(256)S(1)} %dynamic_slice.26, f32[256,768]{1,0:T(8,128)S(1)} %fusion.40, bf16[4096,256]{1,0:T(8,128)(2,1)S(1)} %bitcast.85, bf16[768,4096]{1,0:T(8,128)(2,1)} %param.9), kind=kOutput, calls=%fused_computation.14 | convolution fusion | flops 1614150144 | bytes 9968640 | tf_op jit(solution)/shard_map/dot_general | solution.py:119
  142.7 34.0 %all-gather.2.cloned.1.call-done = bf16[4096,256]{1,0:T(8,128)(2,1)} async-done(((bf16[64,256]{1,0:T(8,128)(2,1)}), bf16[4096,256]{1,0:T(8,128)(2,1)}) %all-gather.2.cloned.1.call-update) | async-done | bytes 2097168 | tf_op jit(solution)/shard_map/all_gather | solution.py:73
  176.7 5.9 %fusion.8 = f32[768]{0:T(1024)S(1)} fusion(f32[256,768]{1,0:T(8,128)S(1)} %fusion.40, bf16[4096,256]{1,0:T(8,128)(2,1)} %all-gather.2.cloned.1.call-done, bf16[768,4096]{1,0:T(8,128)(2,1)} %collective-permute-done.3, f32[256]{0:T(256)S(1)} %dynamic_slice.26), kind=kOutput, calls=%fused_computation.17 | convolution fusion | flops 1612971264 | bytes 9179136 | tf_op jit(solution)/shard_map/dot_general | solution.py:120
  182.6 5.2 %fusion.6 = f32[768]{0:T(1024)S(1)} fusion(bf16[4096,256]{1,0:T(8,128)(2,1)S(1)} %copy-done.8, bf16[768,4096]{1,0:T(8,128)(2,1)} %param.9, f32[256,768]{1,0:T(8,128)S(1)} %get-tuple-element.15, f32[256]{0:T(256)S(1)} %dynamic_slice.26), kind=kOutput, calls=%fused_computation.15 | convolution fusion | flops 1612971264 | bytes 9179136 | tf_op jit(solution)/shard_map/dot_general | solution.py:120
  187.8 0.1 sub.35
  187.9 0.1 reduce_sum.100
  188.0 0.1 sub.33
  188.1 0.1 reduce_sum.97
  188.2 0.1 pad_maximum_fusion
  188.3 0.7 broadcast_in_dim.46
  189.0 11.9 %all-to-all-start.4 = ((f32[256,1,8]{2,1,0:T(1,128)}), f32[256,1,8]{2,1,0:T(1,128)S(1)}, u32[]{:S(2)}, u32[]{:S(2)}) async-start(f32[256,1,8]{2,1,0:T(1,128)} %broadcast_in_dim.46), calls=%async_computation.4 | async-start | bytes 262144 | tf_op jit(solution)/shard_map/all_to_all | solution.py:126
  201.0 1.8 multiply_add_fusion
  202.7 11.2 %all-to-all-done.4 = f32[256,1,8]{2,1,0:T(1,128)S(1)} async-done(((f32[256,1,8]{2,1,0:T(1,128)}), f32[256,1,8]{2,1,0:T(1,128)S(1)}, u32[]{:S(2)}, u32[]{:S(2)}) %all-to-all-start.4) | async-done | bytes 8224 | tf_op jit(solution)/shard_map/all_to_all | solution.py:126
  213.9 0.1 slice.17
  214.1 0.1 broadcast_in_dim.47
  214.2 0.2 fusion.34
  214.4 0.5 multiply_subtract_fusion
  (23 shorter events, 0.2 us)
Async XLA Ops:
  7.2 1.1 copy-start
  12.9 9.2 %collective-permute-start = (bf16[4096,256]{0,1:T(8,128)(2,1)S(1)}, bf16[4096,256]{0,1:T(8,128)(2,1)}, u32[]{:S(2)}, u32[]{:S(2)}) collective-permute-start(bf16[4096,256]{0,1:T(8,128)(2,1)S(1)} %fusion), channel_id=1, source_target_pairs={{0,64},{64,0},{1,65},{65,1},{2,66},{66,2},{3,67},{67,3},{4,68},{68... | collective-permute-start | bytes 6291464 | tf_op jit(solution)/shard_map/ppermute | solution.py:77
  16.3 116.0 %collective-permute-start.3 = (bf16[768,4096]{1,0:T(8,128)(2,1)}, bf16[768,4096]{1,0:T(8,128)(2,1)}, u32[]{:S(2)}, u32[]{:S(2)}) collective-permute-start(bf16[768,4096]{1,0:T(8,128)(2,1)} %param.9), channel_id=1, source_target_pairs={{0,64},{64,0},{1,65},{65,1},{2,66},{66,2},{3,67},{67,3},{4,68},{68... | collective-permute-start | bytes 18874376 | tf_op jit(solution)/shard_map/ppermute | solution.py:79
  33.7 5.2 %copy-start.1 = (f32[64,512]{1,0:T(8,128)S(1)}, f32[64,512]{1,0:T(8,128)}, u32[]{:S(2)}) copy-start(f32[64,512]{1,0:T(8,128)} %param.12) | copy-start | bytes 393220
  33.7 38.3 %all-to-all-start = ((bf16[16,256,256]{2,1,0:T(8,128)(2,1)}), bf16[16,256,256]{2,1,0:T(8,128)(2,1)S(1)}, u32[]{:S(2)}, u32[]{:S(2)}) async-start(bf16[16,256,256]{2,1,0:T(8,128)(2,1)} %bitcast.82), calls=%async_computation | async-start | bytes 4194304 | tf_op jit(solution)/shard_map/all_to_all | solution.py:82
  38.9 50.3 %copy-start.2 = (f32[64,512]{1,0:T(8,128)S(1)}, f32[64,512]{1,0:T(8,128)}, u32[]{:S(2)}) copy-start(f32[64,512]{1,0:T(8,128)} %param.11) | copy-start | bytes 393220
  38.9 50.3 %copy-start.3 = (f32[64,512]{1,0:T(8,128)S(1)}, f32[64,512]{1,0:T(8,128)}, u32[]{:S(2)}) copy-start(f32[64,512]{1,0:T(8,128)} %param.13) | copy-start | bytes 393220
  38.9 50.3 %copy-start.4 = (f32[64,512]{1,0:T(8,128)S(1)}, f32[64,512]{1,0:T(8,128)}, u32[]{:S(2)}) copy-start(f32[64,512]{1,0:T(8,128)} %param.14) | copy-start | bytes 393220
  38.9 137.7 %all-gather.2.cloned.1.call-start = ((), (), s32[]{:S(2)}) async-start(), calls=%async_computation.5 | async-start | bytes 2129920 | tf_op jit(solution)/shard_map/all_gather | solution.py:73
  73.0 16.1 %all-to-all-start.1 = ((bf16[8,32,256]{2,1,0:T(8,128)(2,1)}), bf16[8,32,256]{2,1,0:T(8,128)(2,1)S(1)}, u32[]{:S(2)}, u32[]{:S(2)}) async-start(bf16[8,32,256]{2,1,0:T(8,128)(2,1)} %bitcast.5), calls=%async_computation.1 | async-start | bytes 262144 | tf_op jit(solution)/shard_map/all_to_all | solution.py:84
  101.2 9.8 %copy-start.5 = (s32[2,2]{1,0:T(2,128)S(1)}, s32[2,2]{1,0:T(2,128)}, u32[]{:S(2)}) copy-start(s32[2,2]{1,0:T(2,128)} %param.16) | copy-start | bytes 52
  101.2 10.0 %copy-start.6 = (f32[512]{0:T(512)S(1)}, f32[512]{0:T(512)}, u32[]{:S(2)}) copy-start(f32[512]{0:T(512)} %param.15) | copy-start | bytes 6148
  101.2 30.8 %all-to-all-start.3 = ((bf16[16,256,256]{2,1,0:T(8,128)(2,1)}), bf16[16,256,256]{2,1,0:T(8,128)(2,1)S(1)}, u32[]{:S(2)}, u32[]{:S(2)}) async-start(bf16[16,256,256]{2,1,0:T(8,128)(2,1)} %broadcast_in_dim.45), calls=%async_computation.3 | async-start | bytes 4194304 | tf_op jit(solution)/shard_map/all_to_all | solution.py:93
  106.6 5.3 %collective-permute-start.1 = (f32[32,256]{1,0:T(8,128)S(1)}, f32[32,256]{1,0:T(8,128)S(1)}, u32[]{:S(2)}, u32[]{:S(2)}) collective-permute-start(f32[32,256]{1,0:T(8,128)S(1)} %convert_reduce_fusion), channel_id=1, source_target_pairs={{0,64},{64,0},{1,65},{65,1},{2,66},{66,2},{3,67},{67,3},{4,68},{68... | collective-permute-start | bytes 98312 | tf_op jit(solution)/shard_map/ppermute | solution.py:100
  111.9 89.1 %collective-permute-start.2 = (f32[32,512]{1,0:T(8,128)S(1)}, f32[32,512]{1,0:T(8,128)}, u32[]{:S(2)}, u32[]{:S(2)}) collective-permute-start(f32[32,512]{1,0:T(8,128)S(1)} %maximum_select_fusion.1), channel_id=1, source_target_pairs={{0,128},{128,0},{1,129},{129,1},{2,130},{130,2},{3,131},{131,3},{4... | collective-permute-start | bytes 196616 | tf_op jit(solution)/shard_map/ppermute | solution.py:106
  176.7 5.9 %copy-start.8 = (bf16[4096,256]{1,0:T(8,128)(2,1)S(1)}, bf16[4096,256]{1,0:T(8,128)(2,1)}, u32[]{:S(2)}) copy-start(bf16[4096,256]{1,0:T(8,128)(2,1)} %all-gather.2.cloned.1.call-done) | copy-start | bytes 6291460
  187.8 26.6 %copy-start.7 = (s32[2]{0:T(128)S(1)}, s32[2]{0:T(128)}, u32[]{:S(2)}) copy-start(s32[2]{0:T(128)} %param.17) | copy-start | bytes 28
  189.0 24.9 %all-to-all-start.4 = ((f32[256,1,8]{2,1,0:T(1,128)}), f32[256,1,8]{2,1,0:T(1,128)S(1)}, u32[]{:S(2)}, u32[]{:S(2)}) async-start(f32[256,1,8]{2,1,0:T(1,128)} %broadcast_in_dim.46), calls=%async_computation.4 | async-start | bytes 262144 | tf_op jit(solution)/shard_map/all_to_all | solution.py:126
Sparse Core Ops, SparseCore 0:
  43.9 132.6 all-gather.1

commit v2 on v1

v2 whole, which is shorter than its diff:
```python
import jax
import jax.numpy as jnp
from jax import lax
from jax.experimental import pallas as pl
from jax.experimental.pallas import tpu as pltpu
from jax.sharding import Mesh
from jax.sharding import PartitionSpec as P

LEN = 192


beta_one = 0.9
beta_two = 0.95
step_count = 20
learn_rate = 0.003
adam_epsilon = 1e-08
blend_rate = 0.6
smoothing = 0.1

AXES = ("xlo", "core", "y", "xhi", "z")
PLANE = ("xlo", "y", "xhi")
SWAP = ((0, 1), (1, 0))


def adam_update(gradient, policy, anchor, moment, second):
    moment_new = beta_one * moment + (1.0 - beta_one) * gradient
    second_new = beta_two * second + (1.0 - beta_two) * gradient * gradient
    correct_one = 1.0 - beta_one**step_count
    correct_two = 1.0 - beta_two**step_count
    policy_new = policy - learn_rate * (moment_new / correct_one) / (
        jnp.sqrt(second_new / correct_two) + adam_epsilon
    )
    anchor_new = blend_rate * policy_new + (1.0 - blend_rate) * anchor
    return (policy_new, anchor_new, moment_new, second_new)


def pair_losses(margins, pair_index, noisy_flags):
    sequence_index = jnp.arange(margins.shape[0], dtype=jnp.int32)
    chosen = jnp.sum(
        jnp.where(pair_index[:, 0:1] == sequence_index[None, :], margins[None, :], 0.0), axis=1
    )
    rejected = jnp.sum(
        jnp.where(pair_index[:, 1:2] == sequence_index[None, :], margins[None, :], 0.0), axis=1
    )
    margin_gap = chosen - rejected
    logit_value = jnp.where(noisy_flags == 1, -margin_gap, margin_gap)
    return -(1.0 - smoothing) * jax.nn.log_sigmoid(logit_value) - smoothing * jax.nn.log_sigmoid(
        -logit_value
    )


VMEM = 56 << 20


def gradient_kernel(core, cotangent, tokens, out, turned):
    @pl.when(pl.program_id(0) == 0)
    def _():
        turned[...] = cotangent[...].T

    product = jnp.dot(turned[...], tokens[...], preferred_element_type=jnp.float32)
    quarter = product.shape[0] // 2
    out[0, 0] = product[:quarter].astype(out.dtype)
    out[1, 0] = product[quarter:].astype(out.dtype)


def gradient_blocks(which, cotangent, tokens, dtype):
    count, features = tokens.shape
    half = cotangent.shape[1] // 2
    width = features // 8
    return pl.pallas_call(
        gradient_kernel,
        grid_spec=pltpu.PrefetchScalarGridSpec(
            num_scalar_prefetch=1,
            grid=(8,),
            in_specs=[
                pl.BlockSpec((count, half), lambda i, core: (0, core[0])),
                pl.BlockSpec((count, width), lambda i, core: (0, i)),
            ],
            out_specs=pl.BlockSpec((2, 1, half // 2, width), lambda i, core: (0, i, 0, 0)),
            scratch_shapes=[pltpu.VMEM((half, count), jnp.bfloat16)],
        ),
        out_shape=jax.ShapeDtypeStruct((2, 8, half // 2, width), dtype),
        cost_estimate=pl.CostEstimate(
            flops=2 * count * features * half, bytes_accessed=10 << 20, transcendentals=0
        ),
        compiler_params=pltpu.CompilerParams(vmem_limit_bytes=VMEM),
        name="gradient_blocks",
    )(which, cotangent, tokens)


def select_rows(tokens, sibling):
    return jnp.where(pl.program_id(0) < 2, tokens[...], sibling[...])


def weigh(tokens, sibling, halves, joined):
    quarter = halves.shape[-1]

    @pl.when(pl.program_id(0) == 0)
    def _():
        joined[:, :quarter] = halves[0]
        joined[:, quarter:] = halves[1]

    return jnp.dot(
        select_rows(tokens, sibling), joined[...], preferred_element_type=jnp.float32
    )


def frozen_kernel(place, tokens, sibling, here, left, right, far_left, far_right, out, joined):
    strips, rows, quarter = here.shape

    @pl.when(pl.program_id(0) == 0)
    def _():
        for shift, ref, first in (
            (0, here, 0), (3, left, 0), (1, right, 0), (2, far_left, 0), (2, far_right, strips // 2)
        ):
            chip = (place[0] + shift) % 4
            lanes = pl.ds(pl.multiple_of((chip % 2) * quarter, quarter), quarter)
            for at in range(ref.shape[0]):
                joined[(first + at) * 2 + chip // 2, :, lanes] = ref[at]

    weights = joined[...].reshape(joined.shape[0] * rows, 2 * quarter)
    out[...] = jnp.dot(select_rows(tokens, sibling), weights, preferred_element_type=jnp.float32)


def log_sigmoid(values):
    return jnp.minimum(values, 0.0) - jnp.log(1.0 + jnp.exp(-jnp.abs(values)))


def score_kernel(tokens, sibling, halves, frozen, readout, out, joined):
    policy_values = weigh(tokens, sibling, halves, joined)
    anchor_values = blend_rate * policy_values + (1.0 - blend_rate) * frozen[...]
    weights = readout[...]
    gap = log_sigmoid(policy_values * weights) - log_sigmoid(anchor_values * weights)
    for at in range(out.shape[1]):
        out[0, at] = jnp.sum(gap[at * LEN : (at + 1) * LEN], axis=0)


def token_specs(count, features):
    rows = count // 2
    return [
        pl.BlockSpec((rows, features), lambda i, *_: (jnp.minimum(i, 1), 0)),
        pl.BlockSpec((rows, features), lambda i, *_: (jnp.maximum(i - 2, 0), 0)),
    ]


def frozen_values(place, tokens, sibling, strips):
    count, features = tokens.shape
    width = 2 * strips[0].shape[-1]
    return pl.pallas_call(
        frozen_kernel,
        grid_spec=pltpu.PrefetchScalarGridSpec(
            num_scalar_prefetch=1,
            grid=(4,),
            in_specs=token_specs(count, features)
            + [pl.BlockSpec(strip.shape, lambda i, *_: (0, 0, 0)) for strip in strips],
            out_specs=pl.BlockSpec((count // 2, width), lambda i, *_: (i, 0)),
            scratch_shapes=[pltpu.VMEM((8, features // 8, width), jnp.bfloat16)],
        ),
        out_shape=jax.ShapeDtypeStruct((2 * count, width), jnp.float32),
        cost_estimate=pl.CostEstimate(
            flops=4 * count * features * width, bytes_accessed=16 << 20, transcendentals=0
        ),
        compiler_params=pltpu.CompilerParams(vmem_limit_bytes=VMEM),
        name="frozen_values",
    )(place, tokens, sibling, *strips)


def score_sums(tokens, sibling, halves, frozen, readout):
    count, features = tokens.shape
    width = 2 * halves.shape[-1]
    each = count // 2 // LEN
    return pl.pallas_call(
        score_kernel,
        grid=(4,),
        in_specs=token_specs(count, features)
        + [
            pl.BlockSpec(halves.shape, lambda i: (0, 0, 0)),
            pl.BlockSpec((count // 2, width), lambda i: (i, 0)),
            pl.BlockSpec((1, width), lambda i: (0, 0)),
        ],
        out_specs=pl.BlockSpec((1, each, width), lambda i: (i, 0, 0)),
        out_shape=jax.ShapeDtypeStruct((4, each, width), jnp.float32),
        scratch_shapes=[pltpu.VMEM((features, width), jnp.bfloat16)],
        cost_estimate=pl.CostEstimate(
            flops=4 * count * features * width, bytes_accessed=16 << 20, transcendentals=0
        ),
        compiler_params=pltpu.CompilerParams(vmem_limit_bytes=VMEM),
        name="score_sums",
    )(tokens, sibling, halves, frozen, readout)


def plane_sum_kernel(blocks, out):
    total = blocks[0].astype(jnp.float32)
    for at in range(1, blocks.shape[0]):
        total = total + blocks[at].astype(jnp.float32)
    out[...] = total.T.astype(out.dtype)


def plane_sum(blocks):
    _, channels, features = blocks.shape
    return pl.pallas_call(
        plane_sum_kernel,
        out_shape=jax.ShapeDtypeStruct((features, channels), jnp.bfloat16),
        compiler_params=pltpu.CompilerParams(vmem_limit_bytes=16 << 20),
        name="plane_sum",
    )(blocks)


def to_plane(blocks):
    return lax.all_to_all(blocks, PLANE, 0, 0, tiled=True)


def turn(block, shift):
    def index(x):
        return (x % 2) * 2 + x // 2

    return lax.ppermute(
        block, ("xlo", "xhi"), [(index(x), index((x + shift) % 4)) for x in range(4)]
    )


def along_z(blocks):
    return lax.all_to_all(blocks, "z", 0, 0, tiled=True)


def shards(tokens, cotangent, policy, anchor, moment, second, readout, pair_index, noisy_flags):
    core = lax.axis_index("core")
    low = lax.axis_index("xlo")
    high = lax.axis_index("xhi")
    rows, channels = policy.shape
    half, quarter = channels // 2, channels // 4
    features = tokens.shape[1]

    def piece(array):
        return lax.dynamic_slice_in_dim(array, (core * 2 + low) * quarter, quarter, axis=1)

    def spread_z(block):
        return along_z(jnp.broadcast_to(block[None], (8, rows, quarter))).reshape(8 * rows, quarter)

    def copies(column):
        return jnp.broadcast_to(column[None], (16,) + column.shape)

    def joined_halves(plane):
        return plane.reshape(2, features, quarter)

    strips = lax.all_to_all(
        jnp.broadcast_to(piece(anchor).astype(jnp.bfloat16)[None], (32, rows, quarter)),
        ("y", "z"),
        0,
        0,
        tiled=True,
    ).reshape(4, 8 * rows, quarter)

    sent = gradient_blocks((1 - core)[None], cotangent, tokens, jnp.bfloat16)
    arrived = lax.ppermute(sent, "core", SWAP)
    own = gradient_blocks(core[None], cotangent, tokens, jnp.float32)
    blocks = (own + arrived.astype(jnp.float32)).astype(jnp.bfloat16)
    tokens_out, blocks = lax.optimization_barrier((tokens, blocks))
    sibling = lax.ppermute(tokens_out, "core", SWAP)
    plane = to_plane(blocks.reshape(16, quarter, 8 * rows))
    plane, strips = lax.optimization_barrier((plane, strips))
    left, right = turn(strips, 1), turn(strips, -1)
    column = along_z(plane_sum(plane).reshape(8, rows, quarter))
    gradient_piece = jnp.sum(column.astype(jnp.float32), axis=0)

    gradient_piece, left, right = lax.optimization_barrier((gradient_piece, left, right))
    far_left, far_right = turn(left[:2], 1), turn(right[2:], -1)
    policy_piece = adam_update(
        gradient_piece, piece(policy), piece(anchor), piece(moment), piece(second)
    )[0].astype(jnp.bfloat16)
    policy_copies, far_left, far_right = lax.optimization_barrier(
        (copies(spread_z(policy_piece)), far_left, far_right)
    )
    policy_plane = to_plane(policy_copies)
    frozen = frozen_values(
        (high * 2 + low)[None], tokens, sibling, (strips, left, right, far_left, far_right)
    )

    other = lax.ppermute(gradient_piece, "xlo", SWAP)
    strip = jnp.where(
        low == 0,
        jnp.concatenate([gradient_piece, other], axis=1),
        jnp.concatenate([other, gradient_piece], axis=1),
    )
    other = lax.ppermute(strip, "core", SWAP)
    gradient = jnp.where(
        core == 0,
        jnp.concatenate([strip, other], axis=1),
        jnp.concatenate([other, strip], axis=1),
    )
    policy_next, anchor_next, moment_next, second_next = adam_update(
        gradient, policy, anchor, moment, second
    )

    readout_cols = lax.dynamic_slice_in_dim(readout, core * half, half)[None]
    sums = score_sums(tokens, sibling, joined_halves(policy_plane), frozen, readout_cols)
    parts = jnp.sum(sums, axis=2).reshape(-1) / LEN
    parts = lax.all_to_all(jnp.broadcast_to(parts[None], (256, 8)), AXES, 0, 0, tiled=True)
    parts = parts.reshape(2, 2, 64, 8)
    margins = (parts[:, :, :, :4] + parts[:, ::-1, :, 4:]).reshape(-1)
    pair_loss = pair_losses(margins, pair_index, noisy_flags)
    return (policy_next, anchor_next, moment_next, second_next, pair_loss)


def solution(mesh):
    fine = Mesh(mesh.devices.reshape(2, 2, 4, 2, 8), AXES)
    everywhere = AXES
    owners = ("y", "xhi", "z")
    placed = (
        P(everywhere, None),
        P(everywhere, None),
        P(owners, None),
        P(owners, None),
        P(owners, None),
        P(owners, None),
        P(),
        P(everywhere, None),
        P(everywhere),
    )
    return jax.shard_map(
        shards,
        mesh=fine,
        in_specs=placed,
        out_specs=(
            P(owners, None),
            P(owners, None),
            P(owners, None),
            P(owners, None),
            P(everywhere),
        ),
        check_vma=False,
    )
```

time: 222 us -> 192 us (0.86)
  waiting for transfers between devices: 110 us -> 30.9 us
  blocking collectives: 10.3 us -> 78.9 us
  Pallas kernels: 0 us -> 36.8 us
  matrix products: 32.7 us -> 0 us
  between operations: 14.3 us -> 0.88 us
  starting transfers between devices: 40.4 us -> 31.3 us
  local copies, waits for them, and re-layouts: 9.84 us -> 5.91 us
  other arithmetic: 3.93 us -> 6.22 us
    all_to_all x1 -> x4, blocking collectives: 10.3 us -> 78.9 us  [the longest x1 29.8 us: to_plane(): return lax.all_to_all(blocks, PLANE, 0, 0, tiled=True)]
    all_to_all x3 -> x1, waiting for transfers between devices: 58.7 us -> 0.01 us  [to_plane(): return lax.all_to_all(blocks, PLANE, 0, 0, tiled=True)]
    pallas_call x0 -> x5, Pallas kernels: none -> 36.8 us  [the longest x2 16.6 us: gradient_blocks(): pl.pallas_call(gradient_kernel, grid_spec=pltpu.PrefetchScalarGridSpec(nu...]
    all_gather x1 -> x0, waiting for transfers between devices: 34 us -> none  [shards(): lax.all_gather(columns(anchor, core).astype(jnp.bfloat16), ('y', 'xhi', '...]
    dot_general x6 -> x0, matrix products: 32.7 us -> none  [the longest x2 11.3 us: gradient_product(): lax.dot_general(tokens, cotangent, (((0,), (0,)), ((), ())), preferred_el...]
    ppermute x3 -> x7, waiting for transfers between devices: 0.59 us -> 18.8 us  [the longest x1 18.8 us: shards(): other = lax.ppermute(gradient_piece, 'xlo', SWAP)]
    all_to_all x3 -> x1, starting transfers between devices: 18.7 us -> 3.75 us  [to_plane(): return lax.all_to_all(blocks, PLANE, 0, 0, tiled=True)]
    ppermute x3 -> x7, starting transfers between devices: 6.31 us -> 13.7 us  [the longest x1 6.77 us: shards(): other = lax.ppermute(strip, 'core', SWAP)]
  transfers between devices with their start and end apart: 9 -> 10, of which waited for: 7 -> 2; matrix products, arithmetic and copies ran while one was open for 18% -> 4% of each run, Pallas kernels for 0% -> 15%
where the time goes in v2:
time: 192 us; the launch traced here: 191 us
  blocking collectives  78.9 us (41%)
  Pallas kernels  36.8 us (19%)
  starting transfers between devices  31.3 us (16%)
  waiting for transfers between devices  30.9 us (16%)
  other arithmetic  6.22 us (3%)
  local copies, waits for them, and re-layouts  5.91 us (3%)
    all_to_all x1, blocking collectives, to_plane(): return lax.all_to_all(blocks, PLANE, 0, 0, tiled=True)  29.8 us
    all_to_all x2, blocking collectives, along_z(): return lax.all_to_all(blocks, 'z', 0, 0, tiled=True)  25.7 us
    all_to_all x1, blocking collectives, shards(): lax.all_to_all(jnp.broadcast_to(piece(anchor).astype(jnp.bfloat16)[None],...  23.4 us
    ppermute x1, waiting for transfers between devices, shards(): other = lax.ppermute(gradient_piece, 'xlo', SWAP)  18.8 us
    pallas_call x2, Pallas kernels, gradient_blocks(): pl.pallas_call(gradient_kernel, grid_spec=pltpu.PrefetchScalarGridSpec(nu...  16.6 us
    all_to_all x1, waiting for transfers between devices, shards(): lax.all_to_all(jnp.broadcast_to(parts[None], (256, 8)), AXES, 0, 0, tiled...  12.1 us
    all_to_all x1, starting transfers between devices, shards(): lax.all_to_all(jnp.broadcast_to(parts[None], (256, 8)), AXES, 0, 0, tiled...  10.6 us
    pallas_call x1, Pallas kernels, score_sums(): pl.pallas_call(score_kernel, grid=(4,), in_specs=token_specs(count, featu...  10.3 us
  transfers between devices with their start and end apart: 10, of which 2 were waited for; matrix products, arithmetic and copies ran while one was open for 4% of the time, Pallas kernels for 15%

profile of v2, /device:TPU:1, one launch (start us, length us, event | category | flops | bytes accessed | tf_op | source)
XLA Modules:
  0.0 191.0 jit_solution(16349207926568415945)
XLA Ops:
  0.6 8.1 %gradient_blocks.3 = bf16[2,8,128,512]{3,2,1,0:T(8,128)(2,1)} custom-call(s32[1]{0:T(128)} %bitcast.1.core, bf16[768,512]{1,0:T(8,128)(2,1)} %cotangent.3, bf16[768,4096]{1,0:T(8,128)(2,1)} %tokens.7), custom_call_target="tpu_custom_call" | custom-call | flops 1610612736 | bytes 10485760 | tf_op jit(solution)/shard_map/gradient_blocks/pallas_call | solution.py:70
  8.7 3.2 %collective-permute-start = (bf16[2,8,128,512]{3,2,1,0:T(8,128)(2,1)}, bf16[2,8,128,512]{3,2,1,0:T(8,128)(2,1)S(1)}, u32[]{:S(2)}, u32[]{:S(2)}) collective-permute-start(bf16[2,8,128,512]{3,2,1,0:T(8,128)(2,1)} %gradient_blocks.3), channel_id=1, source_target_pairs={{0,64},{64,0},{1,65},{65,1},{2,66},{66,2},{3,67},{67,3},{4,68},{68... | collective-permute-start | bytes 6291464 | tf_op jit(solution)/shard_map/ppermute | solution.py:255
  12.0 8.4 %gradient_blocks.2 = f32[2,8,128,512]{3,2,1,0:T(8,128)} custom-call(s32[1]{0:T(128)} %bitcast.core, bf16[768,512]{1,0:T(8,128)(2,1)} %cotangent.3, bf16[768,4096]{1,0:T(8,128)(2,1)} %tokens.7), custom_call_target="tpu_custom_call" | custom-call | flops 1610612736 | bytes 10485760 | tf_op jit(solution)/shard_map/gradient_blocks/pallas_call | solution.py:70
  20.4 0.0 collective-permute-done
  20.4 2.9 %add_convert_fusion = bf16[2,8,128,512]{3,2,1,0:T(8,128)(2,1)S(1)} fusion(f32[2,8,128,512]{3,2,1,0:T(8,128)} %gradient_blocks.2, bf16[2,8,128,512]{3,2,1,0:T(8,128)(2,1)S(1)} %collective-permute-done), kind=kLoop, calls=%fused_computation | loop fusion | flops 3145728 | bytes 8388608 | tf_op jit(solution)/shard_map/convert_element_type | solution.py:257
  23.4 0.1 collective-permute-start.5
  23.5 0.8 dynamic-slice_convert_fusion
  24.3 0.1 broadcast_in_dim.59
  24.4 23.4 %all_to_all.31 = bf16[32,64,128]{2,1,0:T(8,128)(2,1)S(1)} all-to-all(bf16[32,64,128]{2,1,0:T(8,128)(2,1)S(1)} %broadcast_in_dim.59), channel_id=1, replica_groups=mesh['xlo'=2,'core'=2,'y'=4,'xhi'=2,'z'=8] {'y','z'}, dimensions={0} | all-to-all | bytes 1048576 | tf_op jit(solution)/shard_map/all_to_all | solution.py:246
  47.8 29.8 %all_to_all.32.blocks = bf16[16,128,512]{2,1,0:T(8,128)(2,1)S(1)} all-to-all(bf16[16,128,512]{2,1,0:T(8,128)(2,1)S(1)} %bitcast.13), channel_id=1, replica_groups=mesh['xlo'=2,'core'=2,'y'=4,'xhi'=2,'z'=8] {'xlo','y','xhi'}, dimensions={0} | all-to-all | bytes 4194304 | tf_op jit(solution)/shard_map/all_to_all | solution.py:210
  77.6 0.6 collective-permute-start.1
  78.2 0.0 copy-done.1
  78.2 2.1 %collective-permute-start.2 = (bf16[4,512,128]{2,1,0:T(8,128)(2,1)S(1)}, bf16[4,512,128]{2,1,0:T(8,128)(2,1)S(1)}, u32[]{:S(2)}, u32[]{:S(2)}) collective-permute-start(bf16[4,512,128]{2,1,0:T(8,128)(2,1)S(1)} %bitcast.16), channel_id=1, source_target_pairs={{0,136},{128,0},{8,128},{136,8},{1,137},{129,1},{9,129},{137,9},{2... | collective-permute-start | bytes 1572872 | tf_op jit(solution)/shard_map/ppermute | solution.py:217
  80.3 0.3 plane_sum.1
  80.6 15.4 %all_to_all.33 = bf16[8,64,128]{2,1,0:T(8,128)(2,1)S(1)} all-to-all(bf16[8,64,128]{2,1,0:T(8,128)(2,1)S(1)} %bitcast.12), channel_id=1, replica_groups=mesh['xlo'=2,'core'=2,'y'=4,'xhi'=2,'z'=8] {'z'}, dimensions={0} | all-to-all | bytes 262144 | tf_op jit(solution)/shard_map/all_to_all | solution.py:223
  96.0 0.0 collective-permute-done.1.left
  96.0 0.0 copy-start.2
  96.0 0.0 collective-permute-done.2.right
  96.1 0.1 collective-permute-start.6
  96.2 2.7 %collective-permute-start.7 = (bf16[2,512,128]{2,1,0:T(8,128)(2,1)S(1)}, bf16[2,512,128]{2,1,0:T(8,128)(2,1)}, u32[]{:S(2)}, u32[]{:S(2)}) collective-permute-start(bf16[2,512,128]{2,1,0:T(8,128)(2,1)S(1)} %slice.20), channel_id=1, source_target_pairs={{0,136},{128,0},{8,128},{136,8},{1,137},{129,1},{9,129},{137,9},{2... | collective-permute-start | bytes 786440 | tf_op jit(solution)/shard_map/ppermute | solution.py:217
  98.9 0.8 fusion.7
  99.8 10.3 %all_to_all.34 = bf16[8,64,128]{2,1,0:T(8,128)(2,1)S(1)} all-to-all(bf16[8,64,128]{2,1,0:T(8,128)(2,1)S(1)} %broadcast_in_dim.60), channel_id=1, replica_groups=mesh['xlo'=2,'core'=2,'y'=4,'xhi'=2,'z'=8] {'z'}, dimensions={0} | all-to-all | bytes 262144 | tf_op jit(solution)/shard_map/all_to_all | solution.py:223
  110.1 0.0 collective-permute-done.6.far_left
  110.1 0.0 collective-permute-done.7.far_right
  110.1 1.8 broadcast_in_dim.62
  111.9 0.0 copy-done.4
  111.9 3.8 %all-to-all-start.4 = ((bf16[16,512,128]{2,1,0:T(8,128)(2,1)}), bf16[16,512,128]{2,1,0:T(8,128)(2,1)S(1)}, u32[]{:S(2)}, u32[]{:S(2)}) async-start(bf16[16,512,128]{2,1,0:T(8,128)(2,1)} %broadcast_in_dim.62), calls=%async_computation.4 | async-start | bytes 4194304 | tf_op jit(solution)/shard_map/all_to_all | solution.py:210
  115.6 1.4 collective-permute-start.3
  117.0 0.2 slice_reduce_fusion
  117.2 0.6 dynamic_slice.19
  117.8 18.8 %collective-permute-done.3 = f32[64,128]{1,0:T(8,128)S(1)} collective-permute-done((f32[64,128]{1,0:T(8,128)S(1)}, f32[64,128]{1,0:T(8,128)S(1)}, u32[]{:S(2)}, u32[]{:S(2)}) %collective-permute-start.3) | collective-permute-done | bytes 32800 | tf_op jit(solution)/shard_map/ppermute | solution.py:279
  136.7 6.8 %collective-permute-start.4 = (f32[64,256]{1,0:T(8,128)S(1)}, f32[64,256]{1,0:T(8,128)S(1)}, u32[]{:S(2)}, u32[]{:S(2)}) collective-permute-start(f32[64,256]{1,0:T(8,128)S(1)} %maximum_select_fusion.1), channel_id=1, source_target_pairs={{0,64},{64,0},{1,65},{65,1},{2,66},{66,2},{3,67},{67,3},{4,68},{68... | collective-permute-start | bytes 196616 | tf_op jit(solution)/shard_map/ppermute | solution.py:285
  143.5 0.0 collective-permute-done.5.sibling
  143.5 9.6 %frozen_values.1.frozen = f32[1536,256]{1,0:T(8,128)} custom-call(s32[1]{0:T(128)} %bitcast.7.place, bf16[768,4096]{1,0:T(8,128)(2,1)} %tokens.7, bf16[768,4096]{1,0:T(8,128)(2,1)} %collective-permute-done.5.sibling, bf16[4,512,128]{2,1,0:T(8,128)(2,1)} %bitcast.17, bf16[4,512,128]{2,1,0:T(8,128)(2,1)} %copy-done.2, bf16[4,512,128]{2,1,0:T(8,128)(2,1)} %copy-done.3, ...), custom_call_target="tpu_custom_call" | custom-call | flops 3221225472 | bytes 16777216 | tf_op jit(solution)/shard_map/frozen_values/pallas_call | solution.py:149
  153.1 0.0 all-to-all-done.4
  153.1 1.3 copy-done
  154.5 10.3 %score_sums.1 = f32[4,2,256]{2,1,0:T(2,128)} custom-call(bf16[768,4096]{1,0:T(8,128)(2,1)} %tokens.7, bf16[768,4096]{1,0:T(8,128)(2,1)} %collective-permute-done.5.sibling, bf16[2,4096,128]{2,1,0:T(8,128)(2,1)} %bitcast.14, f32[1536,256]{1,0:T(8,128)} %frozen_values.1.frozen, f32[1,256]{1,0:T(1,128)} %bitcast.21), custom_call_target="tpu_custom_call" | custom-call | flops 3221225472 | bytes 16777216 | tf_op jit(solution)/shard_map/score_sums/pallas_call | solution.py:172
  164.8 0.8 reduce_sum.37
  165.6 0.1 div.34
  165.7 0.7 broadcast_in_dim.65
  166.4 10.6 %all-to-all-start.5 = ((f32[256,1,8]{2,1,0:T(1,128)}), f32[256,1,8]{2,1,0:T(1,128)S(1)}, u32[]{:S(2)}, u32[]{:S(2)}) async-start(f32[256,1,8]{2,1,0:T(1,128)} %broadcast_in_dim.65), calls=%async_computation.5 | async-start | bytes 262144 | tf_op jit(solution)/shard_map/all_to_all | solution.py:298
  177.0 0.0 collective-permute-done.4
  177.1 0.8 multiply_add_fusion
  177.9 12.1 %all-to-all-done.5 = f32[256,1,8]{2,1,0:T(1,128)S(1)} async-done(((f32[256,1,8]{2,1,0:T(1,128)}), f32[256,1,8]{2,1,0:T(1,128)S(1)}, u32[]{:S(2)}, u32[]{:S(2)}) %all-to-all-start.5) | async-done | bytes 8224 | tf_op jit(solution)/shard_map/all_to_all | solution.py:298
  190.0 0.1 slice.25
  190.1 0.1 broadcast_in_dim.66
  190.3 0.2 fusion.9
  190.5 0.5 multiply_subtract_fusion
  (27 shorter events, 0.2 us)
Async XLA Ops:
  8.7 11.7 %collective-permute-start = (bf16[2,8,128,512]{3,2,1,0:T(8,128)(2,1)}, bf16[2,8,128,512]{3,2,1,0:T(8,128)(2,1)S(1)}, u32[]{:S(2)}, u32[]{:S(2)}) collective-permute-start(bf16[2,8,128,512]{3,2,1,0:T(8,128)(2,1)} %gradient_blocks.3), channel_id=1, source_target_pairs={{0,64},{64,0},{1,65},{65,1},{2,66},{66,2},{3,67},{67,3},{4,68},{68... | collective-permute-start | bytes 6291464 | tf_op jit(solution)/shard_map/ppermute | solution.py:255
  23.4 120.1 %collective-permute-start.5 = (bf16[768,4096]{1,0:T(8,128)(2,1)}, bf16[768,4096]{1,0:T(8,128)(2,1)}, u32[]{:S(2)}, u32[]{:S(2)}) collective-permute-start(bf16[768,4096]{1,0:T(8,128)(2,1)} %tokens.7), channel_id=1, source_target_pairs={{0,64},{64,0},{1,65},{65,1},{2,66},{66,2},{3,67},{67,3},{4,68},{68... | collective-permute-start | bytes 18874376 | tf_op jit(solution)/shard_map/ppermute | solution.py:259
  47.8 30.4 %copy-start.1 = (bf16[32,64,128]{2,1,0:T(8,128)(2,1)}, bf16[32,64,128]{2,1,0:T(8,128)(2,1)S(1)}, u32[]{:S(2)}) copy-start(bf16[32,64,128]{2,1,0:T(8,128)(2,1)S(1)} %all_to_all.31) | copy-start | bytes 1572868
  77.6 18.4 %collective-permute-start.1 = (bf16[4,512,128]{2,1,0:T(8,128)(2,1)S(1)}, bf16[4,512,128]{2,1,0:T(8,128)(2,1)S(1)}, u32[]{:S(2)}, u32[]{:S(2)}) collective-permute-start(bf16[4,512,128]{2,1,0:T(8,128)(2,1)S(1)} %bitcast.15), channel_id=1, source_target_pairs={{0,128},{128,8},{8,136},{136,0},{1,129},{129,9},{9,137},{137,1},{2... | collective-permute-start | bytes 1572872 | tf_op jit(solution)/shard_map/ppermute | solution.py:217
  78.2 17.8 %collective-permute-start.2 = (bf16[4,512,128]{2,1,0:T(8,128)(2,1)S(1)}, bf16[4,512,128]{2,1,0:T(8,128)(2,1)S(1)}, u32[]{:S(2)}, u32[]{:S(2)}) collective-permute-start(bf16[4,512,128]{2,1,0:T(8,128)(2,1)S(1)} %bitcast.16), channel_id=1, source_target_pairs={{0,136},{128,0},{8,128},{136,8},{1,137},{129,1},{9,129},{137,9},{2... | collective-permute-start | bytes 1572872 | tf_op jit(solution)/shard_map/ppermute | solution.py:217
  96.0 15.8 %copy-start.2 = (bf16[4,512,128]{2,1,0:T(8,128)(2,1)}, bf16[4,512,128]{2,1,0:T(8,128)(2,1)S(1)}, u32[]{:S(2)}) copy-start(bf16[4,512,128]{2,1,0:T(8,128)(2,1)S(1)} %collective-permute-done.1.left) | copy-start | bytes 1572868
  96.0 15.8 %copy-start.3 = (bf16[4,512,128]{2,1,0:T(8,128)(2,1)}, bf16[4,512,128]{2,1,0:T(8,128)(2,1)S(1)}, u32[]{:S(2)}) copy-start(bf16[4,512,128]{2,1,0:T(8,128)(2,1)S(1)} %collective-permute-done.2.right) | copy-start | bytes 1572868
  96.1 14.0 %collective-permute-start.6 = (bf16[2,512,128]{2,1,0:T(8,128)(2,1)S(1)}, bf16[2,512,128]{2,1,0:T(8,128)(2,1)S(1)}, u32[]{:S(2)}, u32[]{:S(2)}) collective-permute-start(bf16[2,512,128]{2,1,0:T(8,128)(2,1)S(1)} %slice.19), channel_id=1, source_target_pairs={{0,128},{128,8},{8,136},{136,0},{1,129},{129,9},{9,137},{137,1},{2... | collective-permute-start | bytes 786440 | tf_op jit(solution)/shard_map/ppermute | solution.py:217
  96.2 13.9 %collective-permute-start.7 = (bf16[2,512,128]{2,1,0:T(8,128)(2,1)S(1)}, bf16[2,512,128]{2,1,0:T(8,128)(2,1)}, u32[]{:S(2)}, u32[]{:S(2)}) collective-permute-start(bf16[2,512,128]{2,1,0:T(8,128)(2,1)S(1)} %slice.20), channel_id=1, source_target_pairs={{0,136},{128,0},{8,128},{136,8},{1,137},{129,1},{9,129},{137,9},{2... | collective-permute-start | bytes 786440 | tf_op jit(solution)/shard_map/ppermute | solution.py:217
  110.1 1.8 copy-start.4
  111.9 5.2 %copy-start.9 = (s32[2,2]{1,0:T(2,128)S(1)}, s32[2,2]{1,0:T(2,128)}, u32[]{:S(2)}) copy-start(s32[2,2]{1,0:T(2,128)} %param.16) | copy-start | bytes 52
  111.9 5.3 %copy-start.10 = (f32[512]{0:T(512)S(1)}, f32[512]{0:T(512)}, u32[]{:S(2)}) copy-start(f32[512]{0:T(512)} %param.15) | copy-start | bytes 6148
  111.9 41.2 %all-to-all-start.4 = ((bf16[16,512,128]{2,1,0:T(8,128)(2,1)}), bf16[16,512,128]{2,1,0:T(8,128)(2,1)S(1)}, u32[]{:S(2)}, u32[]{:S(2)}) async-start(bf16[16,512,128]{2,1,0:T(8,128)(2,1)} %broadcast_in_dim.62), calls=%async_computation.4 | async-start | bytes 4194304 | tf_op jit(solution)/shard_map/all_to_all | solution.py:210
  115.6 21.0 %collective-permute-start.3 = (f32[64,128]{1,0:T(8,128)S(1)}, f32[64,128]{1,0:T(8,128)S(1)}, u32[]{:S(2)}, u32[]{:S(2)}) collective-permute-start(f32[64,128]{1,0:T(8,128)S(1)} %convert_reduce_fusion), channel_id=1, source_target_pairs={{0,128},{128,0},{1,129},{129,1},{2,130},{130,2},{3,131},{131,3},{4... | collective-permute-start | bytes 98312 | tf_op jit(solution)/shard_map/ppermute | solution.py:279
  136.7 40.3 %collective-permute-start.4 = (f32[64,256]{1,0:T(8,128)S(1)}, f32[64,256]{1,0:T(8,128)S(1)}, u32[]{:S(2)}, u32[]{:S(2)}) collective-permute-start(f32[64,256]{1,0:T(8,128)S(1)} %maximum_select_fusion.1), channel_id=1, source_target_pairs={{0,64},{64,0},{1,65},{65,1},{2,66},{66,2},{3,67},{67,3},{4,68},{68... | collective-permute-start | bytes 196616 | tf_op jit(solution)/shard_map/ppermute | solution.py:285
  153.1 1.4 copy-start
  154.4 22.6 %copy-start.5 = (f32[64,512]{1,0:T(8,128)S(1)}, f32[64,512]{1,0:T(8,128)}, u32[]{:S(2)}) copy-start(f32[64,512]{1,0:T(8,128)} %param.11) | copy-start | bytes 393220
  154.5 22.6 %copy-start.6 = (f32[64,512]{1,0:T(8,128)S(1)}, f32[64,512]{1,0:T(8,128)}, u32[]{:S(2)}) copy-start(f32[64,512]{1,0:T(8,128)} %param.13) | copy-start | bytes 393220
  154.5 22.6 %copy-start.7 = (f32[64,512]{1,0:T(8,128)S(1)}, f32[64,512]{1,0:T(8,128)}, u32[]{:S(2)}) copy-start(f32[64,512]{1,0:T(8,128)} %param.14) | copy-start | bytes 393220
  154.5 22.6 %copy-start.8 = (f32[64,512]{1,0:T(8,128)S(1)}, f32[64,512]{1,0:T(8,128)}, u32[]{:S(2)}) copy-start(f32[64,512]{1,0:T(8,128)} %param.12) | copy-start | bytes 393220
  164.8 25.7 %copy-start.11 = (s32[2]{0:T(128)S(1)}, s32[2]{0:T(128)}, u32[]{:S(2)}) copy-start(s32[2]{0:T(128)} %param.17) | copy-start | bytes 28
  166.4 23.6 %all-to-all-start.5 = ((f32[256,1,8]{2,1,0:T(1,128)}), f32[256,1,8]{2,1,0:T(1,128)S(1)}, u32[]{:S(2)}, u32[]{:S(2)}) async-start(f32[256,1,8]{2,1,0:T(1,128)} %broadcast_in_dim.65), calls=%async_computation.5 | async-start | bytes 262144 | tf_op jit(solution)/shard_map/all_to_all | solution.py:298

commit v3 on v2

--- a/solution.py
+++ b/solution.py
@@ -49,60 +49,57 @@
     )
 
 
-VMEM = 56 << 20
-
-
-def gradient_kernel(core, cotangent, tokens, out, turned):
+VMEM = 32 << 20
+VMEM_GRADIENT = 32 << 20
+VMEM_SCORE = 32 << 20
+
+
+def gradient_kernel(core, cotangent, tokens, sent, own, turned):
+    half = cotangent.shape[1] // 2
+    quarter = half // 2
+
     @pl.when(pl.program_id(0) == 0)
     def _():
-        turned[...] = cotangent[...].T
+        away = pl.multiple_of((1 - core[0]) * half, half)
+        here = pl.multiple_of(core[0] * half, half)
+        turned[:half] = cotangent[:, pl.ds(away, half)].T
+        turned[half:] = cotangent[:, pl.ds(here, half)].T
 
     product = jnp.dot(turned[...], tokens[...], preferred_element_type=jnp.float32)
-    quarter = product.shape[0] // 2
-    out[0, 0] = product[:quarter].astype(out.dtype)
-    out[1, 0] = product[quarter:].astype(out.dtype)
-
-
-def gradient_blocks(which, cotangent, tokens, dtype):
+    sent[0, 0] = product[:quarter].astype(sent.dtype)
+    sent[1, 0] = product[quarter:half].astype(sent.dtype)
+    own[0, 0] = product[half : half + quarter].astype(own.dtype)
+    own[1, 0] = product[half + quarter :].astype(own.dtype)
+
+
+def gradient_blocks(core, cotangent, tokens):
     count, features = tokens.shape
-    half = cotangent.shape[1] // 2
+    channels = cotangent.shape[1]
+    quarter = channels // 4
     width = features // 8
+    block = pl.BlockSpec((2, 1, quarter, width), lambda i, core: (0, i, 0, 0))
     return pl.pallas_call(
         gradient_kernel,
         grid_spec=pltpu.PrefetchScalarGridSpec(
             num_scalar_prefetch=1,
             grid=(8,),
             in_specs=[
-                pl.BlockSpec((count, half), lambda i, core: (0, core[0])),
+                pl.BlockSpec((count, channels), lambda i, core: (0, 0)),
                 pl.BlockSpec((count, width), lambda i, core: (0, i)),
             ],
-            out_specs=pl.BlockSpec((2, 1, half // 2, width), lambda i, core: (0, i, 0, 0)),
-            scratch_shapes=[pltpu.VMEM((half, count), jnp.bfloat16)],
-        ),
-        out_shape=jax.ShapeDtypeStruct((2, 8, half // 2, width), dtype),
+            out_specs=[block, block],
+            scratch_shapes=[pltpu.VMEM((channels, count), jnp.bfloat16)],
+        ),
+        out_shape=[
+            jax.ShapeDtypeStruct((2, 8, quarter, width), jnp.bfloat16),
+            jax.ShapeDtypeStruct((2, 8, quarter, width), jnp.bfloat16),
+        ],
         cost_estimate=pl.CostEstimate(
-            flops=2 * count * features * half, bytes_accessed=10 << 20, transcendentals=0
-        ),
-        compiler_params=pltpu.CompilerParams(vmem_limit_bytes=VMEM),
+            flops=2 * count * features * channels, bytes_accessed=12 << 20, transcendentals=0
+        ),
+        compiler_params=pltpu.CompilerParams(vmem_limit_bytes=VMEM_GRADIENT),
         name="gradient_blocks",
-    )(which, cotangent, tokens)
-
-
-def select_rows(tokens, sibling):
-    return jnp.where(pl.program_id(0) < 2, tokens[...], sibling[...])
-
-
-def weigh(tokens, sibling, halves, joined):
-    quarter = halves.shape[-1]
-
-    @pl.when(pl.program_id(0) == 0)
-    def _():
-        joined[:, :quarter] = halves[0]
-        joined[:, quarter:] = halves[1]
-
-    return jnp.dot(
-        select_rows(tokens, sibling), joined[...], preferred_element_type=jnp.float32
-    )
+    )(core, cotangent, tokens)
 
 
 def frozen_kernel(place, tokens, sibling, here, left, right, far_left, far_right, out, joined):
@@ -118,21 +115,53 @@
             for at in range(ref.shape[0]):
                 joined[(first + at) * 2 + chip // 2, :, lanes] = ref[at]
 
-    weights = joined[...].reshape(joined.shape[0] * rows, 2 * quarter)
-    out[...] = jnp.dot(select_rows(tokens, sibling), weights, preferred_element_type=jnp.float32)
-
-
-def log_sigmoid(values):
-    return jnp.minimum(values, 0.0) - jnp.log(1.0 + jnp.exp(-jnp.abs(values)))
-
-
-def score_kernel(tokens, sibling, halves, frozen, readout, out, joined):
-    policy_values = weigh(tokens, sibling, halves, joined)
-    anchor_values = blend_rate * policy_values + (1.0 - blend_rate) * frozen[...]
-    weights = readout[...]
-    gap = log_sigmoid(policy_values * weights) - log_sigmoid(anchor_values * weights)
-    for at in range(out.shape[1]):
-        out[0, at] = jnp.sum(gap[at * LEN : (at + 1) * LEN], axis=0)
+    for ref, turn_of in ((tokens, pl.program_id(0) < 2), (sibling, pl.program_id(0) >= 2)):
+
+        @pl.when(turn_of)
+        def _():
+            weights = joined[...].reshape(joined.shape[0] * rows, 2 * quarter)
+            out[...] = jnp.dot(ref[...], weights, preferred_element_type=jnp.float32)
+
+
+def sigmoid_sums(values):
+    rows = values.reshape(LEN // 8, 8, values.shape[1])
+    lows = jnp.minimum(rows, 0.0)
+    factors = 1.0 + jnp.exp(-jnp.abs(rows))
+    low_sum, product = lows[0], factors[0]
+    for step in range(1, LEN // 8):
+        low_sum = low_sum + lows[step]
+        product = product * factors[step]
+    return low_sum - jnp.log(product)
+
+
+def score_kernel(tokens, sibling, halves, frozen, readout, out, joined, held, sems):
+    quarter = halves.shape[-1]
+    count = tokens.shape[0]
+    loads = [
+        pltpu.make_async_copy(
+            source.at[pl.ds(first, LEN)], held.at[pl.ds(base + first, LEN)], sems.at[at]
+        )
+        for at, (source, base, first) in enumerate(
+            (source, base, first)
+            for source, base in ((tokens, 0), (sibling, count))
+            for first in range(0, count, LEN)
+        )
+    ]
+    for load in loads:
+        load.start()
+    joined[:, :quarter] = halves[0]
+    joined[:, quarter:] = halves[1]
+    scale = readout[...]
+    lane = lax.broadcasted_iota(jnp.int32, out.shape, 2)
+    parts = jnp.zeros(out.shape, jnp.float32)
+    for sequence, load in enumerate(loads):
+        load.wait()
+        rows = slice(sequence * LEN, (sequence + 1) * LEN)
+        values = jnp.dot(held[rows], joined[...], preferred_element_type=jnp.float32)
+        blended = blend_rate * values + (1.0 - blend_rate) * frozen[rows]
+        gap = sigmoid_sums(values * scale) - sigmoid_sums(blended * scale)
+        parts = jnp.where(lane == sequence, jnp.sum(gap) / LEN, parts)
+    out[...] = parts
 
 
 def token_specs(count, features):
@@ -168,23 +197,20 @@
 def score_sums(tokens, sibling, halves, frozen, readout):
     count, features = tokens.shape
     width = 2 * halves.shape[-1]
-    each = count // 2 // LEN
     return pl.pallas_call(
         score_kernel,
-        grid=(4,),
-        in_specs=token_specs(count, features)
-        + [
-            pl.BlockSpec(halves.shape, lambda i: (0, 0, 0)),
-            pl.BlockSpec((count // 2, width), lambda i: (i, 0)),
-            pl.BlockSpec((1, width), lambda i: (0, 0)),
+        out_shape=jax.ShapeDtypeStruct((256, 1, 128), jnp.float32),
+        in_specs=[pl.BlockSpec(memory_space=pl.ANY)] * 2
+        + [pl.BlockSpec(memory_space=pltpu.VMEM)] * 3,
+        scratch_shapes=[
+            pltpu.VMEM((features, width), jnp.bfloat16),
+            pltpu.VMEM((2 * count, features), tokens.dtype),
+            pltpu.SemaphoreType.DMA((2 * count // LEN,)),
         ],
-        out_specs=pl.BlockSpec((1, each, width), lambda i: (i, 0, 0)),
-        out_shape=jax.ShapeDtypeStruct((4, each, width), jnp.float32),
-        scratch_shapes=[pltpu.VMEM((features, width), jnp.bfloat16)],
         cost_estimate=pl.CostEstimate(
             flops=4 * count * features * width, bytes_accessed=16 << 20, transcendentals=0
         ),
-        compiler_params=pltpu.CompilerParams(vmem_limit_bytes=VMEM),
+        compiler_params=pltpu.CompilerParams(vmem_limit_bytes=VMEM_SCORE),
         name="score_sums",
     )(tokens, sibling, halves, frozen, readout)
 
@@ -243,22 +269,19 @@
     def joined_halves(plane):
         return plane.reshape(2, features, quarter)
 
-    strips = lax.all_to_all(
-        jnp.broadcast_to(piece(anchor).astype(jnp.bfloat16)[None], (32, rows, quarter)),
-        ("y", "z"),
-        0,
-        0,
-        tiled=True,
-    ).reshape(4, 8 * rows, quarter)
-
-    sent = gradient_blocks((1 - core)[None], cotangent, tokens, jnp.bfloat16)
+    anchor_copies = jnp.broadcast_to(piece(anchor).astype(jnp.bfloat16)[None], (32, rows, quarter))
+    anchor_copies, cotangent = lax.optimization_barrier((anchor_copies, cotangent))
+    strips = lax.all_to_all(anchor_copies, ("y", "z"), 0, 0, tiled=True)
+    strips = strips.reshape(4, 8 * rows, quarter)
+
+    sent, own = gradient_blocks(core[None], cotangent, tokens)
+    sent, strips = lax.optimization_barrier((sent, strips))
     arrived = lax.ppermute(sent, "core", SWAP)
-    own = gradient_blocks(core[None], cotangent, tokens, jnp.float32)
-    blocks = (own + arrived.astype(jnp.float32)).astype(jnp.bfloat16)
-    tokens_out, blocks = lax.optimization_barrier((tokens, blocks))
-    sibling = lax.ppermute(tokens_out, "core", SWAP)
+    blocks = own.astype(jnp.float32) + arrived.astype(jnp.float32)
+    blocks = blocks.astype(jnp.bfloat16)
     plane = to_plane(blocks.reshape(16, quarter, 8 * rows))
-    plane, strips = lax.optimization_barrier((plane, strips))
+    plane, strips, tokens = lax.optimization_barrier((plane, strips, tokens))
+    sibling = lax.ppermute(tokens, "core", SWAP)
     left, right = turn(strips, 1), turn(strips, -1)
     column = along_z(plane_sum(plane).reshape(8, rows, quarter))
     gradient_piece = jnp.sum(column.astype(jnp.float32), axis=0)
@@ -268,15 +291,15 @@
     policy_piece = adam_update(
         gradient_piece, piece(policy), piece(anchor), piece(moment), piece(second)
     )[0].astype(jnp.bfloat16)
-    policy_copies, far_left, far_right = lax.optimization_barrier(
-        (copies(spread_z(policy_piece)), far_left, far_right)
+    other = lax.ppermute(gradient_piece, "xlo", SWAP)
+    policy_copies, far_left, far_right, sibling, other = lax.optimization_barrier(
+        (copies(spread_z(policy_piece)), far_left, far_right, sibling, other)
     )
     policy_plane = to_plane(policy_copies)
     frozen = frozen_values(
         (high * 2 + low)[None], tokens, sibling, (strips, left, right, far_left, far_right)
     )
 
-    other = lax.ppermute(gradient_piece, "xlo", SWAP)
     strip = jnp.where(
         low == 0,
         jnp.concatenate([gradient_piece, other], axis=1),
@@ -293,11 +316,10 @@
     )
 
     readout_cols = lax.dynamic_slice_in_dim(readout, core * half, half)[None]
-    sums = score_sums(tokens, sibling, joined_halves(policy_plane), frozen, readout_cols)
-    parts = jnp.sum(sums, axis=2).reshape(-1) / LEN
-    parts = lax.all_to_all(jnp.broadcast_to(parts[None], (256, 8)), AXES, 0, 0, tiled=True)
-    parts = parts.reshape(2, 2, 64, 8)
-    margins = (parts[:, :, :, :4] + parts[:, ::-1, :, 4:]).reshape(-1)
+    parts = score_sums(tokens, sibling, joined_halves(policy_plane), frozen, readout_cols)
+    parts = lax.all_to_all(parts, AXES, 0, 0, tiled=True)
+    parts = parts.reshape(2, 2, 64, 128)
+    margins = (parts[:, :, :, :4] + parts[:, ::-1, :, 4:8]).reshape(-1)
     pair_loss = pair_losses(margins, pair_index, noisy_flags)
     return (policy_next, anchor_next, moment_next, second_next, pair_loss)
 

time: 192 us -> 171 us (0.89)
  blocking collectives: 78.9 us -> 42.8 us
  starting transfers between devices: 31.3 us -> 42.9 us
  Pallas kernels: 36.8 us -> 28.2 us
  waiting for transfers between devices: 30.9 us -> 39 us
  local copies, waits for them, and re-layouts: 5.91 us -> 12.5 us
  other arithmetic: 6.22 us -> 4.07 us
    all_to_all x1 -> x0, blocking collectives: 23.4 us -> none  [shards(): lax.all_to_all(jnp.broadcast_to(piece(anchor).astype(jnp.bfloat16)[None],...]
    ppermute x1, waiting for transfers between devices: 18.8 us -> 2.76 us  [shards(): other = lax.ppermute(gradient_piece, 'xlo', SWAP)]
    all_to_all x2 -> x1, blocking collectives: 25.7 us -> 11.4 us  [along_z(): return lax.all_to_all(blocks, 'z', 0, 0, tiled=True)]
    all_to_all x1 -> x3, starting transfers between devices: 10.6 us -> 24.8 us  [the longest x1 12 us: shards(): strips = lax.all_to_all(anchor_copies, ('y', 'z'), 0, 0, tiled=True)]
    all_to_all x1, waiting for transfers between devices: 0.01 us -> 11.9 us  [to_plane(): return lax.all_to_all(blocks, PLANE, 0, 0, tiled=True)]
    pallas_call x2 -> x1, Pallas kernels: 16.6 us -> 7.99 us  [gradient_blocks(): pl.pallas_call(gradient_kernel, grid_spec=pltpu.PrefetchScalarGridSpec(nu...]
    all_to_all x1 -> x3, waiting for transfers between devices: 12.1 us -> 20 us  [the longest x1 11 us: shards(): parts = lax.all_to_all(parts, AXES, 0, 0, tiled=True)]
    unnamed x24 -> x30, local copies, waits for them, and re-layouts: 1.39 us -> 7.85 us
  transfers between devices with their start and end apart: 10 -> 12, of which waited for: 2 -> 7; matrix products, arithmetic and copies ran while one was open for 4% -> 2% of each run, Pallas kernels for 15% -> 17%
where the time goes in v3:
time: 171 us; the launch traced here: 170 us
  starting transfers between devices  42.9 us (25%)
  blocking collectives  42.8 us (25%)
  waiting for transfers between devices  39 us (23%)
  Pallas kernels  28.2 us (16%)
  local copies, waits for them, and re-layouts  12.5 us (7%)
  other arithmetic  4.07 us (2%)
    all_to_all x1, blocking collectives, to_plane(): return lax.all_to_all(blocks, PLANE, 0, 0, tiled=True)  31.4 us
    all_to_all x1, starting transfers between devices, shards(): strips = lax.all_to_all(anchor_copies, ('y', 'z'), 0, 0, tiled=True)  12 us
    all_to_all x1, waiting for transfers between devices, to_plane(): return lax.all_to_all(blocks, PLANE, 0, 0, tiled=True)  11.9 us
    pallas_call x1, Pallas kernels, score_sums(): pl.pallas_call(score_kernel, out_shape=jax.ShapeDtypeStruct((256, 1, 128)...  11.7 us
    all_to_all x1, blocking collectives, along_z(): return lax.all_to_all(blocks, 'z', 0, 0, tiled=True)  11.4 us
    all_to_all x1, waiting for transfers between devices, shards(): parts = lax.all_to_all(parts, AXES, 0, 0, tiled=True)  11 us
    all_to_all x1, starting transfers between devices, shards(): parts = lax.all_to_all(parts, AXES, 0, 0, tiled=True)  8.94 us
    pallas_call x1, Pallas kernels, frozen_values(): pl.pallas_call(frozen_kernel, grid_spec=pltpu.PrefetchScalarGridSpec(num_...  8.15 us
  transfers between devices with their start and end apart: 12, of which 7 were waited for; matrix products, arithmetic and copies ran while one was open for 2% of the time, Pallas kernels for 17%

profile of v3, /device:TPU:1, one launch (start us, length us, event | category | flops | bytes accessed | tf_op | source)
XLA Modules:
  0.0 170.3 jit_solution(6445109576639994900)
XLA Ops:
  0.6 0.8 dynamic-slice_convert_fusion
  1.4 0.9 broadcast_in_dim.49
  2.3 12.0 %all-to-all-start = ((bf16[32,64,128]{2,1,0:T(8,128)(2,1)}), bf16[32,64,128]{2,1,0:T(8,128)(2,1)S(1)}, u32[]{:S(2)}, u32[]{:S(2)}) async-start(bf16[32,64,128]{2,1,0:T(8,128)(2,1)} %broadcast_in_dim.49), calls=%async_computation | async-start | bytes 1048576 | tf_op jit(solution)/shard_map/all_to_all | solution.py:274
  14.4 0.0 copy-start.7
  14.4 1.1 copy-done.7
  15.5 8.0 %gradient_blocks.1 = (bf16[2,8,128,512]{3,2,1,0:T(8,128)(2,1)S(1)}, bf16[2,8,128,512]{3,2,1,0:T(8,128)(2,1)S(1)}) custom-call(s32[1]{0:T(128)} %bitcast.core, bf16[768,512]{1,0:T(8,128)(2,1)S(1)} %copy-done.7, bf16[768,4096]{1,0:T(8,128)(2,1)} %tokens.3), custom_call_target="tpu_custom_call" | custom-call | flops 3221225472 | bytes 12582912 | tf_op jit(solution)/shard_map/gradient_blocks/pallas_call | solution.py:81
  23.5 1.3 copy-done.6
  24.8 3.8 %all-to-all-done = bf16[32,64,128]{2,1,0:T(8,128)(2,1)S(1)} async-done(((bf16[32,64,128]{2,1,0:T(8,128)(2,1)}), bf16[32,64,128]{2,1,0:T(8,128)(2,1)S(1)}, u32[]{:S(2)}, u32[]{:S(2)}) %all-to-all-start) | async-done | bytes 524320 | tf_op jit(solution)/shard_map/all_to_all | solution.py:274
  28.7 3.5 %collective-permute-start = (bf16[2,8,128,512]{3,2,1,0:T(8,128)(2,1)}, bf16[2,8,128,512]{3,2,1,0:T(8,128)(2,1)S(1)}, u32[]{:S(2)}, u32[]{:S(2)}) collective-permute-start(bf16[2,8,128,512]{3,2,1,0:T(8,128)(2,1)} %copy-done.6), channel_id=1, source_target_pairs={{0,64},{64,0},{1,65},{65,1},{2,66},{66,2},{3,67},{67,3},{4,68},{68... | collective-permute-start | bytes 6291464 | tf_op jit(solution)/shard_map/ppermute | solution.py:279
  32.2 4.0 %collective-permute-done = bf16[2,8,128,512]{3,2,1,0:T(8,128)(2,1)S(1)} collective-permute-done((bf16[2,8,128,512]{3,2,1,0:T(8,128)(2,1)}, bf16[2,8,128,512]{3,2,1,0:T(8,128)(2,1)S(1)}, u32[]{:S(2)}, u32[]{:S(2)}) %collective-permute-start) | collective-permute-done | bytes 2097184 | tf_op jit(solution)/shard_map/ppermute | solution.py:279
  36.2 0.7 add_convert_fusion
  36.9 31.4 %all_to_all.30.blocks = bf16[16,128,512]{2,1,0:T(8,128)(2,1)S(1)} all-to-all(bf16[16,128,512]{2,1,0:T(8,128)(2,1)S(1)} %bitcast.17), channel_id=1, replica_groups=mesh['xlo'=2,'core'=2,'y'=4,'xhi'=2,'z'=8] {'xlo','y','xhi'}, dimensions={0} | all-to-all | bytes 4194304 | tf_op jit(solution)/shard_map/all_to_all | solution.py:236
  68.3 2.5 %collective-permute-start.5 = (bf16[768,4096]{1,0:T(8,128)(2,1)}, bf16[768,4096]{1,0:T(8,128)(2,1)}, u32[]{:S(2)}, u32[]{:S(2)}) collective-permute-start(bf16[768,4096]{1,0:T(8,128)(2,1)} %tokens.3), channel_id=1, source_target_pairs={{0,64},{64,0},{1,65},{65,1},{2,66},{66,2},{3,67},{67,3},{4,68},{68... | collective-permute-start | bytes 18874376 | tf_op jit(solution)/shard_map/ppermute | solution.py:284
  70.8 0.3 collective-permute-start.1
  71.1 2.4 %collective-permute-start.2 = (bf16[4,512,128]{2,1,0:T(8,128)(2,1)S(1)}, bf16[4,512,128]{2,1,0:T(8,128)(2,1)S(1)}, u32[]{:S(2)}, u32[]{:S(2)}) collective-permute-start(bf16[4,512,128]{2,1,0:T(8,128)(2,1)S(1)} %bitcast.13), channel_id=1, source_target_pairs={{0,136},{128,0},{8,128},{136,8},{1,137},{129,1},{9,129},{137,9},{2... | collective-permute-start | bytes 1572872 | tf_op jit(solution)/shard_map/ppermute | solution.py:243
  73.5 0.3 plane_sum.1
  73.8 11.4 %all_to_all.31 = bf16[8,64,128]{2,1,0:T(8,128)(2,1)S(1)} all-to-all(bf16[8,64,128]{2,1,0:T(8,128)(2,1)S(1)} %bitcast.15), channel_id=1, replica_groups=mesh['xlo'=2,'core'=2,'y'=4,'xhi'=2,'z'=8] {'z'}, dimensions={0} | all-to-all | bytes 262144 | tf_op jit(solution)/shard_map/all_to_all | solution.py:249
  85.2 0.3 collective-permute-done.1.left
  85.6 0.0 collective-permute-done.2.right
  85.6 0.1 collective-permute-start.3
  85.7 0.7 copy-done.2
  86.5 2.4 %collective-permute-start.4 = (bf16[2,512,128]{2,1,0:T(8,128)(2,1)S(1)}, bf16[2,512,128]{2,1,0:T(8,128)(2,1)S(1)}, u32[]{:S(2)}, u32[]{:S(2)}) collective-permute-start(bf16[2,512,128]{2,1,0:T(8,128)(2,1)S(1)} %slice.19), channel_id=1, source_target_pairs={{0,136},{128,0},{8,128},{136,8},{1,137},{129,1},{9,129},{137,9},{2... | collective-permute-start | bytes 786440 | tf_op jit(solution)/shard_map/ppermute | solution.py:243
  88.9 0.8 fusion.7
  89.7 0.7 broadcast_in_dim.50
  90.4 3.8 %all-to-all-start.3 = ((bf16[8,64,128]{2,1,0:T(8,128)(2,1)}), bf16[8,64,128]{2,1,0:T(8,128)(2,1)S(1)}, u32[]{:S(2)}, u32[]{:S(2)}) async-start(bf16[8,64,128]{2,1,0:T(8,128)(2,1)} %broadcast_in_dim.50), calls=%async_computation.3 | async-start | bytes 262144 | tf_op jit(solution)/shard_map/all_to_all | solution.py:249
  94.2 2.8 %collective-permute-done.6 = f32[64,128]{1,0:T(8,128)S(1)} collective-permute-done((f32[64,128]{1,0:T(8,128)S(1)}, f32[64,128]{1,0:T(8,128)S(1)}, u32[]{:S(2)}, u32[]{:S(2)}) %collective-permute-start.6) | collective-permute-done | bytes 32800 | tf_op jit(solution)/shard_map/ppermute | solution.py:294
  97.0 5.2 %all-to-all-done.3 = bf16[8,64,128]{2,1,0:T(8,128)(2,1)S(1)} async-done(((bf16[8,64,128]{2,1,0:T(8,128)(2,1)}), bf16[8,64,128]{2,1,0:T(8,128)(2,1)S(1)}, u32[]{:S(2)}, u32[]{:S(2)}) %all-to-all-start.3) | async-done | bytes 131104 | tf_op jit(solution)/shard_map/all_to_all | solution.py:249
  102.2 1.8 %broadcast_in_dim.52 = bf16[16,512,128]{2,1,0:T(8,128)(2,1)} broadcast(bf16[512,128]{1,0:T(8,128)(2,1)S(1)} %bitcast.20), dimensions={1,2} | broadcast | bytes 2228224 | tf_op jit(solution)/shard_map/broadcast_in_dim | solution.py:267
  103.9 3.8 %all-to-all-start.4 = ((bf16[16,512,128]{2,1,0:T(8,128)(2,1)}), bf16[16,512,128]{2,1,0:T(8,128)(2,1)S(1)}, u32[]{:S(2)}, u32[]{:S(2)}) async-start(bf16[16,512,128]{2,1,0:T(8,128)(2,1)} %broadcast_in_dim.52), calls=%async_computation.4 | async-start | bytes 4194304 | tf_op jit(solution)/shard_map/all_to_all | solution.py:236
  107.8 0.1 dynamic_slice.19
  107.9 3.0 %collective-permute-start.7 = (f32[64,256]{1,0:T(8,128)S(1)}, f32[64,256]{1,0:T(8,128)}, u32[]{:S(2)}, u32[]{:S(2)}) collective-permute-start(f32[64,256]{1,0:T(8,128)S(1)} %maximum_select_fusion.1), channel_id=1, source_target_pairs={{0,64},{64,0},{1,65},{65,1},{2,66},{66,2},{3,67},{67,3},{4,68},{68... | collective-permute-start | bytes 196616 | tf_op jit(solution)/shard_map/ppermute | solution.py:308
  111.0 1.0 copy-done.3
  112.0 0.9 copy-done.5
  112.9 8.1 %frozen_values.1.frozen = f32[1536,256]{1,0:T(8,128)S(1)} custom-call(s32[1]{0:T(128)} %bitcast.6.place, bf16[768,4096]{1,0:T(8,128)(2,1)} %tokens.3, bf16[768,4096]{1,0:T(8,128)(2,1)} %collective-permute-done.5.sibling, bf16[4,512,128]{2,1,0:T(8,128)(2,1)S(1)} %bitcast.14, bf16[4,512,128]{2,1,0:T(8,128)(2,1)S(1)} %collective-permute-done.1.left, ...), custom_call_target="tpu_custom_call" | custom-call | flops 3221225472 | bytes 16777216 | tf_op jit(solution)/shard_map/frozen_values/pallas_call | solution.py:178
  121.1 1.2 copy-done
  122.3 11.9 %all-to-all-done.4 = bf16[16,512,128]{2,1,0:T(8,128)(2,1)S(1)} async-done(((bf16[16,512,128]{2,1,0:T(8,128)(2,1)}), bf16[16,512,128]{2,1,0:T(8,128)(2,1)S(1)}, u32[]{:S(2)}, u32[]{:S(2)}) %all-to-all-start.4) | async-done | bytes 2097184 | tf_op jit(solution)/shard_map/all_to_all | solution.py:236
  134.2 1.4 copy-done.1
  135.6 0.0 copy-start.11
  135.6 11.7 %score_sums.1 = f32[256,1,128]{2,1,0:T(1,128)} custom-call(bf16[768,4096]{1,0:T(8,128)(2,1)} %tokens.3, bf16[768,4096]{1,0:T(8,128)(2,1)} %collective-permute-done.5.sibling, bf16[2,4096,128]{2,1,0:T(8,128)(2,1)S(1)} %bitcast.11, f32[1536,256]{1,0:T(8,128)S(1)} %copy-done.1, f32[1,256]{1,0:T(1,128)S(1)} %bitcast.16), custom_call_target="tpu_custom_call" | custom-call | flops 3221225472 | bytes 16777216 | tf_op jit(solution)/shard_map/score_sums/pallas_call | solution.py:200
  147.3 0.0 copy-start.14
  147.3 8.9 %all-to-all-start.5 = ((f32[256,1,128]{2,1,0:T(1,128)}), f32[256,1,128]{2,1,0:T(1,128)S(1)}, u32[]{:S(2)}, u32[]{:S(2)}) async-start(f32[256,1,128]{2,1,0:T(1,128)} %score_sums.1), calls=%async_computation.5 | async-start | bytes 262144 | tf_op jit(solution)/shard_map/all_to_all | solution.py:320
  156.3 0.2 slice_reduce_fusion
  156.5 1.8 %multiply_add_fusion = (f32[64,512]{1,0:T(8,128)}, f32[64,512]{1,0:T(8,128)}, f32[64,512]{1,0:T(8,128)}, f32[64,512]{1,0:T(8,128)}) fusion(f32[64,512]{1,0:T(8,128)S(1)} %copy-done.11, f32[64,512]{1,0:T(8,128)S(1)} %copy-done.8, f32[64,256]{1,0:T(8,128)S(1)} %maximum_select_fusion.1, f32[64,256]{1,0:T(8,128)} %collective-permute-done.7, pred[]{:T(512)S(6)} %eq.39, ...), kind=kLoop, calls=%fused_computation.6 | loop fusion | flops 589824 | bytes 1179649 | tf_op jit(solution)/shard_map/add | solution.py:33
  158.3 11.0 %all-to-all-done.5 = f32[256,1,128]{2,1,0:T(1,128)S(1)} async-done(((f32[256,1,128]{2,1,0:T(1,128)}), f32[256,1,128]{2,1,0:T(1,128)S(1)}, u32[]{:S(2)}, u32[]{:S(2)}) %all-to-all-start.5) | async-done | bytes 131104 | tf_op jit(solution)/shard_map/all_to_all | solution.py:320
  169.3 0.1 slice.25
  169.4 0.1 broadcast_in_dim.55
  169.5 0.2 fusion.9
  169.7 0.5 multiply_subtract_fusion
  (30 shorter events, 0.1 us)
Async XLA Ops:
  2.3 26.4 %all-to-all-start = ((bf16[32,64,128]{2,1,0:T(8,128)(2,1)}), bf16[32,64,128]{2,1,0:T(8,128)(2,1)S(1)}, u32[]{:S(2)}, u32[]{:S(2)}) async-start(bf16[32,64,128]{2,1,0:T(8,128)(2,1)} %broadcast_in_dim.49), calls=%async_computation | async-start | bytes 1048576 | tf_op jit(solution)/shard_map/all_to_all | solution.py:274
  14.4 1.1 copy-start.7
  23.5 1.3 copy-start.6
  28.7 7.5 %collective-permute-start = (bf16[2,8,128,512]{3,2,1,0:T(8,128)(2,1)}, bf16[2,8,128,512]{3,2,1,0:T(8,128)(2,1)S(1)}, u32[]{:S(2)}, u32[]{:S(2)}) collective-permute-start(bf16[2,8,128,512]{3,2,1,0:T(8,128)(2,1)} %copy-done.6), channel_id=1, source_target_pairs={{0,64},{64,0},{1,65},{65,1},{2,66},{66,2},{3,67},{67,3},{4,68},{68... | collective-permute-start | bytes 6291464 | tf_op jit(solution)/shard_map/ppermute | solution.py:279
  68.3 33.9 %collective-permute-start.5 = (bf16[768,4096]{1,0:T(8,128)(2,1)}, bf16[768,4096]{1,0:T(8,128)(2,1)}, u32[]{:S(2)}, u32[]{:S(2)}) collective-permute-start(bf16[768,4096]{1,0:T(8,128)(2,1)} %tokens.3), channel_id=1, source_target_pairs={{0,64},{64,0},{1,65},{65,1},{2,66},{66,2},{3,67},{67,3},{4,68},{68... | collective-permute-start | bytes 18874376 | tf_op jit(solution)/shard_map/ppermute | solution.py:284
  70.8 14.8 %collective-permute-start.1 = (bf16[4,512,128]{2,1,0:T(8,128)(2,1)S(1)}, bf16[4,512,128]{2,1,0:T(8,128)(2,1)S(1)}, u32[]{:S(2)}, u32[]{:S(2)}) collective-permute-start(bf16[4,512,128]{2,1,0:T(8,128)(2,1)S(1)} %bitcast.12), channel_id=1, source_target_pairs={{0,128},{128,8},{8,136},{136,0},{1,129},{129,9},{9,137},{137,1},{2... | collective-permute-start | bytes 1572872 | tf_op jit(solution)/shard_map/ppermute | solution.py:243
  71.1 14.5 %collective-permute-start.2 = (bf16[4,512,128]{2,1,0:T(8,128)(2,1)S(1)}, bf16[4,512,128]{2,1,0:T(8,128)(2,1)S(1)}, u32[]{:S(2)}, u32[]{:S(2)}) collective-permute-start(bf16[4,512,128]{2,1,0:T(8,128)(2,1)S(1)} %bitcast.13), channel_id=1, source_target_pairs={{0,136},{128,0},{8,128},{136,8},{1,137},{129,1},{9,129},{137,9},{2... | collective-permute-start | bytes 1572872 | tf_op jit(solution)/shard_map/ppermute | solution.py:243
  85.6 0.9 copy-start.2
  85.6 16.5 %collective-permute-start.3 = (bf16[2,512,128]{2,1,0:T(8,128)(2,1)S(1)}, bf16[2,512,128]{2,1,0:T(8,128)(2,1)S(1)}, u32[]{:S(2)}, u32[]{:S(2)}) collective-permute-start(bf16[2,512,128]{2,1,0:T(8,128)(2,1)S(1)} %slice.18), channel_id=1, source_target_pairs={{0,128},{128,8},{8,136},{136,0},{1,129},{129,9},{9,137},{137,1},{2... | collective-permute-start | bytes 786440 | tf_op jit(solution)/shard_map/ppermute | solution.py:243
  86.5 15.7 %collective-permute-start.4 = (bf16[2,512,128]{2,1,0:T(8,128)(2,1)S(1)}, bf16[2,512,128]{2,1,0:T(8,128)(2,1)S(1)}, u32[]{:S(2)}, u32[]{:S(2)}) collective-permute-start(bf16[2,512,128]{2,1,0:T(8,128)(2,1)S(1)} %slice.19), channel_id=1, source_target_pairs={{0,136},{128,0},{8,128},{136,8},{1,137},{129,1},{9,129},{137,9},{2... | collective-permute-start | bytes 786440 | tf_op jit(solution)/shard_map/ppermute | solution.py:243
  90.4 11.8 %all-to-all-start.3 = ((bf16[8,64,128]{2,1,0:T(8,128)(2,1)}), bf16[8,64,128]{2,1,0:T(8,128)(2,1)S(1)}, u32[]{:S(2)}, u32[]{:S(2)}) async-start(bf16[8,64,128]{2,1,0:T(8,128)(2,1)} %broadcast_in_dim.50), calls=%async_computation.3 | async-start | bytes 262144 | tf_op jit(solution)/shard_map/all_to_all | solution.py:249
  94.2 2.8 %collective-permute-start.6 = (f32[64,128]{1,0:T(8,128)S(1)}, f32[64,128]{1,0:T(8,128)S(1)}, u32[]{:S(2)}, u32[]{:S(2)}) collective-permute-start(f32[64,128]{1,0:T(8,128)S(1)} %convert_reduce_fusion), channel_id=1, source_target_pairs={{0,128},{128,0},{1,129},{129,1},{2,130},{130,2},{3,131},{131,3},{4... | collective-permute-start | bytes 98312 | tf_op jit(solution)/shard_map/ppermute | solution.py:294
  102.2 1.8 %copy-start.4 = (bf16[2,512,128]{2,1,0:T(8,128)(2,1)}, bf16[2,512,128]{2,1,0:T(8,128)(2,1)S(1)}, u32[]{:S(2)}) copy-start(bf16[2,512,128]{2,1,0:T(8,128)(2,1)S(1)} %collective-permute-done.4.far_right) | copy-start | bytes 786436
  103.9 3.9 %copy-start.13 = (f32[512]{0:T(512)S(1)}, f32[512]{0:T(512)}, u32[]{:S(2)}) copy-start(f32[512]{0:T(512)} %param.15) | copy-start | bytes 6148
  103.9 30.3 %all-to-all-start.4 = ((bf16[16,512,128]{2,1,0:T(8,128)(2,1)}), bf16[16,512,128]{2,1,0:T(8,128)(2,1)S(1)}, u32[]{:S(2)}, u32[]{:S(2)}) async-start(bf16[16,512,128]{2,1,0:T(8,128)(2,1)} %broadcast_in_dim.52), calls=%async_computation.4 | async-start | bytes 4194304 | tf_op jit(solution)/shard_map/all_to_all | solution.py:236
  107.9 48.6 %collective-permute-start.7 = (f32[64,256]{1,0:T(8,128)S(1)}, f32[64,256]{1,0:T(8,128)}, u32[]{:S(2)}, u32[]{:S(2)}) collective-permute-start(f32[64,256]{1,0:T(8,128)S(1)} %maximum_select_fusion.1), channel_id=1, source_target_pairs={{0,64},{64,0},{1,65},{65,1},{2,66},{66,2},{3,67},{67,3},{4,68},{68... | collective-permute-start | bytes 196616 | tf_op jit(solution)/shard_map/ppermute | solution.py:308
  111.0 1.0 copy-start.3
  112.0 0.9 copy-start.5
  121.1 1.2 copy-start
  134.2 1.4 copy-start.1
  135.6 20.7 %copy-start.12 = (s32[2,2]{1,0:T(2,128)S(1)}, s32[2,2]{1,0:T(2,128)}, u32[]{:S(2)}) copy-start(s32[2,2]{1,0:T(2,128)} %param.16) | copy-start | bytes 52
  135.6 20.9 %copy-start.8 = (f32[64,512]{1,0:T(8,128)S(1)}, f32[64,512]{1,0:T(8,128)}, u32[]{:S(2)}) copy-start(f32[64,512]{1,0:T(8,128)} %param.11) | copy-start | bytes 393220
  135.6 20.9 %copy-start.9 = (f32[64,512]{1,0:T(8,128)S(1)}, f32[64,512]{1,0:T(8,128)}, u32[]{:S(2)}) copy-start(f32[64,512]{1,0:T(8,128)} %param.13) | copy-start | bytes 393220
  135.6 20.9 %copy-start.10 = (f32[64,512]{1,0:T(8,128)S(1)}, f32[64,512]{1,0:T(8,128)}, u32[]{:S(2)}) copy-start(f32[64,512]{1,0:T(8,128)} %param.14) | copy-start | bytes 393220
  135.6 20.9 %copy-start.11 = (f32[64,512]{1,0:T(8,128)S(1)}, f32[64,512]{1,0:T(8,128)}, u32[]{:S(2)}) copy-start(f32[64,512]{1,0:T(8,128)} %param.12) | copy-start | bytes 393220
  147.3 22.4 %copy-start.14 = (s32[2]{0:T(128)S(1)}, s32[2]{0:T(128)}, u32[]{:S(2)}) copy-start(s32[2]{0:T(128)} %param.17) | copy-start | bytes 28
  147.3 21.9 %all-to-all-start.5 = ((f32[256,1,128]{2,1,0:T(1,128)}), f32[256,1,128]{2,1,0:T(1,128)S(1)}, u32[]{:S(2)}, u32[]{:S(2)}) async-start(f32[256,1,128]{2,1,0:T(1,128)} %score_sums.1), calls=%async_computation.5 | async-start | bytes 262144 | tf_op jit(solution)/shard_map/all_to_all | solution.py:320

commit v4 on v3

--- a/solution.py
+++ b/solution.py
@@ -54,52 +54,80 @@
 VMEM_SCORE = 32 << 20
 
 
-def gradient_kernel(core, cotangent, tokens, sent, own, turned):
-    half = cotangent.shape[1] // 2
-    quarter = half // 2
-
-    @pl.when(pl.program_id(0) == 0)
-    def _():
-        away = pl.multiple_of((1 - core[0]) * half, half)
-        here = pl.multiple_of(core[0] * half, half)
-        turned[:half] = cotangent[:, pl.ds(away, half)].T
-        turned[half:] = cotangent[:, pl.ds(here, half)].T
-
-    product = jnp.dot(turned[...], tokens[...], preferred_element_type=jnp.float32)
-    sent[0, 0] = product[:quarter].astype(sent.dtype)
-    sent[1, 0] = product[quarter:half].astype(sent.dtype)
-    own[0, 0] = product[half : half + quarter].astype(own.dtype)
-    own[1, 0] = product[half + quarter :].astype(own.dtype)
-
-
-def gradient_blocks(core, cotangent, tokens):
+def in_hbm(array):
+    return pltpu.with_memory_space_constraint(array, pltpu.HBM)
+
+
+def gradient_kernel(place, cotangent, tokens, anchor, sent, own, message, held, turned, sems):
+    channels = held.shape[1]
+    half, quarter = channels // 2, channels // 4
+    width = sent.shape[3]
+    core = place[0]
+    halves = [
+        pltpu.make_async_copy(
+            cotangent.at[:, pl.ds(pl.multiple_of(which * half, half), half)],
+            held.at[:, pl.ds(at * half, half)],
+            sems.at[at],
+        )
+        for at, which in enumerate((1 - core, core))
+    ]
+    blocks = [
+        pltpu.make_async_copy(
+            tokens.at[:, pl.ds(at * width, width)],
+            turned.at[:, pl.ds(at * width, width)],
+            sems.at[2 + at],
+        )
+        for at in range(8)
+    ]
+    for load in halves + blocks:
+        load.start()
+    lanes = pl.ds(pl.multiple_of(place[1] * quarter, quarter), quarter)
+    piece = anchor[:, lanes].astype(message.dtype)
+    for at in range(message.shape[0]):
+        message[at] = piece
+    for load in halves:
+        load.wait()
+    for at, load in enumerate(blocks):
+        load.wait()
+        product = lax.dot_general(
+            held[...],
+            turned[:, at * width : (at + 1) * width],
+            (((0,), (0,)), ((), ())),
+            preferred_element_type=jnp.float32,
+        ).astype(sent.dtype)
+        sent[0, at] = product[:quarter]
+        sent[1, at] = product[quarter:half]
+        own[0, at] = product[half : half + quarter]
+        own[1, at] = product[half + quarter :]
+
+
+def gradient_blocks(place, cotangent, tokens, anchor):
     count, features = tokens.shape
     channels = cotangent.shape[1]
     quarter = channels // 4
     width = features // 8
-    block = pl.BlockSpec((2, 1, quarter, width), lambda i, core: (0, i, 0, 0))
+    block = pltpu.VMEM((2, 8, quarter, width), jnp.bfloat16)
     return pl.pallas_call(
         gradient_kernel,
-        grid_spec=pltpu.PrefetchScalarGridSpec(
-            num_scalar_prefetch=1,
-            grid=(8,),
-            in_specs=[
-                pl.BlockSpec((count, channels), lambda i, core: (0, 0)),
-                pl.BlockSpec((count, width), lambda i, core: (0, i)),
-            ],
-            out_specs=[block, block],
-            scratch_shapes=[pltpu.VMEM((channels, count), jnp.bfloat16)],
-        ),
-        out_shape=[
-            jax.ShapeDtypeStruct((2, 8, quarter, width), jnp.bfloat16),
-            jax.ShapeDtypeStruct((2, 8, quarter, width), jnp.bfloat16),
+        in_specs=[
+            pl.BlockSpec(memory_space=pltpu.SMEM),
+            pl.BlockSpec(memory_space=pltpu.HBM),
+            pl.BlockSpec(memory_space=pltpu.HBM),
+            pl.BlockSpec(memory_space=pltpu.VMEM),
+        ],
+        out_specs=[pl.BlockSpec(memory_space=pltpu.VMEM)] * 3,
+        out_shape=[block, block, jax.ShapeDtypeStruct((32, anchor.shape[0], quarter), jnp.bfloat16)],
+        scratch_shapes=[
+            pltpu.VMEM(cotangent.shape, cotangent.dtype),
+            pltpu.VMEM(tokens.shape, tokens.dtype),
+            pltpu.SemaphoreType.DMA((10,)),
         ],
         cost_estimate=pl.CostEstimate(
             flops=2 * count * features * channels, bytes_accessed=12 << 20, transcendentals=0
         ),
         compiler_params=pltpu.CompilerParams(vmem_limit_bytes=VMEM_GRADIENT),
         name="gradient_blocks",
-    )(core, cotangent, tokens)
+    )(place, in_hbm(cotangent), in_hbm(tokens), anchor)
 
 
 def frozen_kernel(place, tokens, sibling, here, left, right, far_left, far_right, out, joined):
@@ -134,34 +162,44 @@
     return low_sum - jnp.log(product)
 
 
-def score_kernel(tokens, sibling, halves, frozen, readout, out, joined, held, sems):
+def score_kernel(tokens, sibling, halves, frozen, readout, out, joined, held, still, sems):
     quarter = halves.shape[-1]
     count = tokens.shape[0]
-    loads = [
-        pltpu.make_async_copy(
-            source.at[pl.ds(first, LEN)], held.at[pl.ds(base + first, LEN)], sems.at[at]
+    sizes = (2 * LEN, 2 * LEN, 2 * LEN, LEN, LEN)
+    loads, at = [], 0
+    for step, size in enumerate(sizes):
+        source, first = (tokens, at) if at < count else (sibling, at - count)
+        span = pl.ds(at, size)
+        loads.append(
+            (
+                pltpu.make_async_copy(
+                    source.at[pl.ds(first, size)], held.at[span], sems.at[2 * step]
+                ),
+                pltpu.make_async_copy(frozen.at[span], still.at[span], sems.at[2 * step + 1]),
+            )
         )
-        for at, (source, base, first) in enumerate(
-            (source, base, first)
-            for source, base in ((tokens, 0), (sibling, count))
-            for first in range(0, count, LEN)
-        )
-    ]
-    for load in loads:
-        load.start()
+        at += size
+    for pair in loads:
+        for load in pair:
+            load.start()
     joined[:, :quarter] = halves[0]
     joined[:, quarter:] = halves[1]
     scale = readout[...]
-    lane = lax.broadcasted_iota(jnp.int32, out.shape, 2)
-    parts = jnp.zeros(out.shape, jnp.float32)
-    for sequence, load in enumerate(loads):
-        load.wait()
-        rows = slice(sequence * LEN, (sequence + 1) * LEN)
-        values = jnp.dot(held[rows], joined[...], preferred_element_type=jnp.float32)
-        blended = blend_rate * values + (1.0 - blend_rate) * frozen[rows]
-        gap = sigmoid_sums(values * scale) - sigmoid_sums(blended * scale)
-        parts = jnp.where(lane == sequence, jnp.sum(gap) / LEN, parts)
-    out[...] = parts
+    lane = lax.broadcasted_iota(jnp.int32, (1, 128), 1)
+    parts = jnp.zeros((1, 128), jnp.float32)
+    at = 0
+    for pair, size in zip(loads, sizes):
+        for load in pair:
+            load.wait()
+        values = jnp.dot(held[at : at + size], joined[...], preferred_element_type=jnp.float32)
+        blended = blend_rate * values + (1.0 - blend_rate) * still[at : at + size]
+        values, blended = values * scale, blended * scale
+        for first in range(0, size, LEN):
+            rows = slice(first, first + LEN)
+            gap = sigmoid_sums(values[rows]) - sigmoid_sums(blended[rows])
+            parts = jnp.where(lane == (at + first) // LEN, jnp.sum(gap) / LEN, parts)
+        at += size
+    out[...] = jnp.broadcast_to(parts[None], out.shape)
 
 
 def token_specs(count, features):
@@ -191,7 +229,7 @@
         ),
         compiler_params=pltpu.CompilerParams(vmem_limit_bytes=VMEM),
         name="frozen_values",
-    )(place, tokens, sibling, *strips)
+    )(place, in_hbm(tokens), in_hbm(sibling), *strips)
 
 
 def score_sums(tokens, sibling, halves, frozen, readout):
@@ -200,19 +238,25 @@
     return pl.pallas_call(
         score_kernel,
         out_shape=jax.ShapeDtypeStruct((256, 1, 128), jnp.float32),
-        in_specs=[pl.BlockSpec(memory_space=pl.ANY)] * 2
-        + [pl.BlockSpec(memory_space=pltpu.VMEM)] * 3,
+        in_specs=[
+            pl.BlockSpec(memory_space=pltpu.HBM),
+            pl.BlockSpec(memory_space=pltpu.HBM),
+            pl.BlockSpec(memory_space=pltpu.VMEM),
+            pl.BlockSpec(memory_space=pltpu.HBM),
+            pl.BlockSpec(memory_space=pltpu.VMEM),
+        ],
         scratch_shapes=[
             pltpu.VMEM((features, width), jnp.bfloat16),
             pltpu.VMEM((2 * count, features), tokens.dtype),
-            pltpu.SemaphoreType.DMA((2 * count // LEN,)),
+            pltpu.VMEM(frozen.shape, frozen.dtype),
+            pltpu.SemaphoreType.DMA((10,)),
         ],
         cost_estimate=pl.CostEstimate(
             flops=4 * count * features * width, bytes_accessed=16 << 20, transcendentals=0
         ),
         compiler_params=pltpu.CompilerParams(vmem_limit_bytes=VMEM_SCORE),
         name="score_sums",
-    )(tokens, sibling, halves, frozen, readout)
+    )(in_hbm(tokens), in_hbm(sibling), halves, in_hbm(frozen), readout)
 
 
 def plane_sum_kernel(blocks, out):
@@ -269,16 +313,15 @@
     def joined_halves(plane):
         return plane.reshape(2, features, quarter)
 
-    anchor_copies = jnp.broadcast_to(piece(anchor).astype(jnp.bfloat16)[None], (32, rows, quarter))
-    anchor_copies, cotangent = lax.optimization_barrier((anchor_copies, cotangent))
+    sent, own, anchor_copies = gradient_blocks(
+        jnp.stack([core, core * 2 + low]), cotangent, tokens, anchor
+    )
+    arrived = lax.ppermute(sent, "core", SWAP)
     strips = lax.all_to_all(anchor_copies, ("y", "z"), 0, 0, tiled=True)
     strips = strips.reshape(4, 8 * rows, quarter)
-
-    sent, own = gradient_blocks(core[None], cotangent, tokens)
-    sent, strips = lax.optimization_barrier((sent, strips))
-    arrived = lax.ppermute(sent, "core", SWAP)
     blocks = own.astype(jnp.float32) + arrived.astype(jnp.float32)
     blocks = blocks.astype(jnp.bfloat16)
+    blocks, strips = lax.optimization_barrier((blocks, strips))
     plane = to_plane(blocks.reshape(16, quarter, 8 * rows))
     plane, strips, tokens = lax.optimization_barrier((plane, strips, tokens))
     sibling = lax.ppermute(tokens, "core", SWAP)

time: 171 us -> 171 us (level)
  blocking collectives: 42.8 us -> 31.8 us
  waiting for transfers between devices: 39 us -> 47.5 us
  local copies, waits for them, and re-layouts: 12.5 us -> 7.09 us
  starting transfers between devices: 42.9 us -> 47.6 us
  other arithmetic: 4.07 us -> 7.05 us
    all_to_all x1 -> x0, blocking collectives: 11.4 us -> none  [along_z(): return lax.all_to_all(blocks, 'z', 0, 0, tiled=True)]
    all_to_all x1 -> x2, waiting for transfers between devices: 5.18 us -> 12.8 us  [along_z(): return lax.all_to_all(blocks, 'z', 0, 0, tiled=True)]
    all_to_all x1, waiting for transfers between devices: 3.84 us -> 11.3 us  [shards(): strips = lax.all_to_all(anchor_copies, ('y', 'z'), 0, 0, tiled=True)]
    all_to_all x1 -> x2, starting transfers between devices: 3.81 us -> 8.07 us  [along_z(): return lax.all_to_all(blocks, 'z', 0, 0, tiled=True)]
    ppermute x1, waiting for transfers between devices: 4 us -> 0.01 us  [shards(): arrived = lax.ppermute(sent, 'core', SWAP)]
    unnamed x30 -> x26, local copies, waits for them, and re-layouts: 7.85 us -> 4.15 us
    convert_element_type x1, other arithmetic: 0.68 us -> 3.58 us  [shards(): blocks = blocks.astype(jnp.bfloat16)]
    all_to_all x1, starting transfers between devices: 12 us -> 9.47 us  [shards(): strips = lax.all_to_all(anchor_copies, ('y', 'z'), 0, 0, tiled=True)]
  transfers between devices with their start and end apart: 12 -> 13, of which waited for: 7 -> 6; matrix products, arithmetic and copies ran while one was open for 2% -> 4% of each run, Pallas kernels for 17% -> 12%
where the time goes in v4:
time: 171 us
  starting transfers between devices  47.6 us (28%)
  waiting for transfers between devices  47.5 us (28%)
  blocking collectives  31.8 us (19%)
  Pallas kernels  28.6 us (17%)
  local copies, waits for them, and re-layouts  7.09 us (4%)
  other arithmetic  7.05 us (4%)
    all_to_all x1, blocking collectives, to_plane(): return lax.all_to_all(blocks, PLANE, 0, 0, tiled=True)  31.8 us
    all_to_all x2, waiting for transfers between devices, along_z(): return lax.all_to_all(blocks, 'z', 0, 0, tiled=True)  12.8 us
    pallas_call x1, Pallas kernels, score_sums(): pl.pallas_call(score_kernel, out_shape=jax.ShapeDtypeStruct((256, 1, 128)...  11.4 us
    all_to_all x1, waiting for transfers between devices, shards(): strips = lax.all_to_all(anchor_copies, ('y', 'z'), 0, 0, tiled=True)  11.3 us
    all_to_all x1, waiting for transfers between devices, shards(): parts = lax.all_to_all(parts, AXES, 0, 0, tiled=True)  11 us
    all_to_all x1, waiting for transfers between devices, to_plane(): return lax.all_to_all(blocks, PLANE, 0, 0, tiled=True)  9.71 us
    all_to_all x1, starting transfers between devices, shards(): parts = lax.all_to_all(parts, AXES, 0, 0, tiled=True)  9.57 us
    all_to_all x1, starting transfers between devices, shards(): strips = lax.all_to_all(anchor_copies, ('y', 'z'), 0, 0, tiled=True)  9.47 us
  transfers between devices with their start and end apart: 13, of which 6 were waited for; matrix products, arithmetic and copies ran while one was open for 4% of the time, Pallas kernels for 12%

profile of v4, /device:TPU:1, one launch (start us, length us, event | category | flops | bytes accessed | tf_op | source)
XLA Modules:
  0.0 170.6 jit_solution(9015001221152451714)
XLA Ops:
  0.6 0.1 pad_add_fusion.place
  0.7 0.9 copy-done.5
  1.6 8.1 %gradient_blocks.1 = (bf16[2,8,128,512]{3,2,1,0:T(8,128)(2,1)}, bf16[2,8,128,512]{3,2,1,0:T(8,128)(2,1)S(1)}, bf16[32,64,128]{2,1,0:T(8,128)(2,1)}) custom-call(s32[2]{0:T(128)S(1)} %pad_add_fusion.place, bf16[768,512]{1,0:T(8,128)(2,1)} %cotangent.1, bf16[768,4096]{1,0:T(8,128)(2,1)} %tokens.3, f32[64,512]{1,0:T(8,128)S(1)} %copy-done.5), custom_call_target="tpu_custom_call" | custom-call | flops 3221225472 | bytes 12582912 | tf_op jit(solution)/shard_map/gradient_blocks/pallas_call | solution.py:110
  9.8 3.3 %collective-permute-start = (bf16[2,8,128,512]{3,2,1,0:T(8,128)(2,1)}, bf16[2,8,128,512]{3,2,1,0:T(8,128)(2,1)}, u32[]{:S(2)}, u32[]{:S(2)}) collective-permute-start(bf16[2,8,128,512]{3,2,1,0:T(8,128)(2,1)} %get-tuple-element.22), channel_id=1, source_target_pairs={{0,64},{64,0},{1,65},{65,1},{2,66},{66,2},{3,67},{67,3},{4,68},{68... | collective-permute-start | bytes 6291464 | tf_op jit(solution)/shard_map/ppermute | solution.py:319
  13.1 9.5 %all-to-all-start = ((bf16[32,64,128]{2,1,0:T(8,128)(2,1)}), bf16[32,64,128]{2,1,0:T(8,128)(2,1)S(1)}, u32[]{:S(2)}, u32[]{:S(2)}) async-start(bf16[32,64,128]{2,1,0:T(8,128)(2,1)} %get-tuple-element.23), calls=%async_computation | async-start | bytes 1048576 | tf_op jit(solution)/shard_map/all_to_all | solution.py:320
  22.6 0.0 collective-permute-done
  22.6 3.6 %add_convert_fusion = bf16[2,8,128,512]{3,2,1,0:T(8,128)(2,1)} fusion(bf16[2,8,128,512]{3,2,1,0:T(8,128)(2,1)} %collective-permute-done, bf16[2,8,128,512]{3,2,1,0:T(8,128)(2,1)S(1)} %get-tuple-element.21), kind=kLoop, calls=%fused_computation | loop fusion | flops 4194304 | bytes 6291456 | tf_op jit(solution)/shard_map/convert_element_type | solution.py:323
  26.1 11.3 %all-to-all-done = bf16[32,64,128]{2,1,0:T(8,128)(2,1)S(1)} async-done(((bf16[32,64,128]{2,1,0:T(8,128)(2,1)}), bf16[32,64,128]{2,1,0:T(8,128)(2,1)S(1)}, u32[]{:S(2)}, u32[]{:S(2)}) %all-to-all-start) | async-done | bytes 524320 | tf_op jit(solution)/shard_map/all_to_all | solution.py:320
  37.5 31.8 %all_to_all.30.blocks = bf16[16,128,512]{2,1,0:T(8,128)(2,1)S(1)} all-to-all(bf16[16,128,512]{2,1,0:T(8,128)(2,1)} %bitcast.17), channel_id=1, replica_groups=mesh['xlo'=2,'core'=2,'y'=4,'xhi'=2,'z'=8] {'xlo','y','xhi'}, dimensions={0} | all-to-all | bytes 4194304 | tf_op jit(solution)/shard_map/all_to_all | solution.py:280
  69.3 3.5 %collective-permute-start.5 = (bf16[768,4096]{1,0:T(8,128)(2,1)}, bf16[768,4096]{1,0:T(8,128)(2,1)}, u32[]{:S(2)}, u32[]{:S(2)}) collective-permute-start(bf16[768,4096]{1,0:T(8,128)(2,1)} %tokens.3), channel_id=1, source_target_pairs={{0,64},{64,0},{1,65},{65,1},{2,66},{66,2},{3,67},{67,3},{4,68},{68... | collective-permute-start | bytes 18874376 | tf_op jit(solution)/shard_map/ppermute | solution.py:327
  72.8 1.5 collective-permute-start.1
  74.3 1.2 collective-permute-start.2
  75.4 1.0 plane_sum.1
  76.4 4.7 %all-to-all-start.2 = ((bf16[8,64,128]{2,1,0:T(8,128)(2,1)}), bf16[8,64,128]{2,1,0:T(8,128)(2,1)S(1)}, u32[]{:S(2)}, u32[]{:S(2)}) async-start(bf16[8,64,128]{2,1,0:T(8,128)(2,1)} %bitcast.4), calls=%async_computation.2 | async-start | bytes 262144 | tf_op jit(solution)/shard_map/all_to_all | solution.py:293
  81.1 7.8 %all-to-all-done.2 = bf16[8,64,128]{2,1,0:T(8,128)(2,1)S(1)} async-done(((bf16[8,64,128]{2,1,0:T(8,128)(2,1)}), bf16[8,64,128]{2,1,0:T(8,128)(2,1)S(1)}, u32[]{:S(2)}, u32[]{:S(2)}) %all-to-all-start.2) | async-done | bytes 131104 | tf_op jit(solution)/shard_map/all_to_all | solution.py:293
  88.9 0.0 collective-permute-done.1.left
  88.9 0.0 collective-permute-done.2.right
  89.0 0.3 collective-permute-start.3
  89.3 2.5 %collective-permute-start.4 = (bf16[2,512,128]{2,1,0:T(8,128)(2,1)S(1)}, bf16[2,512,128]{2,1,0:T(8,128)(2,1)S(1)}, u32[]{:S(2)}, u32[]{:S(2)}) collective-permute-start(bf16[2,512,128]{2,1,0:T(8,128)(2,1)S(1)} %slice.19), channel_id=1, source_target_pairs={{0,136},{128,0},{8,128},{136,8},{1,137},{129,1},{9,129},{137,9},{2... | collective-permute-start | bytes 786440 | tf_op jit(solution)/shard_map/ppermute | solution.py:287
  91.8 0.8 fusion.7
  92.7 0.7 broadcast_in_dim.39
  93.3 3.4 %all-to-all-start.3 = ((bf16[8,64,128]{2,1,0:T(8,128)(2,1)}), bf16[8,64,128]{2,1,0:T(8,128)(2,1)S(1)}, u32[]{:S(2)}, u32[]{:S(2)}) async-start(bf16[8,64,128]{2,1,0:T(8,128)(2,1)} %broadcast_in_dim.39), calls=%async_computation.3 | async-start | bytes 262144 | tf_op jit(solution)/shard_map/all_to_all | solution.py:293
  96.7 0.1 collective-permute-start.6
  96.8 2.8 %collective-permute-done.6 = f32[64,128]{1,0:T(8,128)S(1)} collective-permute-done((f32[64,128]{1,0:T(8,128)S(1)}, f32[64,128]{1,0:T(8,128)S(1)}, u32[]{:S(2)}, u32[]{:S(2)}) %collective-permute-start.6) | collective-permute-done | bytes 32800 | tf_op jit(solution)/shard_map/ppermute | solution.py:337
  99.6 5.0 %all-to-all-done.3 = bf16[8,64,128]{2,1,0:T(8,128)(2,1)S(1)} async-done(((bf16[8,64,128]{2,1,0:T(8,128)(2,1)}), bf16[8,64,128]{2,1,0:T(8,128)(2,1)S(1)}, u32[]{:S(2)}, u32[]{:S(2)}) %all-to-all-start.3) | async-done | bytes 131104 | tf_op jit(solution)/shard_map/all_to_all | solution.py:293
  104.6 0.0 collective-permute-done.3.far_left
  104.6 0.0 collective-permute-done.4.far_right
  104.6 0.0 collective-permute-done.5.sibling
  104.6 1.8 %broadcast_in_dim.41 = bf16[16,512,128]{2,1,0:T(8,128)(2,1)} broadcast(bf16[512,128]{1,0:T(8,128)(2,1)S(1)} %bitcast.20), dimensions={1,2} | broadcast | bytes 2228224 | tf_op jit(solution)/shard_map/broadcast_in_dim | solution.py:311
  106.3 3.9 %all-to-all-start.4 = ((bf16[16,512,128]{2,1,0:T(8,128)(2,1)}), bf16[16,512,128]{2,1,0:T(8,128)(2,1)S(1)}, u32[]{:S(2)}, u32[]{:S(2)}) async-start(bf16[16,512,128]{2,1,0:T(8,128)(2,1)} %broadcast_in_dim.41), calls=%async_computation.4 | async-start | bytes 4194304 | tf_op jit(solution)/shard_map/all_to_all | solution.py:280
  110.2 0.1 dynamic_slice.15
  110.3 4.3 %collective-permute-start.7 = (f32[64,256]{1,0:T(8,128)S(1)}, f32[64,256]{1,0:T(8,128)}, u32[]{:S(2)}, u32[]{:S(2)}) collective-permute-start(f32[64,256]{1,0:T(8,128)S(1)} %maximum_select_fusion.1), channel_id=1, source_target_pairs={{0,64},{64,0},{1,65},{65,1},{2,66},{66,2},{3,67},{67,3},{4,68},{68... | collective-permute-start | bytes 196616 | tf_op jit(solution)/shard_map/ppermute | solution.py:351
  114.6 1.0 copy-done.2
  115.6 0.9 copy-done.4
  116.6 8.1 %frozen_values.1.frozen = f32[1536,256]{1,0:T(8,128)S(1)} custom-call(s32[1]{0:T(128)} %bitcast.7.place, bf16[768,4096]{1,0:T(8,128)(2,1)} %tokens.3, bf16[768,4096]{1,0:T(8,128)(2,1)} %collective-permute-done.5.sibling, bf16[4,512,128]{2,1,0:T(8,128)(2,1)S(1)} %bitcast.15, bf16[4,512,128]{2,1,0:T(8,128)(2,1)S(1)} %collective-permute-done.1.left, ...), custom_call_target="tpu_custom_call" | custom-call | flops 3221225472 | bytes 16777216 | tf_op jit(solution)/shard_map/frozen_values/pallas_call | solution.py:216
  124.7 1.2 copy-done
  125.9 9.7 %all-to-all-done.4 = bf16[16,512,128]{2,1,0:T(8,128)(2,1)S(1)} async-done(((bf16[16,512,128]{2,1,0:T(8,128)(2,1)}), bf16[16,512,128]{2,1,0:T(8,128)(2,1)S(1)}, u32[]{:S(2)}, u32[]{:S(2)}) %all-to-all-start.4) | async-done | bytes 2097184 | tf_op jit(solution)/shard_map/all_to_all | solution.py:280
  135.7 0.0 copy-start.9
  135.7 11.4 %score_sums.1 = f32[256,1,128]{2,1,0:T(1,128)} custom-call(bf16[768,4096]{1,0:T(8,128)(2,1)} %tokens.3, bf16[768,4096]{1,0:T(8,128)(2,1)} %collective-permute-done.5.sibling, bf16[2,4096,128]{2,1,0:T(8,128)(2,1)S(1)} %bitcast.12, f32[1536,256]{1,0:T(8,128)} %copy-done, f32[1,256]{1,0:T(1,128)S(1)} %bitcast.16), custom_call_target="tpu_custom_call" | custom-call | flops 3221225472 | bytes 16777216 | tf_op jit(solution)/shard_map/score_sums/pallas_call | solution.py:238
  147.0 0.0 copy-start.12
  147.1 9.6 %all-to-all-start.5 = ((f32[256,1,128]{2,1,0:T(1,128)}), f32[256,1,128]{2,1,0:T(1,128)S(1)}, u32[]{:S(2)}, u32[]{:S(2)}) async-start(f32[256,1,128]{2,1,0:T(1,128)} %score_sums.1), calls=%async_computation.5 | async-start | bytes 262144 | tf_op jit(solution)/shard_map/all_to_all | solution.py:363
  156.6 0.2 slice_reduce_fusion
  156.9 1.8 %multiply_add_fusion = (f32[64,512]{1,0:T(8,128)}, f32[64,512]{1,0:T(8,128)}, f32[64,512]{1,0:T(8,128)}, f32[64,512]{1,0:T(8,128)}) fusion(f32[64,512]{1,0:T(8,128)S(1)} %copy-done.6, f32[64,512]{1,0:T(8,128)S(1)} %copy-done.7, f32[64,256]{1,0:T(8,128)S(1)} %maximum_select_fusion.1, f32[64,256]{1,0:T(8,128)} %collective-permute-done.7, pred[]{:T(512)S(6)} %eq.39, ...), kind=kLoop, calls=%fused_computation.6 | loop fusion | flops 589824 | bytes 1179649 | tf_op jit(solution)/shard_map/add | solution.py:33
  158.6 11.0 %all-to-all-done.5 = f32[256,1,128]{2,1,0:T(1,128)S(1)} async-done(((f32[256,1,128]{2,1,0:T(1,128)}), f32[256,1,128]{2,1,0:T(1,128)S(1)}, u32[]{:S(2)}, u32[]{:S(2)}) %all-to-all-start.5) | async-done | bytes 131104 | tf_op jit(solution)/shard_map/all_to_all | solution.py:363
  169.6 0.1 slice.25
  169.7 0.1 broadcast_in_dim.44
  169.8 0.2 fusion.9
  170.1 0.5 multiply_subtract_fusion
  (26 shorter events, 0.1 us)
Async XLA Ops:
  0.7 0.9 copy-start.5
  9.8 12.8 %collective-permute-start = (bf16[2,8,128,512]{3,2,1,0:T(8,128)(2,1)}, bf16[2,8,128,512]{3,2,1,0:T(8,128)(2,1)}, u32[]{:S(2)}, u32[]{:S(2)}) collective-permute-start(bf16[2,8,128,512]{3,2,1,0:T(8,128)(2,1)} %get-tuple-element.22), channel_id=1, source_target_pairs={{0,64},{64,0},{1,65},{65,1},{2,66},{66,2},{3,67},{67,3},{4,68},{68... | collective-permute-start | bytes 6291464 | tf_op jit(solution)/shard_map/ppermute | solution.py:319
  13.1 24.4 %all-to-all-start = ((bf16[32,64,128]{2,1,0:T(8,128)(2,1)}), bf16[32,64,128]{2,1,0:T(8,128)(2,1)S(1)}, u32[]{:S(2)}, u32[]{:S(2)}) async-start(bf16[32,64,128]{2,1,0:T(8,128)(2,1)} %get-tuple-element.23), calls=%async_computation | async-start | bytes 1048576 | tf_op jit(solution)/shard_map/all_to_all | solution.py:320
  69.3 35.3 %collective-permute-start.5 = (bf16[768,4096]{1,0:T(8,128)(2,1)}, bf16[768,4096]{1,0:T(8,128)(2,1)}, u32[]{:S(2)}, u32[]{:S(2)}) collective-permute-start(bf16[768,4096]{1,0:T(8,128)(2,1)} %tokens.3), channel_id=1, source_target_pairs={{0,64},{64,0},{1,65},{65,1},{2,66},{66,2},{3,67},{67,3},{4,68},{68... | collective-permute-start | bytes 18874376 | tf_op jit(solution)/shard_map/ppermute | solution.py:327
  72.8 16.2 %collective-permute-start.1 = (bf16[4,512,128]{2,1,0:T(8,128)(2,1)S(1)}, bf16[4,512,128]{2,1,0:T(8,128)(2,1)S(1)}, u32[]{:S(2)}, u32[]{:S(2)}) collective-permute-start(bf16[4,512,128]{2,1,0:T(8,128)(2,1)S(1)} %bitcast.13), channel_id=1, source_target_pairs={{0,128},{128,8},{8,136},{136,0},{1,129},{129,9},{9,137},{137,1},{2... | collective-permute-start | bytes 1572872 | tf_op jit(solution)/shard_map/ppermute | solution.py:287
  74.3 14.7 %collective-permute-start.2 = (bf16[4,512,128]{2,1,0:T(8,128)(2,1)S(1)}, bf16[4,512,128]{2,1,0:T(8,128)(2,1)S(1)}, u32[]{:S(2)}, u32[]{:S(2)}) collective-permute-start(bf16[4,512,128]{2,1,0:T(8,128)(2,1)S(1)} %bitcast.14), channel_id=1, source_target_pairs={{0,136},{128,0},{8,128},{136,8},{1,137},{129,1},{9,129},{137,9},{2... | collective-permute-start | bytes 1572872 | tf_op jit(solution)/shard_map/ppermute | solution.py:287
  76.4 12.5 %all-to-all-start.2 = ((bf16[8,64,128]{2,1,0:T(8,128)(2,1)}), bf16[8,64,128]{2,1,0:T(8,128)(2,1)S(1)}, u32[]{:S(2)}, u32[]{:S(2)}) async-start(bf16[8,64,128]{2,1,0:T(8,128)(2,1)} %bitcast.4), calls=%async_computation.2 | async-start | bytes 262144 | tf_op jit(solution)/shard_map/all_to_all | solution.py:293
  89.0 17.4 %copy-start.1 = (bf16[4,512,128]{2,1,0:T(8,128)(2,1)}, bf16[4,512,128]{2,1,0:T(8,128)(2,1)S(1)}, u32[]{:S(2)}) copy-start(bf16[4,512,128]{2,1,0:T(8,128)(2,1)S(1)} %collective-permute-done.2.right) | copy-start | bytes 1572868
  89.0 15.6 %collective-permute-start.3 = (bf16[2,512,128]{2,1,0:T(8,128)(2,1)S(1)}, bf16[2,512,128]{2,1,0:T(8,128)(2,1)S(1)}, u32[]{:S(2)}, u32[]{:S(2)}) collective-permute-start(bf16[2,512,128]{2,1,0:T(8,128)(2,1)S(1)} %slice.18), channel_id=1, source_target_pairs={{0,128},{128,8},{8,136},{136,0},{1,129},{129,9},{9,137},{137,1},{2... | collective-permute-start | bytes 786440 | tf_op jit(solution)/shard_map/ppermute | solution.py:287
  89.3 15.2 %collective-permute-start.4 = (bf16[2,512,128]{2,1,0:T(8,128)(2,1)S(1)}, bf16[2,512,128]{2,1,0:T(8,128)(2,1)S(1)}, u32[]{:S(2)}, u32[]{:S(2)}) collective-permute-start(bf16[2,512,128]{2,1,0:T(8,128)(2,1)S(1)} %slice.19), channel_id=1, source_target_pairs={{0,136},{128,0},{8,128},{136,8},{1,137},{129,1},{9,129},{137,9},{2... | collective-permute-start | bytes 786440 | tf_op jit(solution)/shard_map/ppermute | solution.py:287
  93.3 11.2 %all-to-all-start.3 = ((bf16[8,64,128]{2,1,0:T(8,128)(2,1)}), bf16[8,64,128]{2,1,0:T(8,128)(2,1)S(1)}, u32[]{:S(2)}, u32[]{:S(2)}) async-start(bf16[8,64,128]{2,1,0:T(8,128)(2,1)} %broadcast_in_dim.39), calls=%async_computation.3 | async-start | bytes 262144 | tf_op jit(solution)/shard_map/all_to_all | solution.py:293
  96.7 2.9 %collective-permute-start.6 = (f32[64,128]{1,0:T(8,128)S(1)}, f32[64,128]{1,0:T(8,128)S(1)}, u32[]{:S(2)}, u32[]{:S(2)}) collective-permute-start(f32[64,128]{1,0:T(8,128)S(1)} %convert_reduce_fusion), channel_id=1, source_target_pairs={{0,128},{128,0},{1,129},{129,1},{2,130},{130,2},{3,131},{131,3},{4... | collective-permute-start | bytes 98312 | tf_op jit(solution)/shard_map/ppermute | solution.py:337
  104.6 1.8 %copy-start.3 = (bf16[2,512,128]{2,1,0:T(8,128)(2,1)}, bf16[2,512,128]{2,1,0:T(8,128)(2,1)S(1)}, u32[]{:S(2)}) copy-start(bf16[2,512,128]{2,1,0:T(8,128)(2,1)S(1)} %collective-permute-done.4.far_right) | copy-start | bytes 786436
  106.3 3.9 %copy-start.11 = (f32[512]{0:T(512)S(1)}, f32[512]{0:T(512)}, u32[]{:S(2)}) copy-start(f32[512]{0:T(512)} %param.15) | copy-start | bytes 6148
  106.3 29.3 %all-to-all-start.4 = ((bf16[16,512,128]{2,1,0:T(8,128)(2,1)}), bf16[16,512,128]{2,1,0:T(8,128)(2,1)S(1)}, u32[]{:S(2)}, u32[]{:S(2)}) async-start(bf16[16,512,128]{2,1,0:T(8,128)(2,1)} %broadcast_in_dim.41), calls=%async_computation.4 | async-start | bytes 4194304 | tf_op jit(solution)/shard_map/all_to_all | solution.py:280
  110.3 46.5 %collective-permute-start.7 = (f32[64,256]{1,0:T(8,128)S(1)}, f32[64,256]{1,0:T(8,128)}, u32[]{:S(2)}, u32[]{:S(2)}) collective-permute-start(f32[64,256]{1,0:T(8,128)S(1)} %maximum_select_fusion.1), channel_id=1, source_target_pairs={{0,64},{64,0},{1,65},{65,1},{2,66},{66,2},{3,67},{67,3},{4,68},{68... | collective-permute-start | bytes 196616 | tf_op jit(solution)/shard_map/ppermute | solution.py:351
  114.6 1.0 copy-start.2
  115.6 0.9 copy-start.4
  124.7 1.2 copy-start
  135.7 21.0 %copy-start.10 = (s32[2,2]{1,0:T(2,128)S(1)}, s32[2,2]{1,0:T(2,128)}, u32[]{:S(2)}) copy-start(s32[2,2]{1,0:T(2,128)} %param.16) | copy-start | bytes 52
  135.7 21.2 %copy-start.6 = (f32[64,512]{1,0:T(8,128)S(1)}, f32[64,512]{1,0:T(8,128)}, u32[]{:S(2)}) copy-start(f32[64,512]{1,0:T(8,128)} %anchor.1) | copy-start | bytes 393220
  135.7 21.2 %copy-start.7 = (f32[64,512]{1,0:T(8,128)S(1)}, f32[64,512]{1,0:T(8,128)}, u32[]{:S(2)}) copy-start(f32[64,512]{1,0:T(8,128)} %param.11) | copy-start | bytes 393220
  135.7 21.2 %copy-start.8 = (f32[64,512]{1,0:T(8,128)S(1)}, f32[64,512]{1,0:T(8,128)}, u32[]{:S(2)}) copy-start(f32[64,512]{1,0:T(8,128)} %param.13) | copy-start | bytes 393220
  135.7 21.2 %copy-start.9 = (f32[64,512]{1,0:T(8,128)S(1)}, f32[64,512]{1,0:T(8,128)}, u32[]{:S(2)}) copy-start(f32[64,512]{1,0:T(8,128)} %param.14) | copy-start | bytes 393220
  147.0 23.0 %copy-start.12 = (s32[2]{0:T(128)S(1)}, s32[2]{0:T(128)}, u32[]{:S(2)}) copy-start(s32[2]{0:T(128)} %param.17) | copy-start | bytes 28
  147.1 22.5 %all-to-all-start.5 = ((f32[256,1,128]{2,1,0:T(1,128)}), f32[256,1,128]{2,1,0:T(1,128)S(1)}, u32[]{:S(2)}, u32[]{:S(2)}) async-start(f32[256,1,128]{2,1,0:T(1,128)} %score_sums.1), calls=%async_computation.5 | async-start | bytes 262144 | tf_op jit(solution)/shard_map/all_to_all | solution.py:363

commit v5 on v4

--- a/solution.py
+++ b/solution.py
@@ -58,7 +58,7 @@
     return pltpu.with_memory_space_constraint(array, pltpu.HBM)
 
 
-def gradient_kernel(place, cotangent, tokens, anchor, sent, own, message, held, turned, sems):
+def gradient_kernel(place, cotangent, tokens, sent, own, held, turned, sems):
     channels = held.shape[1]
     half, quarter = channels // 2, channels // 4
     width = sent.shape[3]
@@ -81,10 +81,6 @@
     ]
     for load in halves + blocks:
         load.start()
-    lanes = pl.ds(pl.multiple_of(place[1] * quarter, quarter), quarter)
-    piece = anchor[:, lanes].astype(message.dtype)
-    for at in range(message.shape[0]):
-        message[at] = piece
     for load in halves:
         load.wait()
     for at, load in enumerate(blocks):
@@ -101,7 +97,7 @@
         own[1, at] = product[half + quarter :]
 
 
-def gradient_blocks(place, cotangent, tokens, anchor):
+def gradient_blocks(place, cotangent, tokens):
     count, features = tokens.shape
     channels = cotangent.shape[1]
     quarter = channels // 4
@@ -113,10 +109,9 @@
             pl.BlockSpec(memory_space=pltpu.SMEM),
             pl.BlockSpec(memory_space=pltpu.HBM),
             pl.BlockSpec(memory_space=pltpu.HBM),
-            pl.BlockSpec(memory_space=pltpu.VMEM),
         ],
-        out_specs=[pl.BlockSpec(memory_space=pltpu.VMEM)] * 3,
-        out_shape=[block, block, jax.ShapeDtypeStruct((32, anchor.shape[0], quarter), jnp.bfloat16)],
+        out_specs=[pl.BlockSpec(memory_space=pltpu.VMEM)] * 2,
+        out_shape=[block, block],
         scratch_shapes=[
             pltpu.VMEM(cotangent.shape, cotangent.dtype),
             pltpu.VMEM(tokens.shape, tokens.dtype),
@@ -127,28 +122,31 @@
         ),
         compiler_params=pltpu.CompilerParams(vmem_limit_bytes=VMEM_GRADIENT),
         name="gradient_blocks",
-    )(place, in_hbm(cotangent), in_hbm(tokens), anchor)
+    )(place, in_hbm(cotangent), in_hbm(tokens))
 
 
 def frozen_kernel(place, tokens, sibling, here, left, right, far_left, far_right, out, joined):
-    strips, rows, quarter = here.shape
+    depth, count, rows, quarter = here.shape
 
     @pl.when(pl.program_id(0) == 0)
     def _():
         for shift, ref, first in (
-            (0, here, 0), (3, left, 0), (1, right, 0), (2, far_left, 0), (2, far_right, strips // 2)
+            (0, here, 0), (3, left, 0), (1, right, 0), (2, far_left, 0), (2, far_right, depth // 2)
         ):
             chip = (place[0] + shift) % 4
             lanes = pl.ds(pl.multiple_of((chip % 2) * quarter, quarter), quarter)
             for at in range(ref.shape[0]):
-                joined[(first + at) * 2 + chip // 2, :, lanes] = ref[at]
+                level = (place[2] + first + at) % 8
+                for turn_y in range(count):
+                    owner = ((place[1] + turn_y) % 4) * 16 + (chip // 2) * 8 + level
+                    span = pl.ds(pl.multiple_of(owner * rows, rows), rows)
+                    joined[span, lanes] = ref[at, turn_y]
 
     for ref, turn_of in ((tokens, pl.program_id(0) < 2), (sibling, pl.program_id(0) >= 2)):
 
         @pl.when(turn_of)
         def _():
-            weights = joined[...].reshape(joined.shape[0] * rows, 2 * quarter)
-            out[...] = jnp.dot(ref[...], weights, preferred_element_type=jnp.float32)
+            out[...] = jnp.dot(ref[...], joined[...], preferred_element_type=jnp.float32)
 
 
 def sigmoid_sums(values):
@@ -219,9 +217,9 @@
             num_scalar_prefetch=1,
             grid=(4,),
             in_specs=token_specs(count, features)
-            + [pl.BlockSpec(strip.shape, lambda i, *_: (0, 0, 0)) for strip in strips],
+            + [pl.BlockSpec(strip.shape, lambda i, *_: (0, 0, 0, 0)) for strip in strips],
             out_specs=pl.BlockSpec((count // 2, width), lambda i, *_: (i, 0)),
-            scratch_shapes=[pltpu.VMEM((8, features // 8, width), jnp.bfloat16)],
+            scratch_shapes=[pltpu.VMEM((features, width), jnp.bfloat16)],
         ),
         out_shape=jax.ShapeDtypeStruct((2 * count, width), jnp.float32),
         cost_estimate=pl.CostEstimate(
@@ -289,6 +287,19 @@
     )
 
 
+def shift_ring(block, axis, size, shift):
+    return lax.ppermute(block, axis, [(i, (i - shift) % size) for i in range(size)])
+
+
+def column_strips(piece):
+    pair = jnp.stack([piece, shift_ring(piece, "y", 4, 1)])
+    own = jnp.concatenate([pair, shift_ring(pair, "y", 4, 2)])[None]
+    above, below = shift_ring(own, "z", 8, 1), shift_ring(own, "z", 8, -1)
+    upper = shift_ring(jnp.concatenate([below, own, above]), "z", 8, 3)
+    lower = shift_ring(jnp.concatenate([own, above]), "z", 8, -3)
+    return jnp.concatenate([own, above, upper, lower, below])
+
+
 def along_z(blocks):
     return lax.all_to_all(blocks, "z", 0, 0, tiled=True)
 
@@ -313,15 +324,12 @@
     def joined_halves(plane):
         return plane.reshape(2, features, quarter)
 
-    sent, own, anchor_copies = gradient_blocks(
-        jnp.stack([core, core * 2 + low]), cotangent, tokens, anchor
-    )
+    sent, own = gradient_blocks(core[None], cotangent, tokens)
+    sent, anchor_piece = lax.optimization_barrier((sent, piece(anchor).astype(jnp.bfloat16)))
     arrived = lax.ppermute(sent, "core", SWAP)
-    strips = lax.all_to_all(anchor_copies, ("y", "z"), 0, 0, tiled=True)
-    strips = strips.reshape(4, 8 * rows, quarter)
+    strips = column_strips(anchor_piece)
     blocks = own.astype(jnp.float32) + arrived.astype(jnp.float32)
     blocks = blocks.astype(jnp.bfloat16)
-    blocks, strips = lax.optimization_barrier((blocks, strips))
     plane = to_plane(blocks.reshape(16, quarter, 8 * rows))
     plane, strips, tokens = lax.optimization_barrier((plane, strips, tokens))
     sibling = lax.ppermute(tokens, "core", SWAP)
@@ -329,8 +337,7 @@
     column = along_z(plane_sum(plane).reshape(8, rows, quarter))
     gradient_piece = jnp.sum(column.astype(jnp.float32), axis=0)
 
-    gradient_piece, left, right = lax.optimization_barrier((gradient_piece, left, right))
-    far_left, far_right = turn(left[:2], 1), turn(right[2:], -1)
+    far_left, far_right = turn(left[:4], 1), turn(right[4:], -1)
     policy_piece = adam_update(
         gradient_piece, piece(policy), piece(anchor), piece(moment), piece(second)
     )[0].astype(jnp.bfloat16)
@@ -340,7 +347,7 @@
     )
     policy_plane = to_plane(policy_copies)
     frozen = frozen_values(
-        (high * 2 + low)[None], tokens, sibling, (strips, left, right, far_left, far_right)
+        jnp.stack([high * 2 + low, lax.axis_index("y"), lax.axis_index("z")]), tokens, sibling, (strips, left, right, far_left, far_right)
     )
 
     strip = jnp.where(

time: 171 us -> 184 us (1.076)
  waiting for transfers between devices: 47.5 us -> 72.9 us
  blocking collectives: 31.8 us -> 12.3 us
  starting transfers between devices: 47.6 us -> 56 us
    ppermute x0 -> x6, waiting for transfers between devices: none -> 38.8 us  [shift_ring(): lax.ppermute(block, axis, [(i, (i - shift) % size) for i in range(size)])]
    all_to_all x1, blocking collectives: 31.8 us -> 12.3 us  [along_z(): return lax.all_to_all(blocks, 'z', 0, 0, tiled=True)]
    ppermute x0 -> x6, starting transfers between devices: none -> 12.4 us  [shift_ring(): lax.ppermute(block, axis, [(i, (i - shift) % size) for i in range(size)])]
    all_to_all x1 -> x0, waiting for transfers between devices: 11.3 us -> none  [shards(): strips = lax.all_to_all(anchor_copies, ('y', 'z'), 0, 0, tiled=True)]
    all_to_all x1 -> x0, starting transfers between devices: 9.47 us -> none  [shards(): strips = lax.all_to_all(anchor_copies, ('y', 'z'), 0, 0, tiled=True)]
    all_to_all x2 -> x1, waiting for transfers between devices: 12.8 us -> 4.9 us  [along_z(): return lax.all_to_all(blocks, 'z', 0, 0, tiled=True)]
    all_to_all x1 -> x2, starting transfers between devices: 3.85 us -> 9.15 us  [to_plane(): return lax.all_to_all(blocks, PLANE, 0, 0, tiled=True)]
    ppermute x4, starting transfers between devices: 5.51 us -> 9.63 us  [turn(): lax.ppermute(block, ('xlo', 'xhi'), [(index(x), index((x + shift) % 4)) f...]
  transfers between devices with their start and end apart: 13 -> 18, of which waited for: 6 -> 10; matrix products, arithmetic and copies ran while one was open for 4% -> 4% of each run, Pallas kernels for 12% -> 11%
where the time goes in v5:
time: 184 us
  waiting for transfers between devices  72.9 us (40%)
  starting transfers between devices  56 us (30%)
  Pallas kernels  26.9 us (15%)
  blocking collectives  12.3 us (7%)
  local copies, waits for them, and re-layouts  8.51 us (5%)
  other arithmetic  6.15 us (3%)
    ppermute x6, waiting for transfers between devices, shift_ring(): lax.ppermute(block, axis, [(i, (i - shift) % size) for i in range(size)])  38.8 us
    ppermute x6, starting transfers between devices, shift_ring(): lax.ppermute(block, axis, [(i, (i - shift) % size) for i in range(size)])  12.4 us
    all_to_all x1, blocking collectives, along_z(): return lax.all_to_all(blocks, 'z', 0, 0, tiled=True)  12.3 us
    all_to_all x2, waiting for transfers between devices, to_plane(): return lax.all_to_all(blocks, PLANE, 0, 0, tiled=True)  11.5 us
    pallas_call x1, Pallas kernels, score_sums(): pl.pallas_call(score_kernel, out_shape=jax.ShapeDtypeStruct((256, 1, 128)...  11.3 us
    all_to_all x1, waiting for transfers between devices, shards(): parts = lax.all_to_all(parts, AXES, 0, 0, tiled=True)  11 us
    ppermute x4, starting transfers between devices, turn(): lax.ppermute(block, ('xlo', 'xhi'), [(index(x), index((x + shift) % 4)) f...  9.63 us
    all_to_all x1, starting transfers between devices, shards(): parts = lax.all_to_all(parts, AXES, 0, 0, tiled=True)  9.6 us
  transfers between devices with their start and end apart: 18, of which 10 were waited for; matrix products, arithmetic and copies ran while one was open for 4% of the time, Pallas kernels for 11%

profile of v5, /device:TPU:1, one launch (start us, length us, event | category | flops | bytes accessed | tf_op | source)
XLA Modules:
  0.0 183.7 jit_solution(14093983245080866839)
XLA Ops:
  0.6 0.8 dynamic-slice_convert_fusion
  1.4 6.3 %gradient_blocks.1 = (bf16[2,8,128,512]{3,2,1,0:T(8,128)(2,1)S(1)}, bf16[2,8,128,512]{3,2,1,0:T(8,128)(2,1)S(1)}) custom-call(s32[1]{0:T(128)} %bitcast.place, bf16[768,512]{1,0:T(8,128)(2,1)} %cotangent.1, bf16[768,4096]{1,0:T(8,128)(2,1)} %tokens.3), custom_call_target="tpu_custom_call" | custom-call | flops 3221225472 | bytes 12582912 | tf_op jit(solution)/shard_map/gradient_blocks/pallas_call | solution.py:106
  7.7 3.3 %collective-permute-start = (bf16[2,8,128,512]{3,2,1,0:T(8,128)(2,1)S(1)}, bf16[2,8,128,512]{3,2,1,0:T(8,128)(2,1)S(1)}, u32[]{:S(2)}, u32[]{:S(2)}) collective-permute-start(bf16[2,8,128,512]{3,2,1,0:T(8,128)(2,1)S(1)} %get-tuple-element.19), channel_id=1, source_target_pairs={{0,64},{64,0},{1,65},{65,1},{2,66},{66,2},{3,67},{67,3},{4,68},{68... | collective-permute-start | bytes 6291464 | tf_op jit(solution)/shard_map/ppermute | solution.py:329
  11.0 3.8 %collective-permute-done = bf16[2,8,128,512]{3,2,1,0:T(8,128)(2,1)S(1)} collective-permute-done((bf16[2,8,128,512]{3,2,1,0:T(8,128)(2,1)S(1)}, bf16[2,8,128,512]{3,2,1,0:T(8,128)(2,1)S(1)}, u32[]{:S(2)}, u32[]{:S(2)}) %collective-permute-start) | collective-permute-done | bytes 2097184 | tf_op jit(solution)/shard_map/ppermute | solution.py:329
  14.8 2.0 %add_convert_fusion = bf16[2,8,128,512]{3,2,1,0:T(8,128)(2,1)} fusion(bf16[2,8,128,512]{3,2,1,0:T(8,128)(2,1)S(1)} %collective-permute-done, bf16[2,8,128,512]{3,2,1,0:T(8,128)(2,1)S(1)} %get-tuple-element.17), kind=kLoop, calls=%fused_computation | loop fusion | flops 4194304 | bytes 6291456 | tf_op jit(solution)/shard_map/convert_element_type | solution.py:332
  16.8 5.0 %all-to-all-start = ((bf16[16,128,512]{2,1,0:T(8,128)(2,1)}), bf16[16,128,512]{2,1,0:T(8,128)(2,1)S(1)}, u32[]{:S(2)}, u32[]{:S(2)}) async-start(bf16[16,128,512]{2,1,0:T(8,128)(2,1)} %bitcast.21), calls=%async_computation | async-start | bytes 4194304 | tf_op jit(solution)/shard_map/all_to_all | solution.py:278
  21.8 2.6 %collective-permute-start.1 = (bf16[64,128]{1,0:T(8,128)(2,1)S(1)}, bf16[64,128]{1,0:T(8,128)(2,1)S(1)}, u32[]{:S(2)}, u32[]{:S(2)}) collective-permute-start(bf16[64,128]{1,0:T(8,128)(2,1)S(1)} %dynamic-slice_convert_fusion), channel_id=1, source_target_pairs={{0,48},{16,0},{32,16},{48,32},{1,49},{17,1},{33,17},{49,33},{2,50}... | collective-permute-start | bytes 49160 | tf_op jit(solution)/shard_map/ppermute | solution.py:291
  24.4 20.2 %collective-permute-done.1 = bf16[64,128]{1,0:T(8,128)(2,1)S(1)} collective-permute-done((bf16[64,128]{1,0:T(8,128)(2,1)S(1)}, bf16[64,128]{1,0:T(8,128)(2,1)S(1)}, u32[]{:S(2)}, u32[]{:S(2)}) %collective-permute-start.1) | collective-permute-done | bytes 16416 | tf_op jit(solution)/shard_map/ppermute | solution.py:291
  44.7 0.7 collective-permute-start.2
  45.4 7.3 %collective-permute-done.2 = bf16[2,64,128]{2,1,0:T(8,128)(2,1)S(1)} collective-permute-done((bf16[2,64,128]{2,1,0:T(8,128)(2,1)S(1)}, bf16[2,64,128]{2,1,0:T(8,128)(2,1)S(1)}, u32[]{:S(2)}, u32[]{:S(2)}) %collective-permute-start.2) | collective-permute-done | bytes 32800 | tf_op jit(solution)/shard_map/ppermute | solution.py:291
  52.7 5.7 %collective-permute-start.3 = (bf16[1,4,64,128]{3,2,1,0:T(8,128)(2,1)S(1)}, bf16[1,4,64,128]{3,2,1,0:T(8,128)(2,1)S(1)}, u32[]{:S(2)}, u32[]{:S(2)}) collective-permute-start(bf16[1,4,64,128]{3,2,1,0:T(8,128)(2,1)S(1)} %maximum_bitcast_fusion), channel_id=1, source_target_pairs={{0,7},{1,0},{2,1},{3,2},{4,3},{5,4},{6,5},{7,6},{8,15},{9,8},{10,9... | collective-permute-start | bytes 196616 | tf_op jit(solution)/shard_map/ppermute | solution.py:291
  58.4 0.6 constant_dynamic-update-slice_fusion.4
  59.0 0.7 collective-permute-done.3
  59.7 3.0 %collective-permute-done.4 = bf16[1,4,64,128]{3,2,1,0:T(8,128)(2,1)S(1)} collective-permute-done((bf16[1,4,64,128]{3,2,1,0:T(8,128)(2,1)S(1)}, bf16[1,4,64,128]{3,2,1,0:T(8,128)(2,1)S(1)}, u32[]{:S(2)}, u32[]{:S(2)}) %collective-permute-start.4) | collective-permute-done | bytes 65568 | tf_op jit(solution)/shard_map/ppermute | solution.py:291
  62.7 0.5 collective-permute-start.5
  63.2 2.9 %collective-permute-start.6 = (bf16[2,4,64,128]{3,2,1,0:T(8,128)(2,1)S(1)}, bf16[2,4,64,128]{3,2,1,0:T(8,128)(2,1)S(1)}, u32[]{:S(2)}, u32[]{:S(2)}) collective-permute-start(bf16[2,4,64,128]{3,2,1,0:T(8,128)(2,1)S(1)} %pad_maximum_fusion.1), channel_id=1, source_target_pairs={{0,3},{1,4},{2,5},{3,6},{4,7},{5,0},{6,1},{7,2},{8,11},{9,12},{10,... | collective-permute-start | bytes 393224 | tf_op jit(solution)/shard_map/ppermute | solution.py:291
  66.2 0.6 constant_dynamic-update-slice_fusion.3
  66.8 7.5 %collective-permute-done.5 = bf16[3,4,64,128]{3,2,1,0:T(8,128)(2,1)S(1)} collective-permute-done((bf16[3,4,64,128]{3,2,1,0:T(8,128)(2,1)S(1)}, bf16[3,4,64,128]{3,2,1,0:T(8,128)(2,1)S(1)}, u32[]{:S(2)}, u32[]{:S(2)}) %collective-permute-start.5) | collective-permute-done | bytes 196640 | tf_op jit(solution)/shard_map/ppermute | solution.py:291
  74.3 0.7 constant_dynamic-update-slice_fusion.2
  75.0 0.7 constant_dynamic-update-slice_fusion.1
  75.6 0.6 constant_dynamic-update-slice_fusion.here
  76.3 4.3 %collective-permute-start.11 = (bf16[768,4096]{1,0:T(8,128)(2,1)}, bf16[768,4096]{1,0:T(8,128)(2,1)}, u32[]{:S(2)}, u32[]{:S(2)}) collective-permute-start(bf16[768,4096]{1,0:T(8,128)(2,1)} %tokens.3), channel_id=1, source_target_pairs={{0,64},{64,0},{1,65},{65,1},{2,66},{66,2},{3,67},{67,3},{4,68},{68... | collective-permute-start | bytes 18874376 | tf_op jit(solution)/shard_map/ppermute | solution.py:335
  80.5 6.9 %collective-permute-start.9 = (bf16[8,4,64,128]{3,2,1,0:T(8,128)(2,1)}, bf16[8,4,64,128]{3,2,1,0:T(8,128)(2,1)S(1)}, u32[]{:S(2)}, u32[]{:S(2)}) collective-permute-start(bf16[8,4,64,128]{3,2,1,0:T(8,128)(2,1)} %constant_dynamic-update-slice_fusion.here), channel_id=1, source_target_pairs={{0,136},{128,0},{8,128},{136,8},{1,137},{129,1},{9,129},{137,9},{2... | collective-permute-start | bytes 1572872 | tf_op jit(solution)/shard_map/ppermute | solution.py:285
  87.4 0.3 plane_sum.1
  87.8 12.3 %all_to_all.25 = bf16[8,64,128]{2,1,0:T(8,128)(2,1)S(1)} all-to-all(bf16[8,64,128]{2,1,0:T(8,128)(2,1)S(1)} %bitcast.19), channel_id=1, replica_groups=mesh['xlo'=2,'core'=2,'y'=4,'xhi'=2,'z'=8] {'z'}, dimensions={0} | all-to-all | bytes 262144 | tf_op jit(solution)/shard_map/all_to_all | solution.py:304
  100.2 2.6 %collective-permute-start.10 = (bf16[4,4,64,128]{3,2,1,0:T(8,128)(2,1)S(1)}, bf16[4,4,64,128]{3,2,1,0:T(8,128)(2,1)S(1)}, u32[]{:S(2)}, u32[]{:S(2)}) collective-permute-start(bf16[4,4,64,128]{3,2,1,0:T(8,128)(2,1)S(1)} %slice.25), channel_id=1, source_target_pairs={{0,136},{128,0},{8,128},{136,8},{1,137},{129,1},{9,129},{137,9},{2... | collective-permute-start | bytes 786440 | tf_op jit(solution)/shard_map/ppermute | solution.py:285
  102.8 0.1 collective-permute-start.8
  102.9 0.8 fusion.7
  103.8 0.7 broadcast_in_dim.44
  104.4 4.3 %all-to-all-start.2 = ((bf16[8,64,128]{2,1,0:T(8,128)(2,1)}), bf16[8,64,128]{2,1,0:T(8,128)(2,1)S(1)}, u32[]{:S(2)}, u32[]{:S(2)}) async-start(bf16[8,64,128]{2,1,0:T(8,128)(2,1)} %broadcast_in_dim.44), calls=%async_computation.2 | async-start | bytes 262144 | tf_op jit(solution)/shard_map/all_to_all | solution.py:304
  108.8 3.1 %collective-permute-done.12 = f32[64,128]{1,0:T(8,128)S(1)} collective-permute-done((f32[64,128]{1,0:T(8,128)S(1)}, f32[64,128]{1,0:T(8,128)S(1)}, u32[]{:S(2)}, u32[]{:S(2)}) %collective-permute-start.12) | collective-permute-done | bytes 32800 | tf_op jit(solution)/shard_map/ppermute | solution.py:344
  111.8 4.9 %all-to-all-done.2 = bf16[8,64,128]{2,1,0:T(8,128)(2,1)S(1)} async-done(((bf16[8,64,128]{2,1,0:T(8,128)(2,1)}), bf16[8,64,128]{2,1,0:T(8,128)(2,1)S(1)}, u32[]{:S(2)}, u32[]{:S(2)}) %all-to-all-start.2) | async-done | bytes 131104 | tf_op jit(solution)/shard_map/all_to_all | solution.py:304
  116.8 1.8 broadcast_in_dim.46
  118.5 4.1 %all-to-all-start.3 = ((bf16[16,512,128]{2,1,0:T(8,128)(2,1)}), bf16[16,512,128]{2,1,0:T(8,128)(2,1)S(1)}, u32[]{:S(2)}, u32[]{:S(2)}) async-start(bf16[16,512,128]{2,1,0:T(8,128)(2,1)} %broadcast_in_dim.46), calls=%async_computation.3 | async-start | bytes 4194304 | tf_op jit(solution)/shard_map/all_to_all | solution.py:278
  122.9 3.3 %collective-permute-start.13 = (f32[64,256]{1,0:T(8,128)S(1)}, f32[64,256]{1,0:T(8,128)}, u32[]{:S(2)}, u32[]{:S(2)}) collective-permute-start(f32[64,256]{1,0:T(8,128)S(1)} %maximum_select_fusion.1), channel_id=1, source_target_pairs={{0,64},{64,0},{1,65},{65,1},{2,66},{66,2},{3,67},{67,3},{4,68},{68... | collective-permute-start | bytes 196616 | tf_op jit(solution)/shard_map/ppermute | solution.py:358
  126.2 0.9 copy-done.2
  127.1 8.9 %frozen_values.1.frozen = f32[1536,256]{1,0:T(8,128)S(1)} custom-call(s32[3]{0:T(128)S(1)} %pad_add_fusion.place, bf16[768,4096]{1,0:T(8,128)(2,1)} %tokens.3, bf16[768,4096]{1,0:T(8,128)(2,1)} %collective-permute-done.11.sibling, bf16[8,4,64,128]{3,2,1,0:T(8,128)(2,1)} %constant_dynamic-update-slice_fusion.here, ...), custom_call_target="tpu_custom_call" | custom-call | flops 3221225472 | bytes 16777216 | tf_op jit(solution)/shard_map/frozen_values/pallas_call | solution.py:214
  136.1 1.2 copy-done
  137.3 11.5 %all-to-all-done.3 = bf16[16,512,128]{2,1,0:T(8,128)(2,1)S(1)} async-done(((bf16[16,512,128]{2,1,0:T(8,128)(2,1)}), bf16[16,512,128]{2,1,0:T(8,128)(2,1)S(1)}, u32[]{:S(2)}, u32[]{:S(2)}) %all-to-all-start.3) | async-done | bytes 2097184 | tf_op jit(solution)/shard_map/all_to_all | solution.py:278
  148.7 11.3 %score_sums.1 = f32[256,1,128]{2,1,0:T(1,128)} custom-call(bf16[768,4096]{1,0:T(8,128)(2,1)} %tokens.3, bf16[768,4096]{1,0:T(8,128)(2,1)} %collective-permute-done.11.sibling, bf16[2,4096,128]{2,1,0:T(8,128)(2,1)S(1)} %bitcast.18, f32[1536,256]{1,0:T(8,128)} %copy-done, f32[1,256]{1,0:T(1,128)S(1)} %bitcast.20), custom_call_target="tpu_custom_call" | custom-call | flops 3221225472 | bytes 16777216 | tf_op jit(solution)/shard_map/score_sums/pallas_call | solution.py:236
  160.1 9.6 %all-to-all-start.4 = ((f32[256,1,128]{2,1,0:T(1,128)}), f32[256,1,128]{2,1,0:T(1,128)S(1)}, u32[]{:S(2)}, u32[]{:S(2)}) async-start(f32[256,1,128]{2,1,0:T(1,128)} %score_sums.1), calls=%async_computation.4 | async-start | bytes 262144 | tf_op jit(solution)/shard_map/all_to_all | solution.py:370
  169.7 0.2 slice_reduce_fusion
  170.0 1.8 multiply_add_fusion
  171.7 11.0 %all-to-all-done.4 = f32[256,1,128]{2,1,0:T(1,128)S(1)} async-done(((f32[256,1,128]{2,1,0:T(1,128)}), f32[256,1,128]{2,1,0:T(1,128)S(1)}, u32[]{:S(2)}, u32[]{:S(2)}) %all-to-all-start.4) | async-done | bytes 131104 | tf_op jit(solution)/shard_map/all_to_all | solution.py:370
  182.7 0.1 slice.27
  182.8 0.1 broadcast_in_dim.48
  182.9 0.2 fusion.9
  183.2 0.5 multiply_subtract_fusion
  (40 shorter events, 0.4 us)
Async XLA Ops:
  7.7 7.1 %collective-permute-start = (bf16[2,8,128,512]{3,2,1,0:T(8,128)(2,1)S(1)}, bf16[2,8,128,512]{3,2,1,0:T(8,128)(2,1)S(1)}, u32[]{:S(2)}, u32[]{:S(2)}) collective-permute-start(bf16[2,8,128,512]{3,2,1,0:T(8,128)(2,1)S(1)} %get-tuple-element.19), channel_id=1, source_target_pairs={{0,64},{64,0},{1,65},{65,1},{2,66},{66,2},{3,67},{67,3},{4,68},{68... | collective-permute-start | bytes 6291464 | tf_op jit(solution)/shard_map/ppermute | solution.py:329
  16.8 59.4 %all-to-all-start = ((bf16[16,128,512]{2,1,0:T(8,128)(2,1)}), bf16[16,128,512]{2,1,0:T(8,128)(2,1)S(1)}, u32[]{:S(2)}, u32[]{:S(2)}) async-start(bf16[16,128,512]{2,1,0:T(8,128)(2,1)} %bitcast.21), calls=%async_computation | async-start | bytes 4194304 | tf_op jit(solution)/shard_map/all_to_all | solution.py:278
  21.8 22.8 %collective-permute-start.1 = (bf16[64,128]{1,0:T(8,128)(2,1)S(1)}, bf16[64,128]{1,0:T(8,128)(2,1)S(1)}, u32[]{:S(2)}, u32[]{:S(2)}) collective-permute-start(bf16[64,128]{1,0:T(8,128)(2,1)S(1)} %dynamic-slice_convert_fusion), channel_id=1, source_target_pairs={{0,48},{16,0},{32,16},{48,32},{1,49},{17,1},{33,17},{49,33},{2,50}... | collective-permute-start | bytes 49160 | tf_op jit(solution)/shard_map/ppermute | solution.py:291
  44.7 8.0 %collective-permute-start.2 = (bf16[2,64,128]{2,1,0:T(8,128)(2,1)S(1)}, bf16[2,64,128]{2,1,0:T(8,128)(2,1)S(1)}, u32[]{:S(2)}, u32[]{:S(2)}) collective-permute-start(bf16[2,64,128]{2,1,0:T(8,128)(2,1)S(1)} %pad_maximum_fusion.2), channel_id=1, source_target_pairs={{0,32},{16,48},{32,0},{48,16},{1,33},{17,49},{33,1},{49,17},{2,34}... | collective-permute-start | bytes 98312 | tf_op jit(solution)/shard_map/ppermute | solution.py:291
  52.7 7.0 %collective-permute-start.3 = (bf16[1,4,64,128]{3,2,1,0:T(8,128)(2,1)S(1)}, bf16[1,4,64,128]{3,2,1,0:T(8,128)(2,1)S(1)}, u32[]{:S(2)}, u32[]{:S(2)}) collective-permute-start(bf16[1,4,64,128]{3,2,1,0:T(8,128)(2,1)S(1)} %maximum_bitcast_fusion), channel_id=1, source_target_pairs={{0,7},{1,0},{2,1},{3,2},{4,3},{5,4},{6,5},{7,6},{8,15},{9,8},{10,9... | collective-permute-start | bytes 196616 | tf_op jit(solution)/shard_map/ppermute | solution.py:291
  58.4 4.3 %collective-permute-start.4 = (bf16[1,4,64,128]{3,2,1,0:T(8,128)(2,1)S(1)}, bf16[1,4,64,128]{3,2,1,0:T(8,128)(2,1)S(1)}, u32[]{:S(2)}, u32[]{:S(2)}) collective-permute-start(bf16[1,4,64,128]{3,2,1,0:T(8,128)(2,1)S(1)} %maximum_bitcast_fusion), channel_id=1, source_target_pairs={{0,1},{1,2},{2,3},{3,4},{4,5},{5,6},{6,7},{7,0},{8,9},{9,10},{10,1... | collective-permute-start | bytes 196616 | tf_op jit(solution)/shard_map/ppermute | solution.py:291
  62.7 11.5 %collective-permute-start.5 = (bf16[3,4,64,128]{3,2,1,0:T(8,128)(2,1)S(1)}, bf16[3,4,64,128]{3,2,1,0:T(8,128)(2,1)S(1)}, u32[]{:S(2)}, u32[]{:S(2)}) collective-permute-start(bf16[3,4,64,128]{3,2,1,0:T(8,128)(2,1)S(1)} %pad_maximum_fusion), channel_id=1, source_target_pairs={{0,5},{1,6},{2,7},{3,0},{4,1},{5,2},{6,3},{7,4},{8,13},{9,14},{10,... | collective-permute-start | bytes 589832 | tf_op jit(solution)/shard_map/ppermute | solution.py:291
  63.2 11.7 %collective-permute-start.6 = (bf16[2,4,64,128]{3,2,1,0:T(8,128)(2,1)S(1)}, bf16[2,4,64,128]{3,2,1,0:T(8,128)(2,1)S(1)}, u32[]{:S(2)}, u32[]{:S(2)}) collective-permute-start(bf16[2,4,64,128]{3,2,1,0:T(8,128)(2,1)S(1)} %pad_maximum_fusion.1), channel_id=1, source_target_pairs={{0,3},{1,4},{2,5},{3,6},{4,7},{5,0},{6,1},{7,2},{8,11},{9,12},{10,... | collective-permute-start | bytes 393224 | tf_op jit(solution)/shard_map/ppermute | solution.py:291
  76.3 40.5 %collective-permute-start.11 = (bf16[768,4096]{1,0:T(8,128)(2,1)}, bf16[768,4096]{1,0:T(8,128)(2,1)}, u32[]{:S(2)}, u32[]{:S(2)}) collective-permute-start(bf16[768,4096]{1,0:T(8,128)(2,1)} %tokens.3), channel_id=1, source_target_pairs={{0,64},{64,0},{1,65},{65,1},{2,66},{66,2},{3,67},{67,3},{4,68},{68... | collective-permute-start | bytes 18874376 | tf_op jit(solution)/shard_map/ppermute | solution.py:335
  80.5 19.6 %collective-permute-start.9 = (bf16[8,4,64,128]{3,2,1,0:T(8,128)(2,1)}, bf16[8,4,64,128]{3,2,1,0:T(8,128)(2,1)S(1)}, u32[]{:S(2)}, u32[]{:S(2)}) collective-permute-start(bf16[8,4,64,128]{3,2,1,0:T(8,128)(2,1)} %constant_dynamic-update-slice_fusion.here), channel_id=1, source_target_pairs={{0,136},{128,0},{8,128},{136,8},{1,137},{129,1},{9,129},{137,9},{2... | collective-permute-start | bytes 1572872 | tf_op jit(solution)/shard_map/ppermute | solution.py:285
  87.4 15.4 %collective-permute-start.7 = (bf16[8,4,64,128]{3,2,1,0:T(8,128)(2,1)}, bf16[8,4,64,128]{3,2,1,0:T(8,128)(2,1)S(1)}, u32[]{:S(2)}, u32[]{:S(2)}) collective-permute-start(bf16[8,4,64,128]{3,2,1,0:T(8,128)(2,1)} %constant_dynamic-update-slice_fusion.here), channel_id=1, source_target_pairs={{0,128},{128,8},{8,136},{136,0},{1,129},{129,9},{9,137},{137,1},{2... | collective-permute-start | bytes 1572872 | tf_op jit(solution)/shard_map/ppermute | solution.py:285
  100.2 16.6 %collective-permute-start.10 = (bf16[4,4,64,128]{3,2,1,0:T(8,128)(2,1)S(1)}, bf16[4,4,64,128]{3,2,1,0:T(8,128)(2,1)S(1)}, u32[]{:S(2)}, u32[]{:S(2)}) collective-permute-start(bf16[4,4,64,128]{3,2,1,0:T(8,128)(2,1)S(1)} %slice.25), channel_id=1, source_target_pairs={{0,136},{128,0},{8,128},{136,8},{1,137},{129,1},{9,129},{137,9},{2... | collective-permute-start | bytes 786440 | tf_op jit(solution)/shard_map/ppermute | solution.py:285
  102.8 13.9 %collective-permute-start.8 = (bf16[4,4,64,128]{3,2,1,0:T(8,128)(2,1)S(1)}, bf16[4,4,64,128]{3,2,1,0:T(8,128)(2,1)S(1)}, u32[]{:S(2)}, u32[]{:S(2)}) collective-permute-start(bf16[4,4,64,128]{3,2,1,0:T(8,128)(2,1)S(1)} %slice.24), channel_id=1, source_target_pairs={{0,128},{128,8},{8,136},{136,0},{1,129},{129,9},{9,137},{137,1},{2... | collective-permute-start | bytes 786440 | tf_op jit(solution)/shard_map/ppermute | solution.py:285
  104.4 12.3 %all-to-all-start.2 = ((bf16[8,64,128]{2,1,0:T(8,128)(2,1)}), bf16[8,64,128]{2,1,0:T(8,128)(2,1)S(1)}, u32[]{:S(2)}, u32[]{:S(2)}) async-start(bf16[8,64,128]{2,1,0:T(8,128)(2,1)} %broadcast_in_dim.44), calls=%async_computation.2 | async-start | bytes 262144 | tf_op jit(solution)/shard_map/all_to_all | solution.py:304
  108.8 3.1 %collective-permute-start.12 = (f32[64,128]{1,0:T(8,128)S(1)}, f32[64,128]{1,0:T(8,128)S(1)}, u32[]{:S(2)}, u32[]{:S(2)}) collective-permute-start(f32[64,128]{1,0:T(8,128)S(1)} %convert_reduce_fusion), channel_id=1, source_target_pairs={{0,128},{128,0},{1,129},{129,1},{2,130},{130,2},{3,131},{131,3},{4... | collective-permute-start | bytes 98312 | tf_op jit(solution)/shard_map/ppermute | solution.py:344
  116.8 1.8 copy-start.1
  118.5 4.2 %copy-start.8 = (f32[512]{0:T(512)S(1)}, f32[512]{0:T(512)}, u32[]{:S(2)}) copy-start(f32[512]{0:T(512)} %param.15) | copy-start | bytes 6148
  118.5 30.2 %all-to-all-start.3 = ((bf16[16,512,128]{2,1,0:T(8,128)(2,1)}), bf16[16,512,128]{2,1,0:T(8,128)(2,1)S(1)}, u32[]{:S(2)}, u32[]{:S(2)}) async-start(bf16[16,512,128]{2,1,0:T(8,128)(2,1)} %broadcast_in_dim.46), calls=%async_computation.3 | async-start | bytes 4194304 | tf_op jit(solution)/shard_map/all_to_all | solution.py:278
  122.9 47.0 %collective-permute-start.13 = (f32[64,256]{1,0:T(8,128)S(1)}, f32[64,256]{1,0:T(8,128)}, u32[]{:S(2)}, u32[]{:S(2)}) collective-permute-start(f32[64,256]{1,0:T(8,128)S(1)} %maximum_select_fusion.1), channel_id=1, source_target_pairs={{0,64},{64,0},{1,65},{65,1},{2,66},{66,2},{3,67},{67,3},{4,68},{68... | collective-permute-start | bytes 196616 | tf_op jit(solution)/shard_map/ppermute | solution.py:358
  126.2 0.9 copy-start.2
  136.0 1.2 copy-start
  148.7 21.0 %copy-start.7 = (s32[2,2]{1,0:T(2,128)S(1)}, s32[2,2]{1,0:T(2,128)}, u32[]{:S(2)}) copy-start(s32[2,2]{1,0:T(2,128)} %param.16) | copy-start | bytes 52
  148.7 21.2 %copy-start.3 = (f32[64,512]{1,0:T(8,128)S(1)}, f32[64,512]{1,0:T(8,128)}, u32[]{:S(2)}) copy-start(f32[64,512]{1,0:T(8,128)} %param.11) | copy-start | bytes 393220
  148.7 21.2 %copy-start.4 = (f32[64,512]{1,0:T(8,128)S(1)}, f32[64,512]{1,0:T(8,128)}, u32[]{:S(2)}) copy-start(f32[64,512]{1,0:T(8,128)} %param.13) | copy-start | bytes 393220
  148.7 21.2 %copy-start.5 = (f32[64,512]{1,0:T(8,128)S(1)}, f32[64,512]{1,0:T(8,128)}, u32[]{:S(2)}) copy-start(f32[64,512]{1,0:T(8,128)} %param.14) | copy-start | bytes 393220
  148.7 21.2 %copy-start.6 = (f32[64,512]{1,0:T(8,128)S(1)}, f32[64,512]{1,0:T(8,128)}, u32[]{:S(2)}) copy-start(f32[64,512]{1,0:T(8,128)} %param.12) | copy-start | bytes 393220
  160.1 23.1 %copy-start.9 = (s32[2]{0:T(128)S(1)}, s32[2]{0:T(128)}, u32[]{:S(2)}) copy-start(s32[2]{0:T(128)} %param.17) | copy-start | bytes 28
  160.1 22.6 %all-to-all-start.4 = ((f32[256,1,128]{2,1,0:T(1,128)}), f32[256,1,128]{2,1,0:T(1,128)S(1)}, u32[]{:S(2)}, u32[]{:S(2)}) async-start(f32[256,1,128]{2,1,0:T(1,128)} %score_sums.1), calls=%async_computation.4 | async-start | bytes 262144 | tf_op jit(solution)/shard_map/all_to_all | solution.py:370

commit v6 on v5

--- a/solution.py
+++ b/solution.py
@@ -52,6 +52,7 @@
 VMEM = 32 << 20
 VMEM_GRADIENT = 32 << 20
 VMEM_SCORE = 32 << 20
+AHEAD = 3
 
 
 def in_hbm(array):
@@ -79,12 +80,14 @@
         )
         for at in range(8)
     ]
-    for load in halves + blocks:
+    for load in halves + blocks[:AHEAD]:
         load.start()
     for load in halves:
         load.wait()
     for at, load in enumerate(blocks):
         load.wait()
+        if at + AHEAD < len(blocks):
+            blocks[at + AHEAD].start()
         product = lax.dot_general(
             held[...],
             turned[:, at * width : (at + 1) * width],
@@ -163,7 +166,7 @@
 def score_kernel(tokens, sibling, halves, frozen, readout, out, joined, held, still, sems):
     quarter = halves.shape[-1]
     count = tokens.shape[0]
-    sizes = (2 * LEN, 2 * LEN, 2 * LEN, LEN, LEN)
+    sizes = (LEN,) * 8
     loads, at = [], 0
     for step, size in enumerate(sizes):
         source, first = (tokens, at) if at < count else (sibling, at - count)
@@ -177,7 +180,7 @@
             )
         )
         at += size
-    for pair in loads:
+    for pair in loads[:AHEAD]:
         for load in pair:
             load.start()
     joined[:, :quarter] = halves[0]
@@ -186,9 +189,11 @@
     lane = lax.broadcasted_iota(jnp.int32, (1, 128), 1)
     parts = jnp.zeros((1, 128), jnp.float32)
     at = 0
-    for pair, size in zip(loads, sizes):
-        for load in pair:
+    for step, size in enumerate(sizes):
+        for load in loads[step]:
             load.wait()
+        for load in loads[step + AHEAD] if step + AHEAD < len(sizes) else ():
+            load.start()
         values = jnp.dot(held[at : at + size], joined[...], preferred_element_type=jnp.float32)
         blended = blend_rate * values + (1.0 - blend_rate) * still[at : at + size]
         values, blended = values * scale, blended * scale
@@ -247,7 +252,7 @@
             pltpu.VMEM((features, width), jnp.bfloat16),
             pltpu.VMEM((2 * count, features), tokens.dtype),
             pltpu.VMEM(frozen.shape, frozen.dtype),
-            pltpu.SemaphoreType.DMA((10,)),
+            pltpu.SemaphoreType.DMA((16,)),
         ],
         cost_estimate=pl.CostEstimate(
             flops=4 * count * features * width, bytes_accessed=16 << 20, transcendentals=0
@@ -291,9 +296,8 @@
     return lax.ppermute(block, axis, [(i, (i - shift) % size) for i in range(size)])
 
 
-def column_strips(piece):
-    pair = jnp.stack([piece, shift_ring(piece, "y", 4, 1)])
-    own = jnp.concatenate([pair, shift_ring(pair, "y", 4, 2)])[None]
+def gather_z(own):
+    own = own[None]
     above, below = shift_ring(own, "z", 8, 1), shift_ring(own, "z", 8, -1)
     upper = shift_ring(jnp.concatenate([below, own, above]), "z", 8, 3)
     lower = shift_ring(jnp.concatenate([own, above]), "z", 8, -3)
@@ -325,12 +329,15 @@
         return plane.reshape(2, features, quarter)
 
     sent, own = gradient_blocks(core[None], cotangent, tokens)
-    sent, anchor_piece = lax.optimization_barrier((sent, piece(anchor).astype(jnp.bfloat16)))
+    anchor_piece = piece(anchor).astype(jnp.bfloat16)
+    pair = jnp.stack([anchor_piece, shift_ring(anchor_piece, "y", 4, 1)])
+    sent, pair = lax.optimization_barrier((sent, pair))
     arrived = lax.ppermute(sent, "core", SWAP)
-    strips = column_strips(anchor_piece)
+    strip = jnp.concatenate([pair, shift_ring(pair, "y", 4, 2)])
     blocks = own.astype(jnp.float32) + arrived.astype(jnp.float32)
-    blocks = blocks.astype(jnp.bfloat16)
+    blocks, strip = lax.optimization_barrier((blocks.astype(jnp.bfloat16), strip))
     plane = to_plane(blocks.reshape(16, quarter, 8 * rows))
+    strips = gather_z(strip)
     plane, strips, tokens = lax.optimization_barrier((plane, strips, tokens))
     sibling = lax.ppermute(tokens, "core", SWAP)
     left, right = turn(strips, 1), turn(strips, -1)

time: 184 us -> 159 us (0.86)
  waiting for transfers between devices: 72.9 us -> 51.2 us
  starting transfers between devices: 56 us -> 47.4 us
  blocking collectives: 12.3 us -> 16 us
    ppermute x6, waiting for transfers between devices: 38.8 us -> 15.5 us  [shift_ring(): lax.ppermute(block, axis, [(i, (i - shift) % size) for i in range(size)])]
    all_to_all x2, waiting for transfers between devices: 11.5 us -> 16.8 us  [to_plane(): return lax.all_to_all(blocks, PLANE, 0, 0, tiled=True)]
    ppermute x4, starting transfers between devices: 9.63 us -> 5.01 us  [turn(): lax.ppermute(block, ('xlo', 'xhi'), [(index(x), index((x + shift) % 4)) f...]
    ppermute x1, waiting for transfers between devices: 3.79 us -> 0.01 us  [shards(): arrived = lax.ppermute(sent, 'core', SWAP)]
    all_to_all x1, blocking collectives: 12.3 us -> 16 us  [along_z(): return lax.all_to_all(blocks, 'z', 0, 0, tiled=True)]
    ppermute x1, starting transfers between devices: 3.33 us -> 1.04 us  [shards(): arrived = lax.ppermute(sent, 'core', SWAP)]
    ppermute x1, starting transfers between devices: 4.29 us -> 2.44 us  [shards(): sibling = lax.ppermute(tokens, 'core', SWAP)]
    unnamed x23 -> x24, local copies, waits for them, and re-layouts: 4.17 us -> 4.8 us
  transfers between devices with their start and end apart: 18 -> 18, of which waited for: 10 -> 9; matrix products, arithmetic and copies ran while one was open for 4% -> 5% of each run, Pallas kernels for 11% -> 17%
where the time goes in v6:
time: 159 us; the launch traced here: 158 us
  waiting for transfers between devices  51.2 us (32%)
  starting transfers between devices  47.4 us (30%)
  Pallas kernels  27.3 us (17%)
  blocking collectives  16 us (10%)
  local copies, waits for them, and re-layouts  9.91 us (6%)
  other arithmetic  5.52 us (3%)
    all_to_all x2, waiting for transfers between devices, to_plane(): return lax.all_to_all(blocks, PLANE, 0, 0, tiled=True)  16.8 us
    all_to_all x1, blocking collectives, along_z(): return lax.all_to_all(blocks, 'z', 0, 0, tiled=True)  16 us
    ppermute x6, waiting for transfers between devices, shift_ring(): lax.ppermute(block, axis, [(i, (i - shift) % size) for i in range(size)])  15.5 us
    ppermute x6, starting transfers between devices, shift_ring(): lax.ppermute(block, axis, [(i, (i - shift) % size) for i in range(size)])  13 us
    pallas_call x1, Pallas kernels, score_sums(): pl.pallas_call(score_kernel, out_shape=jax.ShapeDtypeStruct((256, 1, 128)...  11.7 us
    all_to_all x1, waiting for transfers between devices, shards(): parts = lax.all_to_all(parts, AXES, 0, 0, tiled=True)  11 us
    all_to_all x1, starting transfers between devices, shards(): parts = lax.all_to_all(parts, AXES, 0, 0, tiled=True)  9.68 us
    pallas_call x1, Pallas kernels, frozen_values(): pl.pallas_call(frozen_kernel, grid_spec=pltpu.PrefetchScalarGridSpec(num_...  8.91 us
  transfers between devices with their start and end apart: 18, of which 9 were waited for; matrix products, arithmetic and copies ran while one was open for 5% of the time, Pallas kernels for 17%

profile of v6, /device:TPU:1, one launch (start us, length us, event | category | flops | bytes accessed | tf_op | source)
XLA Modules:
  0.0 158.2 jit_solution(5478848238114406725)
XLA Ops:
  0.6 0.8 dynamic-slice_convert_fusion
  1.4 3.6 %collective-permute-start = (bf16[64,128]{1,0:T(8,128)(2,1)S(1)}, bf16[64,128]{1,0:T(8,128)(2,1)S(1)}, u32[]{:S(2)}, u32[]{:S(2)}) collective-permute-start(bf16[64,128]{1,0:T(8,128)(2,1)S(1)} %dynamic-slice_convert_fusion), channel_id=1, source_target_pairs={{0,48},{16,0},{32,16},{48,32},{1,49},{17,1},{33,17},{49,33},{2,50}... | collective-permute-start | bytes 49160 | tf_op jit(solution)/shard_map/ppermute | solution.py:296
  5.0 6.3 %gradient_blocks.1 = (bf16[2,8,128,512]{3,2,1,0:T(8,128)(2,1)S(1)}, bf16[2,8,128,512]{3,2,1,0:T(8,128)(2,1)S(1)}) custom-call(s32[1]{0:T(128)} %bitcast.place, bf16[768,512]{1,0:T(8,128)(2,1)} %cotangent.1, bf16[768,4096]{1,0:T(8,128)(2,1)} %tokens.3), custom_call_target="tpu_custom_call" | custom-call | flops 3221225472 | bytes 12582912 | tf_op jit(solution)/shard_map/gradient_blocks/pallas_call | solution.py:109
  11.3 0.8 fusion.13
  12.1 1.0 collective-permute-start.1
  13.1 0.4 collective-permute-start.2
  13.5 3.9 %collective-permute-done.2 = bf16[2,64,128]{2,1,0:T(8,128)(2,1)S(1)} collective-permute-done((bf16[2,64,128]{2,1,0:T(8,128)(2,1)S(1)}, bf16[2,64,128]{2,1,0:T(8,128)(2,1)S(1)}, u32[]{:S(2)}, u32[]{:S(2)}) %collective-permute-start.2) | collective-permute-done | bytes 32800 | tf_op jit(solution)/shard_map/ppermute | solution.py:296
  17.4 2.0 %add_convert_fusion = bf16[2,8,128,512]{3,2,1,0:T(8,128)(2,1)} fusion(bf16[2,8,128,512]{3,2,1,0:T(8,128)(2,1)S(1)} %collective-permute-done.1, bf16[2,8,128,512]{3,2,1,0:T(8,128)(2,1)S(1)} %get-tuple-element.19), kind=kLoop, calls=%fused_computation | loop fusion | flops 4194304 | bytes 6291456 | tf_op jit(solution)/shard_map/convert_element_type | solution.py:338
  19.4 4.3 %all-to-all-start = ((bf16[16,128,512]{2,1,0:T(8,128)(2,1)}), bf16[16,128,512]{2,1,0:T(8,128)(2,1)S(1)}, u32[]{:S(2)}, u32[]{:S(2)}) async-start(bf16[16,128,512]{2,1,0:T(8,128)(2,1)} %bitcast.20), calls=%async_computation | async-start | bytes 4194304 | tf_op jit(solution)/shard_map/all_to_all | solution.py:283
  23.7 5.6 %collective-permute-start.3 = (bf16[1,4,64,128]{3,2,1,0:T(8,128)(2,1)S(1)}, bf16[1,4,64,128]{3,2,1,0:T(8,128)(2,1)S(1)}, u32[]{:S(2)}, u32[]{:S(2)}) collective-permute-start(bf16[1,4,64,128]{3,2,1,0:T(8,128)(2,1)S(1)} %bitcast.23), channel_id=1, source_target_pairs={{0,7},{1,0},{2,1},{3,2},{4,3},{5,4},{6,5},{7,6},{8,15},{9,8},{10,9... | collective-permute-start | bytes 196616 | tf_op jit(solution)/shard_map/ppermute | solution.py:296
  29.4 0.6 constant_dynamic-update-slice_fusion.4
  30.0 0.7 collective-permute-done.3
  30.7 3.3 %collective-permute-done.4 = bf16[1,4,64,128]{3,2,1,0:T(8,128)(2,1)S(1)} collective-permute-done((bf16[1,4,64,128]{3,2,1,0:T(8,128)(2,1)S(1)}, bf16[1,4,64,128]{3,2,1,0:T(8,128)(2,1)S(1)}, u32[]{:S(2)}, u32[]{:S(2)}) %collective-permute-start.4) | collective-permute-done | bytes 65568 | tf_op jit(solution)/shard_map/ppermute | solution.py:296
  34.0 0.2 collective-permute-start.5
  34.2 3.2 %collective-permute-start.6 = (bf16[2,4,64,128]{3,2,1,0:T(8,128)(2,1)S(1)}, bf16[2,4,64,128]{3,2,1,0:T(8,128)(2,1)S(1)}, u32[]{:S(2)}, u32[]{:S(2)}) collective-permute-start(bf16[2,4,64,128]{3,2,1,0:T(8,128)(2,1)S(1)} %pad_maximum_fusion.1), channel_id=1, source_target_pairs={{0,3},{1,4},{2,5},{3,6},{4,7},{5,0},{6,1},{7,2},{8,11},{9,12},{10,... | collective-permute-start | bytes 393224 | tf_op jit(solution)/shard_map/ppermute | solution.py:296
  37.5 0.6 constant_dynamic-update-slice_fusion.3
  38.1 7.6 %collective-permute-done.5 = bf16[3,4,64,128]{3,2,1,0:T(8,128)(2,1)S(1)} collective-permute-done((bf16[3,4,64,128]{3,2,1,0:T(8,128)(2,1)S(1)}, bf16[3,4,64,128]{3,2,1,0:T(8,128)(2,1)S(1)}, u32[]{:S(2)}, u32[]{:S(2)}) %collective-permute-start.5) | collective-permute-done | bytes 196640 | tf_op jit(solution)/shard_map/ppermute | solution.py:296
  45.6 0.7 constant_dynamic-update-slice_fusion.2
  46.3 0.7 constant_dynamic-update-slice_fusion.1
  47.0 0.6 constant_dynamic-update-slice_fusion.here
  47.6 5.2 %all-to-all-done.blocks = bf16[16,128,512]{2,1,0:T(8,128)(2,1)S(1)} async-done(((bf16[16,128,512]{2,1,0:T(8,128)(2,1)}), bf16[16,128,512]{2,1,0:T(8,128)(2,1)S(1)}, u32[]{:S(2)}, u32[]{:S(2)}) %all-to-all-start) | async-done | bytes 2097184 | tf_op jit(solution)/shard_map/all_to_all | solution.py:283
  52.8 2.4 %collective-permute-start.11 = (bf16[768,4096]{1,0:T(8,128)(2,1)}, bf16[768,4096]{1,0:T(8,128)(2,1)}, u32[]{:S(2)}, u32[]{:S(2)}) collective-permute-start(bf16[768,4096]{1,0:T(8,128)(2,1)} %tokens.3), channel_id=1, source_target_pairs={{0,64},{64,0},{1,65},{65,1},{2,66},{66,2},{3,67},{67,3},{4,68},{68... | collective-permute-start | bytes 18874376 | tf_op jit(solution)/shard_map/ppermute | solution.py:342
  55.3 2.3 %collective-permute-start.9 = (bf16[8,4,64,128]{3,2,1,0:T(8,128)(2,1)}, bf16[8,4,64,128]{3,2,1,0:T(8,128)(2,1)S(1)}, u32[]{:S(2)}, u32[]{:S(2)}) collective-permute-start(bf16[8,4,64,128]{3,2,1,0:T(8,128)(2,1)} %constant_dynamic-update-slice_fusion.here), channel_id=1, source_target_pairs={{0,136},{128,0},{8,128},{136,8},{1,137},{129,1},{9,129},{137,9},{2... | collective-permute-start | bytes 1572872 | tf_op jit(solution)/shard_map/ppermute | solution.py:290
  57.5 0.3 plane_sum.1
  57.9 16.0 %all_to_all.25 = bf16[8,64,128]{2,1,0:T(8,128)(2,1)S(1)} all-to-all(bf16[8,64,128]{2,1,0:T(8,128)(2,1)S(1)} %bitcast.18), channel_id=1, replica_groups=mesh['xlo'=2,'core'=2,'y'=4,'xhi'=2,'z'=8] {'z'}, dimensions={0} | all-to-all | bytes 262144 | tf_op jit(solution)/shard_map/all_to_all | solution.py:308
  74.0 2.6 %collective-permute-start.10 = (bf16[4,4,64,128]{3,2,1,0:T(8,128)(2,1)S(1)}, bf16[4,4,64,128]{3,2,1,0:T(8,128)(2,1)S(1)}, u32[]{:S(2)}, u32[]{:S(2)}) collective-permute-start(bf16[4,4,64,128]{3,2,1,0:T(8,128)(2,1)S(1)} %slice.25), channel_id=1, source_target_pairs={{0,136},{128,0},{8,128},{136,8},{1,137},{129,1},{9,129},{137,9},{2... | collective-permute-start | bytes 786440 | tf_op jit(solution)/shard_map/ppermute | solution.py:290
  76.7 0.1 collective-permute-start.8
  76.7 0.8 fusion.7
  77.6 0.7 broadcast_in_dim.44
  78.3 4.3 %all-to-all-start.2 = ((bf16[8,64,128]{2,1,0:T(8,128)(2,1)}), bf16[8,64,128]{2,1,0:T(8,128)(2,1)S(1)}, u32[]{:S(2)}, u32[]{:S(2)}) async-start(bf16[8,64,128]{2,1,0:T(8,128)(2,1)} %broadcast_in_dim.44), calls=%async_computation.2 | async-start | bytes 262144 | tf_op jit(solution)/shard_map/all_to_all | solution.py:308
  82.6 3.1 %collective-permute-done.12 = f32[64,128]{1,0:T(8,128)S(1)} collective-permute-done((f32[64,128]{1,0:T(8,128)S(1)}, f32[64,128]{1,0:T(8,128)S(1)}, u32[]{:S(2)}, u32[]{:S(2)}) %collective-permute-start.12) | collective-permute-done | bytes 32800 | tf_op jit(solution)/shard_map/ppermute | solution.py:351
  85.7 4.9 %all-to-all-done.2 = bf16[8,64,128]{2,1,0:T(8,128)(2,1)S(1)} async-done(((bf16[8,64,128]{2,1,0:T(8,128)(2,1)}), bf16[8,64,128]{2,1,0:T(8,128)(2,1)S(1)}, u32[]{:S(2)}, u32[]{:S(2)}) %all-to-all-start.2) | async-done | bytes 131104 | tf_op jit(solution)/shard_map/all_to_all | solution.py:308
  90.6 1.8 %broadcast_in_dim.46 = bf16[16,512,128]{2,1,0:T(8,128)(2,1)} broadcast(bf16[512,128]{1,0:T(8,128)(2,1)S(1)} %bitcast.27), dimensions={1,2} | broadcast | bytes 2228224 | tf_op jit(solution)/shard_map/broadcast_in_dim | solution.py:326
  92.4 4.3 %all-to-all-start.3 = ((bf16[16,512,128]{2,1,0:T(8,128)(2,1)}), bf16[16,512,128]{2,1,0:T(8,128)(2,1)S(1)}, u32[]{:S(2)}, u32[]{:S(2)}) async-start(bf16[16,512,128]{2,1,0:T(8,128)(2,1)} %broadcast_in_dim.46), calls=%async_computation.3 | async-start | bytes 4194304 | tf_op jit(solution)/shard_map/all_to_all | solution.py:283
  96.8 3.3 %collective-permute-start.13 = (f32[64,256]{1,0:T(8,128)S(1)}, f32[64,256]{1,0:T(8,128)}, u32[]{:S(2)}, u32[]{:S(2)}) collective-permute-start(f32[64,256]{1,0:T(8,128)S(1)} %maximum_select_fusion.1), channel_id=1, source_target_pairs={{0,64},{64,0},{1,65},{65,1},{2,66},{66,2},{3,67},{67,3},{4,68},{68... | collective-permute-start | bytes 196616 | tf_op jit(solution)/shard_map/ppermute | solution.py:365
  100.1 0.9 copy-done.2
  101.1 8.9 %frozen_values.1.frozen = f32[1536,256]{1,0:T(8,128)S(1)} custom-call(s32[3]{0:T(128)S(1)} %pad_add_fusion.place, bf16[768,4096]{1,0:T(8,128)(2,1)} %tokens.3, bf16[768,4096]{1,0:T(8,128)(2,1)} %collective-permute-done.11.sibling, bf16[8,4,64,128]{3,2,1,0:T(8,128)(2,1)} %constant_dynamic-update-slice_fusion.here, ...), custom_call_target="tpu_custom_call" | custom-call | flops 3221225472 | bytes 16777216 | tf_op jit(solution)/shard_map/frozen_values/pallas_call | solution.py:219
  110.0 1.2 copy-done
  111.2 11.6 %all-to-all-done.3 = bf16[16,512,128]{2,1,0:T(8,128)(2,1)S(1)} async-done(((bf16[16,512,128]{2,1,0:T(8,128)(2,1)}), bf16[16,512,128]{2,1,0:T(8,128)(2,1)S(1)}, u32[]{:S(2)}, u32[]{:S(2)}) %all-to-all-start.3) | async-done | bytes 2097184 | tf_op jit(solution)/shard_map/all_to_all | solution.py:283
  122.8 11.7 %score_sums.1 = f32[256,1,128]{2,1,0:T(1,128)} custom-call(bf16[768,4096]{1,0:T(8,128)(2,1)} %tokens.3, bf16[768,4096]{1,0:T(8,128)(2,1)} %collective-permute-done.11.sibling, bf16[2,4096,128]{2,1,0:T(8,128)(2,1)S(1)} %bitcast.17, f32[1536,256]{1,0:T(8,128)} %copy-done, f32[1,256]{1,0:T(1,128)S(1)} %bitcast.19), custom_call_target="tpu_custom_call" | custom-call | flops 3221225472 | bytes 16777216 | tf_op jit(solution)/shard_map/score_sums/pallas_call | solution.py:241
  134.5 9.7 %all-to-all-start.4 = ((f32[256,1,128]{2,1,0:T(1,128)}), f32[256,1,128]{2,1,0:T(1,128)S(1)}, u32[]{:S(2)}, u32[]{:S(2)}) async-start(f32[256,1,128]{2,1,0:T(1,128)} %score_sums.1), calls=%async_computation.4 | async-start | bytes 262144 | tf_op jit(solution)/shard_map/all_to_all | solution.py:377
  144.2 0.2 slice_reduce_fusion
  144.4 1.8 %multiply_add_fusion = (f32[64,512]{1,0:T(8,128)}, f32[64,512]{1,0:T(8,128)}, f32[64,512]{1,0:T(8,128)}, f32[64,512]{1,0:T(8,128)}) fusion(f32[64,512]{1,0:T(8,128)S(1)} %copy-done.3, f32[64,512]{1,0:T(8,128)S(1)} %copy-done.4, f32[64,256]{1,0:T(8,128)S(1)} %maximum_select_fusion.1, f32[64,256]{1,0:T(8,128)} %collective-permute-done.13, pred[]{:T(512)S(6)} %eq.39, ...), kind=kLoop, calls=%fused_computation.8 | loop fusion | flops 589824 | bytes 1179649 | tf_op jit(solution)/shard_map/add | solution.py:33
  146.2 11.0 %all-to-all-done.4 = f32[256,1,128]{2,1,0:T(1,128)S(1)} async-done(((f32[256,1,128]{2,1,0:T(1,128)}), f32[256,1,128]{2,1,0:T(1,128)S(1)}, u32[]{:S(2)}, u32[]{:S(2)}) %all-to-all-start.4) | async-done | bytes 131104 | tf_op jit(solution)/shard_map/all_to_all | solution.py:377
  157.2 0.1 slice.27
  157.3 0.1 broadcast_in_dim.48
  157.4 0.2 fusion.9
  157.7 0.5 multiply_subtract_fusion
  (41 shorter events, 0.4 us)
Async XLA Ops:
  1.4 10.7 %collective-permute-start = (bf16[64,128]{1,0:T(8,128)(2,1)S(1)}, bf16[64,128]{1,0:T(8,128)(2,1)S(1)}, u32[]{:S(2)}, u32[]{:S(2)}) collective-permute-start(bf16[64,128]{1,0:T(8,128)(2,1)S(1)} %dynamic-slice_convert_fusion), channel_id=1, source_target_pairs={{0,48},{16,0},{32,16},{48,32},{1,49},{17,1},{33,17},{49,33},{2,50}... | collective-permute-start | bytes 49160 | tf_op jit(solution)/shard_map/ppermute | solution.py:296
  12.1 5.3 %collective-permute-start.1 = (bf16[2,8,128,512]{3,2,1,0:T(8,128)(2,1)S(1)}, bf16[2,8,128,512]{3,2,1,0:T(8,128)(2,1)S(1)}, u32[]{:S(2)}, u32[]{:S(2)}) collective-permute-start(bf16[2,8,128,512]{3,2,1,0:T(8,128)(2,1)S(1)} %get-tuple-element.21), channel_id=1, source_target_pairs={{0,64},{64,0},{1,65},{65,1},{2,66},{66,2},{3,67},{67,3},{4,68},{68... | collective-permute-start | bytes 6291464 | tf_op jit(solution)/shard_map/ppermute | solution.py:335
  13.1 4.3 %collective-permute-start.2 = (bf16[2,64,128]{2,1,0:T(8,128)(2,1)S(1)}, bf16[2,64,128]{2,1,0:T(8,128)(2,1)S(1)}, u32[]{:S(2)}, u32[]{:S(2)}) collective-permute-start(bf16[2,64,128]{2,1,0:T(8,128)(2,1)S(1)} %pad_maximum_fusion.3), channel_id=1, source_target_pairs={{0,32},{16,48},{32,0},{48,16},{1,33},{17,49},{33,1},{49,17},{2,34}... | collective-permute-start | bytes 98312 | tf_op jit(solution)/shard_map/ppermute | solution.py:296
  19.4 33.4 %all-to-all-start = ((bf16[16,128,512]{2,1,0:T(8,128)(2,1)}), bf16[16,128,512]{2,1,0:T(8,128)(2,1)S(1)}, u32[]{:S(2)}, u32[]{:S(2)}) async-start(bf16[16,128,512]{2,1,0:T(8,128)(2,1)} %bitcast.20), calls=%async_computation | async-start | bytes 4194304 | tf_op jit(solution)/shard_map/all_to_all | solution.py:283
  23.7 7.0 %collective-permute-start.3 = (bf16[1,4,64,128]{3,2,1,0:T(8,128)(2,1)S(1)}, bf16[1,4,64,128]{3,2,1,0:T(8,128)(2,1)S(1)}, u32[]{:S(2)}, u32[]{:S(2)}) collective-permute-start(bf16[1,4,64,128]{3,2,1,0:T(8,128)(2,1)S(1)} %bitcast.23), channel_id=1, source_target_pairs={{0,7},{1,0},{2,1},{3,2},{4,3},{5,4},{6,5},{7,6},{8,15},{9,8},{10,9... | collective-permute-start | bytes 196616 | tf_op jit(solution)/shard_map/ppermute | solution.py:296
  29.4 4.6 %collective-permute-start.4 = (bf16[1,4,64,128]{3,2,1,0:T(8,128)(2,1)S(1)}, bf16[1,4,64,128]{3,2,1,0:T(8,128)(2,1)S(1)}, u32[]{:S(2)}, u32[]{:S(2)}) collective-permute-start(bf16[1,4,64,128]{3,2,1,0:T(8,128)(2,1)S(1)} %bitcast.24), channel_id=1, source_target_pairs={{0,1},{1,2},{2,3},{3,4},{4,5},{5,6},{6,7},{7,0},{8,9},{9,10},{10,1... | collective-permute-start | bytes 196616 | tf_op jit(solution)/shard_map/ppermute | solution.py:296
  34.0 11.6 %collective-permute-start.5 = (bf16[3,4,64,128]{3,2,1,0:T(8,128)(2,1)S(1)}, bf16[3,4,64,128]{3,2,1,0:T(8,128)(2,1)S(1)}, u32[]{:S(2)}, u32[]{:S(2)}) collective-permute-start(bf16[3,4,64,128]{3,2,1,0:T(8,128)(2,1)S(1)} %pad_maximum_fusion), channel_id=1, source_target_pairs={{0,5},{1,6},{2,7},{3,0},{4,1},{5,2},{6,3},{7,4},{8,13},{9,14},{10,... | collective-permute-start | bytes 589832 | tf_op jit(solution)/shard_map/ppermute | solution.py:296
  34.2 12.1 %collective-permute-start.6 = (bf16[2,4,64,128]{3,2,1,0:T(8,128)(2,1)S(1)}, bf16[2,4,64,128]{3,2,1,0:T(8,128)(2,1)S(1)}, u32[]{:S(2)}, u32[]{:S(2)}) collective-permute-start(bf16[2,4,64,128]{3,2,1,0:T(8,128)(2,1)S(1)} %pad_maximum_fusion.1), channel_id=1, source_target_pairs={{0,3},{1,4},{2,5},{3,6},{4,7},{5,0},{6,1},{7,2},{8,11},{9,12},{10,... | collective-permute-start | bytes 393224 | tf_op jit(solution)/shard_map/ppermute | solution.py:296
  52.8 37.8 %collective-permute-start.11 = (bf16[768,4096]{1,0:T(8,128)(2,1)}, bf16[768,4096]{1,0:T(8,128)(2,1)}, u32[]{:S(2)}, u32[]{:S(2)}) collective-permute-start(bf16[768,4096]{1,0:T(8,128)(2,1)} %tokens.3), channel_id=1, source_target_pairs={{0,64},{64,0},{1,65},{65,1},{2,66},{66,2},{3,67},{67,3},{4,68},{68... | collective-permute-start | bytes 18874376 | tf_op jit(solution)/shard_map/ppermute | solution.py:342
  55.3 18.7 %collective-permute-start.9 = (bf16[8,4,64,128]{3,2,1,0:T(8,128)(2,1)}, bf16[8,4,64,128]{3,2,1,0:T(8,128)(2,1)S(1)}, u32[]{:S(2)}, u32[]{:S(2)}) collective-permute-start(bf16[8,4,64,128]{3,2,1,0:T(8,128)(2,1)} %constant_dynamic-update-slice_fusion.here), channel_id=1, source_target_pairs={{0,136},{128,0},{8,128},{136,8},{1,137},{129,1},{9,129},{137,9},{2... | collective-permute-start | bytes 1572872 | tf_op jit(solution)/shard_map/ppermute | solution.py:290
  57.5 19.1 %collective-permute-start.7 = (bf16[8,4,64,128]{3,2,1,0:T(8,128)(2,1)}, bf16[8,4,64,128]{3,2,1,0:T(8,128)(2,1)S(1)}, u32[]{:S(2)}, u32[]{:S(2)}) collective-permute-start(bf16[8,4,64,128]{3,2,1,0:T(8,128)(2,1)} %constant_dynamic-update-slice_fusion.here), channel_id=1, source_target_pairs={{0,128},{128,8},{8,136},{136,0},{1,129},{129,9},{9,137},{137,1},{2... | collective-permute-start | bytes 1572872 | tf_op jit(solution)/shard_map/ppermute | solution.py:290
  74.0 16.6 %collective-permute-start.10 = (bf16[4,4,64,128]{3,2,1,0:T(8,128)(2,1)S(1)}, bf16[4,4,64,128]{3,2,1,0:T(8,128)(2,1)S(1)}, u32[]{:S(2)}, u32[]{:S(2)}) collective-permute-start(bf16[4,4,64,128]{3,2,1,0:T(8,128)(2,1)S(1)} %slice.25), channel_id=1, source_target_pairs={{0,136},{128,0},{8,128},{136,8},{1,137},{129,1},{9,129},{137,9},{2... | collective-permute-start | bytes 786440 | tf_op jit(solution)/shard_map/ppermute | solution.py:290
  76.7 13.9 %collective-permute-start.8 = (bf16[4,4,64,128]{3,2,1,0:T(8,128)(2,1)S(1)}, bf16[4,4,64,128]{3,2,1,0:T(8,128)(2,1)S(1)}, u32[]{:S(2)}, u32[]{:S(2)}) collective-permute-start(bf16[4,4,64,128]{3,2,1,0:T(8,128)(2,1)S(1)} %slice.24), channel_id=1, source_target_pairs={{0,128},{128,8},{8,136},{136,0},{1,129},{129,9},{9,137},{137,1},{2... | collective-permute-start | bytes 786440 | tf_op jit(solution)/shard_map/ppermute | solution.py:290
  78.3 12.3 %all-to-all-start.2 = ((bf16[8,64,128]{2,1,0:T(8,128)(2,1)}), bf16[8,64,128]{2,1,0:T(8,128)(2,1)S(1)}, u32[]{:S(2)}, u32[]{:S(2)}) async-start(bf16[8,64,128]{2,1,0:T(8,128)(2,1)} %broadcast_in_dim.44), calls=%async_computation.2 | async-start | bytes 262144 | tf_op jit(solution)/shard_map/all_to_all | solution.py:308
  82.6 3.1 %collective-permute-start.12 = (f32[64,128]{1,0:T(8,128)S(1)}, f32[64,128]{1,0:T(8,128)S(1)}, u32[]{:S(2)}, u32[]{:S(2)}) collective-permute-start(f32[64,128]{1,0:T(8,128)S(1)} %convert_reduce_fusion), channel_id=1, source_target_pairs={{0,128},{128,0},{1,129},{129,1},{2,130},{130,2},{3,131},{131,3},{4... | collective-permute-start | bytes 98312 | tf_op jit(solution)/shard_map/ppermute | solution.py:351
  90.6 1.8 %copy-start.1 = (bf16[4,4,64,128]{3,2,1,0:T(8,128)(2,1)}, bf16[4,4,64,128]{3,2,1,0:T(8,128)(2,1)S(1)}, u32[]{:S(2)}) copy-start(bf16[4,4,64,128]{3,2,1,0:T(8,128)(2,1)S(1)} %collective-permute-done.8.far_left) | copy-start | bytes 786436
  92.4 4.3 %copy-start.8 = (f32[512]{0:T(512)S(1)}, f32[512]{0:T(512)}, u32[]{:S(2)}) copy-start(f32[512]{0:T(512)} %param.15) | copy-start | bytes 6148
  92.4 30.4 %all-to-all-start.3 = ((bf16[16,512,128]{2,1,0:T(8,128)(2,1)}), bf16[16,512,128]{2,1,0:T(8,128)(2,1)S(1)}, u32[]{:S(2)}, u32[]{:S(2)}) async-start(bf16[16,512,128]{2,1,0:T(8,128)(2,1)} %broadcast_in_dim.46), calls=%async_computation.3 | async-start | bytes 4194304 | tf_op jit(solution)/shard_map/all_to_all | solution.py:283
  96.8 47.6 %collective-permute-start.13 = (f32[64,256]{1,0:T(8,128)S(1)}, f32[64,256]{1,0:T(8,128)}, u32[]{:S(2)}, u32[]{:S(2)}) collective-permute-start(f32[64,256]{1,0:T(8,128)S(1)} %maximum_select_fusion.1), channel_id=1, source_target_pairs={{0,64},{64,0},{1,65},{65,1},{2,66},{66,2},{3,67},{67,3},{4,68},{68... | collective-permute-start | bytes 196616 | tf_op jit(solution)/shard_map/ppermute | solution.py:365
  100.1 0.9 copy-start.2
  110.0 1.2 copy-start
  122.8 21.5 %copy-start.7 = (s32[2,2]{1,0:T(2,128)S(1)}, s32[2,2]{1,0:T(2,128)}, u32[]{:S(2)}) copy-start(s32[2,2]{1,0:T(2,128)} %param.16) | copy-start | bytes 52
  122.8 21.7 %copy-start.3 = (f32[64,512]{1,0:T(8,128)S(1)}, f32[64,512]{1,0:T(8,128)}, u32[]{:S(2)}) copy-start(f32[64,512]{1,0:T(8,128)} %param.12) | copy-start | bytes 393220
  122.8 21.7 %copy-start.4 = (f32[64,512]{1,0:T(8,128)S(1)}, f32[64,512]{1,0:T(8,128)}, u32[]{:S(2)}) copy-start(f32[64,512]{1,0:T(8,128)} %param.11) | copy-start | bytes 393220
  122.8 21.7 %copy-start.5 = (f32[64,512]{1,0:T(8,128)S(1)}, f32[64,512]{1,0:T(8,128)}, u32[]{:S(2)}) copy-start(f32[64,512]{1,0:T(8,128)} %param.13) | copy-start | bytes 393220
  122.8 21.7 %copy-start.6 = (f32[64,512]{1,0:T(8,128)S(1)}, f32[64,512]{1,0:T(8,128)}, u32[]{:S(2)}) copy-start(f32[64,512]{1,0:T(8,128)} %param.14) | copy-start | bytes 393220
  134.5 23.2 %copy-start.9 = (s32[2]{0:T(128)S(1)}, s32[2]{0:T(128)}, u32[]{:S(2)}) copy-start(s32[2]{0:T(128)} %param.17) | copy-start | bytes 28
  134.5 22.7 %all-to-all-start.4 = ((f32[256,1,128]{2,1,0:T(1,128)}), f32[256,1,128]{2,1,0:T(1,128)S(1)}, u32[]{:S(2)}, u32[]{:S(2)}) async-start(f32[256,1,128]{2,1,0:T(1,128)} %score_sums.1), calls=%async_computation.4 | async-start | bytes 262144 | tf_op jit(solution)/shard_map/all_to_all | solution.py:377

commit v7 on v6

--- a/solution.py
+++ b/solution.py
@@ -22,7 +22,7 @@
 SWAP = ((0, 1), (1, 0))
 
 
-def adam_update(gradient, policy, anchor, moment, second):
+def policy_update(gradient, policy, moment, second):
     moment_new = beta_one * moment + (1.0 - beta_one) * gradient
     second_new = beta_two * second + (1.0 - beta_two) * gradient * gradient
     correct_one = 1.0 - beta_one**step_count
@@ -30,6 +30,11 @@
     policy_new = policy - learn_rate * (moment_new / correct_one) / (
         jnp.sqrt(second_new / correct_two) + adam_epsilon
     )
+    return (policy_new, moment_new, second_new)
+
+
+def adam_update(gradient, policy, anchor, moment, second):
+    policy_new, moment_new, second_new = policy_update(gradient, policy, moment, second)
     anchor_new = blend_rate * policy_new + (1.0 - blend_rate) * anchor
     return (policy_new, anchor_new, moment_new, second_new)
 
@@ -279,6 +284,32 @@
     )(blocks)
 
 
+def policy_kernel(place, column, policy, moment, second, gradient_out, message):
+    quarter = column.shape[2]
+    lanes = pl.ds(pl.multiple_of(place[0] * quarter, quarter), quarter)
+    gradient = column[0].astype(jnp.float32)
+    for at in range(1, column.shape[0]):
+        gradient = gradient + column[at].astype(jnp.float32)
+    gradient_out[...] = gradient
+    updated = policy_update(gradient, policy[:, lanes], moment[:, lanes], second[:, lanes])[0]
+    for at in range(message.shape[0]):
+        message[at] = updated.astype(message.dtype)
+
+
+def policy_message(place, column, policy, moment, second):
+    return pl.pallas_call(
+        policy_kernel,
+        in_specs=[pl.BlockSpec(memory_space=pltpu.SMEM)]
+        + [pl.BlockSpec(memory_space=pltpu.VMEM)] * 4,
+        out_shape=[
+            jax.ShapeDtypeStruct(column.shape[1:], jnp.float32),
+            jax.ShapeDtypeStruct(column.shape, column.dtype),
+        ],
+        compiler_params=pltpu.CompilerParams(vmem_limit_bytes=16 << 20),
+        name="policy_message",
+    )(place, column, policy, moment, second)
+
+
 def to_plane(blocks):
     return lax.all_to_all(blocks, PLANE, 0, 0, tiled=True)
 
@@ -319,9 +350,6 @@
     def piece(array):
         return lax.dynamic_slice_in_dim(array, (core * 2 + low) * quarter, quarter, axis=1)
 
-    def spread_z(block):
-        return along_z(jnp.broadcast_to(block[None], (8, rows, quarter))).reshape(8 * rows, quarter)
-
     def copies(column):
         return jnp.broadcast_to(column[None], (16,) + column.shape)
 
@@ -329,7 +357,7 @@
         return plane.reshape(2, features, quarter)
 
     sent, own = gradient_blocks(core[None], cotangent, tokens)
-    anchor_piece = piece(anchor).astype(jnp.bfloat16)
+    anchor_piece = lax.optimization_barrier(piece(anchor).astype(jnp.bfloat16))
     pair = jnp.stack([anchor_piece, shift_ring(anchor_piece, "y", 4, 1)])
     sent, pair = lax.optimization_barrier((sent, pair))
     arrived = lax.ppermute(sent, "core", SWAP)
@@ -342,15 +370,14 @@
     sibling = lax.ppermute(tokens, "core", SWAP)
     left, right = turn(strips, 1), turn(strips, -1)
     column = along_z(plane_sum(plane).reshape(8, rows, quarter))
-    gradient_piece = jnp.sum(column.astype(jnp.float32), axis=0)
-
     far_left, far_right = turn(left[:4], 1), turn(right[4:], -1)
-    policy_piece = adam_update(
-        gradient_piece, piece(policy), piece(anchor), piece(moment), piece(second)
-    )[0].astype(jnp.bfloat16)
+    gradient_piece, message = policy_message(
+        (core * 2 + low)[None], column, policy, moment, second
+    )
+    policy_column = along_z(message).reshape(8 * rows, quarter)
     other = lax.ppermute(gradient_piece, "xlo", SWAP)
     policy_copies, far_left, far_right, sibling, other = lax.optimization_barrier(
-        (copies(spread_z(policy_piece)), far_left, far_right, sibling, other)
+        (copies(policy_column), far_left, far_right, sibling, other)
     )
     policy_plane = to_plane(policy_copies)
     frozen = frozen_values(

time: 159 us -> 157 us (0.987)
  blocking collectives: 16 us -> 0 us
  starting transfers between devices: 47.4 us -> 57.5 us
  waiting for transfers between devices: 51.2 us -> 53.9 us
    all_to_all x1 -> x0, blocking collectives: 16 us -> none  [along_z(): return lax.all_to_all(blocks, 'z', 0, 0, tiled=True)]
    all_to_all x1 -> x2, starting transfers between devices: 4.35 us -> 14.5 us  [along_z(): return lax.all_to_all(blocks, 'z', 0, 0, tiled=True)]
    ppermute x4, waiting for transfers between devices: 0.01 us -> 2.49 us  [turn(): lax.ppermute(block, ('xlo', 'xhi'), [(index(x), index((x + shift) % 4)) f...]
    all_to_all x1 -> x2, waiting for transfers between devices: 4.9 us -> 7.03 us  [along_z(): return lax.all_to_all(blocks, 'z', 0, 0, tiled=True)]
    all_to_all x2, waiting for transfers between devices: 16.8 us -> 15 us  [to_plane(): return lax.all_to_all(blocks, PLANE, 0, 0, tiled=True)]
    unnamed x24 -> x32, local copies, waits for them, and re-layouts: 4.8 us -> 6.38 us
  transfers between devices with their start and end apart: 18 -> 19, of which waited for: 9 -> 11; matrix products, arithmetic and copies ran while one was open for 5% -> 4% of each run, Pallas kernels for 17% -> 18%
where the time goes in v7:
time: 157 us; the launch traced here: 156 us
  starting transfers between devices  57.5 us (37%)
  waiting for transfers between devices  53.9 us (34%)
  Pallas kernels  28 us (18%)
  local copies, waits for them, and re-layouts  10.1 us (6%)
  other arithmetic  6.15 us (4%)
    ppermute x6, waiting for transfers between devices, shift_ring(): lax.ppermute(block, axis, [(i, (i - shift) % size) for i in range(size)])  15.5 us
    all_to_all x2, waiting for transfers between devices, to_plane(): return lax.all_to_all(blocks, PLANE, 0, 0, tiled=True)  15 us
    all_to_all x2, starting transfers between devices, along_z(): return lax.all_to_all(blocks, 'z', 0, 0, tiled=True)  14.5 us
    ppermute x6, starting transfers between devices, shift_ring(): lax.ppermute(block, axis, [(i, (i - shift) % size) for i in range(size)])  13 us
    pallas_call x1, Pallas kernels, score_sums(): pl.pallas_call(score_kernel, out_shape=jax.ShapeDtypeStruct((256, 1, 128)...  11.7 us
    all_to_all x1, waiting for transfers between devices, shards(): parts = lax.all_to_all(parts, AXES, 0, 0, tiled=True)  11 us
    all_to_all x1, starting transfers between devices, shards(): parts = lax.all_to_all(parts, AXES, 0, 0, tiled=True)  9.15 us
    pallas_call x1, Pallas kernels, frozen_values(): pl.pallas_call(frozen_kernel, grid_spec=pltpu.PrefetchScalarGridSpec(num_...  8.91 us
  transfers between devices with their start and end apart: 19, of which 11 were waited for; matrix products, arithmetic and copies ran while one was open for 4% of the time, Pallas kernels for 18%

profile of v7, /device:TPU:1, one launch (start us, length us, event | category | flops | bytes accessed | tf_op | source)
XLA Modules:
  0.0 156.5 jit_solution(9758748155726847961)
XLA Ops:
  0.6 0.8 dynamic-slice_convert_fusion
  1.4 3.6 %collective-permute-start = (bf16[64,128]{1,0:T(8,128)(2,1)S(1)}, bf16[64,128]{1,0:T(8,128)(2,1)S(1)}, u32[]{:S(2)}, u32[]{:S(2)}) collective-permute-start(bf16[64,128]{1,0:T(8,128)(2,1)S(1)} %dynamic-slice_convert_fusion), channel_id=1, source_target_pairs={{0,48},{16,0},{32,16},{48,32},{1,49},{17,1},{33,17},{49,33},{2,50}... | collective-permute-start | bytes 49160 | tf_op jit(solution)/shard_map/ppermute | solution.py:327
  5.0 6.3 %gradient_blocks.1 = (bf16[2,8,128,512]{3,2,1,0:T(8,128)(2,1)S(1)}, bf16[2,8,128,512]{3,2,1,0:T(8,128)(2,1)S(1)}) custom-call(s32[1]{0:T(128)} %bitcast.1.place, bf16[768,512]{1,0:T(8,128)(2,1)} %cotangent.1, bf16[768,4096]{1,0:T(8,128)(2,1)} %tokens.3), custom_call_target="tpu_custom_call" | custom-call | flops 3221225472 | bytes 12582912 | tf_op jit(solution)/shard_map/gradient_blocks/pallas_call | solution.py:114
  11.3 1.0 collective-permute-start.1
  12.4 0.4 collective-permute-start.2
  12.7 3.9 %collective-permute-done.2 = bf16[2,64,128]{2,1,0:T(8,128)(2,1)S(1)} collective-permute-done((bf16[2,64,128]{2,1,0:T(8,128)(2,1)S(1)}, bf16[2,64,128]{2,1,0:T(8,128)(2,1)S(1)}, u32[]{:S(2)}, u32[]{:S(2)}) %collective-permute-start.2) | collective-permute-done | bytes 32800 | tf_op jit(solution)/shard_map/ppermute | solution.py:327
  16.7 2.0 %add_convert_fusion = bf16[2,8,128,512]{3,2,1,0:T(8,128)(2,1)} fusion(bf16[2,8,128,512]{3,2,1,0:T(8,128)(2,1)S(1)} %collective-permute-done.1, bf16[2,8,128,512]{3,2,1,0:T(8,128)(2,1)S(1)} %get-tuple-element.21), kind=kLoop, calls=%fused_computation | loop fusion | flops 4194304 | bytes 6291456 | tf_op jit(solution)/shard_map/convert_element_type | solution.py:366
  18.7 4.3 %all-to-all-start = ((bf16[16,128,512]{2,1,0:T(8,128)(2,1)}), bf16[16,128,512]{2,1,0:T(8,128)(2,1)S(1)}, u32[]{:S(2)}, u32[]{:S(2)}) async-start(bf16[16,128,512]{2,1,0:T(8,128)(2,1)} %bitcast.20), calls=%async_computation | async-start | bytes 4194304 | tf_op jit(solution)/shard_map/all_to_all | solution.py:314
  23.0 5.6 %collective-permute-start.3 = (bf16[1,4,64,128]{3,2,1,0:T(8,128)(2,1)S(1)}, bf16[1,4,64,128]{3,2,1,0:T(8,128)(2,1)S(1)}, u32[]{:S(2)}, u32[]{:S(2)}) collective-permute-start(bf16[1,4,64,128]{3,2,1,0:T(8,128)(2,1)S(1)} %bitcast.23), channel_id=1, source_target_pairs={{0,7},{1,0},{2,1},{3,2},{4,3},{5,4},{6,5},{7,6},{8,15},{9,8},{10,9... | collective-permute-start | bytes 196616 | tf_op jit(solution)/shard_map/ppermute | solution.py:327
  28.6 0.6 constant_dynamic-update-slice_fusion.4
  29.2 0.7 collective-permute-done.3
  30.0 3.3 %collective-permute-done.4 = bf16[1,4,64,128]{3,2,1,0:T(8,128)(2,1)S(1)} collective-permute-done((bf16[1,4,64,128]{3,2,1,0:T(8,128)(2,1)S(1)}, bf16[1,4,64,128]{3,2,1,0:T(8,128)(2,1)S(1)}, u32[]{:S(2)}, u32[]{:S(2)}) %collective-permute-start.4) | collective-permute-done | bytes 65568 | tf_op jit(solution)/shard_map/ppermute | solution.py:327
  33.3 0.2 collective-permute-start.5
  33.5 3.2 %collective-permute-start.6 = (bf16[2,4,64,128]{3,2,1,0:T(8,128)(2,1)S(1)}, bf16[2,4,64,128]{3,2,1,0:T(8,128)(2,1)S(1)}, u32[]{:S(2)}, u32[]{:S(2)}) collective-permute-start(bf16[2,4,64,128]{3,2,1,0:T(8,128)(2,1)S(1)} %pad_maximum_fusion.1), channel_id=1, source_target_pairs={{0,3},{1,4},{2,5},{3,6},{4,7},{5,0},{6,1},{7,2},{8,11},{9,12},{10,... | collective-permute-start | bytes 393224 | tf_op jit(solution)/shard_map/ppermute | solution.py:327
  36.7 0.6 constant_dynamic-update-slice_fusion.3
  37.3 7.6 %collective-permute-done.5 = bf16[3,4,64,128]{3,2,1,0:T(8,128)(2,1)S(1)} collective-permute-done((bf16[3,4,64,128]{3,2,1,0:T(8,128)(2,1)S(1)}, bf16[3,4,64,128]{3,2,1,0:T(8,128)(2,1)S(1)}, u32[]{:S(2)}, u32[]{:S(2)}) %collective-permute-start.5) | collective-permute-done | bytes 196640 | tf_op jit(solution)/shard_map/ppermute | solution.py:327
  44.9 0.7 constant_dynamic-update-slice_fusion.2
  45.6 0.7 constant_dynamic-update-slice_fusion.1
  46.3 0.6 constant_dynamic-update-slice_fusion.here
  46.9 5.2 %all-to-all-done.blocks = bf16[16,128,512]{2,1,0:T(8,128)(2,1)S(1)} async-done(((bf16[16,128,512]{2,1,0:T(8,128)(2,1)}), bf16[16,128,512]{2,1,0:T(8,128)(2,1)S(1)}, u32[]{:S(2)}, u32[]{:S(2)}) %all-to-all-start) | async-done | bytes 2097184 | tf_op jit(solution)/shard_map/all_to_all | solution.py:314
  52.1 2.4 %collective-permute-start.11 = (bf16[768,4096]{1,0:T(8,128)(2,1)}, bf16[768,4096]{1,0:T(8,128)(2,1)}, u32[]{:S(2)}, u32[]{:S(2)}) collective-permute-start(bf16[768,4096]{1,0:T(8,128)(2,1)} %tokens.3), channel_id=1, source_target_pairs={{0,64},{64,0},{1,65},{65,1},{2,66},{66,2},{3,67},{67,3},{4,68},{68... | collective-permute-start | bytes 18874376 | tf_op jit(solution)/shard_map/ppermute | solution.py:370
  54.5 2.3 %collective-permute-start.9 = (bf16[8,4,64,128]{3,2,1,0:T(8,128)(2,1)}, bf16[8,4,64,128]{3,2,1,0:T(8,128)(2,1)S(1)}, u32[]{:S(2)}, u32[]{:S(2)}) collective-permute-start(bf16[8,4,64,128]{3,2,1,0:T(8,128)(2,1)} %constant_dynamic-update-slice_fusion.here), channel_id=1, source_target_pairs={{0,136},{128,0},{8,128},{136,8},{1,137},{129,1},{9,129},{137,9},{2... | collective-permute-start | bytes 1572872 | tf_op jit(solution)/shard_map/ppermute | solution.py:321
  56.8 0.3 plane_sum.1
  57.2 0.6 copy-done.4
  57.8 8.2 %all-to-all-start.1 = ((bf16[8,64,128]{2,1,0:T(8,128)(2,1)}), bf16[8,64,128]{2,1,0:T(8,128)(2,1)S(1)}, u32[]{:S(2)}, u32[]{:S(2)}) async-start(bf16[8,64,128]{2,1,0:T(8,128)(2,1)} %bitcast.18), calls=%async_computation.1 | async-start | bytes 262144 | tf_op jit(solution)/shard_map/all_to_all | solution.py:339
  66.0 2.5 %collective-permute-done.9.right = bf16[8,4,64,128]{3,2,1,0:T(8,128)(2,1)S(1)} collective-permute-done((bf16[8,4,64,128]{3,2,1,0:T(8,128)(2,1)}, bf16[8,4,64,128]{3,2,1,0:T(8,128)(2,1)S(1)}, u32[]{:S(2)}, u32[]{:S(2)}) %collective-permute-start.9) | collective-permute-done | bytes 524320 | tf_op jit(solution)/shard_map/ppermute | solution.py:321
  68.5 3.6 %collective-permute-start.10 = (bf16[4,4,64,128]{3,2,1,0:T(8,128)(2,1)S(1)}, bf16[4,4,64,128]{3,2,1,0:T(8,128)(2,1)S(1)}, u32[]{:S(2)}, u32[]{:S(2)}) collective-permute-start(bf16[4,4,64,128]{3,2,1,0:T(8,128)(2,1)S(1)} %slice.25), channel_id=1, source_target_pairs={{0,136},{128,0},{8,128},{136,8},{1,137},{129,1},{9,129},{137,9},{2... | collective-permute-start | bytes 786440 | tf_op jit(solution)/shard_map/ppermute | solution.py:321
  72.2 1.9 %all-to-all-done.1.column = bf16[8,64,128]{2,1,0:T(8,128)(2,1)S(1)} async-done(((bf16[8,64,128]{2,1,0:T(8,128)(2,1)}), bf16[8,64,128]{2,1,0:T(8,128)(2,1)S(1)}, u32[]{:S(2)}, u32[]{:S(2)}) %all-to-all-start.1) | async-done | bytes 131104 | tf_op jit(solution)/shard_map/all_to_all | solution.py:339
  74.1 0.7 policy_message.1
  74.8 6.3 %all-to-all-start.2 = ((bf16[8,64,128]{2,1,0:T(8,128)(2,1)}), bf16[8,64,128]{2,1,0:T(8,128)(2,1)S(1)}, u32[]{:S(2)}, u32[]{:S(2)}) async-start(bf16[8,64,128]{2,1,0:T(8,128)(2,1)} %get-tuple-element.29), calls=%async_computation.2 | async-start | bytes 262144 | tf_op jit(solution)/shard_map/all_to_all | solution.py:339
  81.1 2.9 %collective-permute-done.12 = f32[64,128]{1,0:T(8,128)} collective-permute-done((f32[64,128]{1,0:T(8,128)S(1)}, f32[64,128]{1,0:T(8,128)}, u32[]{:S(2)}, u32[]{:S(2)}) %collective-permute-start.12) | collective-permute-done | bytes 32800 | tf_op jit(solution)/shard_map/ppermute | solution.py:378
  84.0 5.2 %all-to-all-done.2 = bf16[8,64,128]{2,1,0:T(8,128)(2,1)S(1)} async-done(((bf16[8,64,128]{2,1,0:T(8,128)(2,1)}), bf16[8,64,128]{2,1,0:T(8,128)(2,1)S(1)}, u32[]{:S(2)}, u32[]{:S(2)}) %all-to-all-start.2) | async-done | bytes 131104 | tf_op jit(solution)/shard_map/all_to_all | solution.py:339
  89.2 1.8 %broadcast_in_dim.43 = bf16[16,512,128]{2,1,0:T(8,128)(2,1)} broadcast(bf16[512,128]{1,0:T(8,128)(2,1)S(1)} %bitcast.27), dimensions={1,2} | broadcast | bytes 2228224 | tf_op jit(solution)/shard_map/broadcast_in_dim | solution.py:354
  91.0 4.2 %all-to-all-start.3 = ((bf16[16,512,128]{2,1,0:T(8,128)(2,1)}), bf16[16,512,128]{2,1,0:T(8,128)(2,1)S(1)}, u32[]{:S(2)}, u32[]{:S(2)}) async-start(bf16[16,512,128]{2,1,0:T(8,128)(2,1)} %broadcast_in_dim.43), calls=%async_computation.3 | async-start | bytes 4194304 | tf_op jit(solution)/shard_map/all_to_all | solution.py:314
  95.3 1.5 maximum_select_fusion.1
  96.8 2.9 %collective-permute-start.13 = (f32[64,256]{1,0:T(8,128)}, f32[64,256]{1,0:T(8,128)}, u32[]{:S(2)}, u32[]{:S(2)}) collective-permute-start(f32[64,256]{1,0:T(8,128)} %maximum_select_fusion.1), channel_id=1, source_target_pairs={{0,64},{64,0},{1,65},{65,1},{2,66},{66,2},{3,67},{67,3},{4,68},{68... | collective-permute-start | bytes 196616 | tf_op jit(solution)/shard_map/ppermute | solution.py:392
  99.7 0.9 copy-done.6
  100.7 0.9 copy-done.8
  101.6 8.9 %frozen_values.1.frozen = f32[1536,256]{1,0:T(8,128)S(1)} custom-call(s32[3]{0:T(128)S(1)} %pad_add_fusion.place, bf16[768,4096]{1,0:T(8,128)(2,1)} %tokens.3, bf16[768,4096]{1,0:T(8,128)(2,1)} %collective-permute-done.11.sibling, bf16[8,4,64,128]{3,2,1,0:T(8,128)(2,1)} %constant_dynamic-update-slice_fusion.here, ...), custom_call_target="tpu_custom_call" | custom-call | flops 3221225472 | bytes 16777216 | tf_op jit(solution)/shard_map/frozen_values/pallas_call | solution.py:224
  110.6 1.2 copy-done
  111.7 9.8 %all-to-all-done.3 = bf16[16,512,128]{2,1,0:T(8,128)(2,1)S(1)} async-done(((bf16[16,512,128]{2,1,0:T(8,128)(2,1)}), bf16[16,512,128]{2,1,0:T(8,128)(2,1)S(1)}, u32[]{:S(2)}, u32[]{:S(2)}) %all-to-all-start.3) | async-done | bytes 2097184 | tf_op jit(solution)/shard_map/all_to_all | solution.py:314
  121.6 11.7 %score_sums.1 = f32[256,1,128]{2,1,0:T(1,128)} custom-call(bf16[768,4096]{1,0:T(8,128)(2,1)} %tokens.3, bf16[768,4096]{1,0:T(8,128)(2,1)} %collective-permute-done.11.sibling, bf16[2,4096,128]{2,1,0:T(8,128)(2,1)S(1)} %bitcast.17, f32[1536,256]{1,0:T(8,128)} %copy-done, f32[1,256]{1,0:T(1,128)S(1)} %bitcast.19), custom_call_target="tpu_custom_call" | custom-call | flops 3221225472 | bytes 16777216 | tf_op jit(solution)/shard_map/score_sums/pallas_call | solution.py:246
  133.3 9.2 %all-to-all-start.4 = ((f32[256,1,128]{2,1,0:T(1,128)}), f32[256,1,128]{2,1,0:T(1,128)S(1)}, u32[]{:S(2)}, u32[]{:S(2)}) async-start(f32[256,1,128]{2,1,0:T(1,128)} %score_sums.1), calls=%async_computation.4 | async-start | bytes 262144 | tf_op jit(solution)/shard_map/all_to_all | solution.py:404
  142.5 0.2 slice_reduce_fusion
  142.7 1.8 %multiply_add_fusion = (f32[64,512]{1,0:T(8,128)}, f32[64,512]{1,0:T(8,128)}, f32[64,512]{1,0:T(8,128)}, f32[64,512]{1,0:T(8,128)}) fusion(f32[64,512]{1,0:T(8,128)S(1)} %copy-done.10, f32[64,512]{1,0:T(8,128)S(1)} %copy-done.1, f32[64,256]{1,0:T(8,128)} %maximum_select_fusion.1, f32[64,256]{1,0:T(8,128)} %collective-permute-done.13, pred[]{:T(512)S(6)} %eq.39, ...), kind=kLoop, calls=%fused_computation.7 | loop fusion | flops 589824 | bytes 1179649 | tf_op jit(solution)/shard_map/add | solution.py:38
  144.4 11.0 %all-to-all-done.4 = f32[256,1,128]{2,1,0:T(1,128)S(1)} async-done(((f32[256,1,128]{2,1,0:T(1,128)}), f32[256,1,128]{2,1,0:T(1,128)S(1)}, u32[]{:S(2)}, u32[]{:S(2)}) %all-to-all-start.4) | async-done | bytes 131104 | tf_op jit(solution)/shard_map/all_to_all | solution.py:404
  155.7 0.2 fusion.2
  155.9 0.5 multiply_subtract_fusion
  (47 shorter events, 0.6 us)
Async XLA Ops:
  1.4 9.9 %collective-permute-start = (bf16[64,128]{1,0:T(8,128)(2,1)S(1)}, bf16[64,128]{1,0:T(8,128)(2,1)S(1)}, u32[]{:S(2)}, u32[]{:S(2)}) collective-permute-start(bf16[64,128]{1,0:T(8,128)(2,1)S(1)} %dynamic-slice_convert_fusion), channel_id=1, source_target_pairs={{0,48},{16,0},{32,16},{48,32},{1,49},{17,1},{33,17},{49,33},{2,50}... | collective-permute-start | bytes 49160 | tf_op jit(solution)/shard_map/ppermute | solution.py:327
  11.3 5.3 %collective-permute-start.1 = (bf16[2,8,128,512]{3,2,1,0:T(8,128)(2,1)S(1)}, bf16[2,8,128,512]{3,2,1,0:T(8,128)(2,1)S(1)}, u32[]{:S(2)}, u32[]{:S(2)}) collective-permute-start(bf16[2,8,128,512]{3,2,1,0:T(8,128)(2,1)S(1)} %get-tuple-element.23), channel_id=1, source_target_pairs={{0,64},{64,0},{1,65},{65,1},{2,66},{66,2},{3,67},{67,3},{4,68},{68... | collective-permute-start | bytes 6291464 | tf_op jit(solution)/shard_map/ppermute | solution.py:363
  12.4 4.3 %collective-permute-start.2 = (bf16[2,64,128]{2,1,0:T(8,128)(2,1)S(1)}, bf16[2,64,128]{2,1,0:T(8,128)(2,1)S(1)}, u32[]{:S(2)}, u32[]{:S(2)}) collective-permute-start(bf16[2,64,128]{2,1,0:T(8,128)(2,1)S(1)} %pad_maximum_fusion.3), channel_id=1, source_target_pairs={{0,32},{16,48},{32,0},{48,16},{1,33},{17,49},{33,1},{49,17},{2,34}... | collective-permute-start | bytes 98312 | tf_op jit(solution)/shard_map/ppermute | solution.py:327
  18.7 33.4 %all-to-all-start = ((bf16[16,128,512]{2,1,0:T(8,128)(2,1)}), bf16[16,128,512]{2,1,0:T(8,128)(2,1)S(1)}, u32[]{:S(2)}, u32[]{:S(2)}) async-start(bf16[16,128,512]{2,1,0:T(8,128)(2,1)} %bitcast.20), calls=%async_computation | async-start | bytes 4194304 | tf_op jit(solution)/shard_map/all_to_all | solution.py:314
  23.0 7.0 %collective-permute-start.3 = (bf16[1,4,64,128]{3,2,1,0:T(8,128)(2,1)S(1)}, bf16[1,4,64,128]{3,2,1,0:T(8,128)(2,1)S(1)}, u32[]{:S(2)}, u32[]{:S(2)}) collective-permute-start(bf16[1,4,64,128]{3,2,1,0:T(8,128)(2,1)S(1)} %bitcast.23), channel_id=1, source_target_pairs={{0,7},{1,0},{2,1},{3,2},{4,3},{5,4},{6,5},{7,6},{8,15},{9,8},{10,9... | collective-permute-start | bytes 196616 | tf_op jit(solution)/shard_map/ppermute | solution.py:327
  28.6 4.6 %collective-permute-start.4 = (bf16[1,4,64,128]{3,2,1,0:T(8,128)(2,1)S(1)}, bf16[1,4,64,128]{3,2,1,0:T(8,128)(2,1)S(1)}, u32[]{:S(2)}, u32[]{:S(2)}) collective-permute-start(bf16[1,4,64,128]{3,2,1,0:T(8,128)(2,1)S(1)} %bitcast.24), channel_id=1, source_target_pairs={{0,1},{1,2},{2,3},{3,4},{4,5},{5,6},{6,7},{7,0},{8,9},{9,10},{10,1... | collective-permute-start | bytes 196616 | tf_op jit(solution)/shard_map/ppermute | solution.py:327
  33.3 11.6 %collective-permute-start.5 = (bf16[3,4,64,128]{3,2,1,0:T(8,128)(2,1)S(1)}, bf16[3,4,64,128]{3,2,1,0:T(8,128)(2,1)S(1)}, u32[]{:S(2)}, u32[]{:S(2)}) collective-permute-start(bf16[3,4,64,128]{3,2,1,0:T(8,128)(2,1)S(1)} %pad_maximum_fusion), channel_id=1, source_target_pairs={{0,5},{1,6},{2,7},{3,0},{4,1},{5,2},{6,3},{7,4},{8,13},{9,14},{10,... | collective-permute-start | bytes 589832 | tf_op jit(solution)/shard_map/ppermute | solution.py:327
  33.5 12.1 %collective-permute-start.6 = (bf16[2,4,64,128]{3,2,1,0:T(8,128)(2,1)S(1)}, bf16[2,4,64,128]{3,2,1,0:T(8,128)(2,1)S(1)}, u32[]{:S(2)}, u32[]{:S(2)}) collective-permute-start(bf16[2,4,64,128]{3,2,1,0:T(8,128)(2,1)S(1)} %pad_maximum_fusion.1), channel_id=1, source_target_pairs={{0,3},{1,4},{2,5},{3,6},{4,7},{5,0},{6,1},{7,2},{8,11},{9,12},{10,... | collective-permute-start | bytes 393224 | tf_op jit(solution)/shard_map/ppermute | solution.py:327
  37.3 36.7 %copy-start.1 = (f32[64,512]{1,0:T(8,128)S(1)}, f32[64,512]{1,0:T(8,128)}, u32[]{:S(2)}) copy-start(f32[64,512]{1,0:T(8,128)} %policy.1) | copy-start | bytes 393220
  37.3 36.7 %copy-start.2 = (f32[64,512]{1,0:T(8,128)S(1)}, f32[64,512]{1,0:T(8,128)}, u32[]{:S(2)}) copy-start(f32[64,512]{1,0:T(8,128)} %moment.1) | copy-start | bytes 393220
  37.3 36.7 %copy-start.3 = (f32[64,512]{1,0:T(8,128)S(1)}, f32[64,512]{1,0:T(8,128)}, u32[]{:S(2)}) copy-start(f32[64,512]{1,0:T(8,128)} %second.1) | copy-start | bytes 393220
  52.1 37.1 %collective-permute-start.11 = (bf16[768,4096]{1,0:T(8,128)(2,1)}, bf16[768,4096]{1,0:T(8,128)(2,1)}, u32[]{:S(2)}, u32[]{:S(2)}) collective-permute-start(bf16[768,4096]{1,0:T(8,128)(2,1)} %tokens.3), channel_id=1, source_target_pairs={{0,64},{64,0},{1,65},{65,1},{2,66},{66,2},{3,67},{67,3},{4,68},{68... | collective-permute-start | bytes 18874376 | tf_op jit(solution)/shard_map/ppermute | solution.py:370
  54.5 13.9 %collective-permute-start.9 = (bf16[8,4,64,128]{3,2,1,0:T(8,128)(2,1)}, bf16[8,4,64,128]{3,2,1,0:T(8,128)(2,1)S(1)}, u32[]{:S(2)}, u32[]{:S(2)}) collective-permute-start(bf16[8,4,64,128]{3,2,1,0:T(8,128)(2,1)} %constant_dynamic-update-slice_fusion.here), channel_id=1, source_target_pairs={{0,136},{128,0},{8,128},{136,8},{1,137},{129,1},{9,129},{137,9},{2... | collective-permute-start | bytes 1572872 | tf_op jit(solution)/shard_map/ppermute | solution.py:321
  56.8 15.3 %collective-permute-start.7 = (bf16[8,4,64,128]{3,2,1,0:T(8,128)(2,1)}, bf16[8,4,64,128]{3,2,1,0:T(8,128)(2,1)S(1)}, u32[]{:S(2)}, u32[]{:S(2)}) collective-permute-start(bf16[8,4,64,128]{3,2,1,0:T(8,128)(2,1)} %constant_dynamic-update-slice_fusion.here), channel_id=1, source_target_pairs={{0,128},{128,8},{8,136},{136,0},{1,129},{129,9},{9,137},{137,1},{2... | collective-permute-start | bytes 1572872 | tf_op jit(solution)/shard_map/ppermute | solution.py:321
  57.1 0.7 copy-start.4
  57.8 16.2 %all-to-all-start.1 = ((bf16[8,64,128]{2,1,0:T(8,128)(2,1)}), bf16[8,64,128]{2,1,0:T(8,128)(2,1)S(1)}, u32[]{:S(2)}, u32[]{:S(2)}) async-start(bf16[8,64,128]{2,1,0:T(8,128)(2,1)} %bitcast.18), calls=%async_computation.1 | async-start | bytes 262144 | tf_op jit(solution)/shard_map/all_to_all | solution.py:339
  68.5 20.7 %collective-permute-start.10 = (bf16[4,4,64,128]{3,2,1,0:T(8,128)(2,1)S(1)}, bf16[4,4,64,128]{3,2,1,0:T(8,128)(2,1)S(1)}, u32[]{:S(2)}, u32[]{:S(2)}) collective-permute-start(bf16[4,4,64,128]{3,2,1,0:T(8,128)(2,1)S(1)} %slice.25), channel_id=1, source_target_pairs={{0,136},{128,0},{8,128},{136,8},{1,137},{129,1},{9,129},{137,9},{2... | collective-permute-start | bytes 786440 | tf_op jit(solution)/shard_map/ppermute | solution.py:321
  72.1 17.1 %collective-permute-start.8 = (bf16[4,4,64,128]{3,2,1,0:T(8,128)(2,1)S(1)}, bf16[4,4,64,128]{3,2,1,0:T(8,128)(2,1)S(1)}, u32[]{:S(2)}, u32[]{:S(2)}) collective-permute-start(bf16[4,4,64,128]{3,2,1,0:T(8,128)(2,1)S(1)} %slice.24), channel_id=1, source_target_pairs={{0,128},{128,8},{8,136},{136,0},{1,129},{129,9},{9,137},{137,1},{2... | collective-permute-start | bytes 786440 | tf_op jit(solution)/shard_map/ppermute | solution.py:321
  74.8 16.2 %copy-start.9 = (f32[64,128]{1,0:T(8,128)}, f32[64,128]{1,0:T(8,128)S(1)}, u32[]{:S(2)}) copy-start(f32[64,128]{1,0:T(8,128)S(1)} %get-tuple-element.28) | copy-start | bytes 98308
  74.8 14.4 %all-to-all-start.2 = ((bf16[8,64,128]{2,1,0:T(8,128)(2,1)}), bf16[8,64,128]{2,1,0:T(8,128)(2,1)S(1)}, u32[]{:S(2)}, u32[]{:S(2)}) async-start(bf16[8,64,128]{2,1,0:T(8,128)(2,1)} %get-tuple-element.29), calls=%async_computation.2 | async-start | bytes 262144 | tf_op jit(solution)/shard_map/all_to_all | solution.py:339
  81.1 2.9 %collective-permute-start.12 = (f32[64,128]{1,0:T(8,128)S(1)}, f32[64,128]{1,0:T(8,128)}, u32[]{:S(2)}, u32[]{:S(2)}) collective-permute-start(f32[64,128]{1,0:T(8,128)S(1)} %get-tuple-element.28), channel_id=1, source_target_pairs={{0,128},{128,0},{1,129},{129,1},{2,130},{130,2},{3,131},{131,3},{4... | collective-permute-start | bytes 98312 | tf_op jit(solution)/shard_map/ppermute | solution.py:378
  89.1 1.8 %copy-start.5 = (bf16[4,4,64,128]{3,2,1,0:T(8,128)(2,1)}, bf16[4,4,64,128]{3,2,1,0:T(8,128)(2,1)S(1)}, u32[]{:S(2)}) copy-start(bf16[4,4,64,128]{3,2,1,0:T(8,128)(2,1)S(1)} %collective-permute-done.10.far_right) | copy-start | bytes 786436
  89.2 1.8 %copy-start.7 = (bf16[4,4,64,128]{3,2,1,0:T(8,128)(2,1)}, bf16[4,4,64,128]{3,2,1,0:T(8,128)(2,1)S(1)}, u32[]{:S(2)}) copy-start(bf16[4,4,64,128]{3,2,1,0:T(8,128)(2,1)S(1)} %collective-permute-done.8.far_left) | copy-start | bytes 786436
  91.0 4.2 %copy-start.12 = (f32[512]{0:T(512)S(1)}, f32[512]{0:T(512)}, u32[]{:S(2)}) copy-start(f32[512]{0:T(512)} %param.15) | copy-start | bytes 6148
  91.0 30.6 %all-to-all-start.3 = ((bf16[16,512,128]{2,1,0:T(8,128)(2,1)}), bf16[16,512,128]{2,1,0:T(8,128)(2,1)S(1)}, u32[]{:S(2)}, u32[]{:S(2)}) async-start(bf16[16,512,128]{2,1,0:T(8,128)(2,1)} %broadcast_in_dim.43), calls=%async_computation.3 | async-start | bytes 4194304 | tf_op jit(solution)/shard_map/all_to_all | solution.py:314
  96.8 45.9 %collective-permute-start.13 = (f32[64,256]{1,0:T(8,128)}, f32[64,256]{1,0:T(8,128)}, u32[]{:S(2)}, u32[]{:S(2)}) collective-permute-start(f32[64,256]{1,0:T(8,128)} %maximum_select_fusion.1), channel_id=1, source_target_pairs={{0,64},{64,0},{1,65},{65,1},{2,66},{66,2},{3,67},{67,3},{4,68},{68... | collective-permute-start | bytes 196616 | tf_op jit(solution)/shard_map/ppermute | solution.py:392
  99.7 0.9 copy-start.6
  100.7 0.9 copy-start.8
  110.6 1.2 copy-start
  121.6 20.9 %copy-start.11 = (s32[2,2]{1,0:T(2,128)S(1)}, s32[2,2]{1,0:T(2,128)}, u32[]{:S(2)}) copy-start(s32[2,2]{1,0:T(2,128)} %param.16) | copy-start | bytes 52
  121.6 21.1 %copy-start.10 = (f32[64,512]{1,0:T(8,128)S(1)}, f32[64,512]{1,0:T(8,128)}, u32[]{:S(2)}) copy-start(f32[64,512]{1,0:T(8,128)} %param.12) | copy-start | bytes 393220
  133.3 22.6 %copy-start.13 = (s32[2]{0:T(128)S(1)}, s32[2]{0:T(128)}, u32[]{:S(2)}) copy-start(s32[2]{0:T(128)} %param.17) | copy-start | bytes 28
  133.3 22.2 %all-to-all-start.4 = ((f32[256,1,128]{2,1,0:T(1,128)}), f32[256,1,128]{2,1,0:T(1,128)S(1)}, u32[]{:S(2)}, u32[]{:S(2)}) async-start(f32[256,1,128]{2,1,0:T(1,128)} %score_sums.1), calls=%async_computation.4 | async-start | bytes 262144 | tf_op jit(solution)/shard_map/all_to_all | solution.py:404

commit v8 on v7

--- a/solution.py
+++ b/solution.py
@@ -56,7 +56,6 @@
 
 VMEM = 32 << 20
 VMEM_GRADIENT = 32 << 20
-VMEM_SCORE = 32 << 20
 AHEAD = 3
 
 
@@ -133,28 +132,39 @@
     )(place, in_hbm(cotangent), in_hbm(tokens))
 
 
-def frozen_kernel(place, tokens, sibling, here, left, right, far_left, far_right, out, joined):
+def chunk_loads(source, target, sems):
+    return [
+        pltpu.make_async_copy(
+            source.at[pl.ds(at * LEN, LEN)], target.at[pl.ds(at * LEN, LEN)], sems.at[at]
+        )
+        for at in range(source.shape[0] // LEN)
+    ]
+
+
+def product_kernel(tokens, own, sibling, out, out_sibling, held, sems):
+    loads = chunk_loads(tokens, held, sems)
+    for load in loads:
+        load.start()
+    for at, load in enumerate(loads):
+        load.wait()
+        span = slice(at * LEN, (at + 1) * LEN)
+        for weights, target in ((own, out), (sibling, out_sibling)):
+            target[span] = jnp.dot(held[span], weights[...], preferred_element_type=jnp.float32)
+
+
+def assemble_kernel(place, here, left, right, far_left, far_right, joined):
     depth, count, rows, quarter = here.shape
-
-    @pl.when(pl.program_id(0) == 0)
-    def _():
-        for shift, ref, first in (
-            (0, here, 0), (3, left, 0), (1, right, 0), (2, far_left, 0), (2, far_right, depth // 2)
-        ):
-            chip = (place[0] + shift) % 4
-            lanes = pl.ds(pl.multiple_of((chip % 2) * quarter, quarter), quarter)
-            for at in range(ref.shape[0]):
-                level = (place[2] + first + at) % 8
-                for turn_y in range(count):
-                    owner = ((place[1] + turn_y) % 4) * 16 + (chip // 2) * 8 + level
-                    span = pl.ds(pl.multiple_of(owner * rows, rows), rows)
-                    joined[span, lanes] = ref[at, turn_y]
-
-    for ref, turn_of in ((tokens, pl.program_id(0) < 2), (sibling, pl.program_id(0) >= 2)):
-
-        @pl.when(turn_of)
-        def _():
-            out[...] = jnp.dot(ref[...], joined[...], preferred_element_type=jnp.float32)
+    for shift, ref, first in (
+        (0, here, 0), (3, left, 0), (1, right, 0), (2, far_left, 0), (2, far_right, depth // 2)
+    ):
+        chip = (place[0] + shift) % 4
+        lanes = pl.ds(pl.multiple_of((chip % 2) * quarter, quarter), quarter)
+        for at in range(ref.shape[0]):
+            level = (place[2] + first + at) % 8
+            for turn_y in range(count):
+                owner = ((place[1] + turn_y) % 4) * 16 + (chip // 2) * 8 + level
+                span = pl.ds(pl.multiple_of(owner * rows, rows), rows)
+                joined[span, lanes] = ref[at, turn_y]
 
 
 def sigmoid_sums(values):
@@ -168,103 +178,138 @@
     return low_sum - jnp.log(product)
 
 
-def score_kernel(tokens, sibling, halves, frozen, readout, out, joined, held, still, sems):
+def chunk_scores(tokens, weights, frozen, scale, at):
+    span = slice(at * LEN, (at + 1) * LEN)
+    values = jnp.dot(tokens[span], weights[...], preferred_element_type=jnp.float32)
+    blended = blend_rate * values + (1.0 - blend_rate) * frozen[span]
+    gap = sigmoid_sums(values * scale) - sigmoid_sums(blended * scale)
+    lane = lax.broadcasted_iota(jnp.int32, (1, 128), 1)
+    return jnp.where(lane == at, jnp.sum(gap) / LEN, 0.0)
+
+
+def join(halves, joined):
     quarter = halves.shape[-1]
-    count = tokens.shape[0]
-    sizes = (LEN,) * 8
-    loads, at = [], 0
-    for step, size in enumerate(sizes):
-        source, first = (tokens, at) if at < count else (sibling, at - count)
-        span = pl.ds(at, size)
-        loads.append(
-            (
-                pltpu.make_async_copy(
-                    source.at[pl.ds(first, size)], held.at[span], sems.at[2 * step]
-                ),
-                pltpu.make_async_copy(frozen.at[span], still.at[span], sems.at[2 * step + 1]),
-            )
-        )
-        at += size
-    for pair in loads[:AHEAD]:
+    joined[:, :quarter] = halves[0]
+    joined[:, quarter:] = halves[1]
+
+
+def own_kernel(tokens, halves, frozen, readout, parts, kept, joined, still, sems, still_sems):
+    loads = chunk_loads(tokens, kept, sems)
+    still_loads = chunk_loads(frozen, still, still_sems)
+    for pair in zip(loads, still_loads):
         for load in pair:
             load.start()
-    joined[:, :quarter] = halves[0]
-    joined[:, quarter:] = halves[1]
+    join(halves, joined)
     scale = readout[...]
-    lane = lax.broadcasted_iota(jnp.int32, (1, 128), 1)
-    parts = jnp.zeros((1, 128), jnp.float32)
-    at = 0
-    for step, size in enumerate(sizes):
-        for load in loads[step]:
-            load.wait()
-        for load in loads[step + AHEAD] if step + AHEAD < len(sizes) else ():
-            load.start()
-        values = jnp.dot(held[at : at + size], joined[...], preferred_element_type=jnp.float32)
-        blended = blend_rate * values + (1.0 - blend_rate) * still[at : at + size]
-        values, blended = values * scale, blended * scale
-        for first in range(0, size, LEN):
-            rows = slice(first, first + LEN)
-            gap = sigmoid_sums(values[rows]) - sigmoid_sums(blended[rows])
-            parts = jnp.where(lane == (at + first) // LEN, jnp.sum(gap) / LEN, parts)
-        at += size
-    out[...] = jnp.broadcast_to(parts[None], out.shape)
-
-
-def token_specs(count, features):
-    rows = count // 2
-    return [
-        pl.BlockSpec((rows, features), lambda i, *_: (jnp.minimum(i, 1), 0)),
-        pl.BlockSpec((rows, features), lambda i, *_: (jnp.maximum(i - 2, 0), 0)),
-    ]
-
-
-def frozen_values(place, tokens, sibling, strips):
+    total = jnp.zeros((1, 128), jnp.float32)
+    for at in range(len(loads)):
+        loads[at].wait()
+        still_loads[at].wait()
+        total = total + chunk_scores(kept, joined, still, scale, at)
+    parts[...] = total
+
+
+def sibling_kernel(tokens, halves, frozen, readout, parts, out, joined, still, sems):
+    loads = chunk_loads(frozen, still, sems)
+    for load in loads:
+        load.start()
+    join(halves, joined)
+    scale = readout[...]
+    total = parts[...]
+    for at in range(len(loads)):
+        loads[at].wait()
+        total = total + chunk_scores(tokens, joined, still, scale, at)
+    out[...] = jnp.broadcast_to(total[None], out.shape)
+
+
+def in_vmem(number):
+    return [pl.BlockSpec(memory_space=pltpu.VMEM)] * number
+
+
+def work(tokens, width, kept):
     count, features = tokens.shape
-    width = 2 * strips[0].shape[-1]
-    return pl.pallas_call(
-        frozen_kernel,
-        grid_spec=pltpu.PrefetchScalarGridSpec(
-            num_scalar_prefetch=1,
-            grid=(4,),
-            in_specs=token_specs(count, features)
-            + [pl.BlockSpec(strip.shape, lambda i, *_: (0, 0, 0, 0)) for strip in strips],
-            out_specs=pl.BlockSpec((count // 2, width), lambda i, *_: (i, 0)),
-            scratch_shapes=[pltpu.VMEM((features, width), jnp.bfloat16)],
-        ),
-        out_shape=jax.ShapeDtypeStruct((2 * count, width), jnp.float32),
-        cost_estimate=pl.CostEstimate(
-            flops=4 * count * features * width, bytes_accessed=16 << 20, transcendentals=0
-        ),
+    return pl.CostEstimate(
+        flops=2 * count * features * width, bytes_accessed=kept << 20, transcendentals=0
+    )
+
+
+def anchor_columns(place, features, strips):
+    return pl.pallas_call(
+        assemble_kernel,
+        in_specs=[pl.BlockSpec(memory_space=pltpu.SMEM)] + in_vmem(5),
+        out_shape=jax.ShapeDtypeStruct((features, 2 * strips[0].shape[-1]), jnp.bfloat16),
+        compiler_params=pltpu.CompilerParams(vmem_limit_bytes=16 << 20),
+        name="anchor_columns",
+    )(place, *strips)
+
+
+def frozen_values(tokens, own, sibling):
+    count, width = tokens.shape[0], own.shape[1]
+    out = jax.ShapeDtypeStruct((count, width), jnp.float32)
+    return pl.pallas_call(
+        product_kernel,
+        in_specs=[pl.BlockSpec(memory_space=pltpu.HBM)] + in_vmem(2),
+        out_shape=[out, out],
+        scratch_shapes=[
+            pltpu.VMEM(tokens.shape, tokens.dtype),
+            pltpu.SemaphoreType.DMA((count // LEN,)),
+        ],
+        cost_estimate=work(tokens, 2 * width, 12),
         compiler_params=pltpu.CompilerParams(vmem_limit_bytes=VMEM),
         name="frozen_values",
-    )(place, in_hbm(tokens), in_hbm(sibling), *strips)
-
-
-def score_sums(tokens, sibling, halves, frozen, readout):
+    )(in_hbm(tokens), own, sibling)
+
+
+def own_scores(tokens, halves, frozen, readout):
     count, features = tokens.shape
     width = 2 * halves.shape[-1]
     return pl.pallas_call(
-        score_kernel,
-        out_shape=jax.ShapeDtypeStruct((256, 1, 128), jnp.float32),
+        own_kernel,
         in_specs=[
-            pl.BlockSpec(memory_space=pltpu.HBM),
             pl.BlockSpec(memory_space=pltpu.HBM),
             pl.BlockSpec(memory_space=pltpu.VMEM),
             pl.BlockSpec(memory_space=pltpu.HBM),
             pl.BlockSpec(memory_space=pltpu.VMEM),
         ],
+        out_specs=in_vmem(2),
+        out_shape=[
+            jax.ShapeDtypeStruct((1, 128), jnp.float32),
+            pltpu.VMEM(tokens.shape, tokens.dtype),
+        ],
         scratch_shapes=[
             pltpu.VMEM((features, width), jnp.bfloat16),
-            pltpu.VMEM((2 * count, features), tokens.dtype),
             pltpu.VMEM(frozen.shape, frozen.dtype),
-            pltpu.SemaphoreType.DMA((16,)),
-        ],
-        cost_estimate=pl.CostEstimate(
-            flops=4 * count * features * width, bytes_accessed=16 << 20, transcendentals=0
-        ),
-        compiler_params=pltpu.CompilerParams(vmem_limit_bytes=VMEM_SCORE),
-        name="score_sums",
-    )(in_hbm(tokens), in_hbm(sibling), halves, in_hbm(frozen), readout)
+            pltpu.SemaphoreType.DMA((count // LEN,)),
+            pltpu.SemaphoreType.DMA((count // LEN,)),
+        ],
+        cost_estimate=work(tokens, width, 9),
+        compiler_params=pltpu.CompilerParams(vmem_limit_bytes=VMEM),
+        name="own_scores",
+    )(in_hbm(tokens), halves, in_hbm(frozen), readout)
+
+
+def sibling_scores(tokens, halves, frozen, readout, parts):
+    count, features = tokens.shape
+    width = 2 * halves.shape[-1]
+    return pl.pallas_call(
+        sibling_kernel,
+        in_specs=in_vmem(2) + [pl.BlockSpec(memory_space=pltpu.HBM)] + in_vmem(2),
+        out_shape=jax.ShapeDtypeStruct((256, 1, 128), jnp.float32),
+        scratch_shapes=[
+            pltpu.VMEM((features, width), jnp.bfloat16),
+            pltpu.VMEM(frozen.shape, frozen.dtype),
+            pltpu.SemaphoreType.DMA((count // LEN,)),
+        ],
+        cost_estimate=work(tokens, width, 3),
+        compiler_params=pltpu.CompilerParams(vmem_limit_bytes=VMEM),
+        name="sibling_scores",
+    )(
+        pltpu.with_memory_space_constraint(tokens, pltpu.VMEM),
+        halves,
+        in_hbm(frozen),
+        readout,
+        parts,
+    )
 
 
 def plane_sum_kernel(blocks, out):
@@ -366,8 +411,7 @@
     blocks, strip = lax.optimization_barrier((blocks.astype(jnp.bfloat16), strip))
     plane = to_plane(blocks.reshape(16, quarter, 8 * rows))
     strips = gather_z(strip)
-    plane, strips, tokens = lax.optimization_barrier((plane, strips, tokens))
-    sibling = lax.ppermute(tokens, "core", SWAP)
+    plane, strips = lax.optimization_barrier((plane, strips))
     left, right = turn(strips, 1), turn(strips, -1)
     column = along_z(plane_sum(plane).reshape(8, rows, quarter))
     far_left, far_right = turn(left[:4], 1), turn(right[4:], -1)
@@ -376,12 +420,17 @@
     )
     policy_column = along_z(message).reshape(8 * rows, quarter)
     other = lax.ppermute(gradient_piece, "xlo", SWAP)
-    policy_copies, far_left, far_right, sibling, other = lax.optimization_barrier(
-        (copies(policy_column), far_left, far_right, sibling, other)
+    policy_copies, far_left, far_right, other = lax.optimization_barrier(
+        (copies(policy_column), far_left, far_right, other)
     )
     policy_plane = to_plane(policy_copies)
-    frozen = frozen_values(
-        jnp.stack([high * 2 + low, lax.axis_index("y"), lax.axis_index("z")]), tokens, sibling, (strips, left, right, far_left, far_right)
+    anchor_half = anchor_columns(
+        jnp.stack([high * 2 + low, lax.axis_index("y"), lax.axis_index("z")]),
+        features,
+        (strips, left, right, far_left, far_right),
+    )
+    frozen, frozen_sibling = frozen_values(
+        tokens, anchor_half, lax.ppermute(anchor_half, "core", SWAP)
     )
 
     strip = jnp.where(
@@ -399,11 +448,17 @@
         gradient, policy, anchor, moment, second
     )
 
-    readout_cols = lax.dynamic_slice_in_dim(readout, core * half, half)[None]
-    parts = score_sums(tokens, sibling, joined_halves(policy_plane), frozen, readout_cols)
-    parts = lax.all_to_all(parts, AXES, 0, 0, tiled=True)
-    parts = parts.reshape(2, 2, 64, 128)
-    margins = (parts[:, :, :, :4] + parts[:, ::-1, :, 4:8]).reshape(-1)
+    def readout_half(which):
+        return lax.dynamic_slice_in_dim(readout, which * half, half)[None]
+
+    policy_plane, frozen, frozen_sibling = lax.optimization_barrier(
+        (policy_plane, frozen, frozen_sibling)
+    )
+    halves = joined_halves(policy_plane)
+    halves_sibling = lax.ppermute(halves, "core", SWAP)
+    parts, kept = own_scores(tokens, halves, frozen, readout_half(core))
+    parts = sibling_scores(kept, halves_sibling, frozen_sibling, readout_half(1 - core), parts)
+    margins = lax.all_to_all(parts, AXES, 0, 0, tiled=True)[:, 0, :4].reshape(-1)
     pair_loss = pair_losses(margins, pair_index, noisy_flags)
     return (policy_next, anchor_next, moment_next, second_next, pair_loss)
 

time: 157 us -> 172 us (1.096)
  waiting for transfers between devices: 53.9 us -> 69.7 us
  Pallas kernels: 28 us -> 32 us
  other arithmetic: 6.15 us -> 3.73 us
    all_to_all x2, waiting for transfers between devices: 15 us -> 30.1 us  [to_plane(): return lax.all_to_all(blocks, PLANE, 0, 0, tiled=True)]
    pallas_call x2 -> x4, Pallas kernels: 20.6 us -> 24.7 us  [the longest x1 8 us: sibling_scores(): pl.pallas_call(sibling_kernel, in_specs=in_vmem(2) + [pl.BlockSpec(memory...]
    ppermute x1, starting transfers between devices: 2.94 us -> 0.31 us  [shards(): other = lax.ppermute(strip, 'core', SWAP)]
    all_to_all x1, starting transfers between devices: 9.15 us -> 7.2 us  [shards(): lax.all_to_all(parts, AXES, 0, 0, tiled=True)[:, 0, :4].reshape(-1)]
    ppermute x1 -> x2, starting transfers between devices: 2.44 us -> 4.26 us  [the longest x1 3.16 us: shards(): lax.ppermute(anchor_half, 'core', SWAP)]
    ppermute x4, starting transfers between devices: 5.92 us -> 7.68 us  [turn(): lax.ppermute(block, ('xlo', 'xhi'), [(index(x), index((x + shift) % 4)) f...]
    unnamed x32 -> x24, local copies, waits for them, and re-layouts: 6.38 us -> 5.09 us
  transfers between devices with their start and end apart: 19 -> 20, of which waited for: 11 -> 11; matrix products, arithmetic and copies ran while one was open for 4% -> 3% of each run, Pallas kernels for 18% -> 17%
where the time goes in v8:
time: 172 us; the launch traced here: 171 us
  waiting for transfers between devices  69.7 us (41%)
  starting transfers between devices  56 us (33%)
  Pallas kernels  32 us (19%)
  local copies, waits for them, and re-layouts  9.01 us (5%)
  other arithmetic  3.73 us (2%)
    all_to_all x2, waiting for transfers between devices, to_plane(): return lax.all_to_all(blocks, PLANE, 0, 0, tiled=True)  30.1 us
    ppermute x6, waiting for transfers between devices, shift_ring(): lax.ppermute(block, axis, [(i, (i - shift) % size) for i in range(size)])  15.5 us
    all_to_all x2, starting transfers between devices, along_z(): return lax.all_to_all(blocks, 'z', 0, 0, tiled=True)  13.9 us
    ppermute x6, starting transfers between devices, shift_ring(): lax.ppermute(block, axis, [(i, (i - shift) % size) for i in range(size)])  13 us
    all_to_all x1, waiting for transfers between devices, shards(): lax.all_to_all(parts, AXES, 0, 0, tiled=True)[:, 0, :4].reshape(-1)  11.9 us
    all_to_all x2, starting transfers between devices, to_plane(): return lax.all_to_all(blocks, PLANE, 0, 0, tiled=True)  8.61 us
    pallas_call x1, Pallas kernels, sibling_scores(): pl.pallas_call(sibling_kernel, in_specs=in_vmem(2) + [pl.BlockSpec(memory...  8 us
    all_to_all x2, waiting for transfers between devices, along_z(): return lax.all_to_all(blocks, 'z', 0, 0, tiled=True)  7.79 us
  transfers between devices with their start and end apart: 20, of which 11 were waited for; matrix products, arithmetic and copies ran while one was open for 3% of the time, Pallas kernels for 17%

profile of v8, /device:TPU:1, one launch (start us, length us, event | category | flops | bytes accessed | tf_op | source)
XLA Modules:
  0.0 171.3 jit_solution(14999035506588115269)
XLA Ops:
  0.6 0.8 dynamic-slice_convert_fusion
  1.4 3.6 %collective-permute-start = (bf16[64,128]{1,0:T(8,128)(2,1)S(1)}, bf16[64,128]{1,0:T(8,128)(2,1)S(1)}, u32[]{:S(2)}, u32[]{:S(2)}) collective-permute-start(bf16[64,128]{1,0:T(8,128)(2,1)S(1)} %dynamic-slice_convert_fusion), channel_id=1, source_target_pairs={{0,48},{16,0},{32,16},{48,32},{1,49},{17,1},{33,17},{49,33},{2,50}... | collective-permute-start | bytes 49160 | tf_op jit(solution)/shard_map/ppermute | solution.py:372
  5.0 6.3 %gradient_blocks.1 = (bf16[2,8,128,512]{3,2,1,0:T(8,128)(2,1)S(1)}, bf16[2,8,128,512]{3,2,1,0:T(8,128)(2,1)S(1)}) custom-call(s32[1]{0:T(128)} %bitcast.1.place, bf16[768,512]{1,0:T(8,128)(2,1)} %cotangent.1, bf16[768,4096]{1,0:T(8,128)(2,1)} %tokens.5), custom_call_target="tpu_custom_call" | custom-call | flops 3221225472 | bytes 12582912 | tf_op jit(solution)/shard_map/gradient_blocks/pallas_call | solution.py:113
  11.3 1.0 collective-permute-start.1
  12.4 0.4 collective-permute-start.2
  12.7 3.9 %collective-permute-done.2 = bf16[2,64,128]{2,1,0:T(8,128)(2,1)S(1)} collective-permute-done((bf16[2,64,128]{2,1,0:T(8,128)(2,1)S(1)}, bf16[2,64,128]{2,1,0:T(8,128)(2,1)S(1)}, u32[]{:S(2)}, u32[]{:S(2)}) %collective-permute-start.2) | collective-permute-done | bytes 32800 | tf_op jit(solution)/shard_map/ppermute | solution.py:372
  16.7 2.0 %add_convert_fusion = bf16[2,8,128,512]{3,2,1,0:T(8,128)(2,1)} fusion(bf16[2,8,128,512]{3,2,1,0:T(8,128)(2,1)S(1)} %collective-permute-done.1, bf16[2,8,128,512]{3,2,1,0:T(8,128)(2,1)S(1)} %get-tuple-element.26), kind=kLoop, calls=%fused_computation | loop fusion | flops 4194304 | bytes 6291456 | tf_op jit(solution)/shard_map/convert_element_type | solution.py:411
  18.7 4.3 %all-to-all-start = ((bf16[16,128,512]{2,1,0:T(8,128)(2,1)}), bf16[16,128,512]{2,1,0:T(8,128)(2,1)S(1)}, u32[]{:S(2)}, u32[]{:S(2)}) async-start(bf16[16,128,512]{2,1,0:T(8,128)(2,1)} %bitcast.20), calls=%async_computation | async-start | bytes 4194304 | tf_op jit(solution)/shard_map/all_to_all | solution.py:359
  23.0 5.6 %collective-permute-start.3 = (bf16[1,4,64,128]{3,2,1,0:T(8,128)(2,1)S(1)}, bf16[1,4,64,128]{3,2,1,0:T(8,128)(2,1)S(1)}, u32[]{:S(2)}, u32[]{:S(2)}) collective-permute-start(bf16[1,4,64,128]{3,2,1,0:T(8,128)(2,1)S(1)} %bitcast.21), channel_id=1, source_target_pairs={{0,7},{1,0},{2,1},{3,2},{4,3},{5,4},{6,5},{7,6},{8,15},{9,8},{10,9... | collective-permute-start | bytes 196616 | tf_op jit(solution)/shard_map/ppermute | solution.py:372
  28.6 0.6 constant_dynamic-update-slice_fusion.4
  29.3 0.7 collective-permute-done.3
  30.0 3.3 %collective-permute-done.4 = bf16[1,4,64,128]{3,2,1,0:T(8,128)(2,1)S(1)} collective-permute-done((bf16[1,4,64,128]{3,2,1,0:T(8,128)(2,1)S(1)}, bf16[1,4,64,128]{3,2,1,0:T(8,128)(2,1)S(1)}, u32[]{:S(2)}, u32[]{:S(2)}) %collective-permute-start.4) | collective-permute-done | bytes 65568 | tf_op jit(solution)/shard_map/ppermute | solution.py:372
  33.5 3.2 %collective-permute-start.6 = (bf16[2,4,64,128]{3,2,1,0:T(8,128)(2,1)S(1)}, bf16[2,4,64,128]{3,2,1,0:T(8,128)(2,1)S(1)}, u32[]{:S(2)}, u32[]{:S(2)}) collective-permute-start(bf16[2,4,64,128]{3,2,1,0:T(8,128)(2,1)S(1)} %pad_maximum_fusion.1), channel_id=1, source_target_pairs={{0,3},{1,4},{2,5},{3,6},{4,7},{5,0},{6,1},{7,2},{8,11},{9,12},{10,... | collective-permute-start | bytes 393224 | tf_op jit(solution)/shard_map/ppermute | solution.py:372
  36.7 0.6 constant_dynamic-update-slice_fusion.3
  37.4 7.5 %collective-permute-done.5 = bf16[3,4,64,128]{3,2,1,0:T(8,128)(2,1)S(1)} collective-permute-done((bf16[3,4,64,128]{3,2,1,0:T(8,128)(2,1)S(1)}, bf16[3,4,64,128]{3,2,1,0:T(8,128)(2,1)S(1)}, u32[]{:S(2)}, u32[]{:S(2)}) %collective-permute-start.5) | collective-permute-done | bytes 196640 | tf_op jit(solution)/shard_map/ppermute | solution.py:372
  44.9 0.7 constant_dynamic-update-slice_fusion.2
  45.6 0.7 constant_dynamic-update-slice_fusion.1
  46.2 0.6 constant_dynamic-update-slice_fusion.here
  46.9 5.2 %all-to-all-done.blocks = bf16[16,128,512]{2,1,0:T(8,128)(2,1)S(1)} async-done(((bf16[16,128,512]{2,1,0:T(8,128)(2,1)}), bf16[16,128,512]{2,1,0:T(8,128)(2,1)S(1)}, u32[]{:S(2)}, u32[]{:S(2)}) %all-to-all-start) | async-done | bytes 2097184 | tf_op jit(solution)/shard_map/all_to_all | solution.py:359
  52.1 4.0 %collective-permute-start.9 = (bf16[8,4,64,128]{3,2,1,0:T(8,128)(2,1)}, bf16[8,4,64,128]{3,2,1,0:T(8,128)(2,1)S(1)}, u32[]{:S(2)}, u32[]{:S(2)}) collective-permute-start(bf16[8,4,64,128]{3,2,1,0:T(8,128)(2,1)} %constant_dynamic-update-slice_fusion.here), channel_id=1, source_target_pairs={{0,136},{128,0},{8,128},{136,8},{1,137},{129,1},{9,129},{137,9},{2... | collective-permute-start | bytes 1572872 | tf_op jit(solution)/shard_map/ppermute | solution.py:366
  56.1 0.3 plane_sum.1
  56.5 0.6 copy-done.5
  57.1 8.2 %all-to-all-start.1 = ((bf16[8,64,128]{2,1,0:T(8,128)(2,1)}), bf16[8,64,128]{2,1,0:T(8,128)(2,1)S(1)}, u32[]{:S(2)}, u32[]{:S(2)}) async-start(bf16[8,64,128]{2,1,0:T(8,128)(2,1)} %bitcast.17), calls=%async_computation.1 | async-start | bytes 262144 | tf_op jit(solution)/shard_map/all_to_all | solution.py:384
  65.3 1.7 %collective-permute-done.9.right = bf16[8,4,64,128]{3,2,1,0:T(8,128)(2,1)S(1)} collective-permute-done((bf16[8,4,64,128]{3,2,1,0:T(8,128)(2,1)}, bf16[8,4,64,128]{3,2,1,0:T(8,128)(2,1)S(1)}, u32[]{:S(2)}, u32[]{:S(2)}) %collective-permute-start.9) | collective-permute-done | bytes 524320 | tf_op jit(solution)/shard_map/ppermute | solution.py:366
  67.0 3.4 %collective-permute-start.10 = (bf16[4,4,64,128]{3,2,1,0:T(8,128)(2,1)S(1)}, bf16[4,4,64,128]{3,2,1,0:T(8,128)(2,1)S(1)}, u32[]{:S(2)}, u32[]{:S(2)}) collective-permute-start(bf16[4,4,64,128]{3,2,1,0:T(8,128)(2,1)S(1)} %slice.21), channel_id=1, source_target_pairs={{0,136},{128,0},{8,128},{136,8},{1,137},{129,1},{9,129},{137,9},{2... | collective-permute-start | bytes 786440 | tf_op jit(solution)/shard_map/ppermute | solution.py:366
  70.4 0.3 collective-permute-start.8
  70.7 2.5 %all-to-all-done.1.column = bf16[8,64,128]{2,1,0:T(8,128)(2,1)S(1)} async-done(((bf16[8,64,128]{2,1,0:T(8,128)(2,1)}), bf16[8,64,128]{2,1,0:T(8,128)(2,1)S(1)}, u32[]{:S(2)}, u32[]{:S(2)}) %all-to-all-start.1) | async-done | bytes 131104 | tf_op jit(solution)/shard_map/all_to_all | solution.py:384
  73.3 0.7 policy_message.1
  74.0 5.7 %all-to-all-start.2 = ((bf16[8,64,128]{2,1,0:T(8,128)(2,1)}), bf16[8,64,128]{2,1,0:T(8,128)(2,1)S(1)}, u32[]{:S(2)}, u32[]{:S(2)}) async-start(bf16[8,64,128]{2,1,0:T(8,128)(2,1)} %get-tuple-element.34), calls=%async_computation.2 | async-start | bytes 262144 | tf_op jit(solution)/shard_map/all_to_all | solution.py:384
  79.7 2.7 %collective-permute-done.11 = f32[64,128]{1,0:T(8,128)S(1)} collective-permute-done((f32[64,128]{1,0:T(8,128)S(1)}, f32[64,128]{1,0:T(8,128)S(1)}, u32[]{:S(2)}, u32[]{:S(2)}) %collective-permute-start.11) | collective-permute-done | bytes 32800 | tf_op jit(solution)/shard_map/ppermute | solution.py:422
  82.4 5.3 %all-to-all-done.2 = bf16[8,64,128]{2,1,0:T(8,128)(2,1)S(1)} async-done(((bf16[8,64,128]{2,1,0:T(8,128)(2,1)}), bf16[8,64,128]{2,1,0:T(8,128)(2,1)S(1)}, u32[]{:S(2)}, u32[]{:S(2)}) %all-to-all-start.2) | async-done | bytes 131104 | tf_op jit(solution)/shard_map/all_to_all | solution.py:384
  87.7 1.8 %broadcast_in_dim.46 = bf16[16,512,128]{2,1,0:T(8,128)(2,1)} broadcast(bf16[512,128]{1,0:T(8,128)(2,1)S(1)} %bitcast.25), dimensions={1,2} | broadcast | bytes 2228224 | tf_op jit(solution)/shard_map/broadcast_in_dim | solution.py:399
  89.5 2.9 %anchor_columns.1.own = bf16[4096,256]{1,0:T(8,128)(2,1)} custom-call(s32[3]{0:T(128)S(1)} %pad_add_fusion.place, bf16[8,4,64,128]{3,2,1,0:T(8,128)(2,1)} %constant_dynamic-update-slice_fusion.here, bf16[8,4,64,128]{3,2,1,0:T(8,128)(2,1)S(1)} %collective-permute-done.7.left, bf16[8,4,64,128]{3,2,1,0:T(8,128)(2,1)S(1)} %collective-permute-done.9.right, ...), custom_call_target="tpu_custom_call" | custom-call | tf_op jit(solution)/shard_map/anchor_columns/pallas_call | solution.py:237
  92.3 3.2 %collective-permute-start.13 = (bf16[4096,256]{1,0:T(8,128)(2,1)}, bf16[4096,256]{1,0:T(8,128)(2,1)}, u32[]{:S(2)}, u32[]{:S(2)}) collective-permute-start(bf16[4096,256]{1,0:T(8,128)(2,1)} %anchor_columns.1.own), channel_id=1, source_target_pairs={{0,64},{64,0},{1,65},{65,1},{2,66},{66,2},{3,67},{67,3},{4,68},{68... | collective-permute-start | bytes 6291464 | tf_op jit(solution)/shard_map/ppermute | solution.py:433
  95.5 4.3 %all-to-all-start.3 = ((bf16[16,512,128]{2,1,0:T(8,128)(2,1)}), bf16[16,512,128]{2,1,0:T(8,128)(2,1)S(1)}, u32[]{:S(2)}, u32[]{:S(2)}) async-start(bf16[16,512,128]{2,1,0:T(8,128)(2,1)} %broadcast_in_dim.46), calls=%async_computation.3 | async-start | bytes 4194304 | tf_op jit(solution)/shard_map/all_to_all | solution.py:359
  99.8 7.6 %frozen_values.1 = (f32[768,256]{1,0:T(8,128)S(1)}, f32[768,256]{1,0:T(8,128)S(1)}) custom-call(bf16[768,4096]{1,0:T(8,128)(2,1)} %tokens.5, bf16[4096,256]{1,0:T(8,128)(2,1)} %anchor_columns.1.own, bf16[4096,256]{1,0:T(8,128)(2,1)} %collective-permute-done.13.sibling), custom_call_target="tpu_custom_call" | custom-call | flops 3221225472 | bytes 12582912 | tf_op jit(solution)/shard_map/frozen_values/pallas_call | solution.py:249
  107.4 0.9 copy-done
  108.3 0.9 copy-done.1
  109.2 24.9 %all-to-all-done.3 = bf16[16,512,128]{2,1,0:T(8,128)(2,1)S(1)} async-done(((bf16[16,512,128]{2,1,0:T(8,128)(2,1)}), bf16[16,512,128]{2,1,0:T(8,128)(2,1)S(1)}, u32[]{:S(2)}, u32[]{:S(2)}) %all-to-all-start.3) | async-done | bytes 2097184 | tf_op jit(solution)/shard_map/all_to_all | solution.py:359
  134.1 1.1 collective-permute-start.14
  135.3 0.3 collective-permute-start.12
  135.6 6.2 %own_scores.1 = (f32[1,128]{1,0:T(1,128)S(1)}, bf16[768,4096]{1,0:T(8,128)(2,1)S(1)}) custom-call(bf16[768,4096]{1,0:T(8,128)(2,1)} %tokens.5, bf16[2,4096,128]{2,1,0:T(8,128)(2,1)S(1)} %bitcast.16, f32[768,256]{1,0:T(8,128)} %copy-done.1, f32[1,256]{1,0:T(1,128)S(1)} %bitcast.19), custom_call_target="tpu_custom_call" | custom-call | flops 1610612736 | bytes 9437184 | tf_op jit(solution)/shard_map/own_scores/pallas_call | solution.py:266
  141.9 8.0 %sibling_scores.1 = f32[256,1,128]{2,1,0:T(1,128)} custom-call(bf16[768,4096]{1,0:T(8,128)(2,1)S(1)} %get-tuple-element.44.tokens, bf16[2,4096,128]{2,1,0:T(8,128)(2,1)} %collective-permute-done.14.halves, f32[768,256]{1,0:T(8,128)} %copy-done, f32[1,256]{1,0:T(1,128)S(1)} %bitcast.18, f32[1,128]{1,0:T(1,128)S(1)} %get-tuple-element.46.parts), custom_call_target="tpu_custom_call" | custom-call | flops 1610612736 | bytes 3145728 | tf_op jit(solution)/shard_map/sibling_scores/pallas_call | solution.py:294
  149.9 7.2 %all-to-all-start.4 = ((f32[256,1,128]{2,1,0:T(1,128)}), f32[256,1,128]{2,1,0:T(1,128)S(1)}, u32[]{:S(2)}, u32[]{:S(2)}) async-start(f32[256,1,128]{2,1,0:T(1,128)} %sibling_scores.1), calls=%async_computation.4 | async-start | bytes 262144 | tf_op jit(solution)/shard_map/all_to_all | solution.py:461
  157.3 0.8 multiply_add_fusion
  158.1 11.9 %all-to-all-done.4 = f32[256,1,128]{2,1,0:T(1,128)S(1)} async-done(((f32[256,1,128]{2,1,0:T(1,128)}), f32[256,1,128]{2,1,0:T(1,128)S(1)}, u32[]{:S(2)}, u32[]{:S(2)}) %all-to-all-start.4) | async-done | bytes 131104 | tf_op jit(solution)/shard_map/all_to_all | solution.py:461
  170.1 0.3 slice_reduce_fusion
  170.8 0.5 multiply_subtract_fusion
  (42 shorter events, 1.0 us)
Async XLA Ops:
  1.4 9.9 %collective-permute-start = (bf16[64,128]{1,0:T(8,128)(2,1)S(1)}, bf16[64,128]{1,0:T(8,128)(2,1)S(1)}, u32[]{:S(2)}, u32[]{:S(2)}) collective-permute-start(bf16[64,128]{1,0:T(8,128)(2,1)S(1)} %dynamic-slice_convert_fusion), channel_id=1, source_target_pairs={{0,48},{16,0},{32,16},{48,32},{1,49},{17,1},{33,17},{49,33},{2,50}... | collective-permute-start | bytes 49160 | tf_op jit(solution)/shard_map/ppermute | solution.py:372
  11.3 5.3 %collective-permute-start.1 = (bf16[2,8,128,512]{3,2,1,0:T(8,128)(2,1)S(1)}, bf16[2,8,128,512]{3,2,1,0:T(8,128)(2,1)S(1)}, u32[]{:S(2)}, u32[]{:S(2)}) collective-permute-start(bf16[2,8,128,512]{3,2,1,0:T(8,128)(2,1)S(1)} %get-tuple-element.28), channel_id=1, source_target_pairs={{0,64},{64,0},{1,65},{65,1},{2,66},{66,2},{3,67},{67,3},{4,68},{68... | collective-permute-start | bytes 6291464 | tf_op jit(solution)/shard_map/ppermute | solution.py:408
  12.4 4.3 %collective-permute-start.2 = (bf16[2,64,128]{2,1,0:T(8,128)(2,1)S(1)}, bf16[2,64,128]{2,1,0:T(8,128)(2,1)S(1)}, u32[]{:S(2)}, u32[]{:S(2)}) collective-permute-start(bf16[2,64,128]{2,1,0:T(8,128)(2,1)S(1)} %pad_maximum_fusion.3), channel_id=1, source_target_pairs={{0,32},{16,48},{32,0},{48,16},{1,33},{17,49},{33,1},{49,17},{2,34}... | collective-permute-start | bytes 98312 | tf_op jit(solution)/shard_map/ppermute | solution.py:372
  18.7 33.4 %all-to-all-start = ((bf16[16,128,512]{2,1,0:T(8,128)(2,1)}), bf16[16,128,512]{2,1,0:T(8,128)(2,1)S(1)}, u32[]{:S(2)}, u32[]{:S(2)}) async-start(bf16[16,128,512]{2,1,0:T(8,128)(2,1)} %bitcast.20), calls=%async_computation | async-start | bytes 4194304 | tf_op jit(solution)/shard_map/all_to_all | solution.py:359
  23.0 7.0 %collective-permute-start.3 = (bf16[1,4,64,128]{3,2,1,0:T(8,128)(2,1)S(1)}, bf16[1,4,64,128]{3,2,1,0:T(8,128)(2,1)S(1)}, u32[]{:S(2)}, u32[]{:S(2)}) collective-permute-start(bf16[1,4,64,128]{3,2,1,0:T(8,128)(2,1)S(1)} %bitcast.21), channel_id=1, source_target_pairs={{0,7},{1,0},{2,1},{3,2},{4,3},{5,4},{6,5},{7,6},{8,15},{9,8},{10,9... | collective-permute-start | bytes 196616 | tf_op jit(solution)/shard_map/ppermute | solution.py:372
  28.6 4.6 %collective-permute-start.4 = (bf16[1,4,64,128]{3,2,1,0:T(8,128)(2,1)S(1)}, bf16[1,4,64,128]{3,2,1,0:T(8,128)(2,1)S(1)}, u32[]{:S(2)}, u32[]{:S(2)}) collective-permute-start(bf16[1,4,64,128]{3,2,1,0:T(8,128)(2,1)S(1)} %bitcast.22), channel_id=1, source_target_pairs={{0,1},{1,2},{2,3},{3,4},{4,5},{5,6},{6,7},{7,0},{8,9},{9,10},{10,1... | collective-permute-start | bytes 196616 | tf_op jit(solution)/shard_map/ppermute | solution.py:372
  33.3 11.6 %collective-permute-start.5 = (bf16[3,4,64,128]{3,2,1,0:T(8,128)(2,1)S(1)}, bf16[3,4,64,128]{3,2,1,0:T(8,128)(2,1)S(1)}, u32[]{:S(2)}, u32[]{:S(2)}) collective-permute-start(bf16[3,4,64,128]{3,2,1,0:T(8,128)(2,1)S(1)} %pad_maximum_fusion), channel_id=1, source_target_pairs={{0,5},{1,6},{2,7},{3,0},{4,1},{5,2},{6,3},{7,4},{8,13},{9,14},{10,... | collective-permute-start | bytes 589832 | tf_op jit(solution)/shard_map/ppermute | solution.py:372
  33.5 12.1 %collective-permute-start.6 = (bf16[2,4,64,128]{3,2,1,0:T(8,128)(2,1)S(1)}, bf16[2,4,64,128]{3,2,1,0:T(8,128)(2,1)S(1)}, u32[]{:S(2)}, u32[]{:S(2)}) collective-permute-start(bf16[2,4,64,128]{3,2,1,0:T(8,128)(2,1)S(1)} %pad_maximum_fusion.1), channel_id=1, source_target_pairs={{0,3},{1,4},{2,5},{3,6},{4,7},{5,0},{6,1},{7,2},{8,11},{9,12},{10,... | collective-permute-start | bytes 393224 | tf_op jit(solution)/shard_map/ppermute | solution.py:372
  37.3 35.9 %copy-start.2 = (f32[64,512]{1,0:T(8,128)S(1)}, f32[64,512]{1,0:T(8,128)}, u32[]{:S(2)}) copy-start(f32[64,512]{1,0:T(8,128)} %policy.1) | copy-start | bytes 393220
  37.3 35.9 %copy-start.3 = (f32[64,512]{1,0:T(8,128)S(1)}, f32[64,512]{1,0:T(8,128)}, u32[]{:S(2)}) copy-start(f32[64,512]{1,0:T(8,128)} %moment.1) | copy-start | bytes 393220
  37.3 35.9 %copy-start.4 = (f32[64,512]{1,0:T(8,128)S(1)}, f32[64,512]{1,0:T(8,128)}, u32[]{:S(2)}) copy-start(f32[64,512]{1,0:T(8,128)} %second.1) | copy-start | bytes 393220
  52.1 14.9 %collective-permute-start.9 = (bf16[8,4,64,128]{3,2,1,0:T(8,128)(2,1)}, bf16[8,4,64,128]{3,2,1,0:T(8,128)(2,1)S(1)}, u32[]{:S(2)}, u32[]{:S(2)}) collective-permute-start(bf16[8,4,64,128]{3,2,1,0:T(8,128)(2,1)} %constant_dynamic-update-slice_fusion.here), channel_id=1, source_target_pairs={{0,136},{128,0},{8,128},{136,8},{1,137},{129,1},{9,129},{137,9},{2... | collective-permute-start | bytes 1572872 | tf_op jit(solution)/shard_map/ppermute | solution.py:366
  56.1 14.3 %collective-permute-start.7 = (bf16[8,4,64,128]{3,2,1,0:T(8,128)(2,1)}, bf16[8,4,64,128]{3,2,1,0:T(8,128)(2,1)S(1)}, u32[]{:S(2)}, u32[]{:S(2)}) collective-permute-start(bf16[8,4,64,128]{3,2,1,0:T(8,128)(2,1)} %constant_dynamic-update-slice_fusion.here), channel_id=1, source_target_pairs={{0,128},{128,8},{8,136},{136,0},{1,129},{129,9},{9,137},{137,1},{2... | collective-permute-start | bytes 1572872 | tf_op jit(solution)/shard_map/ppermute | solution.py:366
  56.5 0.7 copy-start.5
  57.1 16.1 %all-to-all-start.1 = ((bf16[8,64,128]{2,1,0:T(8,128)(2,1)}), bf16[8,64,128]{2,1,0:T(8,128)(2,1)S(1)}, u32[]{:S(2)}, u32[]{:S(2)}) async-start(bf16[8,64,128]{2,1,0:T(8,128)(2,1)} %bitcast.17), calls=%async_computation.1 | async-start | bytes 262144 | tf_op jit(solution)/shard_map/all_to_all | solution.py:384
  67.0 20.7 %collective-permute-start.10 = (bf16[4,4,64,128]{3,2,1,0:T(8,128)(2,1)S(1)}, bf16[4,4,64,128]{3,2,1,0:T(8,128)(2,1)S(1)}, u32[]{:S(2)}, u32[]{:S(2)}) collective-permute-start(bf16[4,4,64,128]{3,2,1,0:T(8,128)(2,1)S(1)} %slice.21), channel_id=1, source_target_pairs={{0,136},{128,0},{8,128},{136,8},{1,137},{129,1},{9,129},{137,9},{2... | collective-permute-start | bytes 786440 | tf_op jit(solution)/shard_map/ppermute | solution.py:366
  70.4 17.3 %collective-permute-start.8 = (bf16[4,4,64,128]{3,2,1,0:T(8,128)(2,1)S(1)}, bf16[4,4,64,128]{3,2,1,0:T(8,128)(2,1)S(1)}, u32[]{:S(2)}, u32[]{:S(2)}) collective-permute-start(bf16[4,4,64,128]{3,2,1,0:T(8,128)(2,1)S(1)} %slice.20), channel_id=1, source_target_pairs={{0,128},{128,8},{8,136},{136,0},{1,129},{129,9},{9,137},{137,1},{2... | collective-permute-start | bytes 786440 | tf_op jit(solution)/shard_map/ppermute | solution.py:366
  74.0 13.7 %all-to-all-start.2 = ((bf16[8,64,128]{2,1,0:T(8,128)(2,1)}), bf16[8,64,128]{2,1,0:T(8,128)(2,1)S(1)}, u32[]{:S(2)}, u32[]{:S(2)}) async-start(bf16[8,64,128]{2,1,0:T(8,128)(2,1)} %get-tuple-element.34), calls=%async_computation.2 | async-start | bytes 262144 | tf_op jit(solution)/shard_map/all_to_all | solution.py:384
  79.7 2.8 %collective-permute-start.11 = (f32[64,128]{1,0:T(8,128)S(1)}, f32[64,128]{1,0:T(8,128)S(1)}, u32[]{:S(2)}, u32[]{:S(2)}) collective-permute-start(f32[64,128]{1,0:T(8,128)S(1)} %get-tuple-element.33), channel_id=1, source_target_pairs={{0,128},{128,0},{1,129},{129,1},{2,130},{130,2},{3,131},{131,3},{4... | collective-permute-start | bytes 98312 | tf_op jit(solution)/shard_map/ppermute | solution.py:422
  92.3 7.5 %collective-permute-start.13 = (bf16[4096,256]{1,0:T(8,128)(2,1)}, bf16[4096,256]{1,0:T(8,128)(2,1)}, u32[]{:S(2)}, u32[]{:S(2)}) collective-permute-start(bf16[4096,256]{1,0:T(8,128)(2,1)} %anchor_columns.1.own), channel_id=1, source_target_pairs={{0,64},{64,0},{1,65},{65,1},{2,66},{66,2},{3,67},{67,3},{4,68},{68... | collective-permute-start | bytes 6291464 | tf_op jit(solution)/shard_map/ppermute | solution.py:433
  95.5 38.6 %all-to-all-start.3 = ((bf16[16,512,128]{2,1,0:T(8,128)(2,1)}), bf16[16,512,128]{2,1,0:T(8,128)(2,1)S(1)}, u32[]{:S(2)}, u32[]{:S(2)}) async-start(bf16[16,512,128]{2,1,0:T(8,128)(2,1)} %broadcast_in_dim.46), calls=%async_computation.3 | async-start | bytes 4194304 | tf_op jit(solution)/shard_map/all_to_all | solution.py:359
  99.8 35.4 %copy-start.8 = (f32[512]{0:T(512)S(1)}, f32[512]{0:T(512)}, u32[]{:S(2)}) copy-start(f32[512]{0:T(512)} %param.15) | copy-start | bytes 6148
  107.4 0.9 copy-start
  108.3 0.9 copy-start.1
  134.1 7.7 %collective-permute-start.14 = (bf16[2,4096,128]{2,1,0:T(8,128)(2,1)S(1)}, bf16[2,4096,128]{2,1,0:T(8,128)(2,1)}, u32[]{:S(2)}, u32[]{:S(2)}) collective-permute-start(bf16[2,4096,128]{2,1,0:T(8,128)(2,1)S(1)} %bitcast.15), channel_id=1, source_target_pairs={{0,64},{64,0},{1,65},{65,1},{2,66},{66,2},{3,67},{67,3},{4,68},{68... | collective-permute-start | bytes 6291464 | tf_op jit(solution)/shard_map/ppermute | solution.py:458
  135.3 22.0 %collective-permute-start.12 = (f32[64,256]{1,0:T(8,128)S(1)}, f32[64,256]{1,0:T(8,128)S(1)}, u32[]{:S(2)}, u32[]{:S(2)}) collective-permute-start(f32[64,256]{1,0:T(8,128)S(1)} %maximum_select_fusion.1), channel_id=1, source_target_pairs={{0,64},{64,0},{1,65},{65,1},{2,66},{66,2},{3,67},{67,3},{4,68},{68... | collective-permute-start | bytes 196616 | tf_op jit(solution)/shard_map/ppermute | solution.py:441
  141.8 15.3 %copy-start.7 = (s32[2,2]{1,0:T(2,128)S(1)}, s32[2,2]{1,0:T(2,128)}, u32[]{:S(2)}) copy-start(s32[2,2]{1,0:T(2,128)} %param.16) | copy-start | bytes 52
  141.8 15.4 %copy-start.6 = (f32[64,512]{1,0:T(8,128)S(1)}, f32[64,512]{1,0:T(8,128)}, u32[]{:S(2)}) copy-start(f32[64,512]{1,0:T(8,128)} %param.12) | copy-start | bytes 393220
  141.8 28.9 %copy-start.9 = (s32[2]{0:T(128)S(1)}, s32[2]{0:T(128)}, u32[]{:S(2)}) copy-start(s32[2]{0:T(128)} %param.17) | copy-start | bytes 28
  149.9 20.2 %all-to-all-start.4 = ((f32[256,1,128]{2,1,0:T(1,128)}), f32[256,1,128]{2,1,0:T(1,128)S(1)}, u32[]{:S(2)}, u32[]{:S(2)}) async-start(f32[256,1,128]{2,1,0:T(1,128)} %sibling_scores.1), calls=%async_computation.4 | async-start | bytes 262144 | tf_op jit(solution)/shard_map/all_to_all | solution.py:461

commit v9 on v7

--- a/solution.py
+++ b/solution.py
@@ -171,7 +171,7 @@
 def score_kernel(tokens, sibling, halves, frozen, readout, out, joined, held, still, sems):
     quarter = halves.shape[-1]
     count = tokens.shape[0]
-    sizes = (LEN,) * 8
+    sizes = (2 * LEN,) * 4
     loads, at = [], 0
     for step, size in enumerate(sizes):
         source, first = (tokens, at) if at < count else (sibling, at - count)
@@ -185,7 +185,7 @@
             )
         )
         at += size
-    for pair in loads[:AHEAD]:
+    for pair in loads[:2]:
         for load in pair:
             load.start()
     joined[:, :quarter] = halves[0]
@@ -197,7 +197,7 @@
     for step, size in enumerate(sizes):
         for load in loads[step]:
             load.wait()
-        for load in loads[step + AHEAD] if step + AHEAD < len(sizes) else ():
+        for load in loads[step + 2] if step + 2 < len(sizes) else ():
             load.start()
         values = jnp.dot(held[at : at + size], joined[...], preferred_element_type=jnp.float32)
         blended = blend_rate * values + (1.0 - blend_rate) * still[at : at + size]
@@ -257,7 +257,7 @@
             pltpu.VMEM((features, width), jnp.bfloat16),
             pltpu.VMEM((2 * count, features), tokens.dtype),
             pltpu.VMEM(frozen.shape, frozen.dtype),
-            pltpu.SemaphoreType.DMA((16,)),
+            pltpu.SemaphoreType.DMA((8,)),
         ],
         cost_estimate=pl.CostEstimate(
             flops=4 * count * features * width, bytes_accessed=16 << 20, transcendentals=0
@@ -310,6 +310,26 @@
     )(place, column, policy, moment, second)
 
 
+def copies_kernel(column, out, sems):
+    sends = [pltpu.make_async_copy(column, out.at[at], sems.at[at]) for at in range(out.shape[0])]
+    for send in sends:
+        send.start()
+    for send in sends:
+        send.wait()
+
+
+def plane_copies(column):
+    return pl.pallas_call(
+        copies_kernel,
+        in_specs=[pl.BlockSpec(memory_space=pltpu.VMEM)],
+        out_specs=pl.BlockSpec(memory_space=pltpu.HBM),
+        out_shape=jax.ShapeDtypeStruct((16,) + column.shape, column.dtype),
+        scratch_shapes=[pltpu.SemaphoreType.DMA((16,))],
+        compiler_params=pltpu.CompilerParams(vmem_limit_bytes=16 << 20),
+        name="plane_copies",
+    )(column)
+
+
 def to_plane(blocks):
     return lax.all_to_all(blocks, PLANE, 0, 0, tiled=True)
 
@@ -349,9 +369,6 @@
 
     def piece(array):
         return lax.dynamic_slice_in_dim(array, (core * 2 + low) * quarter, quarter, axis=1)
-
-    def copies(column):
-        return jnp.broadcast_to(column[None], (16,) + column.shape)
 
     def joined_halves(plane):
         return plane.reshape(2, features, quarter)
@@ -375,15 +392,18 @@
         (core * 2 + low)[None], column, policy, moment, second
     )
     policy_column = along_z(message).reshape(8 * rows, quarter)
-    other = lax.ppermute(gradient_piece, "xlo", SWAP)
-    policy_copies, far_left, far_right, sibling, other = lax.optimization_barrier(
-        (copies(policy_column), far_left, far_right, sibling, other)
+    policy_copies, far_left, far_right, sibling = lax.optimization_barrier(
+        (plane_copies(policy_column), far_left, far_right, sibling)
     )
     policy_plane = to_plane(policy_copies)
     frozen = frozen_values(
         jnp.stack([high * 2 + low, lax.axis_index("y"), lax.axis_index("z")]), tokens, sibling, (strips, left, right, far_left, far_right)
     )
 
+    readout_cols = lax.dynamic_slice_in_dim(readout, core * half, half)[None]
+    parts = score_sums(tokens, sibling, joined_halves(policy_plane), frozen, readout_cols)
+    parts, gradient_piece = lax.optimization_barrier((parts, gradient_piece))
+    other = lax.ppermute(gradient_piece, "xlo", SWAP)
     strip = jnp.where(
         low == 0,
         jnp.concatenate([gradient_piece, other], axis=1),
@@ -399,8 +419,6 @@
         gradient, policy, anchor, moment, second
     )
 
-    readout_cols = lax.dynamic_slice_in_dim(readout, core * half, half)[None]
-    parts = score_sums(tokens, sibling, joined_halves(policy_plane), frozen, readout_cols)
     parts = lax.all_to_all(parts, AXES, 0, 0, tiled=True)
     parts = parts.reshape(2, 2, 64, 128)
     margins = (parts[:, :, :, :4] + parts[:, ::-1, :, 4:8]).reshape(-1)

time: 157 us -> 158 us (level)
  blocking collectives: 0 us -> 14.2 us
  starting transfers between devices: 57.5 us -> 51.5 us
  waiting for transfers between devices: 53.9 us -> 48.9 us
  other arithmetic: 6.15 us -> 3.76 us
    all_to_all x0 -> x1, blocking collectives: none -> 14.2 us  [along_z(): return lax.all_to_all(blocks, 'z', 0, 0, tiled=True)]
    all_to_all x2 -> x1, starting transfers between devices: 14.5 us -> 8.18 us  [along_z(): return lax.all_to_all(blocks, 'z', 0, 0, tiled=True)]
    all_to_all x2 -> x1, waiting for transfers between devices: 7.03 us -> 1.87 us  [along_z(): return lax.all_to_all(blocks, 'z', 0, 0, tiled=True)]
    all_to_all x2, waiting for transfers between devices: 15 us -> 19.4 us  [to_plane(): return lax.all_to_all(blocks, PLANE, 0, 0, tiled=True)]
    ppermute x1, waiting for transfers between devices: 2.86 us -> 0.01 us  [shards(): other = lax.ppermute(gradient_piece, 'xlo', SWAP)]
    all_to_all x1, waiting for transfers between devices: 11 us -> 8.99 us  [shards(): parts = lax.all_to_all(parts, AXES, 0, 0, tiled=True)]
    broadcast_in_dim x1 -> x0, local copies, waits for them, and re-layouts: 1.8 us -> none  [copies(): return jnp.broadcast_to(column[None], (16,) + column.shape)]
    unnamed x32 -> x34, local copies, waits for them, and re-layouts: 6.38 us -> 7.83 us
  transfers between devices with their start and end apart: 19 -> 18, of which waited for: 11 -> 10; matrix products, arithmetic and copies ran while one was open for 4% -> 3% of each run, Pallas kernels for 18% -> 11%
where the time goes in v9:
time: 158 us; the launch traced here: 157 us
  starting transfers between devices  51.5 us (33%)
  waiting for transfers between devices  48.9 us (31%)
  Pallas kernels  28.2 us (18%)
  blocking collectives  14.2 us (9%)
  local copies, waits for them, and re-layouts  9.74 us (6%)
  other arithmetic  3.76 us (2%)
    all_to_all x2, waiting for transfers between devices, to_plane(): return lax.all_to_all(blocks, PLANE, 0, 0, tiled=True)  19.4 us
    ppermute x6, waiting for transfers between devices, shift_ring(): lax.ppermute(block, axis, [(i, (i - shift) % size) for i in range(size)])  15.5 us
    all_to_all x1, blocking collectives, along_z(): return lax.all_to_all(blocks, 'z', 0, 0, tiled=True)  14.2 us
    ppermute x6, starting transfers between devices, shift_ring(): lax.ppermute(block, axis, [(i, (i - shift) % size) for i in range(size)])  13 us
    pallas_call x1, Pallas kernels, score_sums(): pl.pallas_call(score_kernel, out_shape=jax.ShapeDtypeStruct((256, 1, 128)...  11 us
    all_to_all x1, starting transfers between devices, shards(): parts = lax.all_to_all(parts, AXES, 0, 0, tiled=True)  9.76 us
    all_to_all x1, waiting for transfers between devices, shards(): parts = lax.all_to_all(parts, AXES, 0, 0, tiled=True)  8.99 us
    pallas_call x1, Pallas kernels, frozen_values(): pl.pallas_call(frozen_kernel, grid_spec=pltpu.PrefetchScalarGridSpec(num_...  8.91 us
  transfers between devices with their start and end apart: 18, of which 10 were waited for; matrix products, arithmetic and copies ran while one was open for 3% of the time, Pallas kernels for 11%

profile of v9, /device:TPU:1, one launch (start us, length us, event | category | flops | bytes accessed | tf_op | source)
XLA Modules:
  0.0 157.2 jit_solution(2117141279231810376)
XLA Ops:
  0.6 0.8 dynamic-slice_convert_fusion
  1.4 3.6 %collective-permute-start = (bf16[64,128]{1,0:T(8,128)(2,1)S(1)}, bf16[64,128]{1,0:T(8,128)(2,1)S(1)}, u32[]{:S(2)}, u32[]{:S(2)}) collective-permute-start(bf16[64,128]{1,0:T(8,128)(2,1)S(1)} %dynamic-slice_convert_fusion), channel_id=1, source_target_pairs={{0,48},{16,0},{32,16},{48,32},{1,49},{17,1},{33,17},{49,33},{2,50}... | collective-permute-start | bytes 49160 | tf_op jit(solution)/shard_map/ppermute | solution.py:347
  5.0 6.3 %gradient_blocks.1 = (bf16[2,8,128,512]{3,2,1,0:T(8,128)(2,1)S(1)}, bf16[2,8,128,512]{3,2,1,0:T(8,128)(2,1)S(1)}) custom-call(s32[1]{0:T(128)} %bitcast.place, bf16[768,512]{1,0:T(8,128)(2,1)} %cotangent.1, bf16[768,4096]{1,0:T(8,128)(2,1)} %tokens.3), custom_call_target="tpu_custom_call" | custom-call | flops 3221225472 | bytes 12582912 | tf_op jit(solution)/shard_map/gradient_blocks/pallas_call | solution.py:114
  11.3 1.0 collective-permute-start.1
  12.4 0.4 collective-permute-start.2
  12.7 3.9 %collective-permute-done.2 = bf16[2,64,128]{2,1,0:T(8,128)(2,1)S(1)} collective-permute-done((bf16[2,64,128]{2,1,0:T(8,128)(2,1)S(1)}, bf16[2,64,128]{2,1,0:T(8,128)(2,1)S(1)}, u32[]{:S(2)}, u32[]{:S(2)}) %collective-permute-start.2) | collective-permute-done | bytes 32800 | tf_op jit(solution)/shard_map/ppermute | solution.py:347
  16.7 2.0 %add_convert_fusion = bf16[2,8,128,512]{3,2,1,0:T(8,128)(2,1)} fusion(bf16[2,8,128,512]{3,2,1,0:T(8,128)(2,1)S(1)} %collective-permute-done.1, bf16[2,8,128,512]{3,2,1,0:T(8,128)(2,1)S(1)} %get-tuple-element.22), kind=kLoop, calls=%fused_computation | loop fusion | flops 4194304 | bytes 6291456 | tf_op jit(solution)/shard_map/convert_element_type | solution.py:383
  18.7 4.3 %all-to-all-start = ((bf16[16,128,512]{2,1,0:T(8,128)(2,1)}), bf16[16,128,512]{2,1,0:T(8,128)(2,1)S(1)}, u32[]{:S(2)}, u32[]{:S(2)}) async-start(bf16[16,128,512]{2,1,0:T(8,128)(2,1)} %bitcast.21), calls=%async_computation | async-start | bytes 4194304 | tf_op jit(solution)/shard_map/all_to_all | solution.py:334
  23.0 5.6 %collective-permute-start.3 = (bf16[1,4,64,128]{3,2,1,0:T(8,128)(2,1)S(1)}, bf16[1,4,64,128]{3,2,1,0:T(8,128)(2,1)S(1)}, u32[]{:S(2)}, u32[]{:S(2)}) collective-permute-start(bf16[1,4,64,128]{3,2,1,0:T(8,128)(2,1)S(1)} %bitcast.24), channel_id=1, source_target_pairs={{0,7},{1,0},{2,1},{3,2},{4,3},{5,4},{6,5},{7,6},{8,15},{9,8},{10,9... | collective-permute-start | bytes 196616 | tf_op jit(solution)/shard_map/ppermute | solution.py:347
  28.6 0.6 constant_dynamic-update-slice_fusion.4
  29.3 0.7 collective-permute-done.3
  30.0 3.3 %collective-permute-done.4 = bf16[1,4,64,128]{3,2,1,0:T(8,128)(2,1)S(1)} collective-permute-done((bf16[1,4,64,128]{3,2,1,0:T(8,128)(2,1)S(1)}, bf16[1,4,64,128]{3,2,1,0:T(8,128)(2,1)S(1)}, u32[]{:S(2)}, u32[]{:S(2)}) %collective-permute-start.4) | collective-permute-done | bytes 65568 | tf_op jit(solution)/shard_map/ppermute | solution.py:347
  33.3 0.2 collective-permute-start.5
  33.5 3.2 %collective-permute-start.6 = (bf16[2,4,64,128]{3,2,1,0:T(8,128)(2,1)S(1)}, bf16[2,4,64,128]{3,2,1,0:T(8,128)(2,1)S(1)}, u32[]{:S(2)}, u32[]{:S(2)}) collective-permute-start(bf16[2,4,64,128]{3,2,1,0:T(8,128)(2,1)S(1)} %pad_maximum_fusion.1), channel_id=1, source_target_pairs={{0,3},{1,4},{2,5},{3,6},{4,7},{5,0},{6,1},{7,2},{8,11},{9,12},{10,... | collective-permute-start | bytes 393224 | tf_op jit(solution)/shard_map/ppermute | solution.py:347
  36.7 0.6 constant_dynamic-update-slice_fusion.3
  37.4 7.5 %collective-permute-done.5 = bf16[3,4,64,128]{3,2,1,0:T(8,128)(2,1)S(1)} collective-permute-done((bf16[3,4,64,128]{3,2,1,0:T(8,128)(2,1)S(1)}, bf16[3,4,64,128]{3,2,1,0:T(8,128)(2,1)S(1)}, u32[]{:S(2)}, u32[]{:S(2)}) %collective-permute-start.5) | collective-permute-done | bytes 196640 | tf_op jit(solution)/shard_map/ppermute | solution.py:347
  44.9 0.7 constant_dynamic-update-slice_fusion.2
  45.6 0.7 constant_dynamic-update-slice_fusion.1
  46.3 0.6 constant_dynamic-update-slice_fusion.here
  46.9 5.2 %all-to-all-done.blocks = bf16[16,128,512]{2,1,0:T(8,128)(2,1)S(1)} async-done(((bf16[16,128,512]{2,1,0:T(8,128)(2,1)}), bf16[16,128,512]{2,1,0:T(8,128)(2,1)S(1)}, u32[]{:S(2)}, u32[]{:S(2)}) %all-to-all-start) | async-done | bytes 2097184 | tf_op jit(solution)/shard_map/all_to_all | solution.py:334
  52.1 2.4 %collective-permute-start.11 = (bf16[768,4096]{1,0:T(8,128)(2,1)}, bf16[768,4096]{1,0:T(8,128)(2,1)}, u32[]{:S(2)}, u32[]{:S(2)}) collective-permute-start(bf16[768,4096]{1,0:T(8,128)(2,1)} %tokens.3), channel_id=1, source_target_pairs={{0,64},{64,0},{1,65},{65,1},{2,66},{66,2},{3,67},{67,3},{4,68},{68... | collective-permute-start | bytes 18874376 | tf_op jit(solution)/shard_map/ppermute | solution.py:387
  54.5 2.3 %collective-permute-start.9 = (bf16[8,4,64,128]{3,2,1,0:T(8,128)(2,1)}, bf16[8,4,64,128]{3,2,1,0:T(8,128)(2,1)S(1)}, u32[]{:S(2)}, u32[]{:S(2)}) collective-permute-start(bf16[8,4,64,128]{3,2,1,0:T(8,128)(2,1)} %constant_dynamic-update-slice_fusion.here), channel_id=1, source_target_pairs={{0,136},{128,0},{8,128},{136,8},{1,137},{129,1},{9,129},{137,9},{2... | collective-permute-start | bytes 1572872 | tf_op jit(solution)/shard_map/ppermute | solution.py:341
  56.8 0.3 plane_sum.1
  57.2 0.6 copy-done.4
  57.8 8.2 %all-to-all-start.1 = ((bf16[8,64,128]{2,1,0:T(8,128)(2,1)}), bf16[8,64,128]{2,1,0:T(8,128)(2,1)S(1)}, u32[]{:S(2)}, u32[]{:S(2)}) async-start(bf16[8,64,128]{2,1,0:T(8,128)(2,1)} %bitcast.18), calls=%async_computation.1 | async-start | bytes 262144 | tf_op jit(solution)/shard_map/all_to_all | solution.py:359
  66.0 2.5 %collective-permute-done.9.right = bf16[8,4,64,128]{3,2,1,0:T(8,128)(2,1)S(1)} collective-permute-done((bf16[8,4,64,128]{3,2,1,0:T(8,128)(2,1)}, bf16[8,4,64,128]{3,2,1,0:T(8,128)(2,1)S(1)}, u32[]{:S(2)}, u32[]{:S(2)}) %collective-permute-start.9) | collective-permute-done | bytes 524320 | tf_op jit(solution)/shard_map/ppermute | solution.py:341
  68.5 3.6 %collective-permute-start.10 = (bf16[4,4,64,128]{3,2,1,0:T(8,128)(2,1)S(1)}, bf16[4,4,64,128]{3,2,1,0:T(8,128)(2,1)S(1)}, u32[]{:S(2)}, u32[]{:S(2)}) collective-permute-start(bf16[4,4,64,128]{3,2,1,0:T(8,128)(2,1)S(1)} %slice.25), channel_id=1, source_target_pairs={{0,136},{128,0},{8,128},{136,8},{1,137},{129,1},{9,129},{137,9},{2... | collective-permute-start | bytes 786440 | tf_op jit(solution)/shard_map/ppermute | solution.py:341
  72.2 1.9 %all-to-all-done.1.column = bf16[8,64,128]{2,1,0:T(8,128)(2,1)S(1)} async-done(((bf16[8,64,128]{2,1,0:T(8,128)(2,1)}), bf16[8,64,128]{2,1,0:T(8,128)(2,1)S(1)}, u32[]{:S(2)}, u32[]{:S(2)}) %all-to-all-start.1) | async-done | bytes 131104 | tf_op jit(solution)/shard_map/all_to_all | solution.py:359
  74.1 14.2 %all_to_all.25 = bf16[8,64,128]{2,1,0:T(8,128)(2,1)S(1)} all-to-all(bf16[8,64,128]{2,1,0:T(8,128)(2,1)S(1)} %get-tuple-element.30), channel_id=1, replica_groups=mesh['xlo'=2,'core'=2,'y'=4,'xhi'=2,'z'=8] {'z'}, dimensions={0} | all-to-all | bytes 262144 | tf_op jit(solution)/shard_map/all_to_all | solution.py:359
  88.3 1.5 plane_copies.1
  89.9 0.7 copy-done.5
  90.6 0.7 copy-done.7
  91.3 4.1 %all-to-all-start.3 = ((bf16[16,512,128]{2,1,0:T(8,128)(2,1)}), bf16[16,512,128]{2,1,0:T(8,128)(2,1)S(1)}, u32[]{:S(2)}, u32[]{:S(2)}) async-start(bf16[16,512,128]{2,1,0:T(8,128)(2,1)} %plane_copies.1), calls=%async_computation.3 | async-start | bytes 4194304 | tf_op jit(solution)/shard_map/all_to_all | solution.py:334
  95.6 0.9 copy-done.6
  96.6 0.9 copy-done.8
  97.5 8.9 %frozen_values.1.frozen = f32[1536,256]{1,0:T(8,128)S(1)} custom-call(s32[3]{0:T(128)S(1)} %pad_add_fusion.place, bf16[768,4096]{1,0:T(8,128)(2,1)} %tokens.3, bf16[768,4096]{1,0:T(8,128)(2,1)} %collective-permute-done.11.sibling, bf16[8,4,64,128]{3,2,1,0:T(8,128)(2,1)} %constant_dynamic-update-slice_fusion.here, ...), custom_call_target="tpu_custom_call" | custom-call | flops 3221225472 | bytes 16777216 | tf_op jit(solution)/shard_map/frozen_values/pallas_call | solution.py:224
  106.5 1.2 copy-done
  107.6 14.2 %all-to-all-done.3 = bf16[16,512,128]{2,1,0:T(8,128)(2,1)S(1)} async-done(((bf16[16,512,128]{2,1,0:T(8,128)(2,1)}), bf16[16,512,128]{2,1,0:T(8,128)(2,1)S(1)}, u32[]{:S(2)}, u32[]{:S(2)}) %all-to-all-start.3) | async-done | bytes 2097184 | tf_op jit(solution)/shard_map/all_to_all | solution.py:334
  121.9 11.0 %score_sums.1 = f32[256,1,128]{2,1,0:T(1,128)} custom-call(bf16[768,4096]{1,0:T(8,128)(2,1)} %tokens.3, bf16[768,4096]{1,0:T(8,128)(2,1)} %collective-permute-done.11.sibling, bf16[2,4096,128]{2,1,0:T(8,128)(2,1)S(1)} %bitcast.17, f32[1536,256]{1,0:T(8,128)} %copy-done, f32[1,256]{1,0:T(1,128)S(1)} %bitcast.20), custom_call_target="tpu_custom_call" | custom-call | flops 3221225472 | bytes 16777216 | tf_op jit(solution)/shard_map/score_sums/pallas_call | solution.py:246
  132.9 0.5 collective-permute-start.12
  133.4 9.8 %all-to-all-start.4 = ((f32[256,1,128]{2,1,0:T(1,128)}), f32[256,1,128]{2,1,0:T(1,128)S(1)}, u32[]{:S(2)}, u32[]{:S(2)}) async-start(f32[256,1,128]{2,1,0:T(1,128)} %score_sums.1), calls=%async_computation.4 | async-start | bytes 262144 | tf_op jit(solution)/shard_map/all_to_all | solution.py:422
  143.2 2.2 %collective-permute-start.13 = (f32[64,256]{1,0:T(8,128)S(1)}, f32[64,256]{1,0:T(8,128)S(1)}, u32[]{:S(2)}, u32[]{:S(2)}) collective-permute-start(f32[64,256]{1,0:T(8,128)S(1)} %maximum_select_fusion.1), channel_id=1, source_target_pairs={{0,64},{64,0},{1,65},{65,1},{2,66},{66,2},{3,67},{67,3},{4,68},{68... | collective-permute-start | bytes 196616 | tf_op jit(solution)/shard_map/ppermute | solution.py:412
  145.5 0.2 slice_reduce_fusion
  145.6 0.7 collective-permute-done.13
  146.4 0.8 multiply_add_fusion
  147.2 9.0 %all-to-all-done.4 = f32[256,1,128]{2,1,0:T(1,128)S(1)} async-done(((f32[256,1,128]{2,1,0:T(1,128)}), f32[256,1,128]{2,1,0:T(1,128)S(1)}, u32[]{:S(2)}, u32[]{:S(2)}) %all-to-all-start.4) | async-done | bytes 131104 | tf_op jit(solution)/shard_map/all_to_all | solution.py:422
  156.4 0.2 fusion.2
  156.7 0.5 multiply_subtract_fusion
  (48 shorter events, 0.7 us)
Async XLA Ops:
  1.4 9.9 %collective-permute-start = (bf16[64,128]{1,0:T(8,128)(2,1)S(1)}, bf16[64,128]{1,0:T(8,128)(2,1)S(1)}, u32[]{:S(2)}, u32[]{:S(2)}) collective-permute-start(bf16[64,128]{1,0:T(8,128)(2,1)S(1)} %dynamic-slice_convert_fusion), channel_id=1, source_target_pairs={{0,48},{16,0},{32,16},{48,32},{1,49},{17,1},{33,17},{49,33},{2,50}... | collective-permute-start | bytes 49160 | tf_op jit(solution)/shard_map/ppermute | solution.py:347
  11.3 5.3 %collective-permute-start.1 = (bf16[2,8,128,512]{3,2,1,0:T(8,128)(2,1)S(1)}, bf16[2,8,128,512]{3,2,1,0:T(8,128)(2,1)S(1)}, u32[]{:S(2)}, u32[]{:S(2)}) collective-permute-start(bf16[2,8,128,512]{3,2,1,0:T(8,128)(2,1)S(1)} %get-tuple-element.24), channel_id=1, source_target_pairs={{0,64},{64,0},{1,65},{65,1},{2,66},{66,2},{3,67},{67,3},{4,68},{68... | collective-permute-start | bytes 6291464 | tf_op jit(solution)/shard_map/ppermute | solution.py:380
  12.4 4.3 %collective-permute-start.2 = (bf16[2,64,128]{2,1,0:T(8,128)(2,1)S(1)}, bf16[2,64,128]{2,1,0:T(8,128)(2,1)S(1)}, u32[]{:S(2)}, u32[]{:S(2)}) collective-permute-start(bf16[2,64,128]{2,1,0:T(8,128)(2,1)S(1)} %pad_maximum_fusion.3), channel_id=1, source_target_pairs={{0,32},{16,48},{32,0},{48,16},{1,33},{17,49},{33,1},{49,17},{2,34}... | collective-permute-start | bytes 98312 | tf_op jit(solution)/shard_map/ppermute | solution.py:347
  18.7 33.4 %all-to-all-start = ((bf16[16,128,512]{2,1,0:T(8,128)(2,1)}), bf16[16,128,512]{2,1,0:T(8,128)(2,1)S(1)}, u32[]{:S(2)}, u32[]{:S(2)}) async-start(bf16[16,128,512]{2,1,0:T(8,128)(2,1)} %bitcast.21), calls=%async_computation | async-start | bytes 4194304 | tf_op jit(solution)/shard_map/all_to_all | solution.py:334
  23.0 7.0 %collective-permute-start.3 = (bf16[1,4,64,128]{3,2,1,0:T(8,128)(2,1)S(1)}, bf16[1,4,64,128]{3,2,1,0:T(8,128)(2,1)S(1)}, u32[]{:S(2)}, u32[]{:S(2)}) collective-permute-start(bf16[1,4,64,128]{3,2,1,0:T(8,128)(2,1)S(1)} %bitcast.24), channel_id=1, source_target_pairs={{0,7},{1,0},{2,1},{3,2},{4,3},{5,4},{6,5},{7,6},{8,15},{9,8},{10,9... | collective-permute-start | bytes 196616 | tf_op jit(solution)/shard_map/ppermute | solution.py:347
  28.6 4.6 %collective-permute-start.4 = (bf16[1,4,64,128]{3,2,1,0:T(8,128)(2,1)S(1)}, bf16[1,4,64,128]{3,2,1,0:T(8,128)(2,1)S(1)}, u32[]{:S(2)}, u32[]{:S(2)}) collective-permute-start(bf16[1,4,64,128]{3,2,1,0:T(8,128)(2,1)S(1)} %bitcast.25), channel_id=1, source_target_pairs={{0,1},{1,2},{2,3},{3,4},{4,5},{5,6},{6,7},{7,0},{8,9},{9,10},{10,1... | collective-permute-start | bytes 196616 | tf_op jit(solution)/shard_map/ppermute | solution.py:347
  33.3 11.6 %collective-permute-start.5 = (bf16[3,4,64,128]{3,2,1,0:T(8,128)(2,1)S(1)}, bf16[3,4,64,128]{3,2,1,0:T(8,128)(2,1)S(1)}, u32[]{:S(2)}, u32[]{:S(2)}) collective-permute-start(bf16[3,4,64,128]{3,2,1,0:T(8,128)(2,1)S(1)} %pad_maximum_fusion), channel_id=1, source_target_pairs={{0,5},{1,6},{2,7},{3,0},{4,1},{5,2},{6,3},{7,4},{8,13},{9,14},{10,... | collective-permute-start | bytes 589832 | tf_op jit(solution)/shard_map/ppermute | solution.py:347
  33.5 12.1 %collective-permute-start.6 = (bf16[2,4,64,128]{3,2,1,0:T(8,128)(2,1)S(1)}, bf16[2,4,64,128]{3,2,1,0:T(8,128)(2,1)S(1)}, u32[]{:S(2)}, u32[]{:S(2)}) collective-permute-start(bf16[2,4,64,128]{3,2,1,0:T(8,128)(2,1)S(1)} %pad_maximum_fusion.1), channel_id=1, source_target_pairs={{0,3},{1,4},{2,5},{3,6},{4,7},{5,0},{6,1},{7,2},{8,11},{9,12},{10,... | collective-permute-start | bytes 393224 | tf_op jit(solution)/shard_map/ppermute | solution.py:347
  37.4 36.7 %copy-start.1 = (f32[64,512]{1,0:T(8,128)S(1)}, f32[64,512]{1,0:T(8,128)}, u32[]{:S(2)}) copy-start(f32[64,512]{1,0:T(8,128)} %policy.1) | copy-start | bytes 393220
  37.4 36.7 %copy-start.2 = (f32[64,512]{1,0:T(8,128)S(1)}, f32[64,512]{1,0:T(8,128)}, u32[]{:S(2)}) copy-start(f32[64,512]{1,0:T(8,128)} %moment.1) | copy-start | bytes 393220
  37.4 36.7 %copy-start.3 = (f32[64,512]{1,0:T(8,128)S(1)}, f32[64,512]{1,0:T(8,128)}, u32[]{:S(2)}) copy-start(f32[64,512]{1,0:T(8,128)} %second.1) | copy-start | bytes 393220
  52.1 39.2 %collective-permute-start.11 = (bf16[768,4096]{1,0:T(8,128)(2,1)}, bf16[768,4096]{1,0:T(8,128)(2,1)}, u32[]{:S(2)}, u32[]{:S(2)}) collective-permute-start(bf16[768,4096]{1,0:T(8,128)(2,1)} %tokens.3), channel_id=1, source_target_pairs={{0,64},{64,0},{1,65},{65,1},{2,66},{66,2},{3,67},{67,3},{4,68},{68... | collective-permute-start | bytes 18874376 | tf_op jit(solution)/shard_map/ppermute | solution.py:387
  54.5 13.9 %collective-permute-start.9 = (bf16[8,4,64,128]{3,2,1,0:T(8,128)(2,1)}, bf16[8,4,64,128]{3,2,1,0:T(8,128)(2,1)S(1)}, u32[]{:S(2)}, u32[]{:S(2)}) collective-permute-start(bf16[8,4,64,128]{3,2,1,0:T(8,128)(2,1)} %constant_dynamic-update-slice_fusion.here), channel_id=1, source_target_pairs={{0,136},{128,0},{8,128},{136,8},{1,137},{129,1},{9,129},{137,9},{2... | collective-permute-start | bytes 1572872 | tf_op jit(solution)/shard_map/ppermute | solution.py:341
  56.8 15.3 %collective-permute-start.7 = (bf16[8,4,64,128]{3,2,1,0:T(8,128)(2,1)}, bf16[8,4,64,128]{3,2,1,0:T(8,128)(2,1)S(1)}, u32[]{:S(2)}, u32[]{:S(2)}) collective-permute-start(bf16[8,4,64,128]{3,2,1,0:T(8,128)(2,1)} %constant_dynamic-update-slice_fusion.here), channel_id=1, source_target_pairs={{0,128},{128,8},{8,136},{136,0},{1,129},{129,9},{9,137},{137,1},{2... | collective-permute-start | bytes 1572872 | tf_op jit(solution)/shard_map/ppermute | solution.py:341
  57.2 0.7 copy-start.4
  57.8 16.2 %all-to-all-start.1 = ((bf16[8,64,128]{2,1,0:T(8,128)(2,1)}), bf16[8,64,128]{2,1,0:T(8,128)(2,1)S(1)}, u32[]{:S(2)}, u32[]{:S(2)}) async-start(bf16[8,64,128]{2,1,0:T(8,128)(2,1)} %bitcast.18), calls=%async_computation.1 | async-start | bytes 262144 | tf_op jit(solution)/shard_map/all_to_all | solution.py:359
  68.5 21.4 %collective-permute-start.10 = (bf16[4,4,64,128]{3,2,1,0:T(8,128)(2,1)S(1)}, bf16[4,4,64,128]{3,2,1,0:T(8,128)(2,1)S(1)}, u32[]{:S(2)}, u32[]{:S(2)}) collective-permute-start(bf16[4,4,64,128]{3,2,1,0:T(8,128)(2,1)S(1)} %slice.25), channel_id=1, source_target_pairs={{0,136},{128,0},{8,128},{136,8},{1,137},{129,1},{9,129},{137,9},{2... | collective-permute-start | bytes 786440 | tf_op jit(solution)/shard_map/ppermute | solution.py:341
  72.1 18.5 %collective-permute-start.8 = (bf16[4,4,64,128]{3,2,1,0:T(8,128)(2,1)S(1)}, bf16[4,4,64,128]{3,2,1,0:T(8,128)(2,1)S(1)}, u32[]{:S(2)}, u32[]{:S(2)}) collective-permute-start(bf16[4,4,64,128]{3,2,1,0:T(8,128)(2,1)S(1)} %slice.24), channel_id=1, source_target_pairs={{0,128},{128,8},{8,136},{136,0},{1,129},{129,9},{9,137},{137,1},{2... | collective-permute-start | bytes 786440 | tf_op jit(solution)/shard_map/ppermute | solution.py:341
  74.1 14.2 %copy-start.9 = (f32[64,128]{1,0:T(8,128)}, f32[64,128]{1,0:T(8,128)S(1)}, u32[]{:S(2)}) copy-start(f32[64,128]{1,0:T(8,128)S(1)} %get-tuple-element.37) | copy-start | bytes 98308
  89.9 5.6 %copy-start.13 = (f32[512]{0:T(512)S(1)}, f32[512]{0:T(512)}, u32[]{:S(2)}) copy-start(f32[512]{0:T(512)} %param.15) | copy-start | bytes 6148
  89.9 0.7 copy-start.5
  90.6 0.7 copy-start.7
  91.3 30.6 %all-to-all-start.3 = ((bf16[16,512,128]{2,1,0:T(8,128)(2,1)}), bf16[16,512,128]{2,1,0:T(8,128)(2,1)S(1)}, u32[]{:S(2)}, u32[]{:S(2)}) async-start(bf16[16,512,128]{2,1,0:T(8,128)(2,1)} %plane_copies.1), calls=%async_computation.3 | async-start | bytes 4194304 | tf_op jit(solution)/shard_map/all_to_all | solution.py:334
  95.6 1.0 copy-start.6
  96.6 0.9 copy-start.8
  106.4 1.2 copy-start
  121.9 11.1 %copy-start.10 = (f32[64,128]{1,0:T(8,128)S(1)}, f32[64,128]{1,0:T(8,128)}, u32[]{:S(2)}) copy-start(f32[64,128]{1,0:T(8,128)} %copy-done.9) | copy-start | bytes 98308
  121.9 23.6 %copy-start.12 = (s32[2,2]{1,0:T(2,128)S(1)}, s32[2,2]{1,0:T(2,128)}, u32[]{:S(2)}) copy-start(s32[2,2]{1,0:T(2,128)} %param.16) | copy-start | bytes 52
  121.9 24.5 %copy-start.11 = (f32[64,512]{1,0:T(8,128)S(1)}, f32[64,512]{1,0:T(8,128)}, u32[]{:S(2)}) copy-start(f32[64,512]{1,0:T(8,128)} %param.12) | copy-start | bytes 393220
  132.9 23.8 %copy-start.14 = (s32[2]{0:T(128)S(1)}, s32[2]{0:T(128)}, u32[]{:S(2)}) copy-start(s32[2]{0:T(128)} %param.17) | copy-start | bytes 28
  132.9 10.3 %collective-permute-start.12 = (f32[64,128]{1,0:T(8,128)S(1)}, f32[64,128]{1,0:T(8,128)S(1)}, u32[]{:S(2)}, u32[]{:S(2)}) collective-permute-start(f32[64,128]{1,0:T(8,128)S(1)} %copy-done.10), channel_id=1, source_target_pairs={{0,128},{128,0},{1,129},{129,1},{2,130},{130,2},{3,131},{131,3},{4... | collective-permute-start | bytes 98312 | tf_op jit(solution)/shard_map/ppermute | solution.py:406
  133.4 22.8 %all-to-all-start.4 = ((f32[256,1,128]{2,1,0:T(1,128)}), f32[256,1,128]{2,1,0:T(1,128)S(1)}, u32[]{:S(2)}, u32[]{:S(2)}) async-start(f32[256,1,128]{2,1,0:T(1,128)} %score_sums.1), calls=%async_computation.4 | async-start | bytes 262144 | tf_op jit(solution)/shard_map/all_to_all | solution.py:422
  143.2 3.1 %collective-permute-start.13 = (f32[64,256]{1,0:T(8,128)S(1)}, f32[64,256]{1,0:T(8,128)S(1)}, u32[]{:S(2)}, u32[]{:S(2)}) collective-permute-start(f32[64,256]{1,0:T(8,128)S(1)} %maximum_select_fusion.1), channel_id=1, source_target_pairs={{0,64},{64,0},{1,65},{65,1},{2,66},{66,2},{3,67},{67,3},{4,68},{68... | collective-permute-start | bytes 196616 | tf_op jit(solution)/shard_map/ppermute | solution.py:412

commit v10 on v9

--- a/solution.py
+++ b/solution.py
@@ -1,3 +1,5 @@
+import functools
+
 import jax
 import jax.numpy as jnp
 from jax import lax
@@ -64,7 +66,7 @@
     return pltpu.with_memory_space_constraint(array, pltpu.HBM)
 
 
-def gradient_kernel(place, cotangent, tokens, sent, own, held, turned, sems):
+def gradient_kernel(part, place, cotangent, tokens, sent, own, held, turned, sems):
     channels = held.shape[1]
     half, quarter = channels // 2, channels // 4
     width = sent.shape[3]
@@ -79,7 +81,7 @@
     ]
     blocks = [
         pltpu.make_async_copy(
-            tokens.at[:, pl.ds(at * width, width)],
+            tokens.at[:, pl.ds((2 * at + part) * width, width)],
             turned.at[:, pl.ds(at * width, width)],
             sems.at[2 + at],
         )
@@ -105,14 +107,14 @@
         own[1, at] = product[half + quarter :]
 
 
-def gradient_blocks(place, cotangent, tokens):
+def gradient_blocks(part, place, cotangent, tokens):
     count, features = tokens.shape
     channels = cotangent.shape[1]
     quarter = channels // 4
-    width = features // 8
+    width = features // 16
     block = pltpu.VMEM((2, 8, quarter, width), jnp.bfloat16)
     return pl.pallas_call(
-        gradient_kernel,
+        functools.partial(gradient_kernel, part),
         in_specs=[
             pl.BlockSpec(memory_space=pltpu.SMEM),
             pl.BlockSpec(memory_space=pltpu.HBM),
@@ -122,11 +124,11 @@
         out_shape=[block, block],
         scratch_shapes=[
             pltpu.VMEM(cotangent.shape, cotangent.dtype),
-            pltpu.VMEM(tokens.shape, tokens.dtype),
+            pltpu.VMEM((count, features // 2), tokens.dtype),
             pltpu.SemaphoreType.DMA((10,)),
         ],
         cost_estimate=pl.CostEstimate(
-            flops=2 * count * features * channels, bytes_accessed=12 << 20, transcendentals=0
+            flops=count * features * channels, bytes_accessed=6 << 20, transcendentals=0
         ),
         compiler_params=pltpu.CompilerParams(vmem_limit_bytes=VMEM_GRADIENT),
         name="gradient_blocks",
@@ -373,14 +375,23 @@
     def joined_halves(plane):
         return plane.reshape(2, features, quarter)
 
-    sent, own = gradient_blocks(core[None], cotangent, tokens)
+    sent, own = gradient_blocks(0, core[None], cotangent, tokens)
     anchor_piece = lax.optimization_barrier(piece(anchor).astype(jnp.bfloat16))
     pair = jnp.stack([anchor_piece, shift_ring(anchor_piece, "y", 4, 1)])
     sent, pair = lax.optimization_barrier((sent, pair))
     arrived = lax.ppermute(sent, "core", SWAP)
     strip = jnp.concatenate([pair, shift_ring(pair, "y", 4, 2)])
-    blocks = own.astype(jnp.float32) + arrived.astype(jnp.float32)
-    blocks, strip = lax.optimization_barrier((blocks.astype(jnp.bfloat16), strip))
+    sent, own_upper = gradient_blocks(1, core[None], cotangent, tokens)
+    sent, arrived, strip = lax.optimization_barrier((sent, arrived, strip))
+    arrived_upper = lax.ppermute(sent, "core", SWAP)
+    blocks = jnp.concatenate(
+        [
+            (mine.astype(jnp.float32) + other.astype(jnp.float32)).astype(jnp.bfloat16)
+            for mine, other in ((own, arrived), (own_upper, arrived_upper))
+        ],
+        axis=3,
+    )
+    blocks, strip = lax.optimization_barrier((blocks, strip))
     plane = to_plane(blocks.reshape(16, quarter, 8 * rows))
     strips = gather_z(strip)
     plane, strips, tokens = lax.optimization_barrier((plane, strips, tokens))

time: 158 us -> 169 us (1.070)
  Pallas kernels: 28.2 us -> 33.8 us
  waiting for transfers between devices: 48.9 us -> 52.2 us
  starting transfers between devices: 51.5 us -> 54.5 us
    all_to_all x2, starting transfers between devices: 8.45 us -> 14.1 us  [to_plane(): return lax.all_to_all(blocks, PLANE, 0, 0, tiled=True)]
    pallas_call x1 -> x2, Pallas kernels: 6.31 us -> 11.9 us  [gradient_blocks(): pl.pallas_call(functools.partial(gradient_kernel, part), in_specs=[pl.Blo...]
    ppermute x6, waiting for transfers between devices: 15.5 us -> 11.9 us  [shift_ring(): lax.ppermute(block, axis, [(i, (i - shift) % size) for i in range(size)])]
    all_to_all x2, waiting for transfers between devices: 19.4 us -> 22.5 us  [to_plane(): return lax.all_to_all(blocks, PLANE, 0, 0, tiled=True)]
    ppermute x4, starting transfers between devices: 5.92 us -> 3.09 us  [turn(): lax.ppermute(block, ('xlo', 'xhi'), [(index(x), index((x + shift) % 4)) f...]
    ppermute x0 -> x1, waiting for transfers between devices: none -> 1.97 us  [shards(): arrived_upper = lax.ppermute(sent, 'core', SWAP)]
  transfers between devices with their start and end apart: 18 -> 19, of which waited for: 10 -> 10; matrix products, arithmetic and copies ran while one was open for 3% -> 3% of each run, Pallas kernels for 11% -> 14%
where the time goes in v10:
time: 169 us; the launch traced here: 168 us
  starting transfers between devices  54.5 us (32%)
  waiting for transfers between devices  52.2 us (31%)
  Pallas kernels  33.8 us (20%)
  blocking collectives  13 us (8%)
  local copies, waits for them, and re-layouts  9.73 us (6%)
  other arithmetic  3.96 us (2%)
    all_to_all x2, waiting for transfers between devices, to_plane(): return lax.all_to_all(blocks, PLANE, 0, 0, tiled=True)  22.5 us
    all_to_all x2, starting transfers between devices, to_plane(): return lax.all_to_all(blocks, PLANE, 0, 0, tiled=True)  14.1 us
    ppermute x6, starting transfers between devices, shift_ring(): lax.ppermute(block, axis, [(i, (i - shift) % size) for i in range(size)])  13.2 us
    all_to_all x1, blocking collectives, along_z(): return lax.all_to_all(blocks, 'z', 0, 0, tiled=True)  13 us
    ppermute x6, waiting for transfers between devices, shift_ring(): lax.ppermute(block, axis, [(i, (i - shift) % size) for i in range(size)])  11.9 us
    pallas_call x2, Pallas kernels, gradient_blocks(): pl.pallas_call(functools.partial(gradient_kernel, part), in_specs=[pl.Blo...  11.9 us
    pallas_call x1, Pallas kernels, score_sums(): pl.pallas_call(score_kernel, out_shape=jax.ShapeDtypeStruct((256, 1, 128)...  11 us
    all_to_all x1, starting transfers between devices, shards(): parts = lax.all_to_all(parts, AXES, 0, 0, tiled=True)  10.4 us
  transfers between devices with their start and end apart: 19, of which 10 were waited for; matrix products, arithmetic and copies ran while one was open for 3% of the time, Pallas kernels for 14%

profile of v10, /device:TPU:1, one launch (start us, length us, event | category | flops | bytes accessed | tf_op | source)
XLA Modules:
  0.0 168.1 jit_solution(3536668428236453081)
XLA Ops:
  0.6 0.8 dynamic-slice_convert_fusion
  1.4 3.6 %collective-permute-start = (bf16[64,128]{1,0:T(8,128)(2,1)S(1)}, bf16[64,128]{1,0:T(8,128)(2,1)S(1)}, u32[]{:S(2)}, u32[]{:S(2)}) collective-permute-start(bf16[64,128]{1,0:T(8,128)(2,1)S(1)} %dynamic-slice_convert_fusion), channel_id=1, source_target_pairs={{0,48},{16,0},{32,16},{48,32},{1,49},{17,1},{33,17},{49,33},{2,50}... | collective-permute-start | bytes 49160 | tf_op jit(solution)/shard_map/ppermute | solution.py:349
  5.0 5.9 %gradient_blocks.2 = (bf16[2,8,128,256]{3,2,1,0:T(8,128)(2,1)S(1)}, bf16[2,8,128,256]{3,2,1,0:T(8,128)(2,1)S(1)}) custom-call(s32[1]{0:T(128)} %bitcast.place, bf16[768,512]{1,0:T(8,128)(2,1)} %cotangent.3, bf16[768,4096]{1,0:T(8,128)(2,1)} %tokens.5), custom_call_target="tpu_custom_call" | custom-call | flops 1610612736 | bytes 6291456 | tf_op jit(solution)/shard_map/gradient_blocks/pallas_call | solution.py:116
  10.9 1.0 collective-permute-start.1
  12.0 0.4 collective-permute-start.2
  12.4 5.9 %gradient_blocks.3 = (bf16[2,8,128,256]{3,2,1,0:T(8,128)(2,1)S(1)}, bf16[2,8,128,256]{3,2,1,0:T(8,128)(2,1)S(1)}) custom-call(s32[1]{0:T(128)} %bitcast.place, bf16[768,512]{1,0:T(8,128)(2,1)} %cotangent.3, bf16[768,4096]{1,0:T(8,128)(2,1)} %tokens.5), custom_call_target="tpu_custom_call" | custom-call | flops 1610612736 | bytes 6291456 | tf_op jit(solution)/shard_map/gradient_blocks/pallas_call | solution.py:116
  18.4 0.4 collective-permute-start.3
  19.1 2.0 %collective-permute-done.3 = bf16[2,8,128,256]{3,2,1,0:T(8,128)(2,1)S(1)} collective-permute-done((bf16[2,8,128,256]{3,2,1,0:T(8,128)(2,1)S(1)}, bf16[2,8,128,256]{3,2,1,0:T(8,128)(2,1)S(1)}, u32[]{:S(2)}, u32[]{:S(2)}) %collective-permute-start.3) | collective-permute-done | bytes 1048608 | tf_op jit(solution)/shard_map/ppermute | solution.py:386
  21.1 0.3 add_convert_fusion
  21.4 1.5 pad_maximum_fusion
  23.0 6.5 %all-to-all-start = ((bf16[16,128,512]{2,1,0:T(8,128)(2,1)}), bf16[16,128,512]{2,1,0:T(8,128)(2,1)S(1)}, u32[]{:S(2)}, u32[]{:S(2)}) async-start(bf16[16,128,512]{2,1,0:T(8,128)(2,1)} %bitcast.21), calls=%async_computation | async-start | bytes 4194304 | tf_op jit(solution)/shard_map/all_to_all | solution.py:336
  29.4 5.7 %collective-permute-start.4 = (bf16[1,4,64,128]{3,2,1,0:T(8,128)(2,1)S(1)}, bf16[1,4,64,128]{3,2,1,0:T(8,128)(2,1)S(1)}, u32[]{:S(2)}, u32[]{:S(2)}) collective-permute-start(bf16[1,4,64,128]{3,2,1,0:T(8,128)(2,1)S(1)} %bitcast.24), channel_id=1, source_target_pairs={{0,7},{1,0},{2,1},{3,2},{4,3},{5,4},{6,5},{7,6},{8,15},{9,8},{10,9... | collective-permute-start | bytes 196616 | tf_op jit(solution)/shard_map/ppermute | solution.py:349
  35.1 0.6 constant_dynamic-update-slice_fusion.4
  35.7 0.7 collective-permute-done.4
  36.4 3.3 %collective-permute-done.5 = bf16[1,4,64,128]{3,2,1,0:T(8,128)(2,1)S(1)} collective-permute-done((bf16[1,4,64,128]{3,2,1,0:T(8,128)(2,1)S(1)}, bf16[1,4,64,128]{3,2,1,0:T(8,128)(2,1)S(1)}, u32[]{:S(2)}, u32[]{:S(2)}) %collective-permute-start.5) | collective-permute-done | bytes 65568 | tf_op jit(solution)/shard_map/ppermute | solution.py:349
  39.8 0.5 collective-permute-start.6
  40.3 3.1 %collective-permute-start.7 = (bf16[2,4,64,128]{3,2,1,0:T(8,128)(2,1)S(1)}, bf16[2,4,64,128]{3,2,1,0:T(8,128)(2,1)S(1)}, u32[]{:S(2)}, u32[]{:S(2)}) collective-permute-start(bf16[2,4,64,128]{3,2,1,0:T(8,128)(2,1)S(1)} %pad_maximum_fusion.2), channel_id=1, source_target_pairs={{0,3},{1,4},{2,5},{3,6},{4,7},{5,0},{6,1},{7,2},{8,11},{9,12},{10,... | collective-permute-start | bytes 393224 | tf_op jit(solution)/shard_map/ppermute | solution.py:349
  43.4 0.6 constant_dynamic-update-slice_fusion.3
  44.0 7.9 %collective-permute-done.6 = bf16[3,4,64,128]{3,2,1,0:T(8,128)(2,1)S(1)} collective-permute-done((bf16[3,4,64,128]{3,2,1,0:T(8,128)(2,1)S(1)}, bf16[3,4,64,128]{3,2,1,0:T(8,128)(2,1)S(1)}, u32[]{:S(2)}, u32[]{:S(2)}) %collective-permute-start.6) | collective-permute-done | bytes 196640 | tf_op jit(solution)/shard_map/ppermute | solution.py:349
  51.9 0.7 constant_dynamic-update-slice_fusion.2
  52.6 0.7 constant_dynamic-update-slice_fusion.1
  53.3 0.6 constant_dynamic-update-slice_fusion.here
  53.9 8.4 %all-to-all-done.blocks = bf16[16,128,512]{2,1,0:T(8,128)(2,1)S(1)} async-done(((bf16[16,128,512]{2,1,0:T(8,128)(2,1)}), bf16[16,128,512]{2,1,0:T(8,128)(2,1)S(1)}, u32[]{:S(2)}, u32[]{:S(2)}) %all-to-all-start) | async-done | bytes 2097184 | tf_op jit(solution)/shard_map/all_to_all | solution.py:336
  62.4 1.5 collective-permute-start.12
  63.9 1.5 collective-permute-start.8
  65.3 0.3 plane_sum.1
  65.7 0.6 copy-done.4
  66.3 8.2 %all-to-all-start.1 = ((bf16[8,64,128]{2,1,0:T(8,128)(2,1)}), bf16[8,64,128]{2,1,0:T(8,128)(2,1)S(1)}, u32[]{:S(2)}, u32[]{:S(2)}) async-start(bf16[8,64,128]{2,1,0:T(8,128)(2,1)} %bitcast.18), calls=%async_computation.1 | async-start | bytes 262144 | tf_op jit(solution)/shard_map/all_to_all | solution.py:361
  74.5 3.1 %collective-permute-done.10.right = bf16[8,4,64,128]{3,2,1,0:T(8,128)(2,1)S(1)} collective-permute-done((bf16[8,4,64,128]{3,2,1,0:T(8,128)(2,1)}, bf16[8,4,64,128]{3,2,1,0:T(8,128)(2,1)S(1)}, u32[]{:S(2)}, u32[]{:S(2)}) %collective-permute-start.10) | collective-permute-done | bytes 524320 | tf_op jit(solution)/shard_map/ppermute | solution.py:343
  77.7 1.5 collective-permute-start.11
  79.3 3.0 %all-to-all-done.1.column = bf16[8,64,128]{2,1,0:T(8,128)(2,1)S(1)} async-done(((bf16[8,64,128]{2,1,0:T(8,128)(2,1)}), bf16[8,64,128]{2,1,0:T(8,128)(2,1)S(1)}, u32[]{:S(2)}, u32[]{:S(2)}) %all-to-all-start.1) | async-done | bytes 131104 | tf_op jit(solution)/shard_map/all_to_all | solution.py:361
  82.4 13.0 %all_to_all.25 = bf16[8,64,128]{2,1,0:T(8,128)(2,1)S(1)} all-to-all(bf16[8,64,128]{2,1,0:T(8,128)(2,1)S(1)} %get-tuple-element.40), channel_id=1, replica_groups=mesh['xlo'=2,'core'=2,'y'=4,'xhi'=2,'z'=8] {'z'}, dimensions={0} | all-to-all | bytes 262144 | tf_op jit(solution)/shard_map/all_to_all | solution.py:361
  95.3 1.5 plane_copies.1
  96.9 0.7 copy-done.5
  97.6 0.7 copy-done.7
  98.3 7.7 %all-to-all-start.3 = ((bf16[16,512,128]{2,1,0:T(8,128)(2,1)}), bf16[16,512,128]{2,1,0:T(8,128)(2,1)S(1)}, u32[]{:S(2)}, u32[]{:S(2)}) async-start(bf16[16,512,128]{2,1,0:T(8,128)(2,1)} %plane_copies.1), calls=%async_computation.3 | async-start | bytes 4194304 | tf_op jit(solution)/shard_map/all_to_all | solution.py:336
  106.2 0.9 copy-done.6
  107.1 0.9 copy-done.8
  108.1 8.9 %frozen_values.1.frozen = f32[1536,256]{1,0:T(8,128)S(1)} custom-call(s32[3]{0:T(128)S(1)} %pad_add_fusion.place, bf16[768,4096]{1,0:T(8,128)(2,1)} %tokens.5, bf16[768,4096]{1,0:T(8,128)(2,1)} %collective-permute-done.12.sibling, bf16[8,4,64,128]{3,2,1,0:T(8,128)(2,1)} %constant_dynamic-update-slice_fusion.here, ...), custom_call_target="tpu_custom_call" | custom-call | flops 3221225472 | bytes 16777216 | tf_op jit(solution)/shard_map/frozen_values/pallas_call | solution.py:226
  117.0 1.2 copy-done
  118.2 14.1 %all-to-all-done.3 = bf16[16,512,128]{2,1,0:T(8,128)(2,1)S(1)} async-done(((bf16[16,512,128]{2,1,0:T(8,128)(2,1)}), bf16[16,512,128]{2,1,0:T(8,128)(2,1)S(1)}, u32[]{:S(2)}, u32[]{:S(2)}) %all-to-all-start.3) | async-done | bytes 2097184 | tf_op jit(solution)/shard_map/all_to_all | solution.py:336
  132.3 11.0 %score_sums.1 = f32[256,1,128]{2,1,0:T(1,128)} custom-call(bf16[768,4096]{1,0:T(8,128)(2,1)} %tokens.5, bf16[768,4096]{1,0:T(8,128)(2,1)} %collective-permute-done.12.sibling, bf16[2,4096,128]{2,1,0:T(8,128)(2,1)S(1)} %bitcast.17, f32[1536,256]{1,0:T(8,128)} %copy-done, f32[1,256]{1,0:T(1,128)S(1)} %bitcast.20), custom_call_target="tpu_custom_call" | custom-call | flops 3221225472 | bytes 16777216 | tf_op jit(solution)/shard_map/score_sums/pallas_call | solution.py:248
  143.7 10.4 %all-to-all-start.4 = ((f32[256,1,128]{2,1,0:T(1,128)}), f32[256,1,128]{2,1,0:T(1,128)S(1)}, u32[]{:S(2)}, u32[]{:S(2)}) async-start(f32[256,1,128]{2,1,0:T(1,128)} %score_sums.1), calls=%async_computation.4 | async-start | bytes 262144 | tf_op jit(solution)/shard_map/all_to_all | solution.py:433
  154.1 2.2 %collective-permute-start.14 = (f32[64,256]{1,0:T(8,128)S(1)}, f32[64,256]{1,0:T(8,128)S(1)}, u32[]{:S(2)}, u32[]{:S(2)}) collective-permute-start(f32[64,256]{1,0:T(8,128)S(1)} %maximum_select_fusion.1), channel_id=1, source_target_pairs={{0,64},{64,0},{1,65},{65,1},{2,66},{66,2},{3,67},{67,3},{4,68},{68... | collective-permute-start | bytes 196616 | tf_op jit(solution)/shard_map/ppermute | solution.py:423
  156.5 0.7 collective-permute-done.14
  157.2 0.8 multiply_add_fusion
  158.1 9.0 %all-to-all-done.4 = f32[256,1,128]{2,1,0:T(1,128)S(1)} async-done(((f32[256,1,128]{2,1,0:T(1,128)}), f32[256,1,128]{2,1,0:T(1,128)S(1)}, u32[]{:S(2)}, u32[]{:S(2)}) %all-to-all-start.4) | async-done | bytes 131104 | tf_op jit(solution)/shard_map/all_to_all | solution.py:433
  167.5 0.5 multiply_subtract_fusion
  (53 shorter events, 1.8 us)
Async XLA Ops:
  1.4 9.5 %collective-permute-start = (bf16[64,128]{1,0:T(8,128)(2,1)S(1)}, bf16[64,128]{1,0:T(8,128)(2,1)S(1)}, u32[]{:S(2)}, u32[]{:S(2)}) collective-permute-start(bf16[64,128]{1,0:T(8,128)(2,1)S(1)} %dynamic-slice_convert_fusion), channel_id=1, source_target_pairs={{0,48},{16,0},{32,16},{48,32},{1,49},{17,1},{33,17},{49,33},{2,50}... | collective-permute-start | bytes 49160 | tf_op jit(solution)/shard_map/ppermute | solution.py:349
  10.9 7.4 %collective-permute-start.1 = (bf16[2,8,128,256]{3,2,1,0:T(8,128)(2,1)S(1)}, bf16[2,8,128,256]{3,2,1,0:T(8,128)(2,1)S(1)}, u32[]{:S(2)}, u32[]{:S(2)}) collective-permute-start(bf16[2,8,128,256]{3,2,1,0:T(8,128)(2,1)S(1)} %get-tuple-element.30), channel_id=1, source_target_pairs={{0,64},{64,0},{1,65},{65,1},{2,66},{66,2},{3,67},{67,3},{4,68},{68... | collective-permute-start | bytes 3145736 | tf_op jit(solution)/shard_map/ppermute | solution.py:382
  12.0 6.3 %collective-permute-start.2 = (bf16[2,64,128]{2,1,0:T(8,128)(2,1)S(1)}, bf16[2,64,128]{2,1,0:T(8,128)(2,1)S(1)}, u32[]{:S(2)}, u32[]{:S(2)}) collective-permute-start(bf16[2,64,128]{2,1,0:T(8,128)(2,1)S(1)} %pad_maximum_fusion.4), channel_id=1, source_target_pairs={{0,32},{16,48},{32,0},{48,16},{1,33},{17,49},{33,1},{49,17},{2,34}... | collective-permute-start | bytes 98312 | tf_op jit(solution)/shard_map/ppermute | solution.py:349
  18.4 2.7 %collective-permute-start.3 = (bf16[2,8,128,256]{3,2,1,0:T(8,128)(2,1)S(1)}, bf16[2,8,128,256]{3,2,1,0:T(8,128)(2,1)S(1)}, u32[]{:S(2)}, u32[]{:S(2)}) collective-permute-start(bf16[2,8,128,256]{3,2,1,0:T(8,128)(2,1)S(1)} %get-tuple-element.34), channel_id=1, source_target_pairs={{0,64},{64,0},{1,65},{65,1},{2,66},{66,2},{3,67},{67,3},{4,68},{68... | collective-permute-start | bytes 3145736 | tf_op jit(solution)/shard_map/ppermute | solution.py:386
  23.0 39.4 %all-to-all-start = ((bf16[16,128,512]{2,1,0:T(8,128)(2,1)}), bf16[16,128,512]{2,1,0:T(8,128)(2,1)S(1)}, u32[]{:S(2)}, u32[]{:S(2)}) async-start(bf16[16,128,512]{2,1,0:T(8,128)(2,1)} %bitcast.21), calls=%async_computation | async-start | bytes 4194304 | tf_op jit(solution)/shard_map/all_to_all | solution.py:336
  29.4 7.0 %collective-permute-start.4 = (bf16[1,4,64,128]{3,2,1,0:T(8,128)(2,1)S(1)}, bf16[1,4,64,128]{3,2,1,0:T(8,128)(2,1)S(1)}, u32[]{:S(2)}, u32[]{:S(2)}) collective-permute-start(bf16[1,4,64,128]{3,2,1,0:T(8,128)(2,1)S(1)} %bitcast.24), channel_id=1, source_target_pairs={{0,7},{1,0},{2,1},{3,2},{4,3},{5,4},{6,5},{7,6},{8,15},{9,8},{10,9... | collective-permute-start | bytes 196616 | tf_op jit(solution)/shard_map/ppermute | solution.py:349
  35.1 4.6 %collective-permute-start.5 = (bf16[1,4,64,128]{3,2,1,0:T(8,128)(2,1)S(1)}, bf16[1,4,64,128]{3,2,1,0:T(8,128)(2,1)S(1)}, u32[]{:S(2)}, u32[]{:S(2)}) collective-permute-start(bf16[1,4,64,128]{3,2,1,0:T(8,128)(2,1)S(1)} %bitcast.25), channel_id=1, source_target_pairs={{0,1},{1,2},{2,3},{3,4},{4,5},{5,6},{6,7},{7,0},{8,9},{9,10},{10,1... | collective-permute-start | bytes 196616 | tf_op jit(solution)/shard_map/ppermute | solution.py:349
  39.8 12.2 %collective-permute-start.6 = (bf16[3,4,64,128]{3,2,1,0:T(8,128)(2,1)S(1)}, bf16[3,4,64,128]{3,2,1,0:T(8,128)(2,1)S(1)}, u32[]{:S(2)}, u32[]{:S(2)}) collective-permute-start(bf16[3,4,64,128]{3,2,1,0:T(8,128)(2,1)S(1)} %pad_maximum_fusion.1), channel_id=1, source_target_pairs={{0,5},{1,6},{2,7},{3,0},{4,1},{5,2},{6,3},{7,4},{8,13},{9,14},{10,... | collective-permute-start | bytes 589832 | tf_op jit(solution)/shard_map/ppermute | solution.py:349
  40.3 12.4 %collective-permute-start.7 = (bf16[2,4,64,128]{3,2,1,0:T(8,128)(2,1)S(1)}, bf16[2,4,64,128]{3,2,1,0:T(8,128)(2,1)S(1)}, u32[]{:S(2)}, u32[]{:S(2)}) collective-permute-start(bf16[2,4,64,128]{3,2,1,0:T(8,128)(2,1)S(1)} %pad_maximum_fusion.2), channel_id=1, source_target_pairs={{0,3},{1,4},{2,5},{3,6},{4,7},{5,0},{6,1},{7,2},{8,11},{9,12},{10,... | collective-permute-start | bytes 393224 | tf_op jit(solution)/shard_map/ppermute | solution.py:349
  44.0 38.3 %copy-start.1 = (f32[64,512]{1,0:T(8,128)S(1)}, f32[64,512]{1,0:T(8,128)}, u32[]{:S(2)}) copy-start(f32[64,512]{1,0:T(8,128)} %policy.1) | copy-start | bytes 393220
  44.0 38.3 %copy-start.2 = (f32[64,512]{1,0:T(8,128)S(1)}, f32[64,512]{1,0:T(8,128)}, u32[]{:S(2)}) copy-start(f32[64,512]{1,0:T(8,128)} %moment.1) | copy-start | bytes 393220
  44.0 38.3 %copy-start.3 = (f32[64,512]{1,0:T(8,128)S(1)}, f32[64,512]{1,0:T(8,128)}, u32[]{:S(2)}) copy-start(f32[64,512]{1,0:T(8,128)} %second.1) | copy-start | bytes 393220
  62.4 36.0 %collective-permute-start.12 = (bf16[768,4096]{1,0:T(8,128)(2,1)}, bf16[768,4096]{1,0:T(8,128)(2,1)}, u32[]{:S(2)}, u32[]{:S(2)}) collective-permute-start(bf16[768,4096]{1,0:T(8,128)(2,1)} %tokens.5), channel_id=1, source_target_pairs={{0,64},{64,0},{1,65},{65,1},{2,66},{66,2},{3,67},{67,3},{4,68},{68... | collective-permute-start | bytes 18874376 | tf_op jit(solution)/shard_map/ppermute | solution.py:398
  63.9 13.8 %collective-permute-start.10 = (bf16[8,4,64,128]{3,2,1,0:T(8,128)(2,1)}, bf16[8,4,64,128]{3,2,1,0:T(8,128)(2,1)S(1)}, u32[]{:S(2)}, u32[]{:S(2)}) collective-permute-start(bf16[8,4,64,128]{3,2,1,0:T(8,128)(2,1)} %constant_dynamic-update-slice_fusion.here), channel_id=1, source_target_pairs={{0,136},{128,0},{8,128},{136,8},{1,137},{129,1},{9,129},{137,9},{2... | collective-permute-start | bytes 1572872 | tf_op jit(solution)/shard_map/ppermute | solution.py:343
  63.9 15.3 %collective-permute-start.8 = (bf16[8,4,64,128]{3,2,1,0:T(8,128)(2,1)}, bf16[8,4,64,128]{3,2,1,0:T(8,128)(2,1)S(1)}, u32[]{:S(2)}, u32[]{:S(2)}) collective-permute-start(bf16[8,4,64,128]{3,2,1,0:T(8,128)(2,1)} %constant_dynamic-update-slice_fusion.here), channel_id=1, source_target_pairs={{0,128},{128,8},{8,136},{136,0},{1,129},{129,9},{9,137},{137,1},{2... | collective-permute-start | bytes 1572872 | tf_op jit(solution)/shard_map/ppermute | solution.py:343
  65.7 0.7 copy-start.4
  66.3 16.0 %all-to-all-start.1 = ((bf16[8,64,128]{2,1,0:T(8,128)(2,1)}), bf16[8,64,128]{2,1,0:T(8,128)(2,1)S(1)}, u32[]{:S(2)}, u32[]{:S(2)}) async-start(bf16[8,64,128]{2,1,0:T(8,128)(2,1)} %bitcast.18), calls=%async_computation.1 | async-start | bytes 262144 | tf_op jit(solution)/shard_map/all_to_all | solution.py:361
  77.7 19.2 %collective-permute-start.11 = (bf16[4,4,64,128]{3,2,1,0:T(8,128)(2,1)S(1)}, bf16[4,4,64,128]{3,2,1,0:T(8,128)(2,1)S(1)}, u32[]{:S(2)}, u32[]{:S(2)}) collective-permute-start(bf16[4,4,64,128]{3,2,1,0:T(8,128)(2,1)S(1)} %slice.25), channel_id=1, source_target_pairs={{0,136},{128,0},{8,128},{136,8},{1,137},{129,1},{9,129},{137,9},{2... | collective-permute-start | bytes 786440 | tf_op jit(solution)/shard_map/ppermute | solution.py:343
  79.2 18.4 %collective-permute-start.9 = (bf16[4,4,64,128]{3,2,1,0:T(8,128)(2,1)S(1)}, bf16[4,4,64,128]{3,2,1,0:T(8,128)(2,1)S(1)}, u32[]{:S(2)}, u32[]{:S(2)}) collective-permute-start(bf16[4,4,64,128]{3,2,1,0:T(8,128)(2,1)S(1)} %slice.24), channel_id=1, source_target_pairs={{0,128},{128,8},{8,136},{136,0},{1,129},{129,9},{9,137},{137,1},{2... | collective-permute-start | bytes 786440 | tf_op jit(solution)/shard_map/ppermute | solution.py:343
  82.4 13.0 %copy-start.9 = (f32[64,128]{1,0:T(8,128)}, f32[64,128]{1,0:T(8,128)S(1)}, u32[]{:S(2)}) copy-start(f32[64,128]{1,0:T(8,128)S(1)} %get-tuple-element.47) | copy-start | bytes 98308
  96.9 9.1 %copy-start.13 = (f32[512]{0:T(512)S(1)}, f32[512]{0:T(512)}, u32[]{:S(2)}) copy-start(f32[512]{0:T(512)} %param.15) | copy-start | bytes 6148
  96.9 0.7 copy-start.5
  97.6 0.7 copy-start.7
  98.3 34.0 %all-to-all-start.3 = ((bf16[16,512,128]{2,1,0:T(8,128)(2,1)}), bf16[16,512,128]{2,1,0:T(8,128)(2,1)S(1)}, u32[]{:S(2)}, u32[]{:S(2)}) async-start(bf16[16,512,128]{2,1,0:T(8,128)(2,1)} %plane_copies.1), calls=%async_computation.3 | async-start | bytes 4194304 | tf_op jit(solution)/shard_map/all_to_all | solution.py:336
  106.2 1.0 copy-start.6
  107.1 0.9 copy-start.8
  117.0 1.2 copy-start
  132.3 11.1 %copy-start.10 = (f32[64,128]{1,0:T(8,128)S(1)}, f32[64,128]{1,0:T(8,128)}, u32[]{:S(2)}) copy-start(f32[64,128]{1,0:T(8,128)} %copy-done.9) | copy-start | bytes 98308
  132.3 24.0 %copy-start.12 = (s32[2,2]{1,0:T(2,128)S(1)}, s32[2,2]{1,0:T(2,128)}, u32[]{:S(2)}) copy-start(s32[2,2]{1,0:T(2,128)} %param.16) | copy-start | bytes 52
  132.3 24.9 %copy-start.11 = (f32[64,512]{1,0:T(8,128)S(1)}, f32[64,512]{1,0:T(8,128)}, u32[]{:S(2)}) copy-start(f32[64,512]{1,0:T(8,128)} %param.12) | copy-start | bytes 393220
  143.4 24.2 %copy-start.14 = (s32[2]{0:T(128)S(1)}, s32[2]{0:T(128)}, u32[]{:S(2)}) copy-start(s32[2]{0:T(128)} %param.17) | copy-start | bytes 28
  143.4 10.7 %collective-permute-start.13 = (f32[64,128]{1,0:T(8,128)S(1)}, f32[64,128]{1,0:T(8,128)S(1)}, u32[]{:S(2)}, u32[]{:S(2)}) collective-permute-start(f32[64,128]{1,0:T(8,128)S(1)} %copy-done.10), channel_id=1, source_target_pairs={{0,128},{128,0},{1,129},{129,1},{2,130},{130,2},{3,131},{131,3},{4... | collective-permute-start | bytes 98312 | tf_op jit(solution)/shard_map/ppermute | solution.py:417
  143.7 23.4 %all-to-all-start.4 = ((f32[256,1,128]{2,1,0:T(1,128)}), f32[256,1,128]{2,1,0:T(1,128)S(1)}, u32[]{:S(2)}, u32[]{:S(2)}) async-start(f32[256,1,128]{2,1,0:T(1,128)} %score_sums.1), calls=%async_computation.4 | async-start | bytes 262144 | tf_op jit(solution)/shard_map/all_to_all | solution.py:433
  154.1 3.1 %collective-permute-start.14 = (f32[64,256]{1,0:T(8,128)S(1)}, f32[64,256]{1,0:T(8,128)S(1)}, u32[]{:S(2)}, u32[]{:S(2)}) collective-permute-start(f32[64,256]{1,0:T(8,128)S(1)} %maximum_select_fusion.1), channel_id=1, source_target_pairs={{0,64},{64,0},{1,65},{65,1},{2,66},{66,2},{3,67},{67,3},{4,68},{68... | collective-permute-start | bytes 196616 | tf_op jit(solution)/shard_map/ppermute | solution.py:423

commit v11 on v7

--- a/solution.py
+++ b/solution.py
@@ -171,7 +171,7 @@
 def score_kernel(tokens, sibling, halves, frozen, readout, out, joined, held, still, sems):
     quarter = halves.shape[-1]
     count = tokens.shape[0]
-    sizes = (LEN,) * 8
+    sizes = (2 * LEN,) * 4
     loads, at = [], 0
     for step, size in enumerate(sizes):
         source, first = (tokens, at) if at < count else (sibling, at - count)
@@ -185,7 +185,7 @@
             )
         )
         at += size
-    for pair in loads[:AHEAD]:
+    for pair in loads[:2]:
         for load in pair:
             load.start()
     joined[:, :quarter] = halves[0]
@@ -197,7 +197,7 @@
     for step, size in enumerate(sizes):
         for load in loads[step]:
             load.wait()
-        for load in loads[step + AHEAD] if step + AHEAD < len(sizes) else ():
+        for load in loads[step + 2] if step + 2 < len(sizes) else ():
             load.start()
         values = jnp.dot(held[at : at + size], joined[...], preferred_element_type=jnp.float32)
         blended = blend_rate * values + (1.0 - blend_rate) * still[at : at + size]
@@ -257,7 +257,7 @@
             pltpu.VMEM((features, width), jnp.bfloat16),
             pltpu.VMEM((2 * count, features), tokens.dtype),
             pltpu.VMEM(frozen.shape, frozen.dtype),
-            pltpu.SemaphoreType.DMA((16,)),
+            pltpu.SemaphoreType.DMA((8,)),
         ],
         cost_estimate=pl.CostEstimate(
             flops=4 * count * features * width, bytes_accessed=16 << 20, transcendentals=0

time: 157 us -> 156 us (level)
  no operation moved by 1% of the time
where the time goes in v11:
time: 156 us
  starting transfers between devices  57.5 us (37%)
  waiting for transfers between devices  53.9 us (35%)
  Pallas kernels  27.3 us (18%)
  local copies, waits for them, and re-layouts  10.1 us (6%)
  other arithmetic  6.15 us (4%)
    ppermute x6, waiting for transfers between devices, shift_ring(): lax.ppermute(block, axis, [(i, (i - shift) % size) for i in range(size)])  15.5 us
    all_to_all x2, waiting for transfers between devices, to_plane(): return lax.all_to_all(blocks, PLANE, 0, 0, tiled=True)  15 us
    all_to_all x2, starting transfers between devices, along_z(): return lax.all_to_all(blocks, 'z', 0, 0, tiled=True)  14.5 us
    ppermute x6, starting transfers between devices, shift_ring(): lax.ppermute(block, axis, [(i, (i - shift) % size) for i in range(size)])  13 us
    pallas_call x1, Pallas kernels, score_sums(): pl.pallas_call(score_kernel, out_shape=jax.ShapeDtypeStruct((256, 1, 128)...  11 us
    all_to_all x1, waiting for transfers between devices, shards(): parts = lax.all_to_all(parts, AXES, 0, 0, tiled=True)  11 us
    all_to_all x1, starting transfers between devices, shards(): parts = lax.all_to_all(parts, AXES, 0, 0, tiled=True)  9.15 us
    pallas_call x1, Pallas kernels, frozen_values(): pl.pallas_call(frozen_kernel, grid_spec=pltpu.PrefetchScalarGridSpec(num_...  8.91 us
  transfers between devices with their start and end apart: 19, of which 11 were waited for; matrix products, arithmetic and copies ran while one was open for 4% of the time, Pallas kernels for 18%

profile of v11, /device:TPU:1, one launch (start us, length us, event | category | flops | bytes accessed | tf_op | source)
XLA Modules:
  0.0 155.8 jit_solution(6356044113302314915)
XLA Ops:
  0.6 0.8 dynamic-slice_convert_fusion
  1.4 3.6 %collective-permute-start = (bf16[64,128]{1,0:T(8,128)(2,1)S(1)}, bf16[64,128]{1,0:T(8,128)(2,1)S(1)}, u32[]{:S(2)}, u32[]{:S(2)}) collective-permute-start(bf16[64,128]{1,0:T(8,128)(2,1)S(1)} %dynamic-slice_convert_fusion), channel_id=1, source_target_pairs={{0,48},{16,0},{32,16},{48,32},{1,49},{17,1},{33,17},{49,33},{2,50}... | collective-permute-start | bytes 49160 | tf_op jit(solution)/shard_map/ppermute | solution.py:327
  5.0 6.3 %gradient_blocks.1 = (bf16[2,8,128,512]{3,2,1,0:T(8,128)(2,1)S(1)}, bf16[2,8,128,512]{3,2,1,0:T(8,128)(2,1)S(1)}) custom-call(s32[1]{0:T(128)} %bitcast.1.place, bf16[768,512]{1,0:T(8,128)(2,1)} %cotangent.1, bf16[768,4096]{1,0:T(8,128)(2,1)} %tokens.3), custom_call_target="tpu_custom_call" | custom-call | flops 3221225472 | bytes 12582912 | tf_op jit(solution)/shard_map/gradient_blocks/pallas_call | solution.py:114
  11.3 1.0 collective-permute-start.1
  12.4 0.4 collective-permute-start.2
  12.7 3.9 %collective-permute-done.2 = bf16[2,64,128]{2,1,0:T(8,128)(2,1)S(1)} collective-permute-done((bf16[2,64,128]{2,1,0:T(8,128)(2,1)S(1)}, bf16[2,64,128]{2,1,0:T(8,128)(2,1)S(1)}, u32[]{:S(2)}, u32[]{:S(2)}) %collective-permute-start.2) | collective-permute-done | bytes 32800 | tf_op jit(solution)/shard_map/ppermute | solution.py:327
  16.7 2.0 %add_convert_fusion = bf16[2,8,128,512]{3,2,1,0:T(8,128)(2,1)} fusion(bf16[2,8,128,512]{3,2,1,0:T(8,128)(2,1)S(1)} %collective-permute-done.1, bf16[2,8,128,512]{3,2,1,0:T(8,128)(2,1)S(1)} %get-tuple-element.21), kind=kLoop, calls=%fused_computation | loop fusion | flops 4194304 | bytes 6291456 | tf_op jit(solution)/shard_map/convert_element_type | solution.py:366
  18.7 4.3 %all-to-all-start = ((bf16[16,128,512]{2,1,0:T(8,128)(2,1)}), bf16[16,128,512]{2,1,0:T(8,128)(2,1)S(1)}, u32[]{:S(2)}, u32[]{:S(2)}) async-start(bf16[16,128,512]{2,1,0:T(8,128)(2,1)} %bitcast.20), calls=%async_computation | async-start | bytes 4194304 | tf_op jit(solution)/shard_map/all_to_all | solution.py:314
  23.0 5.6 %collective-permute-start.3 = (bf16[1,4,64,128]{3,2,1,0:T(8,128)(2,1)S(1)}, bf16[1,4,64,128]{3,2,1,0:T(8,128)(2,1)S(1)}, u32[]{:S(2)}, u32[]{:S(2)}) collective-permute-start(bf16[1,4,64,128]{3,2,1,0:T(8,128)(2,1)S(1)} %bitcast.23), channel_id=1, source_target_pairs={{0,7},{1,0},{2,1},{3,2},{4,3},{5,4},{6,5},{7,6},{8,15},{9,8},{10,9... | collective-permute-start | bytes 196616 | tf_op jit(solution)/shard_map/ppermute | solution.py:327
  28.6 0.6 constant_dynamic-update-slice_fusion.4
  29.2 0.7 collective-permute-done.3
  30.0 3.3 %collective-permute-done.4 = bf16[1,4,64,128]{3,2,1,0:T(8,128)(2,1)S(1)} collective-permute-done((bf16[1,4,64,128]{3,2,1,0:T(8,128)(2,1)S(1)}, bf16[1,4,64,128]{3,2,1,0:T(8,128)(2,1)S(1)}, u32[]{:S(2)}, u32[]{:S(2)}) %collective-permute-start.4) | collective-permute-done | bytes 65568 | tf_op jit(solution)/shard_map/ppermute | solution.py:327
  33.3 0.2 collective-permute-start.5
  33.5 3.2 %collective-permute-start.6 = (bf16[2,4,64,128]{3,2,1,0:T(8,128)(2,1)S(1)}, bf16[2,4,64,128]{3,2,1,0:T(8,128)(2,1)S(1)}, u32[]{:S(2)}, u32[]{:S(2)}) collective-permute-start(bf16[2,4,64,128]{3,2,1,0:T(8,128)(2,1)S(1)} %pad_maximum_fusion.1), channel_id=1, source_target_pairs={{0,3},{1,4},{2,5},{3,6},{4,7},{5,0},{6,1},{7,2},{8,11},{9,12},{10,... | collective-permute-start | bytes 393224 | tf_op jit(solution)/shard_map/ppermute | solution.py:327
  36.7 0.6 constant_dynamic-update-slice_fusion.3
  37.3 7.6 %collective-permute-done.5 = bf16[3,4,64,128]{3,2,1,0:T(8,128)(2,1)S(1)} collective-permute-done((bf16[3,4,64,128]{3,2,1,0:T(8,128)(2,1)S(1)}, bf16[3,4,64,128]{3,2,1,0:T(8,128)(2,1)S(1)}, u32[]{:S(2)}, u32[]{:S(2)}) %collective-permute-start.5) | collective-permute-done | bytes 196640 | tf_op jit(solution)/shard_map/ppermute | solution.py:327
  44.9 0.7 constant_dynamic-update-slice_fusion.2
  45.6 0.7 constant_dynamic-update-slice_fusion.1
  46.3 0.6 constant_dynamic-update-slice_fusion.here
  46.9 5.2 %all-to-all-done.blocks = bf16[16,128,512]{2,1,0:T(8,128)(2,1)S(1)} async-done(((bf16[16,128,512]{2,1,0:T(8,128)(2,1)}), bf16[16,128,512]{2,1,0:T(8,128)(2,1)S(1)}, u32[]{:S(2)}, u32[]{:S(2)}) %all-to-all-start) | async-done | bytes 2097184 | tf_op jit(solution)/shard_map/all_to_all | solution.py:314
  52.1 2.4 %collective-permute-start.11 = (bf16[768,4096]{1,0:T(8,128)(2,1)}, bf16[768,4096]{1,0:T(8,128)(2,1)}, u32[]{:S(2)}, u32[]{:S(2)}) collective-permute-start(bf16[768,4096]{1,0:T(8,128)(2,1)} %tokens.3), channel_id=1, source_target_pairs={{0,64},{64,0},{1,65},{65,1},{2,66},{66,2},{3,67},{67,3},{4,68},{68... | collective-permute-start | bytes 18874376 | tf_op jit(solution)/shard_map/ppermute | solution.py:370
  54.5 2.3 %collective-permute-start.9 = (bf16[8,4,64,128]{3,2,1,0:T(8,128)(2,1)}, bf16[8,4,64,128]{3,2,1,0:T(8,128)(2,1)S(1)}, u32[]{:S(2)}, u32[]{:S(2)}) collective-permute-start(bf16[8,4,64,128]{3,2,1,0:T(8,128)(2,1)} %constant_dynamic-update-slice_fusion.here), channel_id=1, source_target_pairs={{0,136},{128,0},{8,128},{136,8},{1,137},{129,1},{9,129},{137,9},{2... | collective-permute-start | bytes 1572872 | tf_op jit(solution)/shard_map/ppermute | solution.py:321
  56.8 0.3 plane_sum.1
  57.2 0.6 copy-done.4
  57.8 8.2 %all-to-all-start.1 = ((bf16[8,64,128]{2,1,0:T(8,128)(2,1)}), bf16[8,64,128]{2,1,0:T(8,128)(2,1)S(1)}, u32[]{:S(2)}, u32[]{:S(2)}) async-start(bf16[8,64,128]{2,1,0:T(8,128)(2,1)} %bitcast.18), calls=%async_computation.1 | async-start | bytes 262144 | tf_op jit(solution)/shard_map/all_to_all | solution.py:339
  66.0 2.5 %collective-permute-done.9.right = bf16[8,4,64,128]{3,2,1,0:T(8,128)(2,1)S(1)} collective-permute-done((bf16[8,4,64,128]{3,2,1,0:T(8,128)(2,1)}, bf16[8,4,64,128]{3,2,1,0:T(8,128)(2,1)S(1)}, u32[]{:S(2)}, u32[]{:S(2)}) %collective-permute-start.9) | collective-permute-done | bytes 524320 | tf_op jit(solution)/shard_map/ppermute | solution.py:321
  68.5 3.6 %collective-permute-start.10 = (bf16[4,4,64,128]{3,2,1,0:T(8,128)(2,1)S(1)}, bf16[4,4,64,128]{3,2,1,0:T(8,128)(2,1)S(1)}, u32[]{:S(2)}, u32[]{:S(2)}) collective-permute-start(bf16[4,4,64,128]{3,2,1,0:T(8,128)(2,1)S(1)} %slice.25), channel_id=1, source_target_pairs={{0,136},{128,0},{8,128},{136,8},{1,137},{129,1},{9,129},{137,9},{2... | collective-permute-start | bytes 786440 | tf_op jit(solution)/shard_map/ppermute | solution.py:321
  72.2 1.9 %all-to-all-done.1.column = bf16[8,64,128]{2,1,0:T(8,128)(2,1)S(1)} async-done(((bf16[8,64,128]{2,1,0:T(8,128)(2,1)}), bf16[8,64,128]{2,1,0:T(8,128)(2,1)S(1)}, u32[]{:S(2)}, u32[]{:S(2)}) %all-to-all-start.1) | async-done | bytes 131104 | tf_op jit(solution)/shard_map/all_to_all | solution.py:339
  74.1 0.7 policy_message.1
  74.8 6.3 %all-to-all-start.2 = ((bf16[8,64,128]{2,1,0:T(8,128)(2,1)}), bf16[8,64,128]{2,1,0:T(8,128)(2,1)S(1)}, u32[]{:S(2)}, u32[]{:S(2)}) async-start(bf16[8,64,128]{2,1,0:T(8,128)(2,1)} %get-tuple-element.29), calls=%async_computation.2 | async-start | bytes 262144 | tf_op jit(solution)/shard_map/all_to_all | solution.py:339
  81.1 2.9 %collective-permute-done.12 = f32[64,128]{1,0:T(8,128)} collective-permute-done((f32[64,128]{1,0:T(8,128)S(1)}, f32[64,128]{1,0:T(8,128)}, u32[]{:S(2)}, u32[]{:S(2)}) %collective-permute-start.12) | collective-permute-done | bytes 32800 | tf_op jit(solution)/shard_map/ppermute | solution.py:378
  84.0 5.2 %all-to-all-done.2 = bf16[8,64,128]{2,1,0:T(8,128)(2,1)S(1)} async-done(((bf16[8,64,128]{2,1,0:T(8,128)(2,1)}), bf16[8,64,128]{2,1,0:T(8,128)(2,1)S(1)}, u32[]{:S(2)}, u32[]{:S(2)}) %all-to-all-start.2) | async-done | bytes 131104 | tf_op jit(solution)/shard_map/all_to_all | solution.py:339
  89.2 1.8 %broadcast_in_dim.43 = bf16[16,512,128]{2,1,0:T(8,128)(2,1)} broadcast(bf16[512,128]{1,0:T(8,128)(2,1)S(1)} %bitcast.27), dimensions={1,2} | broadcast | bytes 2228224 | tf_op jit(solution)/shard_map/broadcast_in_dim | solution.py:354
  91.0 4.2 %all-to-all-start.3 = ((bf16[16,512,128]{2,1,0:T(8,128)(2,1)}), bf16[16,512,128]{2,1,0:T(8,128)(2,1)S(1)}, u32[]{:S(2)}, u32[]{:S(2)}) async-start(bf16[16,512,128]{2,1,0:T(8,128)(2,1)} %broadcast_in_dim.43), calls=%async_computation.3 | async-start | bytes 4194304 | tf_op jit(solution)/shard_map/all_to_all | solution.py:314
  95.3 1.5 maximum_select_fusion.1
  96.8 2.9 %collective-permute-start.13 = (f32[64,256]{1,0:T(8,128)}, f32[64,256]{1,0:T(8,128)}, u32[]{:S(2)}, u32[]{:S(2)}) collective-permute-start(f32[64,256]{1,0:T(8,128)} %maximum_select_fusion.1), channel_id=1, source_target_pairs={{0,64},{64,0},{1,65},{65,1},{2,66},{66,2},{3,67},{67,3},{4,68},{68... | collective-permute-start | bytes 196616 | tf_op jit(solution)/shard_map/ppermute | solution.py:392
  99.7 0.9 copy-done.6
  100.7 0.9 copy-done.8
  101.6 8.9 %frozen_values.1.frozen = f32[1536,256]{1,0:T(8,128)S(1)} custom-call(s32[3]{0:T(128)S(1)} %pad_add_fusion.place, bf16[768,4096]{1,0:T(8,128)(2,1)} %tokens.3, bf16[768,4096]{1,0:T(8,128)(2,1)} %collective-permute-done.11.sibling, bf16[8,4,64,128]{3,2,1,0:T(8,128)(2,1)} %constant_dynamic-update-slice_fusion.here, ...), custom_call_target="tpu_custom_call" | custom-call | flops 3221225472 | bytes 16777216 | tf_op jit(solution)/shard_map/frozen_values/pallas_call | solution.py:224
  110.6 1.2 copy-done
  111.7 9.8 %all-to-all-done.3 = bf16[16,512,128]{2,1,0:T(8,128)(2,1)S(1)} async-done(((bf16[16,512,128]{2,1,0:T(8,128)(2,1)}), bf16[16,512,128]{2,1,0:T(8,128)(2,1)S(1)}, u32[]{:S(2)}, u32[]{:S(2)}) %all-to-all-start.3) | async-done | bytes 2097184 | tf_op jit(solution)/shard_map/all_to_all | solution.py:314
  121.6 11.0 %score_sums.1 = f32[256,1,128]{2,1,0:T(1,128)} custom-call(bf16[768,4096]{1,0:T(8,128)(2,1)} %tokens.3, bf16[768,4096]{1,0:T(8,128)(2,1)} %collective-permute-done.11.sibling, bf16[2,4096,128]{2,1,0:T(8,128)(2,1)S(1)} %bitcast.17, f32[1536,256]{1,0:T(8,128)} %copy-done, f32[1,256]{1,0:T(1,128)S(1)} %bitcast.19), custom_call_target="tpu_custom_call" | custom-call | flops 3221225472 | bytes 16777216 | tf_op jit(solution)/shard_map/score_sums/pallas_call | solution.py:246
  132.6 9.2 %all-to-all-start.4 = ((f32[256,1,128]{2,1,0:T(1,128)}), f32[256,1,128]{2,1,0:T(1,128)S(1)}, u32[]{:S(2)}, u32[]{:S(2)}) async-start(f32[256,1,128]{2,1,0:T(1,128)} %score_sums.1), calls=%async_computation.4 | async-start | bytes 262144 | tf_op jit(solution)/shard_map/all_to_all | solution.py:404
  141.8 0.2 slice_reduce_fusion
  142.0 1.8 %multiply_add_fusion = (f32[64,512]{1,0:T(8,128)}, f32[64,512]{1,0:T(8,128)}, f32[64,512]{1,0:T(8,128)}, f32[64,512]{1,0:T(8,128)}) fusion(f32[64,512]{1,0:T(8,128)S(1)} %copy-done.10, f32[64,512]{1,0:T(8,128)S(1)} %copy-done.1, f32[64,256]{1,0:T(8,128)} %maximum_select_fusion.1, f32[64,256]{1,0:T(8,128)} %collective-permute-done.13, pred[]{:T(512)S(6)} %eq.39, ...), kind=kLoop, calls=%fused_computation.7 | loop fusion | flops 589824 | bytes 1179649 | tf_op jit(solution)/shard_map/add | solution.py:38
  143.8 11.0 %all-to-all-done.4 = f32[256,1,128]{2,1,0:T(1,128)S(1)} async-done(((f32[256,1,128]{2,1,0:T(1,128)}), f32[256,1,128]{2,1,0:T(1,128)S(1)}, u32[]{:S(2)}, u32[]{:S(2)}) %all-to-all-start.4) | async-done | bytes 131104 | tf_op jit(solution)/shard_map/all_to_all | solution.py:404
  155.0 0.2 fusion.2
  155.2 0.5 multiply_subtract_fusion
  (47 shorter events, 0.6 us)
Async XLA Ops:
  1.4 9.9 %collective-permute-start = (bf16[64,128]{1,0:T(8,128)(2,1)S(1)}, bf16[64,128]{1,0:T(8,128)(2,1)S(1)}, u32[]{:S(2)}, u32[]{:S(2)}) collective-permute-start(bf16[64,128]{1,0:T(8,128)(2,1)S(1)} %dynamic-slice_convert_fusion), channel_id=1, source_target_pairs={{0,48},{16,0},{32,16},{48,32},{1,49},{17,1},{33,17},{49,33},{2,50}... | collective-permute-start | bytes 49160 | tf_op jit(solution)/shard_map/ppermute | solution.py:327
  11.3 5.3 %collective-permute-start.1 = (bf16[2,8,128,512]{3,2,1,0:T(8,128)(2,1)S(1)}, bf16[2,8,128,512]{3,2,1,0:T(8,128)(2,1)S(1)}, u32[]{:S(2)}, u32[]{:S(2)}) collective-permute-start(bf16[2,8,128,512]{3,2,1,0:T(8,128)(2,1)S(1)} %get-tuple-element.23), channel_id=1, source_target_pairs={{0,64},{64,0},{1,65},{65,1},{2,66},{66,2},{3,67},{67,3},{4,68},{68... | collective-permute-start | bytes 6291464 | tf_op jit(solution)/shard_map/ppermute | solution.py:363
  12.4 4.3 %collective-permute-start.2 = (bf16[2,64,128]{2,1,0:T(8,128)(2,1)S(1)}, bf16[2,64,128]{2,1,0:T(8,128)(2,1)S(1)}, u32[]{:S(2)}, u32[]{:S(2)}) collective-permute-start(bf16[2,64,128]{2,1,0:T(8,128)(2,1)S(1)} %pad_maximum_fusion.3), channel_id=1, source_target_pairs={{0,32},{16,48},{32,0},{48,16},{1,33},{17,49},{33,1},{49,17},{2,34}... | collective-permute-start | bytes 98312 | tf_op jit(solution)/shard_map/ppermute | solution.py:327
  18.7 33.4 %all-to-all-start = ((bf16[16,128,512]{2,1,0:T(8,128)(2,1)}), bf16[16,128,512]{2,1,0:T(8,128)(2,1)S(1)}, u32[]{:S(2)}, u32[]{:S(2)}) async-start(bf16[16,128,512]{2,1,0:T(8,128)(2,1)} %bitcast.20), calls=%async_computation | async-start | bytes 4194304 | tf_op jit(solution)/shard_map/all_to_all | solution.py:314
  23.0 7.0 %collective-permute-start.3 = (bf16[1,4,64,128]{3,2,1,0:T(8,128)(2,1)S(1)}, bf16[1,4,64,128]{3,2,1,0:T(8,128)(2,1)S(1)}, u32[]{:S(2)}, u32[]{:S(2)}) collective-permute-start(bf16[1,4,64,128]{3,2,1,0:T(8,128)(2,1)S(1)} %bitcast.23), channel_id=1, source_target_pairs={{0,7},{1,0},{2,1},{3,2},{4,3},{5,4},{6,5},{7,6},{8,15},{9,8},{10,9... | collective-permute-start | bytes 196616 | tf_op jit(solution)/shard_map/ppermute | solution.py:327
  28.6 4.6 %collective-permute-start.4 = (bf16[1,4,64,128]{3,2,1,0:T(8,128)(2,1)S(1)}, bf16[1,4,64,128]{3,2,1,0:T(8,128)(2,1)S(1)}, u32[]{:S(2)}, u32[]{:S(2)}) collective-permute-start(bf16[1,4,64,128]{3,2,1,0:T(8,128)(2,1)S(1)} %bitcast.24), channel_id=1, source_target_pairs={{0,1},{1,2},{2,3},{3,4},{4,5},{5,6},{6,7},{7,0},{8,9},{9,10},{10,1... | collective-permute-start | bytes 196616 | tf_op jit(solution)/shard_map/ppermute | solution.py:327
  33.3 11.6 %collective-permute-start.5 = (bf16[3,4,64,128]{3,2,1,0:T(8,128)(2,1)S(1)}, bf16[3,4,64,128]{3,2,1,0:T(8,128)(2,1)S(1)}, u32[]{:S(2)}, u32[]{:S(2)}) collective-permute-start(bf16[3,4,64,128]{3,2,1,0:T(8,128)(2,1)S(1)} %pad_maximum_fusion), channel_id=1, source_target_pairs={{0,5},{1,6},{2,7},{3,0},{4,1},{5,2},{6,3},{7,4},{8,13},{9,14},{10,... | collective-permute-start | bytes 589832 | tf_op jit(solution)/shard_map/ppermute | solution.py:327
  33.5 12.1 %collective-permute-start.6 = (bf16[2,4,64,128]{3,2,1,0:T(8,128)(2,1)S(1)}, bf16[2,4,64,128]{3,2,1,0:T(8,128)(2,1)S(1)}, u32[]{:S(2)}, u32[]{:S(2)}) collective-permute-start(bf16[2,4,64,128]{3,2,1,0:T(8,128)(2,1)S(1)} %pad_maximum_fusion.1), channel_id=1, source_target_pairs={{0,3},{1,4},{2,5},{3,6},{4,7},{5,0},{6,1},{7,2},{8,11},{9,12},{10,... | collective-permute-start | bytes 393224 | tf_op jit(solution)/shard_map/ppermute | solution.py:327
  37.3 36.7 %copy-start.1 = (f32[64,512]{1,0:T(8,128)S(1)}, f32[64,512]{1,0:T(8,128)}, u32[]{:S(2)}) copy-start(f32[64,512]{1,0:T(8,128)} %policy.1) | copy-start | bytes 393220
  37.3 36.7 %copy-start.2 = (f32[64,512]{1,0:T(8,128)S(1)}, f32[64,512]{1,0:T(8,128)}, u32[]{:S(2)}) copy-start(f32[64,512]{1,0:T(8,128)} %moment.1) | copy-start | bytes 393220
  37.3 36.7 %copy-start.3 = (f32[64,512]{1,0:T(8,128)S(1)}, f32[64,512]{1,0:T(8,128)}, u32[]{:S(2)}) copy-start(f32[64,512]{1,0:T(8,128)} %second.1) | copy-start | bytes 393220
  52.1 37.1 %collective-permute-start.11 = (bf16[768,4096]{1,0:T(8,128)(2,1)}, bf16[768,4096]{1,0:T(8,128)(2,1)}, u32[]{:S(2)}, u32[]{:S(2)}) collective-permute-start(bf16[768,4096]{1,0:T(8,128)(2,1)} %tokens.3), channel_id=1, source_target_pairs={{0,64},{64,0},{1,65},{65,1},{2,66},{66,2},{3,67},{67,3},{4,68},{68... | collective-permute-start | bytes 18874376 | tf_op jit(solution)/shard_map/ppermute | solution.py:370
  54.5 13.9 %collective-permute-start.9 = (bf16[8,4,64,128]{3,2,1,0:T(8,128)(2,1)}, bf16[8,4,64,128]{3,2,1,0:T(8,128)(2,1)S(1)}, u32[]{:S(2)}, u32[]{:S(2)}) collective-permute-start(bf16[8,4,64,128]{3,2,1,0:T(8,128)(2,1)} %constant_dynamic-update-slice_fusion.here), channel_id=1, source_target_pairs={{0,136},{128,0},{8,128},{136,8},{1,137},{129,1},{9,129},{137,9},{2... | collective-permute-start | bytes 1572872 | tf_op jit(solution)/shard_map/ppermute | solution.py:321
  56.8 15.3 %collective-permute-start.7 = (bf16[8,4,64,128]{3,2,1,0:T(8,128)(2,1)}, bf16[8,4,64,128]{3,2,1,0:T(8,128)(2,1)S(1)}, u32[]{:S(2)}, u32[]{:S(2)}) collective-permute-start(bf16[8,4,64,128]{3,2,1,0:T(8,128)(2,1)} %constant_dynamic-update-slice_fusion.here), channel_id=1, source_target_pairs={{0,128},{128,8},{8,136},{136,0},{1,129},{129,9},{9,137},{137,1},{2... | collective-permute-start | bytes 1572872 | tf_op jit(solution)/shard_map/ppermute | solution.py:321
  57.1 0.7 copy-start.4
  57.8 16.2 %all-to-all-start.1 = ((bf16[8,64,128]{2,1,0:T(8,128)(2,1)}), bf16[8,64,128]{2,1,0:T(8,128)(2,1)S(1)}, u32[]{:S(2)}, u32[]{:S(2)}) async-start(bf16[8,64,128]{2,1,0:T(8,128)(2,1)} %bitcast.18), calls=%async_computation.1 | async-start | bytes 262144 | tf_op jit(solution)/shard_map/all_to_all | solution.py:339
  68.5 20.7 %collective-permute-start.10 = (bf16[4,4,64,128]{3,2,1,0:T(8,128)(2,1)S(1)}, bf16[4,4,64,128]{3,2,1,0:T(8,128)(2,1)S(1)}, u32[]{:S(2)}, u32[]{:S(2)}) collective-permute-start(bf16[4,4,64,128]{3,2,1,0:T(8,128)(2,1)S(1)} %slice.25), channel_id=1, source_target_pairs={{0,136},{128,0},{8,128},{136,8},{1,137},{129,1},{9,129},{137,9},{2... | collective-permute-start | bytes 786440 | tf_op jit(solution)/shard_map/ppermute | solution.py:321
  72.1 17.1 %collective-permute-start.8 = (bf16[4,4,64,128]{3,2,1,0:T(8,128)(2,1)S(1)}, bf16[4,4,64,128]{3,2,1,0:T(8,128)(2,1)S(1)}, u32[]{:S(2)}, u32[]{:S(2)}) collective-permute-start(bf16[4,4,64,128]{3,2,1,0:T(8,128)(2,1)S(1)} %slice.24), channel_id=1, source_target_pairs={{0,128},{128,8},{8,136},{136,0},{1,129},{129,9},{9,137},{137,1},{2... | collective-permute-start | bytes 786440 | tf_op jit(solution)/shard_map/ppermute | solution.py:321
  74.8 16.2 %copy-start.9 = (f32[64,128]{1,0:T(8,128)}, f32[64,128]{1,0:T(8,128)S(1)}, u32[]{:S(2)}) copy-start(f32[64,128]{1,0:T(8,128)S(1)} %get-tuple-element.28) | copy-start | bytes 98308
  74.8 14.4 %all-to-all-start.2 = ((bf16[8,64,128]{2,1,0:T(8,128)(2,1)}), bf16[8,64,128]{2,1,0:T(8,128)(2,1)S(1)}, u32[]{:S(2)}, u32[]{:S(2)}) async-start(bf16[8,64,128]{2,1,0:T(8,128)(2,1)} %get-tuple-element.29), calls=%async_computation.2 | async-start | bytes 262144 | tf_op jit(solution)/shard_map/all_to_all | solution.py:339
  81.1 2.9 %collective-permute-start.12 = (f32[64,128]{1,0:T(8,128)S(1)}, f32[64,128]{1,0:T(8,128)}, u32[]{:S(2)}, u32[]{:S(2)}) collective-permute-start(f32[64,128]{1,0:T(8,128)S(1)} %get-tuple-element.28), channel_id=1, source_target_pairs={{0,128},{128,0},{1,129},{129,1},{2,130},{130,2},{3,131},{131,3},{4... | collective-permute-start | bytes 98312 | tf_op jit(solution)/shard_map/ppermute | solution.py:378
  89.1 1.8 %copy-start.5 = (bf16[4,4,64,128]{3,2,1,0:T(8,128)(2,1)}, bf16[4,4,64,128]{3,2,1,0:T(8,128)(2,1)S(1)}, u32[]{:S(2)}) copy-start(bf16[4,4,64,128]{3,2,1,0:T(8,128)(2,1)S(1)} %collective-permute-done.10.far_right) | copy-start | bytes 786436
  89.2 1.8 %copy-start.7 = (bf16[4,4,64,128]{3,2,1,0:T(8,128)(2,1)}, bf16[4,4,64,128]{3,2,1,0:T(8,128)(2,1)S(1)}, u32[]{:S(2)}) copy-start(bf16[4,4,64,128]{3,2,1,0:T(8,128)(2,1)S(1)} %collective-permute-done.8.far_left) | copy-start | bytes 786436
  91.0 4.2 %copy-start.12 = (f32[512]{0:T(512)S(1)}, f32[512]{0:T(512)}, u32[]{:S(2)}) copy-start(f32[512]{0:T(512)} %param.15) | copy-start | bytes 6148
  91.0 30.6 %all-to-all-start.3 = ((bf16[16,512,128]{2,1,0:T(8,128)(2,1)}), bf16[16,512,128]{2,1,0:T(8,128)(2,1)S(1)}, u32[]{:S(2)}, u32[]{:S(2)}) async-start(bf16[16,512,128]{2,1,0:T(8,128)(2,1)} %broadcast_in_dim.43), calls=%async_computation.3 | async-start | bytes 4194304 | tf_op jit(solution)/shard_map/all_to_all | solution.py:314
  96.8 45.2 %collective-permute-start.13 = (f32[64,256]{1,0:T(8,128)}, f32[64,256]{1,0:T(8,128)}, u32[]{:S(2)}, u32[]{:S(2)}) collective-permute-start(f32[64,256]{1,0:T(8,128)} %maximum_select_fusion.1), channel_id=1, source_target_pairs={{0,64},{64,0},{1,65},{65,1},{2,66},{66,2},{3,67},{67,3},{4,68},{68... | collective-permute-start | bytes 196616 | tf_op jit(solution)/shard_map/ppermute | solution.py:392
  99.7 0.9 copy-start.6
  100.7 0.9 copy-start.8
  110.6 1.2 copy-start
  121.6 20.2 %copy-start.11 = (s32[2,2]{1,0:T(2,128)S(1)}, s32[2,2]{1,0:T(2,128)}, u32[]{:S(2)}) copy-start(s32[2,2]{1,0:T(2,128)} %param.16) | copy-start | bytes 52
  121.6 20.4 %copy-start.10 = (f32[64,512]{1,0:T(8,128)S(1)}, f32[64,512]{1,0:T(8,128)}, u32[]{:S(2)}) copy-start(f32[64,512]{1,0:T(8,128)} %param.12) | copy-start | bytes 393220
  132.6 22.6 %copy-start.13 = (s32[2]{0:T(128)S(1)}, s32[2]{0:T(128)}, u32[]{:S(2)}) copy-start(s32[2]{0:T(128)} %param.17) | copy-start | bytes 28
  132.6 22.2 %all-to-all-start.4 = ((f32[256,1,128]{2,1,0:T(1,128)}), f32[256,1,128]{2,1,0:T(1,128)S(1)}, u32[]{:S(2)}, u32[]{:S(2)}) async-start(f32[256,1,128]{2,1,0:T(1,128)} %score_sums.1), calls=%async_computation.4 | async-start | bytes 262144 | tf_op jit(solution)/shard_map/all_to_all | solution.py:404
